TPU v7x, 32 devices: a whole 2x2x4 slice. The times are simulated.
32 devices in a mesh: seq: 4 (over y, x), fsdp: 8 (over z, core).
Axes of the slice: x: 2, y: 2, z: 4, core: 2. Of those that a mesh axis runs over, the one named last changes fastest.
Arguments:
- tokens: bfloat16 [2, 4096, 2048], P(None, ('seq', 'fsdp')), may hold values from -6 to 6
- cotangent: bfloat16 [2, 4096, 2048], P(None, ('seq', 'fsdp')), may hold values from -6 to 6
- lengths: int32 [2, 4], replicated, may hold values from 1 to 2048, 4096 in all within a row
- gain_attn: bfloat16 [2048], P(('seq', 'fsdp')), may hold values from 0.5 to 1.5
- w_query: bfloat16 [2048, 2048], P(('seq', 'fsdp')), may hold values from -0.1875 to 0.1875
- w_key: bfloat16 [2048, 2048], P(('seq', 'fsdp')), may hold values from -0.1875 to 0.1875
- w_value: bfloat16 [2048, 2048], P(('seq', 'fsdp')), may hold values from -0.125 to 0.125
- w_out: bfloat16 [2048, 2048], P(('seq', 'fsdp')), may hold values from -0.75 to 0.75
- gain_mlp: bfloat16 [2048], P(('seq', 'fsdp')), may hold values from 0.5 to 1.5
- w_gate: bfloat16 [2048, 8192], P(('seq', 'fsdp')), may hold values from -0.125 to 0.125
- w_up: bfloat16 [2048, 8192], P(('seq', 'fsdp')), may hold values from -0.125 to 0.125
- w_down: bfloat16 [8192, 2048], P(('seq', 'fsdp')), may hold values from -0.125 to 0.125
Outputs:
- layer_out: bfloat16 [2, 4096, 2048], P(None, ('seq', 'fsdp'))
- input_grad: float32 [2, 4096, 2048], P(None, ('seq', 'fsdp'))
- gain_attn_grad: float32 [2048], P(('seq', 'fsdp'))
- w_query_grad: float32 [2048, 2048], P(('seq', 'fsdp'))
- w_key_grad: float32 [2048, 2048], P(('seq', 'fsdp'))
- w_value_grad: float32 [2048, 2048], P(('seq', 'fsdp'))
- w_out_grad: float32 [2048, 2048], P(('seq', 'fsdp'))
- gain_mlp_grad: float32 [2048], P(('seq', 'fsdp'))
- w_gate_grad: float32 [2048, 8192], P(('seq', 'fsdp'))
- w_up_grad: float32 [2048, 8192], P(('seq', 'fsdp'))
- w_down_grad: float32 [8192, 2048], P(('seq', 'fsdp'))
Inputs may be any that keep to these rules, and one draw needn't show every extreme that they name: Row r lists in order the lengths of the 4 documents packed into sequence r, which is sequence r % 1 of micro-batch r; each row sums to 4096 and its longest document has exactly 2048 tokens.
All inputs are finite; a program needn't handle non-finite values.
Results may differ from a plain program's by a relative error of at most 0.02.
Values may be sent and summed in bfloat16 or wider, within the bound.
A program may use at most 256 MiB of HBM per device.

v0:
```python
import jax
import jax.numpy as jnp
from jax import lax
from jax.sharding import PartitionSpec as P

HEAD = 64
FF = 8192
WINDOW = 1024


EPS = 1e-05


def passed_along(value, axis, steps):
    count = lax.axis_size(axis)
    leading, last = (max(0, -steps), min(count, count - steps))
    return lax.ppermute(value, axis, [(source, source + steps) for source in range(leading, last)])


def to_half(values):
    return values.astype(jnp.bfloat16)


def normalize(values, gain):
    return values * lax.rsqrt(jnp.mean(values * values, axis=-1, keepdims=True) + EPS) * gain


def contract_rows(left, right):
    return lax.dot_general(
        left, right, (((0,), (0,)), ((), ())), preferred_element_type=jnp.float32
    )


def contract_cols(left, right):
    return lax.dot_general(
        left, right, (((1,), (1,)), ((), ())), preferred_element_type=jnp.float32
    )


def doc_numbers(lengths, positions, batches, seq_len):
    table = lengths.reshape(batches, -1, lengths.shape[1])
    seq_count = table.shape[1]
    starts = jnp.cumsum(table, axis=2) - table
    valid = positions >= 0
    safe = jnp.maximum(positions, 0)
    which = safe // seq_len
    offset = safe % seq_len
    pick = which[:, None] == jnp.arange(seq_count, dtype=jnp.int32)[None, :]
    row_starts = jnp.sum(jnp.where(pick[None, :, :, None], starts[:, None, :, :], 0), axis=2)
    count = jnp.sum((row_starts[:, :, 1:] <= offset[None, :, None]).astype(jnp.int32), axis=2)
    batch_ids = jnp.arange(batches, dtype=jnp.int32)[:, None]
    number = (batch_ids * seq_count + which[None, :]) * lengths.shape[1] + count
    return jnp.where(valid[None, :], number, -1)


def gate_back(gate, up, d_hidden):
    sigma = jax.nn.sigmoid(gate)
    d_gate = d_hidden * up * sigma * (1.0 + gate * (1.0 - sigma))
    d_up = d_hidden * gate * sigma
    return (to_half(d_gate), to_half(d_up))


def body(
    tokens,
    cotangent,
    lengths,
    gain_attn,
    w_query,
    w_key,
    w_value,
    w_out,
    gain_mlp,
    w_gate,
    w_up,
    w_down,
):
    batches, piece, width = tokens.shape
    devices = lax.axis_size(("seq", "fsdp"))
    seq_len = piece * devices
    rows = batches * piece
    scale = HEAD ** (-0.5)
    seq_count = lax.axis_size("seq")
    group_count = lax.axis_size("fsdp")
    share = w_query.shape[0]
    inputs = tokens.astype(jnp.float32).reshape(rows, width)
    upstream = cotangent.astype(jnp.float32).reshape(rows, width)
    g_attn, g_mlp = (
        lax.all_gather(gain_attn, ("seq", "fsdp"), axis=0, tiled=True),
        lax.all_gather(gain_mlp, ("seq", "fsdp"), axis=0, tiled=True),
    )
    gain_one = g_attn.astype(jnp.float32)
    gain_two = g_mlp.astype(jnp.float32)
    normed_a = to_half(normalize(inputs, gain_one))
    span = width // group_count
    head_part = span // HEAD
    group_len = group_count * piece
    group_rows_all = batches * group_len
    qblock = min(512, group_len)
    qblocks = group_len // qblock
    group_start = lax.axis_index("seq") * group_len
    group_docs = doc_numbers(
        lengths, group_start + jnp.arange(group_len, dtype=jnp.int32), batches, seq_len
    )
    pad_docs = doc_numbers(
        lengths,
        group_start - WINDOW + jnp.arange(group_len + WINDOW, dtype=jnp.int32),
        batches,
        seq_len,
    )
    block_gap = (
        jnp.arange(qblock, dtype=jnp.int32)[:, None]
        - jnp.arange(qblock + WINDOW, dtype=jnp.int32)[None, :]
        + WINDOW
    )
    block_starts = jnp.arange(qblocks, dtype=jnp.int32) * qblock

    def head_weights():
        moved = (
            lax.all_to_all(
                w_query.reshape(share, group_count, span),
                "fsdp",
                split_axis=1,
                concat_axis=0,
                tiled=True,
            ),
            lax.all_to_all(
                w_key.reshape(share, group_count, span),
                "fsdp",
                split_axis=1,
                concat_axis=0,
                tiled=True,
            ),
            lax.all_to_all(
                w_value.reshape(share, group_count, span),
                "fsdp",
                split_axis=1,
                concat_axis=0,
                tiled=True,
            ),
            lax.all_to_all(
                w_out.reshape(share, group_count, span),
                "fsdp",
                split_axis=1,
                concat_axis=0,
                tiled=True,
            ),
        )
        flat = [item.reshape(group_count * share, span) for item in moved]
        return (
            lax.all_gather(flat[0], "seq", axis=0, tiled=True),
            lax.all_gather(flat[1], "seq", axis=0, tiled=True),
            lax.all_gather(flat[2], "seq", axis=0, tiled=True),
            lax.all_gather(flat[3], "seq", axis=0, tiled=True),
        )

    def block_parts(begin, query_g, key_pad, value_pad):
        q_four = lax.dynamic_slice_in_dim(query_g, begin, qblock, 1).reshape(
            batches, qblock, head_part, HEAD
        )
        k_four = lax.dynamic_slice_in_dim(key_pad, begin, qblock + WINDOW, 1).reshape(
            batches, qblock + WINDOW, head_part, HEAD
        )
        v_four = lax.dynamic_slice_in_dim(value_pad, begin, qblock + WINDOW, 1).reshape(
            batches, qblock + WINDOW, head_part, HEAD
        )
        q_docs = lax.dynamic_slice_in_dim(group_docs, begin, qblock, 1)
        k_docs = lax.dynamic_slice_in_dim(pad_docs, begin, qblock + WINDOW, 1)
        seen = (
            (q_docs[:, :, None] == k_docs[:, None, :])
            & (block_gap >= 0)[None]
            & (block_gap < WINDOW)[None]
        )[:, None]
        raw = (
            jnp.einsum("bqhd,bkhd->bhqk", q_four, k_four, preferred_element_type=jnp.float32)
            * scale
        )
        return (q_four, k_four, v_four, jnp.where(seen, raw, -1e30))

    wq_c, wk_c, wv_c, wo_c = head_weights()
    group_a = lax.all_gather(normed_a.reshape(batches, piece, width), "fsdp", axis=1, tiled=True)
    group_flat = group_a.reshape(group_rows_all, width)
    query_g = to_half(jnp.dot(group_flat, wq_c, preferred_element_type=jnp.float32)).reshape(
        batches, group_len, span
    )
    key_g = to_half(jnp.dot(group_flat, wk_c, preferred_element_type=jnp.float32)).reshape(
        batches, group_len, span
    )
    value_g = to_half(jnp.dot(group_flat, wv_c, preferred_element_type=jnp.float32)).reshape(
        batches, group_len, span
    )
    tail_key, tail_value = passed_along(
        (key_g[:, group_len - WINDOW :], value_g[:, group_len - WINDOW :]), "seq", 1
    )
    key_pad = jnp.concatenate([tail_key, key_g], axis=1)
    value_pad = jnp.concatenate([tail_value, value_g], axis=1)

    def forward_block(begin):
        q_four, k_four, v_four, masked = block_parts(begin, query_g, key_pad, value_pad)
        top = jnp.max(masked, axis=3, keepdims=True)
        expo = jnp.exp(masked - top)
        total = jnp.sum(expo, axis=3, keepdims=True)
        probs_low = to_half(expo / total)
        mixed = jnp.einsum("bhqk,bkhd->bqhd", probs_low, v_four, preferred_element_type=jnp.float32)
        return (to_half(mixed.reshape(batches, qblock, span)), top + jnp.log(total))

    att_blocks, log_totals = lax.map(forward_block, block_starts)
    attended_g = jnp.moveaxis(att_blocks, 0, 1).reshape(batches, group_len, span)
    attended_full = lax.all_gather(attended_g, "fsdp", axis=2, tiled=True).reshape(
        group_rows_all, width
    )
    out_cols = jnp.dot(attended_full, wo_c, preferred_element_type=jnp.float32).reshape(
        batches, group_len, span
    )
    branch = lax.all_to_all(out_cols, "fsdp", split_axis=1, concat_axis=2, tiled=True)
    middle = inputs + branch.reshape(rows, width)
    normed_b = to_half(normalize(middle, gain_two))
    d_mlp = to_half(upstream)
    row_share = w_gate.shape[0]
    block = FF // (seq_count * group_count)

    def unit_weights():
        moved = (
            lax.all_to_all(
                w_gate.reshape(row_share, seq_count, group_count, block),
                "fsdp",
                split_axis=2,
                concat_axis=0,
                tiled=True,
            ),
            lax.all_to_all(
                w_up.reshape(row_share, seq_count, group_count, block),
                "fsdp",
                split_axis=2,
                concat_axis=0,
                tiled=True,
            ),
        )
        gate_cols = moved[0].reshape(group_count * row_share, seq_count * block)
        up_cols = moved[1].reshape(group_count * row_share, seq_count * block)
        return (
            lax.all_gather(gate_cols, "seq", axis=0, tiled=True),
            lax.all_gather(up_cols, "seq", axis=0, tiled=True),
            lax.all_gather(w_down, "seq", axis=0, tiled=True),
        )

    def group_rows(values):
        return lax.all_gather(values, "fsdp", axis=0, tiled=True)

    def group_sums(values):
        return lax.psum_scatter(values, "fsdp", scatter_dimension=0, tiled=True)

    wg_part, wu_part, wd_part = unit_weights()
    group_b = group_rows(normed_b)
    gate = jnp.dot(group_b, wg_part, preferred_element_type=jnp.float32)
    up = jnp.dot(group_b, wu_part, preferred_element_type=jnp.float32)
    hidden = to_half(gate * jax.nn.sigmoid(gate) * up)
    outputs = middle + group_sums(jnp.dot(hidden, wd_part, preferred_element_type=jnp.float32))
    wg_part, wu_part, wd_part = unit_weights()
    group_d = group_rows(d_mlp)
    d_hidden = contract_cols(group_d, wd_part)
    d_gate, d_up = gate_back(gate, up, d_hidden)
    d_normed_b = group_sums(contract_cols(d_gate, wg_part) + contract_cols(d_up, wu_part))
    gate_sum, up_sum, w_down_grad = (
        lax.psum_scatter(
            contract_rows(group_b, d_gate).astype(jnp.bfloat16),
            "seq",
            scatter_dimension=0,
            tiled=True,
        ).astype(jnp.float32),
        lax.psum_scatter(
            contract_rows(group_b, d_up).astype(jnp.bfloat16),
            "seq",
            scatter_dimension=0,
            tiled=True,
        ).astype(jnp.float32),
        lax.psum_scatter(
            contract_rows(hidden, group_d).astype(jnp.bfloat16),
            "seq",
            scatter_dimension=0,
            tiled=True,
        ).astype(jnp.float32),
    )
    gate_back_cols, up_back_cols = (
        lax.all_to_all(
            gate_sum.reshape(group_count, row_share, seq_count, 1, block).astype(jnp.bfloat16),
            "fsdp",
            split_axis=0,
            concat_axis=3,
            tiled=True,
        ).astype(jnp.float32),
        lax.all_to_all(
            up_sum.reshape(group_count, row_share, seq_count, 1, block).astype(jnp.bfloat16),
            "fsdp",
            split_axis=0,
            concat_axis=3,
            tiled=True,
        ).astype(jnp.float32),
    )
    w_gate_grad = gate_back_cols.reshape(row_share, FF)
    w_up_grad = up_back_cols.reshape(row_share, FF)
    mlp_pull = jax.vjp(normalize, middle, gain_two)[1]
    d_middle_norm, gain_two_grad = mlp_pull(d_normed_b)
    d_middle = upstream + d_middle_norm
    d_branch = to_half(d_middle)
    wq_c, wk_c, wv_c, wo_c = head_weights()
    d_cols = lax.all_to_all(
        d_branch.reshape(batches, piece, width), "fsdp", split_axis=2, concat_axis=1, tiled=True
    )
    d_cols_flat = d_cols.reshape(group_rows_all, span)
    w_out_cols = contract_rows(attended_full, d_cols_flat)
    d_att_part = contract_cols(d_cols_flat, wo_c).reshape(batches, group_len, width)
    d_attended_g = to_half(lax.psum_scatter(d_att_part, "fsdp", scatter_dimension=2, tiled=True))

    def backward_block(carry, item):
        begin, log_total_blk = item
        key_acc, value_acc = carry
        q_four, k_four, v_four, masked = block_parts(begin, query_g, key_pad, value_pad)
        d_att = lax.dynamic_slice_in_dim(d_attended_g, begin, qblock, 1).reshape(
            batches, qblock, head_part, HEAD
        )
        d_probs = jnp.einsum("bqhd,bkhd->bhqk", d_att, v_four, preferred_element_type=jnp.float32)
        probs = jnp.exp(masked - log_total_blk)
        along = jnp.sum(probs * d_probs, axis=3, keepdims=True)
        d_scores = to_half(probs * (d_probs - along))
        d_query_blk = to_half(
            (
                jnp.einsum("bhqk,bkhd->bqhd", d_scores, k_four, preferred_element_type=jnp.float32)
                * scale
            ).reshape(batches, qblock, span)
        )
        d_key_blk = (
            jnp.einsum("bhqk,bqhd->bkhd", d_scores, q_four, preferred_element_type=jnp.float32)
            * scale
        ).reshape(batches, qblock + WINDOW, span)
        d_value_blk = jnp.einsum(
            "bhqk,bqhd->bkhd", to_half(probs), d_att, preferred_element_type=jnp.float32
        ).reshape(batches, qblock + WINDOW, span)
        key_acc = lax.dynamic_update_slice_in_dim(
            key_acc,
            lax.dynamic_slice_in_dim(key_acc, begin, qblock + WINDOW, 1) + d_key_blk,
            begin,
            1,
        )
        value_acc = lax.dynamic_update_slice_in_dim(
            value_acc,
            lax.dynamic_slice_in_dim(value_acc, begin, qblock + WINDOW, 1) + d_value_blk,
            begin,
            1,
        )
        return ((key_acc, value_acc), d_query_blk)

    empty = jnp.zeros((batches, group_len + WINDOW, span), jnp.float32)
    (key_acc, value_acc), dq_blocks = lax.scan(
        backward_block, (empty, empty), (block_starts, log_totals)
    )
    back_key, back_value = (
        passed_along(key_acc[:, :WINDOW].astype(jnp.bfloat16), "seq", -1).astype(jnp.float32),
        passed_along(value_acc[:, :WINDOW].astype(jnp.bfloat16), "seq", -1).astype(jnp.float32),
    )
    own_key = key_acc[:, WINDOW:]
    own_value = value_acc[:, WINDOW:]
    own_key = jnp.concatenate(
        [own_key[:, : group_len - WINDOW], own_key[:, group_len - WINDOW :] + back_key], axis=1
    )
    own_value = jnp.concatenate(
        [own_value[:, : group_len - WINDOW], own_value[:, group_len - WINDOW :] + back_value],
        axis=1,
    )
    d_key_g = to_half(own_key).reshape(group_rows_all, span)
    d_value_g = to_half(own_value).reshape(group_rows_all, span)
    d_query_g = jnp.moveaxis(dq_blocks, 0, 1).reshape(group_rows_all, span)
    wq_cols_grad = contract_rows(group_flat, d_query_g)
    wk_cols_grad = contract_rows(group_flat, d_key_g)
    wv_cols_grad = contract_rows(group_flat, d_value_g)
    d_part = (
        contract_cols(d_query_g, wq_c)
        + contract_cols(d_key_g, wk_c)
        + contract_cols(d_value_g, wv_c)
    ).reshape(batches, group_len, width)
    d_normed_a = (
        lax.psum_scatter(d_part.astype(jnp.bfloat16), "fsdp", scatter_dimension=1, tiled=True)
        .astype(jnp.float32)
        .reshape(rows, width)
    )
    attn_pull = jax.vjp(normalize, inputs, gain_one)[1]
    d_input_norm, gain_one_grad = attn_pull(d_normed_a)
    input_grad = (d_middle + d_input_norm).reshape(batches, piece, width)
    layer_out = to_half(outputs).reshape(batches, piece, width)
    summed_cols = (
        lax.psum_scatter(
            wq_cols_grad.astype(jnp.bfloat16), "seq", scatter_dimension=0, tiled=True
        ).astype(jnp.float32),
        lax.psum_scatter(
            wk_cols_grad.astype(jnp.bfloat16), "seq", scatter_dimension=0, tiled=True
        ).astype(jnp.float32),
        lax.psum_scatter(
            wv_cols_grad.astype(jnp.bfloat16), "seq", scatter_dimension=0, tiled=True
        ).astype(jnp.float32),
        lax.psum_scatter(
            w_out_cols.astype(jnp.bfloat16), "seq", scatter_dimension=0, tiled=True
        ).astype(jnp.float32),
    )
    returned = (
        lax.all_to_all(
            summed_cols[0].reshape(group_count, share, 1, span).astype(jnp.bfloat16),
            "fsdp",
            split_axis=0,
            concat_axis=2,
            tiled=True,
        ).astype(jnp.float32),
        lax.all_to_all(
            summed_cols[1].reshape(group_count, share, 1, span).astype(jnp.bfloat16),
            "fsdp",
            split_axis=0,
            concat_axis=2,
            tiled=True,
        ).astype(jnp.float32),
        lax.all_to_all(
            summed_cols[2].reshape(group_count, share, 1, span).astype(jnp.bfloat16),
            "fsdp",
            split_axis=0,
            concat_axis=2,
            tiled=True,
        ).astype(jnp.float32),
        lax.all_to_all(
            summed_cols[3].reshape(group_count, share, 1, span).astype(jnp.bfloat16),
            "fsdp",
            split_axis=0,
            concat_axis=2,
            tiled=True,
        ).astype(jnp.float32),
    )
    gain_sums = (
        lax.psum_scatter(gain_one_grad, ("seq", "fsdp"), scatter_dimension=0, tiled=True),
        lax.psum_scatter(gain_two_grad, ("seq", "fsdp"), scatter_dimension=0, tiled=True),
    )
    return (
        layer_out,
        input_grad,
        gain_sums[0],
        returned[0].reshape(share, width),
        returned[1].reshape(share, width),
        returned[2].reshape(share, width),
        returned[3].reshape(share, width),
        gain_sums[1],
        w_gate_grad,
        w_up_grad,
        w_down_grad,
    )


def solution(mesh):
    in_specs = (
        P(None, ("seq", "fsdp"), None),
        P(None, ("seq", "fsdp"), None),
        P(),
        P(("seq", "fsdp")),
        P(("seq", "fsdp"), None),
        P(("seq", "fsdp"), None),
        P(("seq", "fsdp"), None),
        P(("seq", "fsdp"), None),
        P(("seq", "fsdp")),
        P(("seq", "fsdp"), None),
        P(("seq", "fsdp"), None),
        P(("seq", "fsdp"), None),
    )
    out_specs = (
        P(None, ("seq", "fsdp"), None),
        P(None, ("seq", "fsdp"), None),
        P(("seq", "fsdp")),
        P(("seq", "fsdp"), None),
        P(("seq", "fsdp"), None),
        P(("seq", "fsdp"), None),
        P(("seq", "fsdp"), None),
        P(("seq", "fsdp")),
        P(("seq", "fsdp"), None),
        P(("seq", "fsdp"), None),
        P(("seq", "fsdp"), None),
    )
    return jax.shard_map(body, mesh=mesh, in_specs=in_specs, out_specs=out_specs, check_vma=False)
```

profile of v0, /device:TPU:9, one launch (start us, length us, event | category | flops | bytes accessed | tf_op | source)
XLA Modules:
  0.0 2050.2 jit_solution(8817122043817867746)
XLA Ops:
  9.0 40.1 %all-reduce.5 = (bf16[2048]{0:T(1024)(128)(2,1)S(1)}, bf16[2048]{0:T(1024)(128)(2,1)}) all-reduce(bf16[2048]{0:T(1024)(128)(2,1)S(1)} %dynamic-update-slice, bf16[2048]{0:T(1024)(128)(2,1)S(1)} %dynamic-update-slice.1), channel_id=1, replica_groups=mesh['seq'=4,'fsdp'=8] {'seq','fsdp'}, use_global_device_ids=true, to_apply=%add | all-reduce | flops 4096 | bytes 16384
  52.5 23.0 %all_to_all.204 = bf16[64,8,256]{2,0,1:T(8,128)(2,1)} all-to-all(bf16[64,8,256]{2,0,1:T(8,128)(2,1)S(1)} %bitcast.423), channel_id=1, replica_groups=mesh['seq'=4,'fsdp'=8] {'fsdp'}, dimensions={1} | all-to-all | bytes 524288 | tf_op jit(solution)/shard_map/all_to_all | solution.py:133
  84.2 19.2 all-to-all-done.2
  127.2 24.3 %all-gather.12.cloned.1.call-done = bf16[2,1024,2048]{1,2,0:T(8,128)(2,1)} async-done(((bf16[2,128,2048]{1,2,0:T(8,128)(2,1)}), bf16[2,1024,2048]{1,2,0:T(8,128)(2,1)}) %all-gather.12.cloned.1.call-update) | async-done | bytes 8388624 | tf_op jit(solution)/shard_map/all_gather | solution.py:180
  163.2 18.8 all-gather.14.cloned.1.call-done
  192.6 27.1 %all-gather.18.cloned.1.call-done = bf16[2048,256]{1,0:T(8,128)(2,1)} async-done(((bf16[512,256]{1,0:T(8,128)(2,1)}), bf16[2048,256]{1,0:T(8,128)(2,1)}) %all-gather.18.cloned.1.call-update) | async-done | bytes 1048592 | tf_op jit(solution)/shard_map/all_gather | solution.py:151
  231.0 26.1 %all-gather.16.cloned.1.call-done = bf16[2048,256]{1,0:T(8,128)(2,1)} async-done(((bf16[512,256]{1,0:T(8,128)(2,1)}), bf16[2048,256]{1,0:T(8,128)(2,1)}) %all-gather.16.cloned.1.call-update) | async-done | bytes 1048592 | tf_op jit(solution)/shard_map/all_gather | solution.py:150
  269.2 92.8 %while.30 = (s32[]{:T(128)}, bf16[2,2,512,256]{2,3,1,0:T(8,128)(2,1)}, f32[2,2,4,512,1]{3,2,1,4,0:T(4,128)S(1)}, s32[2]{0:T(128)S(1)}, bf16[2,2048,256]{1,2,0:T(...) while((s32[]{:T(128)}, ...), condition=%wide.region_7.8_spmd.clone.clone, body=%wide.region_4.7_spmd.clone.clone.sunk | while | flops 1694232576 | bytes 120766800 | solution.py:206
  366.2 60.4 %all_to_all.205 = bf16[64,4,8,256]{3,1,0,2:T(4,128)(2,1)S(1)} all-to-all(bf16[64,4,8,256]{3,1,0,2:T(4,128)(2,1)S(1)} %copy.205), channel_id=1, replica_groups=mesh['seq'=4,'fsdp'=8] {'fsdp'}, dimensions={2} | all-to-all | bytes 2097152 | tf_op jit(solution)/shard_map/all_to_all | solution.py:230
  427.9 41.0 %all-gather.20.cloned.1.call-done = bf16[2,1024,2048]{2,1,0:T(8,128)(2,1)} async-done(((bf16[2,1024,256]{2,1,0:T(8,128)(2,1)}), bf16[2,1024,2048]{2,1,0:T(8,128)(2,1)}) %all-gather.20.cloned.1.call-update) | async-done | bytes 8388624 | tf_op jit(solution)/shard_map/all_gather | solution.py:208
  484.6 43.8 %all-to-all-done.4 = f32[2,1024,256]{2,0,1:T(2,128)S(1)} async-done(((f32[2,1024,256]{2,0,1:T(2,128)}), f32[2,1024,256]{2,0,1:T(2,128)S(1)}, u32[]{:S(2)}, u32[]{:S(2)}) %all-to-all-start.4) | async-done | bytes 2097184 | tf_op jit(solution)/shard_map/all_to_all | solution.py:214
  535.7 55.0 %all_to_all.206 = bf16[64,4,8,256]{3,1,0,2:T(4,128)(2,1)S(1)} all-to-all(bf16[64,4,8,256]{3,1,0,2:T(4,128)(2,1)S(1)} %copy.204), channel_id=1, replica_groups=mesh['seq'=4,'fsdp'=8] {'fsdp'}, dimensions={2} | all-to-all | bytes 2097152 | tf_op jit(solution)/shard_map/all_to_all | solution.py:223
  593.5 38.9 %all-gather.24.cloned.1.call-done = bf16[2048,2048]{1,0:T(8,128)(2,1)} async-done(((bf16[256,2048]{1,0:T(8,128)(2,1)}), bf16[2048,2048]{1,0:T(8,128)(2,1)}) %all-gather.24.cloned.1.call-update) | async-done | bytes 8388624 | tf_op jit(solution)/shard_map/all_gather | solution.py:247
  646.8 43.1 %all-gather.26.cloned.1.call-done = bf16[2048,1024]{1,0:T(8,128)(2,1)} async-done(((bf16[512,1024]{1,0:T(8,128)(2,1)}), bf16[2048,1024]{1,0:T(8,128)(2,1)}) %all-gather.26.cloned.1.call-update) | async-done | bytes 4194320 | tf_op jit(solution)/shard_map/all_gather | solution.py:241
  704.3 40.0 %all-gather.30.cloned.1.call-done = bf16[1024,2048]{1,0:T(8,128)(2,1)} async-done(((bf16[256,2048]{1,0:T(8,128)(2,1)}), bf16[1024,2048]{1,0:T(8,128)(2,1)}) %all-gather.30.cloned.1.call-update) | async-done | bytes 4194320 | tf_op jit(solution)/shard_map/all_gather | solution.py:243
  744.3 81.5 %all-gather.32.cloned.1.call-done = bf16[2048,2048]{1,0:T(8,128)(2,1)} async-done(((bf16[256,2048]{1,0:T(8,128)(2,1)}), bf16[2048,2048]{1,0:T(8,128)(2,1)}) %all-gather.32.cloned.1.call-update) | async-done | bytes 8388624 | tf_op jit(solution)/shard_map/all_gather | solution.py:247
  825.7 23.0 %multiply_convert_fusion.1 = (bf16[2048,1024]{1,0:T(8,128)(2,1)}, bf16[2048,1024]{1,0:T(8,128)(2,1)}, bf16[2048,1024]{1,0:T(8,128)(2,1)}) fusion(f32[2048,1024]{1,0:T(8,128)} %fusion.52, f32[2048,1024]{1,0:T(8,128)} %fusion.53, bf16[2048,2048]{1,0:T(8,128)(2,1)} %all-gather.32.cloned.1.call-done, bf16[1024,2048]{1,0:T(8,128)(2,1)} %all-gather.30.cloned.1.call-done), kind=kOutput, calls=%fused_computation.47 | convolution fusion | flops 8623489024 | bytes 41943040 | tf_op jit(solution)/shard_map/dot_general | solution.py:35
  864.5 17.2 convolution_add_fusion
  881.8 167.6 %reduce-scatter.16.cloned.1.call-done = f32[256,2048]{1,0:T(8,128)} async-done(((f32[2048,2048]{1,0:T(8,128)}), f32[256,2048]{1,0:T(8,128)}) %reduce-scatter.16.cloned.1.call-update) | async-done | bytes 2097168 | tf_op jit(solution)/shard_map/reduce_scatter | solution.py:250
  1056.4 28.7 %all_to_all.207 = bf16[2,128,2048]{1,0,2:T(2,128)(2,1)S(1)} all-to-all(bf16[2,128,2048]{1,0,2:T(2,128)(2,1)S(1)} %copy.206), channel_id=1, replica_groups=mesh['seq'=4,'fsdp'=8] {'fsdp'}, dimensions={2} | all-to-all | bytes 2097152 | tf_op jit(solution)/shard_map/all_to_all | solution.py:306
  1129.5 132.6 %reduce-scatter.18.cloned.1.call-done = f32[2,1024,256]{2,1,0:T(8,128)} async-done(((f32[2,1024,2048]{2,1,0:T(8,128)}), f32[2,1024,256]{2,1,0:T(8,128)}) %reduce-scatter.18.cloned.1.call-update) | async-done | bytes 2097168 | tf_op jit(solution)/shard_map/reduce_scatter | solution.py:312
  1269.5 269.5 %while.31 = (s32[]{:T(128)}, f32[2,2048,256]{2,1,0:T(8,128)}, f32[2,2048,256]{2,1,0:T(8,128)}, bf16[2,2,512,256]{3,2,0,1:T(8,128)(2,1)}, s32[2]{0:T(128)S(1)}, /...) while((s32[]{:T(128)}, f32[2,2048,256]{2,1,0:T(8,128)}, ...), condition=%wide.region_15.16_spmd.clone.clone, body=%wide.region_13.15_spmd.clone.clone.sunk | while | flops 4093898752 | bytes 344064416 | solution.py:353
  1307.5 22.3 %multiply_reduce_fusion.7 = (f32[2,4,512]{2,1,0:T(4,128)S(1)}, f32[2,4,512,1536]{3,2,1,0:T(8,128)}) fusion(f32[2,4,512,1536]{3,2,1,0:T(8,128)} %fusion.148, f32[2,4,512]{2,1,0:T(4,128)S(1)} %dynamic-slice_bitcast_fusion.2, bf16[2,512,4,64]{1,3,2,0:T(8,128)(2,1)} %bitcast.376, bf16[2,1536,4,64]{1,3,2,0:T(8,128)(2,1)S(1)} %bitcast.370, ...), kind=kOutput, calls=%fused_computation.23.clone.1 | convolution fusion | flops 836759552 | bytes 54034432 | tf_op jit(solution)/shard_map/while/body/eval_jaxpr/bqhd,bkhd->bhqk/dot_general | solution.py:174
  1329.9 17.5 multiply_convert_fusion.7
  1443.2 22.2 %multiply_reduce_fusion.7 = (f32[2,4,512]{2,1,0:T(4,128)S(1)}, f32[2,4,512,1536]{3,2,1,0:T(8,128)}) fusion(f32[2,4,512,1536]{3,2,1,0:T(8,128)} %fusion.148, f32[2,4,512]{2,1,0:T(4,128)S(1)} %dynamic-slice_bitcast_fusion.2, bf16[2,512,4,64]{1,3,2,0:T(8,128)(2,1)} %bitcast.376, bf16[2,1536,4,64]{1,3,2,0:T(8,128)(2,1)S(1)} %bitcast.370, ...), kind=kOutput, calls=%fused_computation.23.clone.1 | convolution fusion | flops 836759552 | bytes 54034432 | tf_op jit(solution)/shard_map/while/body/eval_jaxpr/bqhd,bkhd->bhqk/dot_general | solution.py:174
  1567.6 27.6 %collective-permute-done.3 = bf16[2,1024,256]{2,1,0:T(8,128)(2,1)S(1)} collective-permute-done((bf16[2,1024,256]{2,1,0:T(8,128)(2,1)S(1)}, bf16[2,1024,256]{2,1,0:T(8,128)(2,1)S(1)}, u32[]{:S(2)}, u32[]{:S(2)}) %collective-permute-start.3) | collective-permute-done | bytes 1048608 | tf_op jit(solution)/shard_map/ppermute | solution.py:17
  1610.7 26.3 %collective-permute-done.2 = bf16[2,1024,256]{2,1,0:T(8,128)(2,1)} collective-permute-done((bf16[2,1024,256]{2,1,0:T(8,128)(2,1)}, bf16[2,1024,256]{2,1,0:T(8,128)(2,1)}, u32[]{:S(2)}, u32[]{:S(2)}) %collective-permute-start.2) | collective-permute-done | bytes 1048608 | tf_op jit(solution)/shard_map/ppermute | solution.py:17
  1725.1 37.0 %all-to-all-done.13 = bf16[8,64,4,1,256]{4,2,1,3,0:T(4,128)(2,1)S(1)} async-done(((bf16[8,64,4,1,256]{4,2,1,3,0:T(4,128)(2,1)}), bf16[8,64,4,1,256]{4,2,1,3,0:T(4,128)(2,1)S(1)}, u32[]{:S(2)}, u32[]{:S(2)}) %all-to-all-start.13) | async-done | bytes 1048608 | tf_op jit(solution)/shard_map/all_to_all | solution.py:291
  1762.1 46.2 %all_to_all.208 = bf16[8,64,4,1,256]{4,2,1,3,0:T(4,128)(2,1)S(1)} all-to-all(bf16[8,64,4,1,256]{4,2,1,3,0:T(4,128)(2,1)S(1)} %bitcast.401), channel_id=1, replica_groups=mesh['seq'=4,'fsdp'=8] {'fsdp'}, dimensions={0} | all-to-all | bytes 2097152 | tf_op jit(solution)/shard_map/all_to_all | solution.py:284
  1808.2 20.5 %all_to_all.209 = bf16[8,64,1,256]{3,1,2,0:T(8,128)(2,1)} all-to-all(bf16[8,64,1,256]{3,1,2,0:T(8,128)(2,1)} %bitcast.432), channel_id=1, replica_groups=mesh['seq'=4,'fsdp'=8] {'fsdp'}, dimensions={0} | all-to-all | bytes 524288 | tf_op jit(solution)/shard_map/all_to_all | solution.py:425
  1887.0 41.9 %all-reduce.4 = (f32[2048]{0:T(1024)S(1)}, f32[2048]{0:T(1024)S(1)}) all-reduce(f32[2048]{0:T(1024)S(1)} %get-tuple-element.372, f32[2048]{0:T(1024)S(1)} %copy-done.46), channel_id=6, replica_groups=mesh['seq'=4,'fsdp'=8] {'seq','fsdp'}, use_global_device_ids=true, to_apply=%region_19.20.clone | all-reduce | flops 4096 | bytes 32768
  1930.0 106.4 %reduce-scatter.14.cloned.1.call-done = f32[256,2048]{1,0:T(8,128)} async-done(((f32[2048,2048]{1,0:T(8,128)}), f32[256,2048]{1,0:T(8,128)}) %reduce-scatter.14.cloned.1.call-update) | async-done | bytes 2097168 | tf_op jit(solution)/shard_map/reduce_scatter | solution.py:250
  (401 shorter events, 701.4 us)
Async XLA Ops:
  7.2 144.3 %all-gather.12.cloned.1.call-start = ((), (), s32[]{:S(2)}) async-start(), calls=%async_computation.25 | async-start | bytes 9437184 | tf_op jit(solution)/shard_map/all_gather | solution.py:180
  52.4 129.6 %all-gather.14.cloned.1.call-start = ((), (), s32[]{:S(2)}) async-start(), calls=%async_computation.26 | async-start | bytes 1310720 | tf_op jit(solution)/shard_map/all_gather | solution.py:152
  76.3 27.1 %all-to-all-start.2 = ((bf16[64,8,256]{2,0,1:T(8,128)(2,1)}), bf16[64,8,256]{2,0,1:T(8,128)(2,1)S(1)}, u32[]{:S(2)}, u32[]{:S(2)}) async-start(bf16[64,8,256]{2,0,1:T(8,128)(2,1)} %bitcast.313), calls=%async_computation.2 | async-start | bytes 524288 | tf_op jit(solution)/shard_map/all_to_all | solution.py:126
  103.4 19.1 all-to-all-start.1
  110.7 109.1 %all-gather.18.cloned.1.call-start = ((), (), s32[]{:S(2)}) async-start(), calls=%async_computation.28 | async-start | bytes 1310720 | tf_op jit(solution)/shard_map/all_gather | solution.py:151
  122.5 107.7 %all-to-all-start.3 = ((bf16[64,8,256]{2,0,1:T(8,128)(2,1)}), bf16[64,8,256]{2,0,1:T(8,128)(2,1)S(1)}, u32[]{:S(2)}, u32[]{:S(2)}) async-start(bf16[64,8,256]{2,0,1:T(8,128)(2,1)} %bitcast.312), calls=%async_computation.3 | async-start | bytes 524288 | tf_op jit(solution)/shard_map/all_to_all | solution.py:140
  126.6 130.5 %all-gather.16.cloned.1.call-start = ((), (), s32[]{:S(2)}) async-start(), calls=%async_computation.27 | async-start | bytes 1310720 | tf_op jit(solution)/shard_map/all_gather | solution.py:150
  127.1 300.7 %all-gather.22.cloned.1.call-start = ((), (), s32[]{:S(2)}) async-start(), calls=%async_computation.30 | async-start | bytes 1310720 | tf_op jit(solution)/shard_map/all_gather | solution.py:153
  188.5 76.1 %collective-permute-start = (bf16[2,1024,256]{1,2,0:T(8,128)(2,1)S(1)}, bf16[2,1024,256]{1,2,0:T(8,128)(2,1)}, u32[]{:S(2)}, u32[]{:S(2)}) collective-permute-start(bf16[2,1024,256]{1,2,0:T(8,128)(2,1)S(1)} %copy.190), channel_id=1, source_target_pairs={{0,8},{8,16},{16,24},{1,9},{9,17},{17,25},{2,10},{10,18},{18,26},{... | collective-permute-start | bytes 3145736 | tf_op jit(solution)/shard_map/ppermute | solution.py:17
  227.0 39.0 %collective-permute-start.1 = (bf16[2,1024,256]{1,2,0:T(8,128)(2,1)}, bf16[2,1024,256]{1,2,0:T(8,128)(2,1)}, u32[]{:S(2)}, u32[]{:S(2)}) collective-permute-start(bf16[2,1024,256]{1,2,0:T(8,128)(2,1)} %copy.196), channel_id=1, source_target_pairs={{0,8},{8,16},{16,24},{1,9},{9,17},{17,25},{2,10},{10,18},{18,26},{... | collective-permute-start | bytes 3145736 | tf_op jit(solution)/shard_map/ppermute | solution.py:17
  230.9 238.0 %all-gather.20.cloned.1.call-start = ((), (), s32[]{:S(2)}) async-start(), calls=%async_computation.29 | async-start | bytes 9437184 | tf_op jit(solution)/shard_map/all_gather | solution.py:208
  365.0 228.5 %all-gather.28.cloned.1.call-start = ((), (), s32[]{:S(2)}) async-start(), calls=%async_computation.33 | async-start | bytes 5242880 | tf_op jit(solution)/shard_map/all_gather | solution.py:242
  477.9 50.6 %all-to-all-start.4 = ((f32[2,1024,256]{2,0,1:T(2,128)}), f32[2,1024,256]{2,0,1:T(2,128)S(1)}, u32[]{:S(2)}, u32[]{:S(2)}) async-start(f32[2,1024,256]{2,0,1:T(2,128)} %copy.201), calls=%async_computation.4 | async-start | bytes 4194304 | tf_op jit(solution)/shard_map/all_to_all | solution.py:214
  482.9 149.5 %all-gather.24.cloned.1.call-start = ((), (), s32[]{:S(2)}) async-start(), calls=%async_computation.31 | async-start | bytes 9437184 | tf_op jit(solution)/shard_map/all_gather | solution.py:247
  535.0 154.8 %all-gather.26.cloned.1.call-start = ((), (), s32[]{:S(2)}) async-start(), calls=%async_computation.32 | async-start | bytes 5242880 | tf_op jit(solution)/shard_map/all_gather | solution.py:241
  592.0 152.3 %all-gather.30.cloned.1.call-start = ((), (), s32[]{:S(2)}) async-start(), calls=%async_computation.34 | async-start | bytes 5242880 | tf_op jit(solution)/shard_map/all_gather | solution.py:243
  592.5 233.2 %all-gather.32.cloned.1.call-start = ((), (), s32[]{:S(2)}) async-start(), calls=%async_computation.36 | async-start | bytes 9437184 | tf_op jit(solution)/shard_map/all_gather | solution.py:247
  593.3 456.1 %reduce-scatter.16.cloned.1.call-start = ((), (), s32[]{:S(2)}) async-start(), calls=%async_computation.37 | async-start | bytes 18874368 | tf_op jit(solution)/shard_map/reduce_scatter | solution.py:250
  881.7 380.5 %reduce-scatter.18.cloned.1.call-start = ((), (), s32[]{:S(2)}) async-start(), calls=%async_computation.38 | async-start | bytes 18874368 | tf_op jit(solution)/shard_map/reduce_scatter | solution.py:312
  1094.1 621.3 %reduce-scatter.30.cloned.1.call-start = ((), (), s32[]{:S(2)}) async-start(), calls=%async_computation.44 | async-start | bytes 5242880 | tf_op jit(solution)/shard_map/reduce_scatter | solution.py:270
  1108.3 615.0 %reduce-scatter.28.cloned.1.call-start = ((), (), s32[]{:S(2)}) async-start(), calls=%async_computation.43 | async-start | bytes 5242880 | tf_op jit(solution)/shard_map/reduce_scatter | solution.py:264
  1122.5 685.7 %reduce-scatter.26.cloned.1.call-start = ((), (), s32[]{:S(2)}) async-start(), calls=%async_computation.42 | async-start | bytes 1310720 | tf_op jit(solution)/shard_map/reduce_scatter | solution.py:399
  1129.5 699.3 %reduce-scatter.20.cloned.1.call-start = ((), (), s32[]{:S(2)}) async-start(), calls=%async_computation.39 | async-start | bytes 1310720 | tf_op jit(solution)/shard_map/reduce_scatter | solution.py:390
  1546.1 288.3 %reduce-scatter.32.cloned.1.call-start = ((), (), s32[]{:S(2)}) async-start(), calls=%async_computation.45 | async-start | bytes 5242880 | tf_op jit(solution)/shard_map/reduce_scatter | solution.py:276
  1560.3 285.5 %reduce-scatter.24.cloned.1.call-start = ((), (), s32[]{:S(2)}) async-start(), calls=%async_computation.41 | async-start | bytes 1310720 | tf_op jit(solution)/shard_map/reduce_scatter | solution.py:396
  1562.2 32.9 %collective-permute-start.3 = (bf16[2,1024,256]{2,1,0:T(8,128)(2,1)S(1)}, bf16[2,1024,256]{2,1,0:T(8,128)(2,1)S(1)}, u32[]{:S(2)}, u32[]{:S(2)}) collective-permute-start(bf16[2,1024,256]{2,1,0:T(8,128)(2,1)S(1)} %slice.34), channel_id=1, source_target_pairs={{8,0},{16,8},{24,16},{9,1},{17,9},{25,17},{10,2},{18,10},{26,18},{... | collective-permute-start | bytes 3145736 | tf_op jit(solution)/shard_map/ppermute | solution.py:17
  1566.3 70.6 %collective-permute-start.2 = (bf16[2,1024,256]{2,1,0:T(8,128)(2,1)}, bf16[2,1024,256]{2,1,0:T(8,128)(2,1)}, u32[]{:S(2)}, u32[]{:S(2)}) collective-permute-start(bf16[2,1024,256]{2,1,0:T(8,128)(2,1)} %slice.35), channel_id=1, source_target_pairs={{8,0},{16,8},{24,16},{9,1},{17,9},{25,17},{10,2},{18,10},{26,18},{... | collective-permute-start | bytes 3145736 | tf_op jit(solution)/shard_map/ppermute | solution.py:17
  1602.4 253.6 %reduce-scatter.22.cloned.1.call-start = ((), (), s32[]{:S(2)}) async-start(), calls=%async_computation.40 | async-start | bytes 1310720 | tf_op jit(solution)/shard_map/reduce_scatter | solution.py:393
  1646.0 229.4 %reduce-scatter.34.cloned.1.call-start = ((), (), s32[]{:S(2)}) async-start(), calls=%async_computation.46 | async-start | bytes 9437184
  1699.7 336.7 %reduce-scatter.14.cloned.1.call-start = ((), (), s32[]{:S(2)}) async-start(), calls=%async_computation.35 | async-start | bytes 18874368 | tf_op jit(solution)/shard_map/reduce_scatter | solution.py:250
  1718.1 43.9 %all-to-all-start.13 = ((bf16[8,64,4,1,256]{4,2,1,3,0:T(4,128)(2,1)}), bf16[8,64,4,1,256]{4,2,1,3,0:T(4,128)(2,1)S(1)}, u32[]{:S(2)}, u32[]{:S(2)}) async-start(bf16[8,64,4,1,256]{4,2,1,3,0:T(4,128)(2,1)} %bitcast.68), calls=%async_computation.22 | async-start | bytes 2097152 | tf_op jit(solution)/shard_map/all_to_all | solution.py:291
  1828.8 17.0 all-to-all-start.8
  (72 other events, 3705.1 us)
Sparse Core Ops, SparseCore 0:
  52.6 98.8 all-gather.11
  153.3 28.6 all-gather.13
  184.4 35.2 all-gather.17
  222.0 35.0 all-gather.15
  259.3 26.4 all-gather.21
  365.1 103.7 all-gather.19
  470.7 52.1 all-gather.27
  535.1 97.2 all-gather.23
  634.8 54.9 all-gather.25
  691.5 52.6 all-gather.29
  745.9 79.8 all-gather.31
  881.8 167.4 reduce-scatter.15
  1094.3 167.8 reduce-scatter.17
  1265.0 52.5 reduce-scatter.29
  1320.7 52.6 reduce-scatter.27
  1376.2 27.7 reduce-scatter.25
  1546.2 30.9 reduce-scatter.19
  1580.0 74.9 reduce-scatter.31
  1658.2 27.6 reduce-scatter.23
  1689.2 27.7 reduce-scatter.21
  1719.4 147.9 reduce-scatter.33
  1869.8 166.5 reduce-scatter.13
where the time goes:
time: 2070 us; the launch traced here: 2050 us
  waiting for transfers between devices  928 us (45%)
  matrix products  393 us (19%)
  blocking collectives  316 us (15%)
  local copies, waits for them, and re-layouts  211 us (10%)
  other arithmetic  113 us (5%)
  starting transfers between devices  59.2 us (3%)
    reduce_scatter x2, waiting for transfers between devices, group_sums(): return lax.psum_scatter(values, 'fsdp', scatter_dimension=0, tiled=True)  274 us
    reduce_scatter x1, waiting for transfers between devices, body(): lax.psum_scatter(d_att_part, 'fsdp', scatter_dimension=2, tiled=True)  133 us
    all_gather x2, waiting for transfers between devices, group_rows(): return lax.all_gather(values, 'fsdp', axis=0, tiled=True)  120 us
    dot_general x7, matrix products, contract_cols(): lax.dot_general(left, right, (((1,), (1,)), ((), ())), preferred_element_...  97.3 us
    unnamed x2, blocking collectives  81.9 us
    dot_general x7, matrix products, contract_rows(): lax.dot_general(left, right, (((0,), (0,)), ((), ())), preferred_element_...  70.6 us
    dot_general x4, matrix products, block_parts(): jnp.einsum('bqhd,bkhd->bhqk', q_four, k_four, preferred_element_type=jnp....  66 us
    all_to_all x1, blocking collectives, unit_weights(): lax.all_to_all(w_up.reshape(row_share, seq_count, group_count, block), 'f...  60.4 us
  transfers between devices with their start and end apart: 34, of which 21 were waited for; matrix products, arithmetic and copies ran while one was open for 31% of the time, Pallas kernels for 0%

commit v1 on v0

v1 whole, which is shorter than its diff:
```python
import functools

import jax
import jax.numpy as jnp
from jax import lax
from jax.experimental import pallas as pl
from jax.experimental.pallas import tpu as pltpu
from jax.sharding import PartitionSpec as P

HEAD = 64
FF = 8192
WINDOW = 1024
PAIR = 128
TILE = 512
LOW = -1e30
EPS = 1e-05
MESH = pl.DeviceIdType.MESH
MIB = 2**20


def to_half(values):
    return values.astype(jnp.bfloat16)


def normalize(values, gain):
    return values * lax.rsqrt(jnp.mean(values * values, axis=-1, keepdims=True) + EPS) * gain


def contract_rows(left, right):
    return lax.dot_general(
        left, right, (((0,), (0,)), ((), ())), preferred_element_type=jnp.float32
    )


def dot_nt(left, right):
    return lax.dot_general(
        left, right, (((1,), (1,)), ((), ())), preferred_element_type=jnp.float32
    )


def dot_nn(left, right):
    return jnp.dot(left, right, preferred_element_type=jnp.float32)


def gate_back(gate, up, d_hidden):
    sigma = jax.nn.sigmoid(gate)
    d_gate = d_hidden * up * sigma * (1.0 + gate * (1.0 - sigma))
    d_up = d_hidden * gate * sigma
    return (to_half(d_gate), to_half(d_up))


def head_lanes(values, half):
    lane = lax.broadcasted_iota(jnp.int32, values.shape, 1)
    return jnp.where((lane >= HEAD) == (half == 1), values, jnp.zeros_like(values))


def masked_scores(k_rows, q_head, low):
    keys, block = k_rows.shape[0], q_head.shape[0]
    scores = dot_nt(k_rows, q_head)
    at = lax.broadcasted_iota(jnp.int32, (keys, block), 0)
    query = lax.broadcasted_iota(jnp.int32, (keys, block), 1)
    seen = (at >= low) & (at <= query + WINDOW)
    return jnp.where(seen, scores, LOW)


def attend_kernel(block, q_ref, k_ref, v_ref, low_ref, out_ref, lse_ref, vt_ref):
    step = pl.program_id(1)
    span = q_ref.shape[2]

    @pl.when(step == 0)
    def _():
        vt_ref[...] = v_ref[0].T

    begin = pl.multiple_of(step * block, block)
    keys = pl.ds(begin, block + WINDOW)
    low = low_ref[0]
    for pair in range(span // PAIR):
        lanes = slice(pair * PAIR, (pair + 1) * PAIR)
        q_pair = q_ref[0, :, lanes] * jnp.asarray(HEAD**-0.5, jnp.bfloat16)
        k_rows = k_ref[0, keys, lanes]
        vt = vt_ref[lanes, keys]
        mixed = []
        for half in range(2):
            scores = masked_scores(k_rows, head_lanes(q_pair, half), low)
            top = jnp.max(scores, axis=0, keepdims=True)
            expo = jnp.exp(scores - top)
            total = jnp.sum(expo, axis=0, keepdims=True)
            mixed.append(dot_nn(vt, expo.astype(jnp.bfloat16)) / total)
            row = pair * 2 + half
            lse_ref[0, row : row + 1, :] = top + jnp.log(total)
        row = lax.broadcasted_iota(jnp.int32, mixed[0].shape, 0)
        out_ref[0, :, lanes] = jnp.where(row < HEAD, mixed[0], mixed[1]).T.astype(jnp.bfloat16)


def attend(query, kv_pad, low, block):
    batches, length, span = query.shape
    padded = kv_pad.shape[1]
    heads = span // HEAD
    return pl.pallas_call(
        functools.partial(attend_kernel, block),
        grid=(batches, length // block),
        in_specs=[
            pl.BlockSpec((1, block, span), lambda b, i: (b, i, 0)),
            pl.BlockSpec((1, padded, span), lambda b, i: (b, 0, 0)),
            pl.BlockSpec((1, padded, span), lambda b, i: (b, 0, 1)),
            pl.BlockSpec((1, 1, block), lambda b, i: (b, 0, i)),
        ],
        out_specs=[
            pl.BlockSpec((1, block, span), lambda b, i: (b, i, 0)),
            pl.BlockSpec((1, heads, block), lambda b, i: (b, 0, i)),
        ],
        out_shape=[
            jax.ShapeDtypeStruct((batches, length, span), jnp.bfloat16),
            jax.ShapeDtypeStruct((batches, heads, length), jnp.float32),
        ],
        scratch_shapes=[pltpu.VMEM((span, padded), jnp.bfloat16)],
        compiler_params=pltpu.CompilerParams(vmem_limit_bytes=48 * 2**20),
        name="attend",
    )(query, kv_pad, kv_pad, low)


def attend_back_kernel(
    block, q_ref, k_ref, v_ref, low_ref, lse_ref, d_ref, dq_ref, dk_ref, dv_ref, kt_ref
):
    step = pl.program_id(1)
    span = q_ref.shape[2]
    scale = jnp.asarray(HEAD**-0.5, jnp.bfloat16)

    @pl.when(step == 0)
    def _():
        kt_ref[...] = k_ref[0].T * scale
        dk_ref[...] = jnp.zeros_like(dk_ref)
        dv_ref[...] = jnp.zeros_like(dv_ref)

    begin = pl.multiple_of(step * block, block)
    keys = pl.ds(begin, block + WINDOW)
    low = low_ref[0]
    for pair in range(span // PAIR):
        lanes = slice(pair * PAIR, (pair + 1) * PAIR)
        q_pair = q_ref[0, :, lanes] * scale
        d_pair = d_ref[0, :, lanes]
        k_rows = k_ref[0, keys, lanes]
        v_rows = v_ref[0, keys, lanes]
        kt = kt_ref[lanes, keys]
        back = []
        for half in range(2):
            row = pair * 2 + half
            q_head = head_lanes(q_pair, half)
            d_head = head_lanes(d_pair, half)
            scores = masked_scores(k_rows, q_head, low)
            probs = jnp.exp(scores - lse_ref[0, row : row + 1, :])
            d_probs = dot_nt(v_rows, d_head)
            along = jnp.sum(probs * d_probs, axis=0, keepdims=True)
            d_scores = (probs * (d_probs - along)).astype(jnp.bfloat16)
            dv_ref[0, keys, lanes] += dot_nn(probs.astype(jnp.bfloat16), d_head)
            dk_ref[0, keys, lanes] += dot_nn(d_scores, q_head)
            back.append(dot_nn(kt, d_scores))
        at = lax.broadcasted_iota(jnp.int32, back[0].shape, 0)
        dq_ref[0, :, lanes] = jnp.where(at < HEAD, back[0], back[1]).T.astype(jnp.bfloat16)


def attend_back(query, kv_pad, low, lse, d_att, block):
    batches, length, span = query.shape
    padded = kv_pad.shape[1]
    heads = span // HEAD
    rows = pl.BlockSpec((1, block, span), lambda b, i: (b, i, 0))
    whole = pl.BlockSpec((1, padded, span), lambda b, i: (b, 0, 0))
    return pl.pallas_call(
        functools.partial(attend_back_kernel, block),
        grid=(batches, length // block),
        in_specs=[
            rows,
            whole,
            pl.BlockSpec((1, padded, span), lambda b, i: (b, 0, 1)),
            pl.BlockSpec((1, 1, block), lambda b, i: (b, 0, i)),
            pl.BlockSpec((1, heads, block), lambda b, i: (b, 0, i)),
            rows,
        ],
        out_specs=[rows, whole, whole],
        out_shape=[
            jax.ShapeDtypeStruct((batches, length, span), jnp.bfloat16),
            jax.ShapeDtypeStruct((batches, padded, span), jnp.float32),
            jax.ShapeDtypeStruct((batches, padded, span), jnp.float32),
        ],
        scratch_shapes=[pltpu.VMEM((span, padded), jnp.bfloat16)],
        compiler_params=pltpu.CompilerParams(vmem_limit_bytes=48 * 2**20),
        name="attend_back",
    )(query, kv_pad, kv_pad, low, lse, d_att)


def line_place():
    own = lax.axis_index("fsdp")
    chip = own // 2
    core = lax.rem(own, 2)
    return own, chip, core, own + 1 - 2 * core


def greet_line(chips, own, chip, other):
    barrier = pltpu.get_barrier_semaphore()
    has_left = chip > 0
    has_right = chip < chips - 1

    def greet(peer):
        pl.semaphore_signal(barrier, inc=1, device_id={"fsdp": peer}, device_id_type=MESH)

    greet(other)
    pl.when(has_left)(lambda: greet(own - 2))
    pl.when(has_right)(lambda: greet(own + 2))
    pl.semaphore_wait(barrier, 1 + has_left.astype(jnp.int32) + has_right.astype(jnp.int32))
    return has_left, has_right


def spread_line(chips, x_ref, buf, send_sem, recv_sem, use):
    own, chip, core, other = line_place()
    has_left, has_right = greet_line(chips, own, chip, other)

    def move(slot, way, peer):
        return pltpu.make_async_remote_copy(
            src_ref=buf.at[slot],
            dst_ref=buf.at[slot],
            send_sem=send_sem.at[way, slot],
            recv_sem=recv_sem.at[slot],
            device_id={"fsdp": peer},
            device_id_type=MESH,
        )

    buf[own] = x_ref[...]
    pl.when(has_right)(lambda: move(own, 1, own + 2).start())
    pl.when(has_left)(lambda: move(own, 0, own - 2).start())
    move(own, 2, other).start()

    @pl.loop(0, chips + 1)
    def _(far):
        @pl.when((far > 0) & (chip - far >= 0))
        def _():
            slot = (chip - far) * 2 + core
            move(slot, 1, own).wait_recv()
            pl.when(has_right)(lambda: move(slot, 1, own + 2).start())
            move(slot, 2, other).start()

        @pl.when((far > 0) & (chip + far < chips))
        def _():
            slot = (chip + far) * 2 + core
            move(slot, 0, own).wait_recv()
            pl.when(has_left)(lambda: move(slot, 0, own - 2).start())
            move(slot, 2, other).start()

        @pl.loop(0, 4)
        def _(turn):
            side = lax.rem(turn, 2)
            across = turn // 2
            away = far - across
            source = chip + away * (2 * side - 1)
            valid = (away >= 0) & (away < chips) & (source >= 0) & (source < chips)
            valid = valid & ((side == 0) | (away > 0))

            @pl.when(valid)
            def _():
                slot = source * 2 + core + across * (1 - 2 * core)
                pl.when(across == 1)(lambda: move(slot, 2, own).wait_recv())
                use(slot)

    @pl.loop(0, chips)
    def _(place):
        slot = place * 2 + core
        move(slot, 2, other).wait_send()
        pl.when(has_right & (place <= chip))(lambda: move(slot, 1, own + 2).wait_send())
        pl.when(has_left & (place >= chip))(lambda: move(slot, 0, own - 2).wait_send())


def reduce_line(chips, width, product, out_ref, acc, outs, ins, send_sem, recv_sem):
    own, chip, core, other = line_place()
    has_left, has_right = greet_line(chips, own, chip, other)
    cross_out, line_out = outs
    cross_in, line_in = ins
    tiles = width // TILE

    def cross(place):
        return pltpu.make_async_remote_copy(
            src_ref=cross_out.at[place],
            dst_ref=cross_in.at[place],
            send_sem=send_sem.at[0, place],
            recv_sem=recv_sem.at[0, place],
            device_id={"fsdp": other},
            device_id_type=MESH,
        )

    def along(place, landing, peer):
        return pltpu.make_async_remote_copy(
            src_ref=line_out.at[place],
            dst_ref=line_in.at[landing],
            send_sem=send_sem.at[1, place],
            recv_sem=recv_sem.at[1, landing],
            device_id={"fsdp": peer},
            device_id_type=MESH,
        )

    def columns(tile):
        return pl.ds(pl.multiple_of(tile * TILE, TILE), TILE)

    @pl.loop(0, 2 * chips - 1)
    def _(step):
        away = chips - 1 - step // 2
        side = lax.rem(step, 2)
        place = chip + away * (1 - 2 * side)

        @pl.when((place >= 0) & (place < chips))
        def _():
            @pl.loop(0, tiles)
            def _(tile):
                cross_out[place, :, columns(tile)] = to_half(product(place * 2 + 1 - core, tile))

            cross(place).start()

            @pl.loop(0, tiles)
            def _(tile):
                acc[:, columns(tile)] = product(place * 2 + core, tile)

            cross(place).wait_recv()

            @pl.when(away > 0)
            def _():
                rightward = side == 0
                upstream = (rightward & has_left) | (jnp.logical_not(rightward) & has_right)

                @pl.when(upstream)
                def _():
                    along(place, place, own).wait_recv()
                    line_out[place] = to_half(
                        acc[...]
                        + cross_in[place].astype(jnp.float32)
                        + line_in[place].astype(jnp.float32)
                    )

                @pl.when(jnp.logical_not(upstream))
                def _():
                    line_out[place] = to_half(acc[...] + cross_in[place].astype(jnp.float32))

                @pl.when(rightward)
                def _():
                    along(place, place, own + 2).start()

                @pl.when(jnp.logical_not(rightward))
                def _():
                    landing = jnp.where(away == 1, chips, place)
                    along(place, landing, own - 2).start()

            @pl.when(away == 0)
            def _():
                out_ref[...] = acc[...] + cross_in[place].astype(jnp.float32)

                @pl.when(has_left)
                def _():
                    along(place, place, own).wait_recv()
                    out_ref[...] += line_in[place].astype(jnp.float32)

                @pl.when(has_right)
                def _():
                    along(place, chips, own).wait_recv()
                    out_ref[...] += line_in[chips].astype(jnp.float32)

    @pl.loop(0, chips)
    def _(place):
        cross(place).wait_send()
        pl.when(place != chip)(lambda: along(place, place, own).wait_send())


def project_kernel(chips, batches, x_ref, w_ref, g_ref, q_ref, kv_ref, buf, send, recv, keep):
    piece = x_ref.shape[0] // batches
    span = q_ref.shape[2]

    def kept(slot, batch):
        return pltpu.make_async_copy(
            buf.at[slot, pl.ds(batch * piece, piece)],
            g_ref.at[batch, pl.ds(pl.multiple_of(slot * piece, piece), piece)],
            keep.at[slot, batch],
        )

    def use(slot):
        for batch in range(batches):
            kept(slot, batch).start()
        rows = pl.ds(pl.multiple_of(slot * piece, piece), piece)
        values = buf[slot]
        for part in range(3):
            got = to_half(dot_nn(values, w_ref[:, part * span : (part + 1) * span]))
            for batch in range(batches):
                own = got[batch * piece : (batch + 1) * piece]
                if part == 0:
                    q_ref[batch, rows, :] = own
                else:
                    kv_ref[batch, rows, (part - 1) * span : part * span] = own

    spread_line(chips, x_ref, buf, send, recv, use)

    @pl.loop(0, 2 * chips)
    def _(slot):
        for batch in range(batches):
            kept(slot, batch).wait()


def project_heads(chips, batches, x, w, collective):
    rows, width = x.shape
    slots = 2 * chips
    length = slots * rows // batches
    span = w.shape[1] // 3
    vmem = pl.BlockSpec(memory_space=pltpu.VMEM)
    return pl.pallas_call(
        functools.partial(project_kernel, chips, batches),
        out_shape=[
            jax.ShapeDtypeStruct((batches, length, width), jnp.bfloat16),
            jax.ShapeDtypeStruct((batches, length, span), jnp.bfloat16),
            jax.ShapeDtypeStruct((batches, length, 2 * span), jnp.bfloat16),
        ],
        in_specs=[vmem, vmem],
        out_specs=[pl.BlockSpec(memory_space=pl.ANY), vmem, vmem],
        scratch_shapes=[
            pltpu.VMEM((slots, rows, width), jnp.bfloat16),
            pltpu.SemaphoreType.DMA((3, slots)),
            pltpu.SemaphoreType.DMA((slots,)),
            pltpu.SemaphoreType.DMA((slots, batches)),
        ],
        compiler_params=pltpu.CompilerParams(
            collective_id=collective, has_side_effects=True, vmem_limit_bytes=56 * MIB
        ),
        cost_estimate=line_cost(slots, rows, width, w.shape[1]),
        name="project_heads",
    )(x, w)


def line_cost(slots, rows, width, depth):
    moved = slots * rows * width * 2
    return pl.CostEstimate(
        flops=2 * slots * rows * width * depth,
        bytes_accessed=24 * moved,
        transcendentals=0,
        remote_bytes_transferred=moved,
    )


def units_kernel(chips, x_ref, w_ref, g_ref, gate_ref, up_ref, hidden_ref, buf, send, recv, keep):
    rows = x_ref.shape[0]
    units = gate_ref.shape[1]

    def kept(slot):
        return pltpu.make_async_copy(buf.at[slot], g_ref.at[slot], keep.at[slot])

    def use(slot):
        kept(slot).start()
        place = pl.ds(pl.multiple_of(slot * rows, rows), rows)

        @pl.loop(0, units // TILE)
        def _(tile):
            first = pl.multiple_of(tile * TILE, TILE)
            columns = pl.ds(first, TILE)
            values = buf[slot]
            gate = dot_nn(values, w_ref[:, columns])
            up = dot_nn(values, w_ref[:, pl.ds(pl.multiple_of(units + first, TILE), TILE)])
            gate_ref[place, columns] = to_half(gate)
            up_ref[place, columns] = to_half(up)
            hidden_ref[place, columns] = to_half(gate * jax.nn.sigmoid(gate) * up)

    spread_line(chips, x_ref, buf, send, recv, use)

    @pl.loop(0, 2 * chips)
    def _(slot):
        kept(slot).wait()


def hidden_units(chips, x, w, collective):
    rows, width = x.shape
    slots = 2 * chips
    units = w.shape[1] // 2
    vmem = pl.BlockSpec(memory_space=pltpu.VMEM)
    part = jax.ShapeDtypeStruct((slots * rows, units), jnp.bfloat16)
    return pl.pallas_call(
        functools.partial(units_kernel, chips),
        out_shape=[jax.ShapeDtypeStruct((slots, rows, width), jnp.bfloat16), part, part, part],
        in_specs=[vmem, vmem],
        out_specs=[pl.BlockSpec(memory_space=pl.ANY), vmem, vmem, vmem],
        scratch_shapes=[
            pltpu.VMEM((slots, rows, width), jnp.bfloat16),
            pltpu.SemaphoreType.DMA((3, slots)),
            pltpu.SemaphoreType.DMA((slots,)),
            pltpu.SemaphoreType.DMA((slots,)),
        ],
        compiler_params=pltpu.CompilerParams(
            collective_id=collective, has_side_effects=True, vmem_limit_bytes=58 * MIB
        ),
        cost_estimate=line_cost(slots, rows, width, w.shape[1]),
        name="hidden_units",
    )(x, w)


def branch_back_kernel(chips, batches, x_ref, w_ref, g_ref, d_ref, buf, send, recv, keep):
    piece = x_ref.shape[0] // batches

    def kept(slot, batch):
        return pltpu.make_async_copy(
            buf.at[slot, pl.ds(batch * piece, piece)],
            g_ref.at[batch, pl.ds(pl.multiple_of(slot * piece, piece), piece)],
            keep.at[slot, batch],
        )

    def use(slot):
        for batch in range(batches):
            kept(slot, batch).start()
        rows = pl.ds(pl.multiple_of(slot * piece, piece), piece)
        got = to_half(dot_nt(buf[slot], w_ref[...]))
        for batch in range(batches):
            d_ref[batch, rows, :] = got[batch * piece : (batch + 1) * piece]

    spread_line(chips, x_ref, buf, send, recv, use)

    @pl.loop(0, 2 * chips)
    def _(slot):
        for batch in range(batches):
            kept(slot, batch).wait()


def branch_back(chips, batches, x, w, collective):
    rows, width = x.shape
    slots = 2 * chips
    length = slots * rows // batches
    span = w.shape[0]
    vmem = pl.BlockSpec(memory_space=pltpu.VMEM)
    return pl.pallas_call(
        functools.partial(branch_back_kernel, chips, batches),
        out_shape=[
            jax.ShapeDtypeStruct((batches, length, width), jnp.bfloat16),
            jax.ShapeDtypeStruct((batches, length, span), jnp.bfloat16),
        ],
        in_specs=[vmem, vmem],
        out_specs=[pl.BlockSpec(memory_space=pl.ANY), vmem],
        scratch_shapes=[
            pltpu.VMEM((slots, rows, width), jnp.bfloat16),
            pltpu.SemaphoreType.DMA((3, slots)),
            pltpu.SemaphoreType.DMA((slots,)),
            pltpu.SemaphoreType.DMA((slots, batches)),
        ],
        compiler_params=pltpu.CompilerParams(
            collective_id=collective, has_side_effects=True, vmem_limit_bytes=56 * MIB
        ),
        cost_estimate=line_cost(slots, rows, width, span),
        name="branch_back",
    )(x, w)


def sum_kernel(chips, across, a_ref, w_ref, out_ref, acc, *scratch):
    width = out_ref.shape[1]
    rows = out_ref.shape[0]
    outs, ins, send, recv = scratch[0:2], scratch[2:4], scratch[4], scratch[5]

    def product(slot, tile):
        if len(a_ref.shape) == 3:
            piece = rows // a_ref.shape[0]
            place = pl.ds(pl.multiple_of(slot * piece, piece), piece)
            left = jnp.concatenate([a_ref[batch, place, :] for batch in range(a_ref.shape[0])], axis=0)
        else:
            left = a_ref[pl.ds(pl.multiple_of(slot * rows, rows), rows), :]
        part = pl.ds(pl.multiple_of(tile * TILE, TILE), TILE)
        if across:
            return dot_nt(left, w_ref[part, :])
        return dot_nn(left, w_ref[:, part])

    reduce_line(chips, width, product, out_ref, acc, outs, ins, send, recv)


def sum_products(chips, a, w, across, name, collective):
    slots = 2 * chips
    width = w.shape[0] if across else w.shape[1]
    rows = (a.shape[0] * a.shape[1] if a.ndim == 3 else a.shape[0]) // slots
    vmem = pl.BlockSpec(memory_space=pltpu.VMEM)
    half = functools.partial(pltpu.VMEM, dtype=jnp.bfloat16)
    return pl.pallas_call(
        functools.partial(sum_kernel, chips, across),
        out_shape=jax.ShapeDtypeStruct((rows, width), jnp.float32),
        in_specs=[vmem, vmem],
        out_specs=vmem,
        scratch_shapes=[
            pltpu.VMEM((rows, width), jnp.float32),
            half((chips, rows, width)),
            half((chips, rows, width)),
            half((chips, rows, width)),
            half((chips + 1, rows, width)),
            pltpu.SemaphoreType.DMA((2, chips)),
            pltpu.SemaphoreType.DMA((2, chips + 1)),
        ],
        compiler_params=pltpu.CompilerParams(
            collective_id=collective, has_side_effects=True, vmem_limit_bytes=60 * MIB
        ),
        cost_estimate=line_cost(slots, rows, width, a.shape[-1]),
        name=name,
    )(a, w)


def swap_kernel(group, count, *refs):
    sources, targets = refs[:count], refs[count : 2 * count]
    send, recv, keep = refs[2 * count :]
    own = lax.axis_index("fsdp")
    barrier = pltpu.get_barrier_semaphore()

    @pl.loop(1, group)
    def _(ahead):
        peer = lax.rem(own + ahead, group)
        pl.semaphore_signal(barrier, inc=1, device_id={"fsdp": peer}, device_id_type=MESH)

    pl.semaphore_wait(barrier, group - 1)

    def move(item, peer, source):
        return pltpu.make_async_remote_copy(
            src_ref=sources[item].at[peer],
            dst_ref=targets[item].at[source],
            send_sem=send.at[item, peer],
            recv_sem=recv.at[item, source],
            device_id={"fsdp": peer},
            device_id_type=MESH,
        )

    for item in range(count):
        pltpu.make_async_copy(sources[item].at[own], targets[item].at[own], keep.at[item]).start()

        @pl.loop(1, group)
        def _(ahead, item=item):
            move(item, lax.rem(own + ahead, group), own).start()

    for item in range(count):
        pltpu.make_async_copy(sources[item].at[own], targets[item].at[own], keep.at[item]).wait()

        @pl.loop(1, group)
        def _(ahead, item=item):
            peer = lax.rem(own + ahead, group)
            move(item, peer, peer).wait_recv()
            move(item, peer, own).wait_send()


def swap_blocks(group, arrays, name, collective):
    count = len(arrays)
    anywhere = pl.BlockSpec(memory_space=pl.ANY)
    moved = sum(item.size * 2 for item in arrays)
    return pl.pallas_call(
        functools.partial(swap_kernel, group, count),
        out_shape=[jax.ShapeDtypeStruct(item.shape, item.dtype) for item in arrays],
        in_specs=[anywhere] * count,
        out_specs=[anywhere] * count,
        scratch_shapes=[
            pltpu.SemaphoreType.DMA((count, group)),
            pltpu.SemaphoreType.DMA((count, group)),
            pltpu.SemaphoreType.DMA((count,)),
        ],
        compiler_params=pltpu.CompilerParams(collective_id=collective, has_side_effects=True),
        cost_estimate=pl.CostEstimate(
            flops=0,
            bytes_accessed=40 * moved,
            transcendentals=0,
            remote_bytes_transferred=moved,
        ),
        name=name,
    )(*arrays)


def tiles_kernel(seqs, group, same, x_ref, out_ref, send, recv):
    devices = seqs * group
    own = lax.axis_index("seq") * group + lax.axis_index("fsdp")
    barrier = pltpu.get_barrier_semaphore()

    def place(peer):
        return {"seq": peer // group, "fsdp": lax.rem(peer, group)}

    @pl.loop(1, devices)
    def _(ahead):
        peer = lax.rem(own + ahead, devices)
        pl.semaphore_signal(barrier, inc=1, device_id=place(peer), device_id_type=MESH)

    pl.semaphore_wait(barrier, devices - 1)
    out_ref[own] = x_ref[0] if same else x_ref[own]

    def move(peer, source):
        return pltpu.make_async_remote_copy(
            src_ref=x_ref.at[0 if same else peer],
            dst_ref=out_ref.at[source],
            send_sem=send.at[peer],
            recv_sem=recv.at[source],
            device_id=place(peer),
            device_id_type=MESH,
        )

    @pl.loop(1, devices)
    def _(ahead):
        move(lax.rem(own + ahead, devices), own).start()

    @pl.loop(1, devices)
    def _(ahead):
        peer = lax.rem(own + ahead, devices)
        move(peer, peer).wait_recv()
        move(peer, own).wait_send()


def swap_tiles(seqs, group, x, same, name, collective):
    devices = seqs * group
    vmem = pl.BlockSpec(memory_space=pltpu.VMEM)
    return pl.pallas_call(
        functools.partial(tiles_kernel, seqs, group, same),
        out_shape=jax.ShapeDtypeStruct((devices, 8, 128), jnp.float32),
        in_specs=[vmem],
        out_specs=vmem,
        scratch_shapes=[
            pltpu.SemaphoreType.DMA((devices,)),
            pltpu.SemaphoreType.DMA((devices,)),
        ],
        compiler_params=pltpu.CompilerParams(collective_id=collective, has_side_effects=True),
        name=name,
    )(x)


def doc_starts(lengths, positions, batches, seq_len):
    table = lengths.reshape(batches, -1, lengths.shape[1])
    starts = jnp.cumsum(table, axis=2) - table
    per_batch = seq_len // table.shape[1]
    begins = (starts + (jnp.arange(table.shape[1], dtype=jnp.int32) * per_batch)[None, :, None]).reshape(
        batches, -1
    )
    before = begins[:, None, :] <= positions[None, :, None]
    return jnp.max(jnp.where(before, begins[:, None, :], 0), axis=2)


def body(
    tokens,
    cotangent,
    lengths,
    gain_attn,
    w_query,
    w_key,
    w_value,
    w_out,
    gain_mlp,
    w_gate,
    w_up,
    w_down,
):
    batches, piece, width = tokens.shape
    seqs = lax.axis_size("seq")
    group = lax.axis_size("fsdp")
    chips = group // 2
    devices = seqs * group
    seq_len = piece * devices
    rows = batches * piece
    share = w_query.shape[0]
    span = width // group
    length = group * piece
    group_rows = group * rows
    units = FF // group
    aligned = share == HEAD
    member = lax.axis_index("fsdp")

    def blocks(weight):
        part = weight.shape[1] // devices
        if part < HEAD:
            return weight.reshape(share, group, -1).transpose(1, 0, 2)
        return weight.reshape(share, seqs, group, part).transpose(2, 0, 1, 3).reshape(group, share, -1)

    def unblock(cols, total):
        part = total // devices
        if part < HEAD:
            return cols.transpose(1, 0, 2).reshape(share, total)
        return cols.reshape(group, share, seqs, part).transpose(1, 2, 0, 3).reshape(share, total)

    tile = jnp.zeros((1, 8, 128), jnp.float32)
    tile = tile.at[0, 0, :share].set(gain_attn.astype(jnp.float32))
    tile = tile.at[0, 0, 64 : 64 + share].set(gain_mlp.astype(jnp.float32))
    gains = swap_tiles(seqs, group, tile, True, "gains", 1)
    gain_one = gains[:, 0, :share].reshape(width)
    gain_two = gains[:, 0, 64 : 64 + share].reshape(width)

    inputs = tokens.astype(jnp.float32).reshape(rows, width)
    upstream = cotangent.astype(jnp.float32).reshape(rows, width)
    group_d = lax.all_gather(cotangent.reshape(rows, width), "fsdp", axis=0, tiled=True)
    wd_part = lax.all_gather(w_down, "seq", axis=0, tiled=True)
    if aligned:
        wo_part = lax.all_gather(w_out, "seq", axis=0, tiled=True)
    else:
        wo_all = lax.all_gather(w_out, ("seq", "fsdp"), axis=0, tiled=True)
        wo_part = lax.dynamic_slice_in_dim(wo_all, member * span, span, 0)

    attn_blocks = jnp.concatenate([blocks(w_query), blocks(w_key), blocks(w_value)], axis=2)
    unit_blocks = jnp.concatenate([blocks(w_gate), blocks(w_up)], axis=2)
    attn_own, unit_own = swap_blocks(group, [attn_blocks, unit_blocks], "weights", 2)
    w_heads = lax.all_gather(attn_own.reshape(group * share, -1), "seq", axis=0, tiled=True)
    w_units = lax.all_gather(unit_own.reshape(group * share, -1), "seq", axis=0, tiled=True)

    group_start = lax.axis_index("seq") * length
    positions = group_start + jnp.arange(length, dtype=jnp.int32)
    begins = doc_starts(lengths, positions, batches, seq_len)
    at = jnp.arange(length, dtype=jnp.int32)
    block = min(256, length)
    low = jnp.maximum(begins - group_start + WINDOW, at[None, :] + 1) - (at // block * block)[None, :]
    low = low[:, None, :]

    normed_a = to_half(normalize(inputs, gain_one))
    group_a, query, key_value = project_heads(chips, batches, normed_a, w_heads, 3)
    ahead = [(source, source + 1) for source in range(seqs - 1)]
    behind = [(source + 1, source) for source in range(seqs - 1)]
    tail = lax.ppermute(key_value[:, length - WINDOW :], "seq", ahead)
    kv_pad = jnp.concatenate([tail, key_value], axis=1)
    attended, lse = attend(query, kv_pad, low, block)
    branch = sum_products(chips, attended, wo_part, False, "branch", 4)
    middle = inputs + branch
    normed_b = to_half(normalize(middle, gain_two))
    group_b, gate, up, hidden = hidden_units(chips, normed_b, w_units, 5)
    d_hidden = dot_nt(group_d, wd_part)
    d_gate, d_up = gate_back(gate.astype(jnp.float32), up.astype(jnp.float32), d_hidden)
    d_units = jnp.concatenate([d_gate, d_up], axis=1)
    d_normed_b = sum_products(chips, d_units, w_units, True, "units_back", 6)
    mlp_out = lax.psum_scatter(
        to_half(dot_nn(hidden, wd_part)), "fsdp", scatter_dimension=0, tiled=True
    )
    outputs = middle + mlp_out.astype(jnp.float32)
    mlp_pull = jax.vjp(normalize, middle, gain_two)[1]
    d_middle_norm, gain_two_grad = mlp_pull(d_normed_b)
    d_middle = upstream + d_middle_norm
    d_branch = to_half(d_middle)

    def over_seq(values):
        return lax.psum_scatter(to_half(values), "seq", scatter_dimension=0, tiled=True)

    down_sum = over_seq(contract_rows(hidden, group_d))
    unit_sums = over_seq(contract_rows(group_b.reshape(group_rows, width), d_units))

    group_branch, d_attended = branch_back(chips, batches, d_branch, wo_part, 7)
    d_query, d_key_pad, d_value_pad = attend_back(query, kv_pad, low, lse, d_attended, block)
    back = lax.ppermute(
        to_half(jnp.concatenate([d_key_pad[:, :WINDOW], d_value_pad[:, :WINDOW]], axis=2)),
        "seq",
        behind,
    ).astype(jnp.float32)
    back = jnp.pad(back, ((0, 0), (length - WINDOW, 0), (0, 0)))
    d_heads = jnp.concatenate(
        [
            d_query,
            to_half(d_key_pad[:, WINDOW:] + back[:, :, :span]),
            to_half(d_value_pad[:, WINDOW:] + back[:, :, span:]),
        ],
        axis=2,
    )
    d_normed_a = sum_products(chips, d_heads, w_heads, True, "heads_back", 8)
    flat_a = group_a.reshape(group_rows, width)
    out_grad = contract_rows(
        attended.reshape(group_rows, span), group_branch.reshape(group_rows, width)
    )
    if aligned:
        out_sum = over_seq(out_grad)
    else:
        whole = lax.dynamic_update_slice_in_dim(
            jnp.zeros((width, width), jnp.bfloat16), to_half(out_grad), member * span, 0
        )
        out_sum = lax.psum_scatter(whole, ("seq", "fsdp"), scatter_dimension=0, tiled=True)
    head_sums = over_seq(contract_rows(flat_a, d_heads.reshape(group_rows, 3 * span)))
    head_cols, unit_cols = swap_blocks(
        group,
        [head_sums.reshape(group, share, -1), unit_sums.reshape(group, share, -1)],
        "weight_grads",
        9,
    )

    attn_pull = jax.vjp(normalize, inputs, gain_one)[1]
    d_input_norm, gain_one_grad = attn_pull(d_normed_a)
    input_grad = (d_middle + d_input_norm).reshape(batches, piece, width)
    layer_out = to_half(outputs).reshape(batches, piece, width)

    def lanes(values):
        return jnp.pad(values.reshape(devices, 1, share), ((0, 0), (0, 7), (0, 64 - share)))

    grad_tiles = jnp.concatenate([lanes(gain_one_grad), lanes(gain_two_grad)], axis=2)
    grad_sums = jnp.sum(swap_tiles(seqs, group, grad_tiles, False, "gain_grads", 10)[:, 0], axis=0)

    def whole_rows(cols, part, total):
        size = total // group
        return unblock(cols[:, :, part * size : (part + 1) * size], total).astype(jnp.float32)

    return (
        layer_out,
        input_grad,
        grad_sums[:share],
        whole_rows(head_cols, 0, width),
        whole_rows(head_cols, 1, width),
        whole_rows(head_cols, 2, width),
        out_sum.astype(jnp.float32),
        grad_sums[64 : 64 + share],
        whole_rows(unit_cols, 0, FF),
        whole_rows(unit_cols, 1, FF),
        down_sum.astype(jnp.float32),
    )


def solution(mesh):
    spread = ("seq", "fsdp")
    tokens, rows, gains = P(None, spread, None), P(spread, None), P(spread)
    in_specs = (tokens, tokens, P(), gains, rows, rows, rows, rows, gains, rows, rows, rows)
    out_specs = (tokens, tokens, gains, rows, rows, rows, rows, gains, rows, rows, rows)
    return jax.shard_map(body, mesh=mesh, in_specs=in_specs, out_specs=out_specs, check_vma=False)
```

time: 2070 us -> 1210 us (0.58)
  Pallas kernels: 0 us -> 796 us
  waiting for transfers between devices: 928 us -> 212 us
  blocking collectives: 316 us -> 0 us
  matrix products: 393 us -> 89.7 us
  local copies, waits for them, and re-layouts: 211 us -> 44.1 us
  other arithmetic: 113 us -> 42.8 us
  starting transfers between devices: 59.2 us -> 7.44 us
    pallas_call x0 -> x12, Pallas kernels: none -> 796 us  [the longest x3 346 us: sum_products(): pl.pallas_call(functools.partial(sum_kernel, chips, across), out_shape=ja...]
    reduce_scatter x10 -> x5, waiting for transfers between devices: 407 us -> 44 us  [the longest x4 44 us: over_seq(): lax.psum_scatter(to_half(values), 'seq', scatter_dimension=0, tiled=True)]
    all_gather x11 -> x5, waiting for transfers between devices: 341 us -> 28 us  [the longest x1 27.9 us: body(): lax.all_gather(attn_own.reshape(group * share, -1), 'seq', axis=0, tiled=...]
    dot_general x28 -> x2, matrix products: 322 us -> 34.6 us  [the longest x1 20.6 us: dot_nt(): lax.dot_general(left, right, (((1,), (1,)), ((), ())), preferred_element_...]
    all_to_all x6 -> x0, blocking collectives: 234 us -> none  [the longest x1 60.4 us: unit_weights(): lax.all_to_all(w_up.reshape(row_share, seq_count, group_count, block), 'f...]
    all_to_all x8 -> x0, waiting for transfers between devices: 124 us -> none  [the longest x1 43.8 us: body(): lax.all_to_all(out_cols, 'fsdp', split_axis=1, concat_axis=2, tiled=True)]
    ppermute x4 -> x2, waiting for transfers between devices: 53.8 us -> 138 us  [the longest x1 80.3 us: body(): tail = lax.ppermute(key_value[:, length - WINDOW:], 'seq', ahead)]
    unnamed x2 -> x0, blocking collectives: 81.9 us -> none
  transfers between devices with their start and end apart: 34 -> 12, of which waited for: 21 -> 4; matrix products, arithmetic and copies ran while one was open for 31% -> 8% of each run, Pallas kernels for 0% -> 40%
where the time goes in v1:
time: 1210 us
  Pallas kernels  796 us (66%)
  waiting for transfers between devices  212 us (18%)
  matrix products  89.7 us (7%)
  local copies, waits for them, and re-layouts  44.1 us (4%)
  other arithmetic  42.8 us (4%)
  between operations  15 us (1%)
    pallas_call x3, Pallas kernels, sum_products(): pl.pallas_call(functools.partial(sum_kernel, chips, across), out_shape=ja...  346 us
    pallas_call x2, Pallas kernels, swap_blocks(): pl.pallas_call(functools.partial(swap_kernel, group, count), out_shape=[j...  133 us
    ppermute x1, waiting for transfers between devices, body(): tail = lax.ppermute(key_value[:, length - WINDOW:], 'seq', ahead)  80.3 us
    pallas_call x1, Pallas kernels, hidden_units(): pl.pallas_call(functools.partial(units_kernel, chips), out_shape=[jax.Sha...  77.5 us
    pallas_call x1, Pallas kernels, project_heads(): pl.pallas_call(functools.partial(project_kernel, chips, batches), out_sha...  74.5 us
    pallas_call x1, Pallas kernels, branch_back(): pl.pallas_call(functools.partial(branch_back_kernel, chips, batches), out...  72.9 us
    ppermute x1, waiting for transfers between devices, body(): lax.ppermute(to_half(jnp.concatenate([d_key_pad[:, :WINDOW], d_value_pad[...  57.2 us
    dot_general x4, matrix products, contract_rows(): lax.dot_general(left, right, (((0,), (0,)), ((), ())), preferred_element_...  55.1 us
  transfers between devices with their start and end apart: 12, of which 4 were waited for; matrix products, arithmetic and copies ran while one was open for 8% of the time, Pallas kernels for 40%

profile of v1, /device:TPU:9, one launch (start us, length us, event | category | flops | bytes accessed | tf_op | source)
XLA Modules:
  0.0 1206.8 jit_solution(13434930681813756823)
XLA Ops:
  19.2 66.6 %weights.1 = (bf16[8,64,768]{2,1,0:T(8,128)(2,1)}, bf16[8,64,2048]{2,1,0:T(8,128)(2,1)}) custom-call(bf16[8,64,768]{2,1,0:T(8,128)(2,1)} %pad_maximum_fusion.4.refs_0_, bf16[8,64,2048]{2,1,0:T(8,128)(2,1)} %pad_maximum_fusion.2.refs_1_), custom_call_target="tpu_custom_call" | custom-call | bytes 115343360 | tf_op jit(solution)/shard_map/weights/pallas_call | solution.py:640
  89.4 10.7 gains.1
  102.9 27.9 %all-gather.6.cloned.1.call-done.w_ref = bf16[2048,768]{1,0:T(8,128)(2,1)} async-done(((bf16[512,768]{1,0:T(8,128)(2,1)}), bf16[2048,768]{1,0:T(8,128)(2,1)}) %all-gather.6.cloned.1.call-update) | async-done | bytes 3145744 | tf_op jit(solution)/shard_map/all_gather | solution.py:787
  130.9 74.5 %project_heads.1 = (bf16[2,1024,2048]{2,1,0:T(8,128)(2,1)}, bf16[2,1024,256]{2,1,0:T(8,128)(2,1)}, bf16[2,1024,512]{2,1,0:T(8,128)(2,1)}) custom-call(bf16[256,2048]{1,0:T(8,128)(2,1)} %fusion.15.x_ref, bf16[2048,768]{1,0:T(8,128)(2,1)} %all-gather.6.cloned.1.call-done.w_ref), custom_call_target="tpu_custom_call" | custom-call | flops 6442450944 | bytes 201326592 | tf_op jit(solution)/shard_map/project_heads/pallas_call | solution.py:407
  205.5 4.9 collective-permute-start
  210.8 80.3 %collective-permute-done = bf16[2,1024,512]{2,1,0:T(8,128)(2,1)} collective-permute-done((bf16[2,1024,512]{2,1,0:T(8,128)(2,1)}, bf16[2,1024,512]{2,1,0:T(8,128)(2,1)}, u32[]{:S(2)}, u32[]{:S(2)}) %collective-permute-start) | collective-permute-done | bytes 2097184 | tf_op jit(solution)/shard_map/ppermute | solution.py:802
  295.0 30.3 %attend.1 = (bf16[2,1024,256]{2,1,0:T(8,128)(2,1)S(1)}, f32[2,4,1024]{2,1,0:T(4,128)S(1)}) custom-call(bf16[2,1024,256]{2,1,0:T(8,128)(2,1)S(1)} %copy-done, bf16[2,2048,512]{2,1,0:T(8,128)(2,1)} %copy-done.4, bf16[2,2048,512]{2,1,0:T(8,128)(2,1)} %copy-done.4, s32[2,1,1024]{2,1,0:T(1,128)S(1)} %maximum_subtract_fusion.low_ref), custom_call_target="tpu_custom_call" | custom-call | tf_op jit(solution)/shard_map/attend/pallas_call | solution.py:99
  326.2 147.4 %branch.1 = f32[256,2048]{1,0:T(8,128)} custom-call(bf16[2,1024,256]{2,1,0:T(8,128)(2,1)} %copy-done.1, bf16[256,2048]{1,0:T(8,128)(2,1)} %all-gather.8.cloned.1.call-done.w_ref), custom_call_target="tpu_custom_call" | custom-call | flops 2147483648 | bytes 201326592 | tf_op jit(solution)/shard_map/branch/pallas_call | solution.py:574
  477.3 77.5 %hidden_units.1 = (bf16[8,256,2048]{2,1,0:T(8,128)(2,1)}, bf16[2048,1024]{1,0:T(8,128)(2,1)}, bf16[2048,1024]{1,0:T(8,128)(2,1)}, bf16[2048,1024]{1,0:T(8,128)(2,1)}) custom-call(bf16[256,2048]{1,0:T(8,128)(2,1)} %multiply_convert_fusion.x_ref, bf16[2048,2048]{1,0:T(8,128)(2,1)} %all-gather.10.cloned.1.call-done.w_ref), custom_call_target="tpu_custom_call" | custom-call | flops 17179869184 | bytes 201326592 | tf_op jit(solution)/shard_map/hidden_units/pallas_call | solution.py:475
  554.9 20.6 %fusion.5 = (bf16[2048,1024]{1,0:T(8,128)(2,1)}, bf16[2048,1024]{1,0:T(8,128)(2,1)}) fusion(bf16[2048,1024]{1,0:T(8,128)(2,1)} %get-tuple-element.60, bf16[2048,1024]{1,0:T(8,128)(2,1)} %get-tuple-element.59, bf16[2048,2048]{1,0:T(8,128)(2,1)} %all-gather.14.cloned.1.call-done, bf16[1024,2048]{1,0:T(8,128)(2,1)} %all-gather.12.cloned.1.call-done), kind=kOutput, calls=%fused_computation.8 | convolution fusion | flops 8621391872 | bytes 29360128 | tf_op jit(solution)/shard_map/dot_general | solution.py:36
  575.5 8.2 pad_maximum_fusion.a_ref
  583.6 103.8 %units_back.1 = f32[256,2048]{1,0:T(8,128)} custom-call(bf16[2048,2048]{1,0:T(8,128)(2,1)} %pad_maximum_fusion.a_ref, bf16[2048,2048]{1,0:T(8,128)(2,1)} %all-gather.10.cloned.1.call-done.w_ref), custom_call_target="tpu_custom_call" | custom-call | flops 17179869184 | bytes 201326592 | tf_op jit(solution)/shard_map/units_back/pallas_call | solution.py:574
  691.6 72.9 %branch_back.1 = (bf16[2,1024,2048]{2,1,0:T(8,128)(2,1)}, bf16[2,1024,256]{2,1,0:T(8,128)(2,1)}) custom-call(bf16[256,2048]{1,0:T(8,128)(2,1)} %fusion.24.x_ref, bf16[256,2048]{1,0:T(8,128)(2,1)} %all-gather.8.cloned.1.call-done.w_ref), custom_call_target="tpu_custom_call" | custom-call | flops 2147483648 | bytes 201326592 | tf_op jit(solution)/shard_map/branch_back/pallas_call | solution.py:526
  764.5 6.7 fusion.8
  771.3 14.0 %convolution_convert_fusion.2 = bf16[1024,2048]{1,0:T(8,128)(2,1)} fusion(bf16[2048,1024]{1,0:T(8,128)(2,1)} %get-tuple-element.58, bf16[2048,2048]{1,0:T(8,128)(2,1)} %all-gather.14.cloned.1.call-done), kind=kOutput, calls=%fused_computation.15 | convolution fusion | flops 8592031744 | bytes 16777216 | tf_op jit(solution)/shard_map/dot_general | solution.py:30
  785.4 14.0 %convolution_convert_fusion.1 = bf16[2048,2048]{1,0:T(8,128)(2,1)} fusion(bf16[2048,1024]{1,0:T(8,128)(2,1)} %get-tuple-element.58, bf16[1024,2048]{1,0:T(8,128)(2,1)} %all-gather.12.cloned.1.call-done), kind=kOutput, calls=%fused_computation.13 | convolution fusion | flops 8594128896 | bytes 16777216 | tf_op jit(solution)/shard_map/dot_general | solution.py:42
  800.6 40.4 %attend_back.1 = (bf16[2,1024,256]{2,1,0:T(8,128)(2,1)S(1)}, f32[2,2048,256]{2,1,0:T(8,128)}, f32[2,2048,256]{2,1,0:T(8,128)}) custom-call(bf16[2,1024,256]{2,1,0:T(8,128)(2,1)S(1)} %copy-done, bf16[2,2048,512]{2,1,0:T(8,128)(2,1)} %copy-done.4, bf16[2,2048,512]{2,1,0:T(8,128)(2,1)} %copy-done.4, s32[2,1,1024]{2,1,0:T(1,128)S(1)} %maximum_subtract_fusion.low_ref, ...), custom_call_target="tpu_custom_call" | custom-call | tf_op jit(solution)/shard_map/attend_back/pallas_call | solution.py:168
  846.2 57.2 %collective-permute-done.1 = bf16[2,1024,512]{2,1,0:T(8,128)(2,1)S(1)} collective-permute-done((bf16[2,1024,512]{2,1,0:T(8,128)(2,1)S(1)}, bf16[2,1024,512]{2,1,0:T(8,128)(2,1)S(1)}, u32[]{:S(2)}, u32[]{:S(2)}) %collective-permute-start.1) | collective-permute-done | bytes 2097184 | tf_op jit(solution)/shard_map/ppermute | solution.py:830
  904.8 10.5 bitcast_convert_fusion
  915.7 23.9 %convolution_convert_fusion = bf16[2048,2048]{1,0:T(8,128)(2,1)} fusion(bf16[2048,2048]{1,0:T(8,128)(2,1)} %bitcast.122, bf16[2048,1024]{1,0:T(8,128)(2,1)} %get-tuple-element.80, bf16[2048,1024]{1,0:T(8,128)(2,1)} %get-tuple-element.79), kind=kOutput, calls=%fused_computation.12 | convolution fusion | flops 17200840704 | bytes 25165824 | tf_op jit(solution)/shard_map/dot_general | solution.py:30
  941.6 94.7 %heads_back.1 = f32[256,2048]{1,0:T(8,128)} custom-call(bf16[2,1024,768]{2,1,0:T(8,128)(2,1)} %pad_maximum_fusion.1.a_ref, bf16[2048,768]{1,0:T(8,128)(2,1)} %all-gather.6.cloned.1.call-done.w_ref), custom_call_target="tpu_custom_call" | custom-call | flops 6442450944 | bytes 201326592 | tf_op jit(solution)/shard_map/heads_back/pallas_call | solution.py:574
  1039.6 10.4 gain_grads.1
  1053.4 2.8 convert_element_type.166
  1056.2 5.9 fusion.10
  1062.1 44.0 %reduce-scatter.10.cloned.1.call-done = bf16[512,2048]{1,0:T(8,128)(2,1)} async-done(((bf16[2048,2048]{1,0:T(8,128)(2,1)}), bf16[512,2048]{1,0:T(8,128)(2,1)}) %reduce-scatter.10.cloned.1.call-update) | async-done | bytes 2097168 | tf_op jit(solution)/shard_map/reduce_scatter | solution.py:823
  1106.0 66.5 %weight_grads.1 = (bf16[8,64,768]{2,1,0:T(8,128)(2,1)}, bf16[8,64,2048]{2,1,0:T(8,128)(2,1)}) custom-call(bf16[8,64,768]{2,1,0:T(8,128)(2,1)} %bitcast.120, bf16[8,64,2048]{2,1,0:T(8,128)(2,1)} %bitcast.109), custom_call_target="tpu_custom_call" | custom-call | bytes 115343360 | tf_op jit(solution)/shard_map/weight_grads/pallas_call | solution.py:640
  1180.5 3.3 slice_convert_fusion.2
  1183.8 3.3 reshape.359
  1187.1 2.8 copy.50
  1189.9 2.5 copy.57
  1194.4 2.8 copy.49
  1197.2 2.5 copy.56
  (153 shorter events, 58.0 us)
Async XLA Ops:
  7.2 4.9 copy-start.18
  7.2 123.7 %all-gather.6.cloned.1.call-start = ((), (), s32[]{:S(2)}) async-start(), calls=%async_computation.5 | async-start | bytes 3932160 | tf_op jit(solution)/shard_map/all_gather | solution.py:787
  8.9 4.9 copy-start.14
  85.8 2.8 copy-start.27
  85.8 2.8 copy-start.28
  85.8 15.6 %copy-start.7 = (bf16[2,128,2048]{2,1,0:T(8,128)(2,1)S(1)}, bf16[2,128,2048]{2,1,0:T(8,128)(2,1)}, u32[]{:S(2)}) copy-start(bf16[2,128,2048]{2,1,0:T(8,128)(2,1)} %param.16) | copy-start | bytes 3145732
  85.8 240.4 %all-gather.8.cloned.1.call-start = ((), (), s32[]{:S(2)}) async-start(), calls=%async_computation.6 | async-start | bytes 1310720 | tf_op jit(solution)/shard_map/all_gather | solution.py:779
  86.6 390.8 %all-gather.10.cloned.1.call-start = ((), (), s32[]{:S(2)}) async-start(), calls=%async_computation.7 | async-start | bytes 10485760 | tf_op jit(solution)/shard_map/all_gather | solution.py:788
  87.3 467.5 %all-gather.12.cloned.1.call-start = ((), (), s32[]{:S(2)}) async-start(), calls=%async_computation.8 | async-start | bytes 5242880 | tf_op jit(solution)/shard_map/all_gather | solution.py:777
  87.9 467.0 %all-gather.14.cloned.1.call-start = ((), (), s32[]{:S(2)}) async-start(), calls=%async_computation.10 | async-start | bytes 9437184 | tf_op jit(solution)/shard_map/all_gather | solution.py:776
  88.5 961.6 %reduce-scatter.12.cloned.1.call-start = ((), (), s32[]{:S(2)}) async-start(), calls=%async_computation.13 | async-start | bytes 1310720 | tf_op jit(solution)/shard_map/reduce_scatter | solution.py:823
  101.3 104.1 %copy-start.19 = (f32[2048]{0:T(1024)}, f32[2048]{0:T(1024)S(1)}, u32[]{:S(2)}) copy-start(f32[2048]{0:T(1024)S(1)} %mul.153) | copy-start | bytes 24580
  101.6 29.3 %copy-start.24 = (f32[2,128]{1,0:T(2,128)}, f32[2,128]{1,0:T(2,128)S(1)}, u32[]{:S(2)}) copy-start(f32[2,128]{1,0:T(2,128)S(1)} %fusion.17) | copy-start | bytes 3076
  101.6 29.2 %copy-start.21 = (f32[256]{0:T(256)}, f32[256]{0:T(256)S(1)}, u32[]{:S(2)}) copy-start(f32[256]{0:T(256)S(1)} %bitcast_rsqrt_fusion) | copy-start | bytes 3076
  102.9 107.4 %copy-start.26 = (s32[2,4]{1,0:T(2,128)S(1)}, s32[2,4]{1,0:T(2,128)}, u32[]{:S(2)}) copy-start(s32[2,4]{1,0:T(2,128)} %param.18) | copy-start | bytes 100
  205.4 87.4 %copy-start.13 = (bf16[2,1024,512]{2,1,0:T(8,128)(2,1)S(1)}, bf16[2,1024,512]{2,1,0:T(8,128)(2,1)}, u32[]{:S(2)}) copy-start(bf16[2,1024,512]{2,1,0:T(8,128)(2,1)} %get-tuple-element.55) | copy-start | bytes 6291460
  205.5 85.6 %collective-permute-start = (bf16[2,1024,512]{2,1,0:T(8,128)(2,1)}, bf16[2,1024,512]{2,1,0:T(8,128)(2,1)}, u32[]{:S(2)}, u32[]{:S(2)}) collective-permute-start(bf16[2,1024,512]{2,1,0:T(8,128)(2,1)} %get-tuple-element.55), channel_id=1, source_target_pairs={{0,8},{8,16},{16,24},{1,9},{9,17},{17,25},{2,10},{10,18},{18,26},{... | collective-permute-start | bytes 6291464 | tf_op jit(solution)/shard_map/ppermute | solution.py:802
  475.9 214.0 %copy-start.5 = (f32[256,2048]{1,0:T(8,128)}, f32[256,2048]{1,0:T(8,128)S(1)}, u32[]{:S(2)}) copy-start(f32[256,2048]{1,0:T(8,128)S(1)} %get-tuple-element.78) | copy-start | bytes 6291460
  687.5 2.5 copy-start.10
  691.6 72.9 %copy-start.2 = (bf16[2,1024,256]{2,1,0:T(8,128)(2,1)S(1)}, bf16[2,1024,256]{2,1,0:T(8,128)(2,1)}, u32[]{:S(2)}) copy-start(bf16[2,1024,256]{2,1,0:T(8,128)(2,1)} %copy-done.1) | copy-start | bytes 3145732
  771.2 282.2 %reduce-scatter.14.cloned.1.call-start = ((), (), s32[]{:S(2)}) async-start(), calls=%async_computation.14 | async-start | bytes 5242880 | tf_op jit(solution)/shard_map/reduce_scatter | solution.py:823
  785.3 270.9 %reduce-scatter.6.cloned.1.call-start = ((), (), s32[]{:S(2)}) async-start(), calls=%async_computation.9 | async-start | bytes 9437184 | tf_op jit(solution)/shard_map/reduce_scatter | solution.py:813
  799.4 262.7 %reduce-scatter.8.cloned.1.call-start = ((), (), s32[]{:S(2)}) async-start(), calls=%async_computation.11 | async-start | bytes 3932160 | tf_op jit(solution)/shard_map/reduce_scatter | solution.py:823
  844.4 59.5 %copy-start.12 = (f32[2,2048,256]{2,1,0:T(8,128)S(1)}, f32[2,2048,256]{2,1,0:T(8,128)}, u32[]{:S(2)}) copy-start(f32[2,2048,256]{2,1,0:T(8,128)} %get-tuple-element.65) | copy-start | bytes 12582916
  844.6 59.4 %copy-start.11 = (f32[2,2048,256]{2,1,0:T(8,128)S(1)}, f32[2,2048,256]{2,1,0:T(8,128)}, u32[]{:S(2)}) copy-start(f32[2,2048,256]{2,1,0:T(8,128)} %get-tuple-element.64) | copy-start | bytes 12582916
  844.6 58.8 %collective-permute-start.1 = (bf16[2,1024,512]{2,1,0:T(8,128)(2,1)S(1)}, bf16[2,1024,512]{2,1,0:T(8,128)(2,1)S(1)}, u32[]{:S(2)}, u32[]{:S(2)}) collective-permute-start(bf16[2,1024,512]{2,1,0:T(8,128)(2,1)S(1)} %pad_maximum_fusion.3), channel_id=1, source_target_pairs={{8,0},{16,8},{24,16},{9,1},{17,9},{25,17},{10,2},{18,10},{26,18},{... | collective-permute-start | bytes 6291464 | tf_op jit(solution)/shard_map/ppermute | solution.py:830
  915.3 190.7 %reduce-scatter.10.cloned.1.call-start = ((), (), s32[]{:S(2)}) async-start(), calls=%async_computation.12 | async-start | bytes 10485760 | tf_op jit(solution)/shard_map/reduce_scatter | solution.py:823
  941.5 94.7 %copy-start.8 = (bf16[2,128,2048]{2,1,0:T(8,128)(2,1)S(1)}, bf16[2,128,2048]{2,1,0:T(8,128)(2,1)}, u32[]{:S(2)}) copy-start(bf16[2,128,2048]{2,1,0:T(8,128)(2,1)} %param.16) | copy-start | bytes 3145732
  941.5 94.7 %copy-start.20 = (f32[2048]{0:T(1024)S(1)}, f32[2048]{0:T(1024)}, u32[]{:S(2)}) copy-start(f32[2048]{0:T(1024)} %copy-done.19) | copy-start | bytes 24580
  941.5 94.7 %copy-start.22 = (f32[256]{0:T(256)S(1)}, f32[256]{0:T(256)}, u32[]{:S(2)}) copy-start(f32[256]{0:T(256)} %copy-done.21) | copy-start | bytes 3076
  1036.3 17.1 %copy-start.25 = (f32[2,128]{1,0:T(2,128)S(1)}, f32[2,128]{1,0:T(2,128)}, u32[]{:S(2)}) copy-start(f32[2,128]{1,0:T(2,128)} %copy-done.24) | copy-start | bytes 3076
  1036.3 19.9 %copy-start.6 = (f32[256,2048]{1,0:T(8,128)S(1)}, f32[256,2048]{1,0:T(8,128)}, u32[]{:S(2)}) copy-start(f32[256,2048]{1,0:T(8,128)} %copy-done.5) | copy-start | bytes 6291460
  (9 other events, 13.8 us)
Sparse Core Ops, SparseCore 0:
  85.9 44.8 all-gather.5
  132.7 26.6 all-gather.7
  161.2 124.0 all-gather.9
  287.0 55.4 all-gather.11
  344.0 127.1 all-gather.13
  771.3 33.2 reduce-scatter.11
  807.9 61.2 reduce-scatter.13
  871.5 87.3 reduce-scatter.5
  961.9 53.3 reduce-scatter.7
  1018.2 87.7 reduce-scatter.9

commit v2 on v1

v2 whole, which is shorter than its diff:
```python
import functools

import jax
import jax.numpy as jnp
from jax import lax
from jax.experimental import pallas as pl
from jax.experimental.pallas import tpu as pltpu
from jax.sharding import PartitionSpec as P

HEAD = 64
FF = 8192
WINDOW = 1024
PAIR = 128
TILE = 512
LOW = -1e30
EPS = 1e-05
MESH = pl.DeviceIdType.MESH
MIB = 2**20


def to_half(values):
    return values.astype(jnp.bfloat16)


def normalize(values, gain):
    return values * lax.rsqrt(jnp.mean(values * values, axis=-1, keepdims=True) + EPS) * gain


def contract_rows(left, right):
    return lax.dot_general(
        left, right, (((0,), (0,)), ((), ())), preferred_element_type=jnp.float32
    )


def dot_nt(left, right):
    return lax.dot_general(
        left, right, (((1,), (1,)), ((), ())), preferred_element_type=jnp.float32
    )


def dot_nn(left, right):
    return jnp.dot(left, right, preferred_element_type=jnp.float32)


def gate_back(gate, up, d_hidden):
    sigma = jax.nn.sigmoid(gate)
    d_gate = d_hidden * up * sigma * (1.0 + gate * (1.0 - sigma))
    d_up = d_hidden * gate * sigma
    return (to_half(d_gate), to_half(d_up))


def head_lanes(values, half):
    lane = lax.broadcasted_iota(jnp.int32, values.shape, 1)
    return jnp.where((lane >= HEAD) == (half == 1), values, jnp.zeros_like(values))


def masked_scores(k_rows, q_head, low):
    keys, block = k_rows.shape[0], q_head.shape[0]
    scores = dot_nt(k_rows, q_head)
    at = lax.broadcasted_iota(jnp.int32, (keys, block), 0)
    query = lax.broadcasted_iota(jnp.int32, (keys, block), 1)
    seen = (at >= low) & (at <= query + WINDOW)
    return jnp.where(seen, scores, LOW)


class Line:
    def __init__(self, chips):
        self.chips = chips
        self.own = lax.axis_index("fsdp")
        self.chip = self.own // 2
        self.core = lax.rem(self.own, 2)
        self.other = self.own + 1 - 2 * self.core
        self.has_left = self.chip > 0
        self.has_right = self.chip < chips - 1

    def greet(self):
        signal_group(self.other)
        pl.when(self.has_left)(lambda: signal_group(self.own - 2))
        pl.when(self.has_right)(lambda: signal_group(self.own + 2))
        return 1 + self.has_left.astype(jnp.int32) + self.has_right.astype(jnp.int32)


def signal_group(peer):
    barrier = pltpu.get_barrier_semaphore()
    pl.semaphore_signal(barrier, inc=1, device_id={"fsdp": peer}, device_id_type=MESH)


def signal_seq(peer):
    barrier = pltpu.get_barrier_semaphore()
    pl.semaphore_signal(barrier, inc=1, device_id={"seq": peer}, device_id_type=MESH)


def greet_group(group):
    own = lax.axis_index("fsdp")
    pl.loop(1, group)(lambda ahead: signal_group(lax.rem(own + ahead, group)))
    return group - 1


def greet_seq(seqs):
    own = lax.axis_index("seq")
    pl.loop(1, seqs)(lambda ahead: signal_seq(lax.rem(own + ahead, seqs)))
    return seqs - 1


def meet(count):
    pl.semaphore_wait(pltpu.get_barrier_semaphore(), count)


def rows_at(index, size):
    return pl.ds(pl.multiple_of(index * size, size), size)


class Spread:
    def __init__(self, line, first, buf, send, recv):
        self.line, self.first, self.buf, self.send, self.recv = line, first, buf, send, recv

    def move(self, slot, way, peer, source=None):
        return pltpu.make_async_remote_copy(
            src_ref=self.buf.at[slot] if source is None else source,
            dst_ref=self.buf.at[slot],
            send_sem=self.send.at[way, slot],
            recv_sem=self.recv.at[slot],
            device_id={"fsdp": peer},
            device_id_type=MESH,
        )

    def begin(self):
        line = self.line
        pl.when(line.has_right)(lambda: self.move(line.own, 1, line.own + 2, self.first).start())
        pl.when(line.has_left)(lambda: self.move(line.own, 0, line.own - 2, self.first).start())
        self.move(line.own, 2, line.other, self.first).start()

    def relay(self, far):
        line = self.line

        @pl.when(line.chip - far >= 0)
        def _():
            slot = (line.chip - far) * 2 + line.core
            self.move(slot, 1, line.own).wait_recv()
            pl.when(line.has_right)(lambda: self.move(slot, 1, line.own + 2).start())
            self.move(slot, 2, line.other).start()

        @pl.when(line.chip + far < line.chips)
        def _():
            slot = (line.chip + far) * 2 + line.core
            self.move(slot, 0, line.own).wait_recv()
            pl.when(line.has_left)(lambda: self.move(slot, 0, line.own - 2).start())
            self.move(slot, 2, line.other).start()

    def each(self, far, use):
        line = self.line

        @pl.loop(0, 4)
        def _(turn):
            side = lax.rem(turn, 2)
            across = turn // 2
            away = far - across
            source = line.chip + away * (2 * side - 1)
            valid = (away >= 0) & (away < line.chips) & (source >= 0) & (source < line.chips)
            valid = valid & ((side == 0) | (away > 0))

            @pl.when(valid)
            def _():
                slot = source * 2 + line.core + across * (1 - 2 * line.core)
                pl.when(across == 1)(lambda: self.move(slot, 2, line.own).wait_recv())
                use(slot)

    def whole(self, use):
        @pl.loop(0, self.line.chips + 1)
        def _(far):
            pl.when(far > 0)(lambda: self.relay(far))
            self.each(far, use)

    def rest(self):
        pl.loop(0, self.line.chips)(
            lambda place: self.move(place * 2 + 1 - self.line.core, 2, self.line.own).wait_recv()
        )

    def sent(self):
        line = self.line

        @pl.loop(0, line.chips)
        def _(place):
            slot = place * 2 + line.core
            self.move(slot, 2, line.other).wait_send()
            pl.when(line.has_right & (place <= line.chip))(
                lambda: self.move(slot, 1, line.own + 2).wait_send()
            )
            pl.when(line.has_left & (place >= line.chip))(
                lambda: self.move(slot, 0, line.own - 2).wait_send()
            )


class Reduce:
    def __init__(self, line, product, out, acc, cross_out, line_out, cross_in, line_in, send, recv):
        self.line, self.product, self.out, self.acc = line, product, out, acc
        self.cross_out, self.line_out, self.cross_in, self.line_in = cross_out, line_out, cross_in, line_in
        self.send, self.recv = send, recv

    @staticmethod
    def scratch(chips, rows, width):
        part = pltpu.VMEM((chips, rows, width), jnp.bfloat16)
        return [
            pltpu.VMEM((rows, width), jnp.float32),
            part,
            part,
            part,
            pltpu.VMEM((chips + 1, rows, width), jnp.bfloat16),
            pltpu.SemaphoreType.DMA((2, chips)),
            pltpu.SemaphoreType.DMA((2, chips + 1)),
        ]

    def cross(self, place):
        return pltpu.make_async_remote_copy(
            src_ref=self.cross_out.at[place],
            dst_ref=self.cross_in.at[place],
            send_sem=self.send.at[0, place],
            recv_sem=self.recv.at[0, place],
            device_id={"fsdp": self.line.other},
            device_id_type=MESH,
        )

    def along(self, place, landing, peer):
        return pltpu.make_async_remote_copy(
            src_ref=self.line_out.at[place],
            dst_ref=self.line_in.at[landing],
            send_sem=self.send.at[1, place],
            recv_sem=self.recv.at[1, landing],
            device_id={"fsdp": peer},
            device_id_type=MESH,
        )

    def steps(self):
        return 2 * self.line.chips - 1

    def step(self, step):
        line, acc = self.line, self.acc
        tiles = acc.shape[1] // TILE
        away = line.chips - 1 - step // 2
        side = lax.rem(step, 2)
        place = line.chip + away * (1 - 2 * side)

        @pl.when((place >= 0) & (place < line.chips))
        def _():
            @pl.loop(0, tiles)
            def _(tile):
                got = self.product(place * 2 + 1 - line.core, tile)
                self.cross_out[place, :, rows_at(tile, TILE)] = to_half(got)

            self.cross(place).start()

            @pl.loop(0, tiles)
            def _(tile):
                acc[:, rows_at(tile, TILE)] = self.product(place * 2 + line.core, tile)

            self.cross(place).wait_recv()

            @pl.when(away > 0)
            def _():
                rightward = side == 0
                upstream = (rightward & line.has_left) | (jnp.logical_not(rightward) & line.has_right)

                @pl.when(upstream)
                def _():
                    self.along(place, place, line.own).wait_recv()
                    self.line_out[place] = to_half(
                        acc[...]
                        + self.cross_in[place].astype(jnp.float32)
                        + self.line_in[place].astype(jnp.float32)
                    )

                @pl.when(jnp.logical_not(upstream))
                def _():
                    self.line_out[place] = to_half(
                        acc[...] + self.cross_in[place].astype(jnp.float32)
                    )

                @pl.when(rightward)
                def _():
                    self.along(place, place, line.own + 2).start()

                @pl.when(jnp.logical_not(rightward))
                def _():
                    landing = jnp.where(away == 1, line.chips, place)
                    self.along(place, landing, line.own - 2).start()

            @pl.when(away == 0)
            def _():
                self.out[...] = acc[...] + self.cross_in[place].astype(jnp.float32)

                @pl.when(line.has_left)
                def _():
                    self.along(place, place, line.own).wait_recv()
                    self.out[...] += self.line_in[place].astype(jnp.float32)

                @pl.when(line.has_right)
                def _():
                    self.along(place, line.chips, line.own).wait_recv()
                    self.out[...] += self.line_in[line.chips].astype(jnp.float32)

    def sent(self):
        @pl.loop(0, self.line.chips)
        def _(place):
            self.cross(place).wait_send()
            pl.when(place != self.line.chip)(
                lambda: self.along(place, place, self.line.own).wait_send()
            )


class Swap:
    def __init__(self, group, source, target, send, recv, keep):
        self.group, self.source, self.target = group, source, target
        self.send, self.recv, self.keep = send, recv, keep
        self.own = lax.axis_index("fsdp")

    def move(self, peer, source):
        return pltpu.make_async_remote_copy(
            src_ref=self.source.at[peer],
            dst_ref=self.target.at[source],
            send_sem=self.send.at[peer],
            recv_sem=self.recv.at[source],
            device_id={"fsdp": peer},
            device_id_type=MESH,
        )

    def kept(self):
        return pltpu.make_async_copy(self.source.at[self.own], self.target.at[self.own], self.keep)

    def begin(self):
        self.kept().start()
        pl.loop(1, self.group)(
            lambda ahead: self.move(lax.rem(self.own + ahead, self.group), self.own).start()
        )

    def end(self):
        self.kept().wait()

        @pl.loop(1, self.group)
        def _(ahead):
            peer = lax.rem(self.own + ahead, self.group)
            self.move(peer, peer).wait_recv()
            self.move(peer, self.own).wait_send()


class Share:
    def __init__(self, seqs, source, target, send, recv, keep):
        self.seqs, self.source, self.target = seqs, source, target
        self.send, self.recv, self.keep = send, recv, keep
        self.own = lax.axis_index("seq")

    def move(self, peer, place):
        return pltpu.make_async_remote_copy(
            src_ref=self.source,
            dst_ref=self.target.at[place],
            send_sem=self.send.at[peer],
            recv_sem=self.recv.at[place],
            device_id={"seq": peer},
            device_id_type=MESH,
        )

    def kept(self):
        return pltpu.make_async_copy(self.source, self.target.at[self.own], self.keep)

    def begin(self):
        self.kept().start()
        pl.loop(1, self.seqs)(
            lambda ahead: self.move(lax.rem(self.own + ahead, self.seqs), self.own).start()
        )

    def end(self):
        self.kept().wait()

        @pl.loop(1, self.seqs)
        def _(ahead):
            peer = lax.rem(self.own + ahead, self.seqs)
            self.move(peer, peer).wait_recv()
            self.move(peer, self.own).wait_send()


VMEM_SPEC = pl.BlockSpec(memory_space=pltpu.VMEM)
ANY_SPEC = pl.BlockSpec(memory_space=pl.ANY)


def comm_params(collective, mib=58):
    return pltpu.CompilerParams(
        collective_id=collective, has_side_effects=True, vmem_limit_bytes=mib * MIB
    )


def cost(flops, local, remote):
    return pl.CostEstimate(
        flops=flops, bytes_accessed=local, transcendentals=0, remote_bytes_transferred=remote
    )


def sems(*shape):
    return pltpu.SemaphoreType.DMA(shape)


def start_kernel(
    seqs, chips, batches, tile_ref, x_ref, blocks_ref, g_ref, q_ref, kv_ref, gains_ref, w_out_ref,
    buf, normed, gain, gains, w, send, recv, keep, swap_send, share_send, w_recv,
    tile_send, tile_across, tile_recv, tile_back, w_keep, gain_keep,
):
    line = Line(chips)
    group = 2 * chips
    seq = lax.axis_index("seq")
    own = line.own
    share = blocks_ref.shape[1]
    piece = x_ref.shape[0] // batches
    span = q_ref.shape[2]
    width = x_ref.shape[1]
    per = 128 * seqs * group // width
    meet(greet_group(group) + greet_seq(seqs))

    def block_at(run, member):
        return w.at[rows_at(run * group + member, share)]

    def block_swap(peer, member):
        return pltpu.make_async_remote_copy(
            src_ref=blocks_ref.at[peer],
            dst_ref=block_at(seq, member),
            send_sem=swap_send.at[peer],
            recv_sem=w_recv.at[seq, member],
            device_id={"fsdp": peer},
            device_id_type=MESH,
        )

    def block_share(run, member, peer):
        return pltpu.make_async_remote_copy(
            src_ref=block_at(run, member),
            dst_ref=block_at(run, member),
            send_sem=share_send.at[peer, member],
            recv_sem=w_recv.at[run, member],
            device_id={"seq": peer},
            device_id_type=MESH,
        )

    def tile_to_seq(peer, place):
        return pltpu.make_async_remote_copy(
            src_ref=tile_ref.at[0],
            dst_ref=gains.at[own, place],
            send_sem=tile_send.at[peer],
            recv_sem=tile_recv.at[place],
            device_id={"seq": peer},
            device_id_type=MESH,
        )

    def tiles_to_group(peer, member):
        return pltpu.make_async_remote_copy(
            src_ref=gains.at[member],
            dst_ref=gains.at[member],
            send_sem=tile_across.at[peer],
            recv_sem=tile_back.at[member],
            device_id={"fsdp": peer},
            device_id_type=MESH,
        )

    def others(count, me, act):
        pl.loop(1, count)(lambda ahead: act(lax.rem(me + ahead, count)))

    others(seqs, seq, lambda peer: tile_to_seq(peer, seq).start())
    others(group, own, lambda peer: block_swap(peer, own).start())
    spread = Spread(line, x_ref, buf, send, recv)
    spread.begin()
    gains[own, seq] = tile_ref[0]
    w[rows_at(seq * group + own, share), :] = blocks_ref[own]
    others(seqs, seq, lambda peer: block_share(seq, own, peer).start())
    buf[own] = x_ref[...]
    others(seqs, seq, lambda peer: tile_to_seq(peer, peer).wait_recv())
    others(group, own, lambda peer: tiles_to_group(peer, own).start())

    def pass_block(member):
        block_swap(member, member).wait_recv()
        others(seqs, seq, lambda peer: block_share(seq, member, peer).start())

    others(group, own, pass_block)
    others(group, own, lambda peer: tiles_to_group(peer, peer).wait_recv())
    for column in range(width // 128):
        total = 0.0
        for place in range(column * per, (column + 1) * per):
            total = total + gains[place % group, place // group, 0:1, :]
        gain[0:1, column * 128 : (column + 1) * 128] = total

    def kept(slot, batch):
        return pltpu.make_async_copy(
            normed.at[slot, pl.ds(batch * piece, piece)],
            g_ref.at[batch, rows_at(slot, piece)],
            keep.at[slot, batch],
        )

    def use(slot):
        @pl.loop(0, x_ref.shape[0] // 16)
        def _(chunk):
            rows = rows_at(chunk, 16)
            values = buf[slot, rows, :].astype(jnp.float32)
            normed[slot, rows, :] = to_half(normalize(values, gain[0:1, :]))

        for batch in range(batches):
            kept(slot, batch).start()
        rows = rows_at(slot, piece)
        values = normed[slot]
        for part in range(3):
            got = to_half(dot_nn(values, w[:, part * span : (part + 1) * span]))
            for batch in range(batches):
                mine = got[batch * piece : (batch + 1) * piece]
                if part == 0:
                    q_ref[batch, rows, :] = mine
                else:
                    kv_ref[batch, rows, (part - 1) * span : part * span] = mine

    pl.loop(1, chips - 1)(spread.relay)

    def have_block(run, member):
        block_share(run, member, seq).wait_recv()

    others(seqs, seq, lambda run: pl.loop(0, group)(lambda member: have_block(run, member)))
    w_kept = pltpu.make_async_copy(w, w_out_ref, w_keep)
    w_kept.start()
    gains_kept = pltpu.make_async_copy(gains, gains_ref, gain_keep)
    gains_kept.start()

    pl.loop(0, chips - 1)(lambda far: spread.each(far, use))
    spread.relay(chips - 1)
    spread.each(chips - 1, use)
    spread.each(chips, use)
    spread.sent()
    others(seqs, seq, lambda peer: tile_to_seq(peer, seq).wait_send())
    others(group, own, lambda peer: block_swap(peer, own).wait_send())
    others(group, own, lambda peer: tiles_to_group(peer, own).wait_send())
    others(
        seqs,
        seq,
        lambda peer: pl.loop(0, group)(lambda member: block_share(seq, member, peer).wait_send()),
    )
    w_kept.wait()
    gains_kept.wait()

    @pl.loop(0, group)
    def _(slot):
        for batch in range(batches):
            kept(slot, batch).wait()


def start(seqs, chips, batches, tile, x, blocks, collective):
    rows, width = x.shape
    group = 2 * chips
    length = group * rows // batches
    share, cols = blocks.shape[1:]
    span = cols // 3
    half = jnp.bfloat16
    return pl.pallas_call(
        functools.partial(start_kernel, seqs, chips, batches),
        out_shape=[
            jax.ShapeDtypeStruct((batches, length, width), half),
            jax.ShapeDtypeStruct((batches, length, span), half),
            jax.ShapeDtypeStruct((batches, length, 2 * span), half),
            jax.ShapeDtypeStruct((group, seqs, 8, 128), jnp.float32),
            jax.ShapeDtypeStruct((width, cols), half),
        ],
        in_specs=[VMEM_SPEC] * 3,
        out_specs=[ANY_SPEC, VMEM_SPEC, VMEM_SPEC, ANY_SPEC, ANY_SPEC],
        scratch_shapes=[
            pltpu.VMEM((group, rows, width), half),
            pltpu.VMEM((group, rows, width), half),
            pltpu.VMEM((8, width), jnp.float32),
            pltpu.VMEM((group, seqs, 8, 128), jnp.float32),
            pltpu.VMEM((width, cols), half),
            sems(3, group),
            sems(group),
            sems(group, batches),
            sems(group),
            sems(seqs, group),
            sems(seqs, group),
            sems(seqs),
            sems(group),
            sems(seqs),
            sems(group),
            pltpu.SemaphoreType.DMA,
            pltpu.SemaphoreType.DMA,
        ],
        compiler_params=comm_params(collective),
        cost_estimate=cost(2 * group * rows * width * cols, 200 * MIB, group * rows * width * 2),
        name="start",
    )(tile, x, blocks)


def attend_kernel(
    seqs, group, block, q_ref, kv_ref, low_ref, units_ref, out_ref, lse_ref, pad_ref, own_units_ref,
    pad, vt, halo_send, halo_recv, pad_keep, swap_send, swap_recv, swap_keep,
):
    seq = lax.axis_index("seq")
    batches, length, span = q_ref.shape
    has_left, has_right = seq > 0, seq < seqs - 1
    pl.when(has_left)(lambda: signal_seq(seq - 1))
    pl.when(has_right)(lambda: signal_seq(seq + 1))
    meet(greet_group(group) + has_left.astype(jnp.int32) + has_right.astype(jnp.int32))

    def halo(batch, peer):
        return pltpu.make_async_remote_copy(
            src_ref=kv_ref.at[batch, pl.ds(length - WINDOW, WINDOW)],
            dst_ref=pad.at[batch, pl.ds(0, WINDOW)],
            send_sem=halo_send.at[batch],
            recv_sem=halo_recv.at[batch],
            device_id={"seq": peer},
            device_id_type=MESH,
        )

    for batch in range(batches):
        pl.when(has_right)(lambda batch=batch: halo(batch, seq + 1).start())
    swap = Swap(group, units_ref, own_units_ref, swap_send, swap_recv, swap_keep)
    swap.begin()
    pad[:, WINDOW:, :] = kv_ref[...]

    @pl.when(jnp.logical_not(has_left))
    def _():
        pad[:, :WINDOW, :] = jnp.zeros((batches, WINDOW, 2 * span), jnp.bfloat16)

    def kept(batch):
        return pltpu.make_async_copy(pad.at[batch], pad_ref.at[batch], pad_keep.at[batch])

    for batch in range(batches):
        pl.when(has_left)(lambda batch=batch: halo(batch, seq).wait_recv())
        kept(batch).start()
        vt[...] = pad[batch, :, span:].T

        @pl.loop(0, length // block)
        def _(step, batch=batch):
            begin = pl.multiple_of(step * block, block)
            keys = pl.ds(begin, block + WINDOW)
            rows = pl.ds(begin, block)
            low = low_ref[batch, :, rows]
            for pair in range(span // PAIR):
                lanes = slice(pair * PAIR, (pair + 1) * PAIR)
                q_pair = q_ref[batch, rows, lanes] * jnp.asarray(HEAD**-0.5, jnp.bfloat16)
                k_rows = pad[batch, keys, lanes]
                values = vt[lanes, keys]
                mixed = []
                for half in range(2):
                    scores = masked_scores(k_rows, head_lanes(q_pair, half), low)
                    top = jnp.max(scores, axis=0, keepdims=True)
                    expo = jnp.exp(scores - top)
                    total = jnp.sum(expo, axis=0, keepdims=True)
                    mixed.append(dot_nn(values, to_half(expo)) / total)
                    row = pair * 2 + half
                    lse_ref[batch, row : row + 1, rows] = top + jnp.log(total)
                lane = lax.broadcasted_iota(jnp.int32, mixed[0].shape, 0)
                out_ref[batch, rows, lanes] = to_half(jnp.where(lane < HEAD, mixed[0], mixed[1]).T)

    for batch in range(batches):
        kept(batch).wait()
        pl.when(has_right)(lambda batch=batch: halo(batch, seq + 1).wait_send())
    swap.end()


def attend(seqs, group, query, key_value, low, block, units, collective):
    batches, length, span = query.shape
    padded = length + WINDOW
    heads = span // HEAD
    half = jnp.bfloat16
    return pl.pallas_call(
        functools.partial(attend_kernel, seqs, group, block),
        in_specs=[VMEM_SPEC, VMEM_SPEC, VMEM_SPEC, ANY_SPEC],
        out_specs=[VMEM_SPEC, VMEM_SPEC, ANY_SPEC, ANY_SPEC],
        out_shape=[
            jax.ShapeDtypeStruct((batches, length, span), half),
            jax.ShapeDtypeStruct((batches, heads, length), jnp.float32),
            jax.ShapeDtypeStruct((batches, padded, 2 * span), half),
            jax.ShapeDtypeStruct(units.shape, half),
        ],
        scratch_shapes=[
            pltpu.VMEM((batches, padded, 2 * span), half),
            pltpu.VMEM((span, padded), half),
            sems(batches),
            sems(batches),
            sems(batches),
            sems(group),
            sems(group),
            pltpu.SemaphoreType.DMA,
        ],
        compiler_params=comm_params(collective),
        cost_estimate=cost(
            8 * batches * length * span * (WINDOW + block), 150 * MIB, units.size * 2
        ),
        name="attend",
    )(query, key_value, low, units)


def left_rows(a_ref, slot, rows):
    if len(a_ref.shape) == 2:
        return a_ref[rows_at(slot, rows), :]
    piece = rows // a_ref.shape[0]
    return jnp.concatenate(
        [a_ref[batch, rows_at(slot, piece), :] for batch in range(a_ref.shape[0])], axis=0
    )


def branch_kernel(
    seqs, chips, a_ref, w_ref, d_ref, units_ref, out_ref, gd_ref, w_units_ref,
    acc, cross_out, line_out, cross_in, line_in, sum_send, sum_recv,
    send, recv, d_keep, share_send, share_recv, share_keep,
):
    line = Line(chips)
    rows = out_ref.shape[0]

    def product(slot, tile):
        return dot_nn(left_rows(a_ref, slot, rows), w_ref[:, rows_at(tile, TILE)])

    meet(line.greet() + greet_seq(seqs))
    reduce = Reduce(
        line, product, out_ref, acc, cross_out, line_out, cross_in, line_in, sum_send, sum_recv
    )
    spread = Spread(line, d_ref, gd_ref, send, recv)
    units = Share(seqs, units_ref, w_units_ref, share_send, share_recv, share_keep)
    d_kept = pltpu.make_async_copy(d_ref, gd_ref.at[line.own], d_keep)
    units.begin()
    spread.begin()
    d_kept.start()

    @pl.loop(0, reduce.steps())
    def _(step):
        reduce.step(step)
        pl.when(lax.rem(step, 2) == 1)(lambda: spread.relay((step + 1) // 2))

    spread.rest()
    spread.sent()
    reduce.sent()
    d_kept.wait()
    units.end()


def branch_sum(seqs, chips, a, w, d_rows, units, collective):
    rows, width = d_rows.shape
    group = 2 * chips
    half = jnp.bfloat16
    return pl.pallas_call(
        functools.partial(branch_kernel, seqs, chips),
        out_shape=[
            jax.ShapeDtypeStruct((rows, width), jnp.float32),
            jax.ShapeDtypeStruct((group, rows, width), half),
            jax.ShapeDtypeStruct((seqs,) + units.shape, half),
        ],
        in_specs=[VMEM_SPEC, VMEM_SPEC, ANY_SPEC, ANY_SPEC],
        out_specs=[VMEM_SPEC, ANY_SPEC, ANY_SPEC],
        scratch_shapes=Reduce.scratch(chips, rows, width)
        + [sems(3, group), sems(group), pltpu.SemaphoreType.DMA]
        + [sems(seqs), sems(seqs), pltpu.SemaphoreType.DMA],
        compiler_params=comm_params(collective),
        cost_estimate=cost(
            2 * group * rows * width * w.shape[0], 250 * MIB, 3 * group * rows * width * 2
        ),
        name="branch_sum",
    )(a, w, d_rows, units)


def units_kernel(
    chips, x_ref, w_ref, wd_ref, gd_ref, g_ref, hidden_ref, d_ref, buf, d_buf, send, recv, keep, d_sem
):
    line = Line(chips)
    rows = x_ref.shape[0]
    units = hidden_ref.shape[1]
    part = min(units, 256)
    meet(line.greet())
    spread = Spread(line, x_ref, buf, send, recv)
    spread.begin()
    buf[line.own] = x_ref[...]

    def kept(slot):
        return pltpu.make_async_copy(buf.at[slot], g_ref.at[slot], keep.at[slot])

    def use(slot):
        kept(slot).start()
        fetch = pltpu.make_async_copy(gd_ref.at[slot], d_buf, d_sem)
        fetch.start()
        fetch.wait()
        place = rows_at(slot, rows)

        @pl.loop(0, units // part)
        def _(tile):
            here = rows_at(tile, part)
            there = rows_at(units // part + tile, part)
            values = buf[slot]
            gate = dot_nn(values, w_ref[:, here])
            up = dot_nn(values, w_ref[:, there])
            d_hidden = dot_nt(d_buf[...], wd_ref[here, :])
            sigma = jax.nn.sigmoid(gate)
            swish = gate * sigma
            hidden_ref[place, here] = to_half(swish * up)
            d_ref[place, here] = to_half(d_hidden * up * sigma * (1.0 + gate * (1.0 - sigma)))
            d_ref[place, there] = to_half(d_hidden * swish)

    spread.whole(use)
    spread.sent()
    pl.loop(0, 2 * chips)(lambda slot: kept(slot).wait())


def hidden_units(chips, x, w, wd, group_d, collective):
    rows, width = x.shape
    group = 2 * chips
    units = wd.shape[0]
    half = jnp.bfloat16
    return pl.pallas_call(
        functools.partial(units_kernel, chips),
        out_shape=[
            jax.ShapeDtypeStruct((group, rows, width), half),
            jax.ShapeDtypeStruct((group * rows, units), half),
            jax.ShapeDtypeStruct((group * rows, 2 * units), half),
        ],
        in_specs=[VMEM_SPEC, VMEM_SPEC, VMEM_SPEC, ANY_SPEC],
        out_specs=[ANY_SPEC, VMEM_SPEC, VMEM_SPEC],
        scratch_shapes=[
            pltpu.VMEM((group, rows, width), half),
            pltpu.VMEM((rows, width), half),
            sems(3, group),
            sems(group),
            sems(group),
            pltpu.SemaphoreType.DMA,
        ],
        compiler_params=comm_params(collective),
        cost_estimate=cost(
            6 * group * rows * width * units, 200 * MIB, group * rows * width * 2
        ),
        name="hidden_units",
    )(x, w, wd, group_d)


def branch_back_kernel(
    chips, batches, x_ref, w_ref, hidden_ref, wd_ref, g_ref, d_ref, out_ref,
    acc, cross_out, line_out, cross_in, line_in, sum_send, sum_recv, buf, send, recv, keep,
):
    line = Line(chips)
    rows = x_ref.shape[0]
    piece = rows // batches

    def product(slot, tile):
        return dot_nn(left_rows(hidden_ref, slot, rows), wd_ref[:, rows_at(tile, TILE)])

    meet(line.greet())
    spread = Spread(line, x_ref, buf, send, recv)
    reduce = Reduce(
        line, product, out_ref, acc, cross_out, line_out, cross_in, line_in, sum_send, sum_recv
    )
    spread.begin()
    buf[line.own] = x_ref[...]

    def kept(slot, batch):
        return pltpu.make_async_copy(
            buf.at[slot, pl.ds(batch * piece, piece)],
            g_ref.at[batch, rows_at(slot, piece)],
            keep.at[slot, batch],
        )

    def use(slot):
        for batch in range(batches):
            kept(slot, batch).start()
        got = to_half(dot_nt(buf[slot], w_ref[...]))
        for batch in range(batches):
            d_ref[batch, rows_at(slot, piece), :] = got[batch * piece : (batch + 1) * piece]

    @pl.loop(0, reduce.steps())
    def _(step):
        reduce.step(step)

        @pl.when(lax.rem(step, 2) == 1)
        def _():
            far = (step + 1) // 2
            spread.relay(far)
            spread.each(far - 1, use)

    spread.each(chips - 1, use)
    spread.each(chips, use)
    spread.sent()
    reduce.sent()

    @pl.loop(0, 2 * chips)
    def _(slot):
        for batch in range(batches):
            kept(slot, batch).wait()


def branch_back(chips, batches, x, w, hidden, wd, collective):
    rows, width = x.shape
    group = 2 * chips
    length = group * rows // batches
    span = w.shape[0]
    half = jnp.bfloat16
    return pl.pallas_call(
        functools.partial(branch_back_kernel, chips, batches),
        out_shape=[
            jax.ShapeDtypeStruct((batches, length, width), half),
            jax.ShapeDtypeStruct((batches, length, span), half),
            jax.ShapeDtypeStruct((rows, width), jnp.float32),
        ],
        in_specs=[VMEM_SPEC] * 4,
        out_specs=[ANY_SPEC, VMEM_SPEC, VMEM_SPEC],
        scratch_shapes=Reduce.scratch(chips, rows, width)
        + [
            pltpu.VMEM((group, rows, width), half),
            sems(3, group),
            sems(group),
            sems(group, batches),
        ],
        compiler_params=comm_params(collective, 62),
        cost_estimate=cost(
            2 * group * rows * width * (span + wd.shape[0]), 250 * MIB, 2 * group * rows * width * 2
        ),
        name="branch_back",
    )(x, w, hidden, wd)


def sum_kernel(chips, a_ref, w_ref, out_ref, *scratch):
    line = Line(chips)
    rows = out_ref.shape[0]

    def product(slot, tile):
        return dot_nt(left_rows(a_ref, slot, rows), w_ref[rows_at(tile, TILE), :])

    meet(line.greet())
    reduce = Reduce(line, product, out_ref, *scratch)
    pl.loop(0, reduce.steps())(reduce.step)
    reduce.sent()


def sum_products(chips, a, w, name, collective):
    group = 2 * chips
    width, depth = w.shape
    rows = a.size // depth // group
    return pl.pallas_call(
        functools.partial(sum_kernel, chips),
        out_shape=jax.ShapeDtypeStruct((rows, width), jnp.float32),
        in_specs=[VMEM_SPEC, VMEM_SPEC],
        out_specs=VMEM_SPEC,
        scratch_shapes=Reduce.scratch(chips, rows, width),
        compiler_params=comm_params(collective),
        cost_estimate=cost(2 * group * rows * width * depth, 200 * MIB, group * rows * width * 2),
        name=name,
    )(a, w)


def swap_kernel(group, count, *refs):
    sources, targets = refs[:count], refs[count : 2 * count]
    send, recv, keep = refs[2 * count :]
    meet(greet_group(group))
    swaps = [
        Swap(group, sources[item], targets[item], send.at[item], recv.at[item], keep.at[item])
        for item in range(count)
    ]
    for item in swaps:
        item.begin()
    for item in swaps:
        item.end()


def swap_blocks(group, arrays, name, collective):
    count = len(arrays)
    return pl.pallas_call(
        functools.partial(swap_kernel, group, count),
        out_shape=[jax.ShapeDtypeStruct(item.shape, item.dtype) for item in arrays],
        in_specs=[ANY_SPEC] * count,
        out_specs=[ANY_SPEC] * count,
        scratch_shapes=[sems(count, group), sems(count, group), sems(count)],
        compiler_params=comm_params(collective, 16),
        cost_estimate=cost(0, 150 * MIB, sum(item.size * 2 for item in arrays)),
        name=name,
    )(*arrays)


def tiles_kernel(seqs, group, x_ref, out_ref, send, recv):
    devices = seqs * group
    own = lax.axis_index("seq") * group + lax.axis_index("fsdp")
    barrier = pltpu.get_barrier_semaphore()

    def place(peer):
        return {"seq": peer // group, "fsdp": lax.rem(peer, group)}

    @pl.loop(1, devices)
    def _(ahead):
        peer = lax.rem(own + ahead, devices)
        pl.semaphore_signal(barrier, inc=1, device_id=place(peer), device_id_type=MESH)

    meet(devices - 1)
    out_ref[own] = x_ref[own]

    def move(peer, source):
        return pltpu.make_async_remote_copy(
            src_ref=x_ref.at[peer],
            dst_ref=out_ref.at[source],
            send_sem=send.at[peer],
            recv_sem=recv.at[source],
            device_id=place(peer),
            device_id_type=MESH,
        )

    pl.loop(1, devices)(lambda ahead: move(lax.rem(own + ahead, devices), own).start())

    @pl.loop(1, devices)
    def _(ahead):
        peer = lax.rem(own + ahead, devices)
        move(peer, peer).wait_recv()
        move(peer, own).wait_send()


def swap_tiles(seqs, group, x, name, collective):
    devices = seqs * group
    return pl.pallas_call(
        functools.partial(tiles_kernel, seqs, group),
        out_shape=jax.ShapeDtypeStruct((devices, 8, 128), jnp.float32),
        in_specs=[VMEM_SPEC],
        out_specs=VMEM_SPEC,
        scratch_shapes=[sems(devices), sems(devices)],
        compiler_params=comm_params(collective, 16),
        name=name,
    )(x)


def attend_back_kernel(
    block, q_ref, k_ref, v_ref, low_ref, lse_ref, d_ref, dq_ref, dk_ref, dv_ref, kt_ref
):
    step = pl.program_id(1)
    span = q_ref.shape[2]
    scale = jnp.asarray(HEAD**-0.5, jnp.bfloat16)

    @pl.when(step == 0)
    def _():
        kt_ref[...] = k_ref[0].T * scale
        dk_ref[...] = jnp.zeros_like(dk_ref)
        dv_ref[...] = jnp.zeros_like(dv_ref)

    begin = pl.multiple_of(step * block, block)
    keys = pl.ds(begin, block + WINDOW)
    low = low_ref[0]
    for pair in range(span // PAIR):
        lanes = slice(pair * PAIR, (pair + 1) * PAIR)
        q_pair = q_ref[0, :, lanes] * scale
        d_pair = d_ref[0, :, lanes]
        k_rows = k_ref[0, keys, lanes]
        v_rows = v_ref[0, keys, lanes]
        kt = kt_ref[lanes, keys]
        back = []
        for half in range(2):
            row = pair * 2 + half
            q_head = head_lanes(q_pair, half)
            d_head = head_lanes(d_pair, half)
            scores = masked_scores(k_rows, q_head, low)
            probs = jnp.exp(scores - lse_ref[0, row : row + 1, :])
            d_probs = dot_nt(v_rows, d_head)
            along = jnp.sum(probs * d_probs, axis=0, keepdims=True)
            d_scores = (probs * (d_probs - along)).astype(jnp.bfloat16)
            dv_ref[0, keys, lanes] += dot_nn(probs.astype(jnp.bfloat16), d_head)
            dk_ref[0, keys, lanes] += dot_nn(d_scores, q_head)
            back.append(dot_nn(kt, d_scores))
        at = lax.broadcasted_iota(jnp.int32, back[0].shape, 0)
        dq_ref[0, :, lanes] = jnp.where(at < HEAD, back[0], back[1]).T.astype(jnp.bfloat16)


def attend_back(query, kv_pad, low, lse, d_att, block):
    batches, length, span = query.shape
    padded = kv_pad.shape[1]
    heads = span // HEAD
    rows = pl.BlockSpec((1, block, span), lambda b, i: (b, i, 0))
    whole = pl.BlockSpec((1, padded, span), lambda b, i: (b, 0, 0))
    return pl.pallas_call(
        functools.partial(attend_back_kernel, block),
        grid=(batches, length // block),
        in_specs=[
            rows,
            whole,
            pl.BlockSpec((1, padded, span), lambda b, i: (b, 0, 1)),
            pl.BlockSpec((1, 1, block), lambda b, i: (b, 0, i)),
            pl.BlockSpec((1, heads, block), lambda b, i: (b, 0, i)),
            rows,
        ],
        out_specs=[rows, whole, whole],
        out_shape=[
            jax.ShapeDtypeStruct((batches, length, span), jnp.bfloat16),
            jax.ShapeDtypeStruct((batches, padded, span), jnp.float32),
            jax.ShapeDtypeStruct((batches, padded, span), jnp.float32),
        ],
        scratch_shapes=[pltpu.VMEM((span, padded), jnp.bfloat16)],
        compiler_params=pltpu.CompilerParams(vmem_limit_bytes=48 * 2**20),
        name="attend_back",
    )(query, kv_pad, kv_pad, low, lse, d_att)


def doc_starts(lengths, positions, batches, seq_len):
    table = lengths.reshape(batches, -1, lengths.shape[1])
    starts = jnp.cumsum(table, axis=2) - table
    per_batch = seq_len // table.shape[1]
    begins = (starts + (jnp.arange(table.shape[1], dtype=jnp.int32) * per_batch)[None, :, None]).reshape(
        batches, -1
    )
    before = begins[:, None, :] <= positions[None, :, None]
    return jnp.max(jnp.where(before, begins[:, None, :], 0), axis=2)


def body(
    tokens,
    cotangent,
    lengths,
    gain_attn,
    w_query,
    w_key,
    w_value,
    w_out,
    gain_mlp,
    w_gate,
    w_up,
    w_down,
):
    batches, piece, width = tokens.shape
    seqs = lax.axis_size("seq")
    group = lax.axis_size("fsdp")
    chips = group // 2
    devices = seqs * group
    seq_len = piece * devices
    rows = batches * piece
    share = w_query.shape[0]
    span = width // group
    length = group * piece
    group_rows = group * rows
    units = FF // group
    aligned = share == HEAD
    member = lax.axis_index("fsdp")

    def blocks(weight):
        part = weight.shape[1] // devices
        if part < HEAD:
            return weight.reshape(share, group, -1).transpose(1, 0, 2)
        return weight.reshape(share, seqs, group, part).transpose(2, 0, 1, 3).reshape(group, share, -1)

    def unblock(cols, total):
        part = total // devices
        if part < HEAD:
            return cols.transpose(1, 0, 2).reshape(share, total)
        return cols.reshape(group, share, seqs, part).transpose(1, 2, 0, 3).reshape(share, total)

    inputs = tokens.astype(jnp.float32).reshape(rows, width)
    upstream = cotangent.astype(jnp.float32).reshape(rows, width)
    wd_part = lax.all_gather(w_down, "seq", axis=0, tiled=True)
    if aligned:
        wo_part = lax.all_gather(w_out, "seq", axis=0, tiled=True)
    else:
        wo_all = lax.all_gather(w_out, ("seq", "fsdp"), axis=0, tiled=True)
        wo_part = lax.dynamic_slice_in_dim(wo_all, member * span, span, 0)

    attn_blocks = jnp.concatenate([blocks(w_query), blocks(w_key), blocks(w_value)], axis=2)
    unit_blocks = jnp.concatenate([blocks(w_gate), blocks(w_up)], axis=2)
    group_start = lax.axis_index("seq") * length
    positions = group_start + jnp.arange(length, dtype=jnp.int32)
    begins = doc_starts(lengths, positions, batches, seq_len)
    at = jnp.arange(length, dtype=jnp.int32)
    block = min(256, length)
    low = jnp.maximum(begins - group_start + WINDOW, at[None, :] + 1) - (at // block * block)[None, :]
    low = low[:, None, :]

    lane = jnp.arange(128, dtype=jnp.int32)
    device = lax.axis_index("seq") * group + member
    fold = 128 // share
    here = lane // share == lax.rem(device, fold)
    both = jnp.stack([gain_attn, gain_mlp]).astype(jnp.float32)
    tile = jnp.where(here[None], jnp.tile(both, (1, fold)), 0.0)
    tile = jnp.pad(tile, ((0, 6), (0, 0)))[None]
    group_a, query, key_value, gains, w_heads = start(
        seqs, chips, batches, tile, tokens.reshape(rows, width), attn_blocks, 1
    )
    gains = gains.transpose(1, 0, 2, 3).reshape(devices // fold, fold, 8, 128).sum(axis=1)
    gain_one = gains[:, 0].reshape(width)
    gain_two = gains[:, 1].reshape(width)
    attended, lse, kv_pad, unit_own = attend(
        seqs, group, query, key_value, low, block, unit_blocks, 2
    )
    branch, group_d, w_units = branch_sum(
        seqs, chips, attended, wo_part, cotangent.reshape(rows, width),
        unit_own.reshape(group * share, -1), 3,
    )
    w_units = w_units.reshape(width, -1)
    middle = inputs + branch
    normed_b = to_half(normalize(middle, gain_two))
    group_b, hidden, d_units = hidden_units(chips, normed_b, w_units, wd_part, group_d, 4)
    group_d = group_d.reshape(group_rows, width)
    d_normed_b = sum_products(chips, d_units, w_units, "units_back", 5)
    mlp_pull = jax.vjp(normalize, middle, gain_two)[1]
    d_middle_norm, gain_two_grad = mlp_pull(d_normed_b)
    d_middle = upstream + d_middle_norm
    d_branch = to_half(d_middle)

    def over_seq(values):
        return lax.psum_scatter(to_half(values), "seq", scatter_dimension=0, tiled=True)

    down_sum = over_seq(contract_rows(hidden, group_d))
    unit_sums = over_seq(contract_rows(group_b.reshape(group_rows, width), d_units))

    group_branch, d_attended, mlp_out = branch_back(
        chips, batches, d_branch, wo_part, hidden, wd_part, 6
    )
    outputs = middle + mlp_out
    d_query, d_key_pad, d_value_pad = attend_back(query, kv_pad, low, lse, d_attended, block)
    behind = [(source + 1, source) for source in range(seqs - 1)]
    back = lax.ppermute(
        to_half(jnp.concatenate([d_key_pad[:, :WINDOW], d_value_pad[:, :WINDOW]], axis=2)),
        "seq",
        behind,
    ).astype(jnp.float32)
    back = jnp.pad(back, ((0, 0), (length - WINDOW, 0), (0, 0)))
    d_heads = jnp.concatenate(
        [
            d_query,
            to_half(d_key_pad[:, WINDOW:] + back[:, :, :span]),
            to_half(d_value_pad[:, WINDOW:] + back[:, :, span:]),
        ],
        axis=2,
    )
    d_normed_a = sum_products(chips, d_heads, w_heads, "heads_back", 7)
    flat_a = group_a.reshape(group_rows, width)
    out_grad = contract_rows(
        attended.reshape(group_rows, span), group_branch.reshape(group_rows, width)
    )
    if aligned:
        out_sum = over_seq(out_grad)
    else:
        whole = lax.dynamic_update_slice_in_dim(
            jnp.zeros((width, width), jnp.bfloat16), to_half(out_grad), member * span, 0
        )
        out_sum = lax.psum_scatter(whole, ("seq", "fsdp"), scatter_dimension=0, tiled=True)
    head_sums = over_seq(contract_rows(flat_a, d_heads.reshape(group_rows, 3 * span)))
    head_cols, unit_cols = swap_blocks(
        group,
        [head_sums.reshape(group, share, -1), unit_sums.reshape(group, share, -1)],
        "weight_grads",
        8,
    )

    attn_pull = jax.vjp(normalize, inputs, gain_one)[1]
    d_input_norm, gain_one_grad = attn_pull(d_normed_a)
    input_grad = (d_middle + d_input_norm).reshape(batches, piece, width)
    layer_out = to_half(outputs).reshape(batches, piece, width)

    def lanes(values):
        return jnp.pad(values.reshape(devices, 1, share), ((0, 0), (0, 7), (0, 64 - share)))

    grad_tiles = jnp.concatenate([lanes(gain_one_grad), lanes(gain_two_grad)], axis=2)
    grad_sums = jnp.sum(swap_tiles(seqs, group, grad_tiles, "gain_grads", 9)[:, 0], axis=0)

    def whole_rows(cols, part, total):
        size = total // group
        return unblock(cols[:, :, part * size : (part + 1) * size], total).astype(jnp.float32)

    return (
        layer_out,
        input_grad,
        grad_sums[:share],
        whole_rows(head_cols, 0, width),
        whole_rows(head_cols, 1, width),
        whole_rows(head_cols, 2, width),
        out_sum.astype(jnp.float32),
        grad_sums[64 : 64 + share],
        whole_rows(unit_cols, 0, FF),
        whole_rows(unit_cols, 1, FF),
        down_sum.astype(jnp.float32),
    )


def solution(mesh):
    spread = ("seq", "fsdp")
    tokens, rows, gains = P(None, spread, None), P(spread, None), P(spread)
    in_specs = (tokens, tokens, P(), gains, rows, rows, rows, rows, gains, rows, rows, rows)
    out_specs = (tokens, tokens, gains, rows, rows, rows, rows, gains, rows, rows, rows)
    return jax.shard_map(body, mesh=mesh, in_specs=in_specs, out_specs=out_specs, check_vma=False)
```

time: 1210 us -> 1010 us (0.83)
  waiting for transfers between devices: 212 us -> 60 us
  matrix products: 89.7 us -> 55 us
    ppermute x1 -> x0, waiting for transfers between devices: 80.3 us -> none  [body(): tail = lax.ppermute(key_value[:, length - WINDOW:], 'seq', ahead)]
    pallas_call x2 -> x1, Pallas kernels: 133 us -> 65.9 us  [swap_blocks(): pl.pallas_call(functools.partial(swap_kernel, group, count), out_shape=[j...]
    reduce_scatter x4, waiting for transfers between devices: 44 us -> 0.03 us  [over_seq(): lax.psum_scatter(to_half(values), 'seq', scatter_dimension=0, tiled=True)]
    pallas_call x1, Pallas kernels: 72.9 us -> 108 us  [branch_back(): pl.pallas_call(functools.partial(branch_back_kernel, chips, batches), out...]
    dot_general x2 -> x0, matrix products: 34.6 us -> none  [the longest x1 20.6 us: dot_nt(): lax.dot_general(left, right, (((1,), (1,)), ((), ())), preferred_element_...]
    all_gather x3 -> x0, waiting for transfers between devices: 28 us -> none  [the longest x1 27.9 us: body(): lax.all_gather(attn_own.reshape(group * share, -1), 'seq', axis=0, tiled=...]
    pallas_call x7 -> x6, Pallas kernels: 472 us -> 488 us  [the longest x2 201 us: sum_products(): pl.pallas_call(functools.partial(sum_kernel, chips), out_shape=jax.ShapeD...]
  transfers between devices with their start and end apart: 12 -> 7, of which waited for: 4 -> 1; matrix products, arithmetic and copies ran while one was open for 8% -> 9% of each run, Pallas kernels for 40% -> 42%
where the time goes in v2:
time: 1010 us; the launch traced here: 1000 us
  Pallas kernels  785 us (78%)
  waiting for transfers between devices  60 us (6%)
  matrix products  55 us (5%)
  local copies, waits for them, and re-layouts  50.6 us (5%)
  other arithmetic  35.2 us (3%)
  between operations  15.1 us (1%)
    pallas_call x2, Pallas kernels, sum_products(): pl.pallas_call(functools.partial(sum_kernel, chips), out_shape=jax.ShapeD...  201 us
    pallas_call x1, Pallas kernels, branch_sum(): pl.pallas_call(functools.partial(branch_kernel, seqs, chips), out_shape=[...  118 us
    pallas_call x1, Pallas kernels, branch_back(): pl.pallas_call(functools.partial(branch_back_kernel, chips, batches), out...  108 us
    pallas_call x1, Pallas kernels, start(): pl.pallas_call(functools.partial(start_kernel, seqs, chips, batches), out...  99.3 us
    pallas_call x1, Pallas kernels, hidden_units(): pl.pallas_call(functools.partial(units_kernel, chips), out_shape=[jax.Sha...  82.8 us
    pallas_call x1, Pallas kernels, swap_blocks(): pl.pallas_call(functools.partial(swap_kernel, group, count), out_shape=[j...  65.9 us
    pallas_call x1, Pallas kernels, attend(): pl.pallas_call(functools.partial(attend_kernel, seqs, group, block), in_s...  61.5 us
    ppermute x1, waiting for transfers between devices, body(): lax.ppermute(to_half(jnp.concatenate([d_key_pad[:, :WINDOW], d_value_pad[...  58.6 us
  transfers between devices with their start and end apart: 7, of which 1 were waited for; matrix products, arithmetic and copies ran while one was open for 9% of the time, Pallas kernels for 42%

profile of v2, /device:TPU:9, one launch (start us, length us, event | category | flops | bytes accessed | tf_op | source)
XLA Modules:
  0.0 1003.3 jit_solution(18062051447233145712)
XLA Ops:
  20.2 2.0 pad_maximum_fusion.3.blocks_ref
  22.2 99.3 %start.1 = (bf16[2,1024,2048]{2,1,0:T(8,128)(2,1)}, bf16[2,1024,256]{2,1,0:T(8,128)(2,1)}, bf16[2,1024,512]{2,1,0:T(8,128)(2,1)}, f32[8,4,8,128]{3,2,1,0:T(8,128)}, bf16[2048,768]{1,0:T(8,128)(2,1)}) custom-call(f32[1,8,128]{2,1,0:T(8,128)} %pad_bitcast_fusion.tile_ref, bf16[256,2048]{1,0:T(8,128)(2,1)} %bitcast.97, ...), custom_call_target="tpu_custom_call" | custom-call | flops 6442450944 | bytes 209715200 | tf_op jit(solution)/shard_map/start/pallas_call | solution.py:552
  124.7 61.5 %attend.1 = (bf16[2,1024,256]{2,1,0:T(8,128)(2,1)}, f32[2,4,1024]{2,1,0:T(4,128)}, bf16[2,2048,512]{2,1,0:T(8,128)(2,1)}, bf16[8,64,2048]{2,1,0:T(8,128)(2,1)}) custom-call(bf16[2,1024,256]{2,1,0:T(8,128)(2,1)} %get-tuple-element.34.q_ref, bf16[2,1024,512]{2,1,0:T(8,128)(2,1)} %get-tuple-element.35.kv_ref, s32[2,1,1024]{2,1,0:T(1,128)} %maximum_subtract_fusion.low_ref, ...), custom_call_target="tpu_custom_call" | custom-call | flops 5368709120 | bytes 157286400 | tf_op jit(solution)/shard_map/attend/pallas_call | solution.py:661
  186.2 117.5 %branch_sum.1 = (f32[256,2048]{1,0:T(8,128)}, bf16[8,256,2048]{2,1,0:T(8,128)(2,1)}, bf16[4,512,2048]{2,1,0:T(8,128)(2,1)}) custom-call(bf16[2,1024,256]{2,1,0:T(8,128)(2,1)} %get-tuple-element.36.a_ref, bf16[256,2048]{1,0:T(8,128)(2,1)} %all-gather.3.cloned.1.call-done.w_ref, bf16[256,2048]{1,0:T(8,128)(2,1)} %bitcast.102, bf16[512,2048]{1,0:T(8,128)(2,1)} %bitcast.133), custom_call_target="tpu_custom_call" | custom-call | flops 2147483648 | bytes 262144000 | tf_op jit(solution)/shard_map/branch_sum/pallas_call | solution.py:736
  303.8 1.9 multiply_reduce_fusion.2
  307.2 82.8 %hidden_units.1 = (bf16[8,256,2048]{2,1,0:T(8,128)(2,1)}, bf16[2048,1024]{1,0:T(8,128)(2,1)}, bf16[2048,2048]{1,0:T(8,128)(2,1)}) custom-call(bf16[256,2048]{1,0:T(8,128)(2,1)} %multiply_convert_fusion.x_ref, bf16[2048,2048]{1,0:T(8,128)(2,1)} %bitcast.131, bf16[1024,2048]{1,0:T(8,128)(2,1)} %all-gather.5.cloned.1.call-done.wd_ref, ...), custom_call_target="tpu_custom_call" | custom-call | flops 25769803776 | bytes 209715200 | tf_op jit(solution)/shard_map/hidden_units/pallas_call | solution.py:802
  389.9 110.8 %units_back.1 = f32[256,2048]{1,0:T(8,128)} custom-call(bf16[2048,2048]{1,0:T(8,128)(2,1)} %get-tuple-element.42.a_ref, bf16[2048,2048]{1,0:T(8,128)(2,1)} %bitcast.132), custom_call_target="tpu_custom_call" | custom-call | flops 17179869184 | bytes 209715200 | tf_op jit(solution)/shard_map/units_back/pallas_call | solution.py:928
  500.7 2.3 multiply_reduce_fusion
  504.8 107.6 %branch_back.1 = (bf16[2,1024,2048]{2,1,0:T(8,128)(2,1)}, bf16[2,1024,256]{2,1,0:T(8,128)(2,1)}, f32[256,2048]{1,0:T(8,128)}) custom-call(bf16[256,2048]{1,0:T(8,128)(2,1)} %fusion.15.x_ref, bf16[256,2048]{1,0:T(8,128)(2,1)} %all-gather.3.cloned.1.call-done.w_ref, bf16[2048,1024]{1,0:T(8,128)(2,1)} %get-tuple-element.43.hidden_ref, ...), custom_call_target="tpu_custom_call" | custom-call | flops 10737418240 | bytes 262144000 | tf_op jit(solution)/shard_map/branch_back/pallas_call | solution.py:887
  612.5 6.7 fusion
  619.4 14.1 %convolution_convert_fusion.1 = bf16[1024,2048]{1,0:T(8,128)(2,1)} fusion(bf16[2048,1024]{1,0:T(8,128)(2,1)} %get-tuple-element.43.hidden_ref, bf16[2048,2048]{1,0:T(8,128)(2,1)} %bitcast.130), kind=kOutput, calls=%fused_computation.2 | convolution fusion | flops 8592031744 | bytes 16777216 | tf_op jit(solution)/shard_map/dot_general | solution.py:30
  635.1 40.3 %attend_back.1 = (bf16[2,1024,256]{2,1,0:T(8,128)(2,1)S(1)}, f32[2,2048,256]{2,1,0:T(8,128)}, f32[2,2048,256]{2,1,0:T(8,128)}) custom-call(bf16[2,1024,256]{2,1,0:T(8,128)(2,1)S(1)} %copy-done.1, bf16[2,2048,512]{2,1,0:T(8,128)(2,1)} %get-tuple-element.45.k_ref.v_ref, bf16[2,2048,512]{2,1,0:T(8,128)(2,1)} %get-tuple-element.45.k_ref.v_ref, ...), custom_call_target="tpu_custom_call" | custom-call | tf_op jit(solution)/shard_map/attend_back/pallas_call | solution.py:1062
  680.9 58.6 %collective-permute-done = bf16[2,1024,512]{2,1,0:T(8,128)(2,1)S(1)} collective-permute-done((bf16[2,1024,512]{2,1,0:T(8,128)(2,1)S(1)}, bf16[2,1024,512]{2,1,0:T(8,128)(2,1)S(1)}, u32[]{:S(2)}, u32[]{:S(2)}) %collective-permute-start) | collective-permute-done | bytes 2097184 | tf_op jit(solution)/shard_map/ppermute | solution.py:1199
  741.8 10.5 %bitcast_convert_fusion = bf16[2048,768]{1,0:T(8,128)(2,1)} fusion(bf16[2,1024,2048]{2,1,0:T(8,128)(2,1)} %get-tuple-element.52, bf16[2,1024,256]{2,1,0:T(8,128)(2,1)S(1)} %get-tuple-element.64, bf16[2,1024,256]{2,1,0:T(8,128)(2,1)S(1)} %get-tuple-element.63, bf16[2,1024,256]{2,1,0:T(8,128)(2,1)S(1)} %get-tuple-element.48), kind=kOutput, calls=%fused_computation.1 | convolution fusion | flops 6453460992 | bytes 14680064 | tf_op jit(solution)/shard_map/dot_general | solution.py:30
  752.3 23.7 %convolution_convert_fusion = bf16[2048,2048]{1,0:T(8,128)(2,1)} fusion(bf16[2048,2048]{1,0:T(8,128)(2,1)} %bitcast.129, bf16[2048,2048]{1,0:T(8,128)(2,1)} %get-tuple-element.42.a_ref), kind=kOutput, calls=%fused_computation | convolution fusion | flops 17184063488 | bytes 25165824 | tf_op jit(solution)/shard_map/dot_general | solution.py:30
  777.7 2.9 pad_maximum_fusion.a_ref
  780.6 90.4 %heads_back.1 = f32[256,2048]{1,0:T(8,128)} custom-call(bf16[2,1024,768]{2,1,0:T(8,128)(2,1)} %pad_maximum_fusion.a_ref, bf16[2048,768]{1,0:T(8,128)(2,1)} %get-tuple-element.51.w_ref), custom_call_target="tpu_custom_call" | custom-call | flops 6442450944 | bytes 209715200 | tf_op jit(solution)/shard_map/heads_back/pallas_call | solution.py:928
  871.0 2.4 fusion.8
  873.7 8.9 gain_grads.1
  882.6 1.8 convert_element_type.136
  885.0 5.9 fusion.2
  891.0 2.8 convert_element_type.146
  896.5 65.9 %weight_grads.1 = (bf16[8,64,768]{2,1,0:T(8,128)(2,1)S(1)}, bf16[8,64,2048]{2,1,0:T(8,128)(2,1)S(1)}) custom-call(bf16[8,64,768]{2,1,0:T(8,128)(2,1)S(1)} %bitcast.96, bf16[8,64,2048]{2,1,0:T(8,128)(2,1)S(1)} %bitcast.95), custom_call_target="tpu_custom_call" | custom-call | bytes 157286400 | tf_op jit(solution)/shard_map/weight_grads/pallas_call | solution.py:956
  966.6 2.4 reshape.328
  972.1 2.4 reshape.327
  977.5 2.4 reshape.326
  979.9 2.5 slice_convert_fusion.2
  982.4 2.5 reshape.335
  986.1 2.5 copy.66
  988.6 2.0 reshape.334
  990.6 2.8 copy.59
  993.4 2.5 copy.65
  (118 shorter events, 45.7 us)
Async XLA Ops:
  7.2 5.9 copy-start.19
  7.2 179.0 %all-gather.3.cloned.1.call-start = ((), (), s32[]{:S(2)}) async-start(), calls=%async_computation.4 | async-start | bytes 1310720 | tf_op jit(solution)/shard_map/all_gather | solution.py:1141
  7.9 299.2 %all-gather.5.cloned.1.call-start = ((), (), s32[]{:S(2)}) async-start(), calls=%async_computation.5 | async-start | bytes 5242880 | tf_op jit(solution)/shard_map/all_gather | solution.py:1139
  8.7 873.9 %reduce-scatter.9.cloned.1.call-start = ((), (), s32[]{:S(2)}) async-start(), calls=%async_computation.8 | async-start | bytes 1310720 | tf_op jit(solution)/shard_map/reduce_scatter | solution.py:1188
  12.5 2.4 copy-start.20
  13.6 3.1 copy-start.17
  16.9 1.2 copy-start.18
  186.2 117.6 %copy-start.9 = (bf16[2,128,2048]{2,1,0:T(8,128)(2,1)S(1)}, bf16[2,128,2048]{2,1,0:T(8,128)(2,1)}, u32[]{:S(2)}) copy-start(bf16[2,128,2048]{2,1,0:T(8,128)(2,1)} %param.12) | copy-start | bytes 3145732
  305.7 197.3 %copy-start.6 = (f32[256,2048]{1,0:T(8,128)}, f32[256,2048]{1,0:T(8,128)S(1)}, u32[]{:S(2)}) copy-start(f32[256,2048]{1,0:T(8,128)S(1)} %get-tuple-element.62) | copy-start | bytes 6291460
  500.7 2.3 copy-start.8
  500.7 2.5 copy-start.12
  504.8 107.6 %copy-start.14 = (bf16[2,1024,256]{2,1,0:T(8,128)(2,1)S(1)}, bf16[2,1024,256]{2,1,0:T(8,128)(2,1)}, u32[]{:S(2)}) copy-start(bf16[2,1024,256]{2,1,0:T(8,128)(2,1)} %get-tuple-element.36.a_ref) | copy-start | bytes 3145732
  619.2 271.7 %reduce-scatter.11.cloned.1.call-start = ((), (), s32[]{:S(2)}) async-start(), calls=%async_computation.9 | async-start | bytes 5242880 | tf_op jit(solution)/shard_map/reduce_scatter | solution.py:1188
  633.5 1.2 copy-start.1
  633.5 1.6 copy-start.2
  633.5 1.6 copy-start.4
  633.6 1.6 copy-start.5
  633.6 260.2 %reduce-scatter.5.cloned.1.call-start = ((), (), s32[]{:S(2)}) async-start(), calls=%async_computation.6 | async-start | bytes 3932160 | tf_op jit(solution)/shard_map/reduce_scatter | solution.py:1188
  678.9 61.1 %copy-start.16 = (f32[2,2048,256]{2,1,0:T(8,128)S(1)}, f32[2,2048,256]{2,1,0:T(8,128)}, u32[]{:S(2)}) copy-start(f32[2,2048,256]{2,1,0:T(8,128)} %get-tuple-element.50) | copy-start | bytes 12582916
  679.1 60.9 %copy-start.15 = (f32[2,2048,256]{2,1,0:T(8,128)S(1)}, f32[2,2048,256]{2,1,0:T(8,128)}, u32[]{:S(2)}) copy-start(f32[2,2048,256]{2,1,0:T(8,128)} %get-tuple-element.49) | copy-start | bytes 12582916
  679.1 60.3 %collective-permute-start = (bf16[2,1024,512]{2,1,0:T(8,128)(2,1)S(1)}, bf16[2,1024,512]{2,1,0:T(8,128)(2,1)S(1)}, u32[]{:S(2)}, u32[]{:S(2)}) collective-permute-start(bf16[2,1024,512]{2,1,0:T(8,128)(2,1)S(1)} %pad_maximum_fusion.2), channel_id=1, source_target_pairs={{8,0},{16,8},{24,16},{9,1},{17,9},{25,17},{10,2},{18,10},{26,18},{... | collective-permute-start | bytes 6291464 | tf_op jit(solution)/shard_map/ppermute | solution.py:1199
  740.8 1.0 copy-start.13
  752.3 141.5 %reduce-scatter.7.cloned.1.call-start = ((), (), s32[]{:S(2)}) async-start(), calls=%async_computation.7 | async-start | bytes 10485760 | tf_op jit(solution)/shard_map/reduce_scatter | solution.py:1188
  776.1 1.2 copy-start.10
  871.0 14.0 %copy-start.7 = (f32[256,2048]{1,0:T(8,128)S(1)}, f32[256,2048]{1,0:T(8,128)}, u32[]{:S(2)}) copy-start(f32[256,2048]{1,0:T(8,128)} %copy-done.6) | copy-start | bytes 6291460
  893.7 1.6 copy-start
  895.3 1.1 copy-start.3
  986.1 2.5 copy-start.11
Sparse Core Ops, SparseCore 0:
  9.9 31.5 all-gather.2
  43.3 69.6 all-gather.4
  619.3 27.2 reduce-scatter.8
  649.7 67.8 reduce-scatter.10
  752.4 44.9 reduce-scatter.4
  800.3 87.7 reduce-scatter.6

commit v3 on v2

--- a/solution.py
+++ b/solution.py
@@ -40,13 +40,6 @@
 
 def dot_nn(left, right):
     return jnp.dot(left, right, preferred_element_type=jnp.float32)
-
-
-def gate_back(gate, up, d_hidden):
-    sigma = jax.nn.sigmoid(gate)
-    d_gate = d_hidden * up * sigma * (1.0 + gate * (1.0 - sigma))
-    d_up = d_hidden * gate * sigma
-    return (to_half(d_gate), to_half(d_up))
 
 
 def head_lanes(values, half):
@@ -202,7 +195,7 @@
         part = pltpu.VMEM((chips, rows, width), jnp.bfloat16)
         return [
             pltpu.VMEM((rows, width), jnp.float32),
-            part,
+            pltpu.VMEM((rows, width), jnp.bfloat16),
             part,
             part,
             pltpu.VMEM((chips + 1, rows, width), jnp.bfloat16),
@@ -212,7 +205,7 @@
 
     def cross(self, place):
         return pltpu.make_async_remote_copy(
-            src_ref=self.cross_out.at[place],
+            src_ref=self.cross_out,
             dst_ref=self.cross_in.at[place],
             send_sem=self.send.at[0, place],
             recv_sem=self.recv.at[0, place],
@@ -245,7 +238,7 @@
             @pl.loop(0, tiles)
             def _(tile):
                 got = self.product(place * 2 + 1 - line.core, tile)
-                self.cross_out[place, :, rows_at(tile, TILE)] = to_half(got)
+                self.cross_out[:, rows_at(tile, TILE)] = to_half(got)
 
             self.cross(place).start()
 
@@ -253,7 +246,7 @@
             def _(tile):
                 acc[:, rows_at(tile, TILE)] = self.product(place * 2 + line.core, tile)
 
-            self.cross(place).wait_recv()
+            self.cross(place).wait()
 
             @pl.when(away > 0)
             def _():
@@ -301,7 +294,6 @@
     def sent(self):
         @pl.loop(0, self.line.chips)
         def _(place):
-            self.cross(place).wait_send()
             pl.when(place != self.line.chip)(
                 lambda: self.along(place, place, self.line.own).wait_send()
             )
@@ -395,6 +387,32 @@
 
 def sems(*shape):
     return pltpu.SemaphoreType.DMA(shape)
+
+
+def left_rows(a_ref, slot, rows):
+    if len(a_ref.shape) == 2:
+        return a_ref[rows_at(slot, rows), :]
+    piece = rows // a_ref.shape[0]
+    return jnp.concatenate(
+        [a_ref[batch, rows_at(slot, piece), :] for batch in range(a_ref.shape[0])], axis=0
+    )
+
+
+def norm_back(rows, v_ref, e_ref, gain_ref, gain_acc, put):
+    gain_acc[...] = jnp.zeros_like(gain_acc)
+
+    @pl.loop(0, rows // 16)
+    def _(chunk):
+        here = rows_at(chunk, 16)
+        values = v_ref[here, :].astype(jnp.float32)
+        error = e_ref[here, :]
+        rate = lax.rsqrt(jnp.mean(values * values, axis=-1, keepdims=True) + EPS)
+        unit = values * rate
+        product = error * unit
+        gain = gain_ref[0:1, :]
+        mean = jnp.mean(product * gain, axis=-1, keepdims=True)
+        gain_acc[...] += product[0:8] + product[8:16]
+        put(here, rate * (gain * error - unit * mean))
 
 
 def start_kernel(
@@ -686,15 +704,6 @@
     )(query, key_value, low, units)
 
 
-def left_rows(a_ref, slot, rows):
-    if len(a_ref.shape) == 2:
-        return a_ref[rows_at(slot, rows), :]
-    piece = rows // a_ref.shape[0]
-    return jnp.concatenate(
-        [a_ref[batch, rows_at(slot, piece), :] for batch in range(a_ref.shape[0])], axis=0
-    )
-
-
 def branch_kernel(
     seqs, chips, a_ref, w_ref, d_ref, units_ref, out_ref, gd_ref, w_units_ref,
     acc, cross_out, line_out, cross_in, line_in, sum_send, sum_recv,
@@ -754,26 +763,39 @@
 
 
 def units_kernel(
-    chips, x_ref, w_ref, wd_ref, gd_ref, g_ref, hidden_ref, d_ref, buf, d_buf, send, recv, keep, d_sem
+    chips, x_ref, w_hbm, wd_hbm, gd_ref, g_ref, hidden_hbm, d_hbm,
+    buf, d_buf, w_ref, wd_ref, hidden_ref, d_ref, send, recv, keep, d_sem, load, store,
 ):
     line = Line(chips)
     rows = x_ref.shape[0]
     units = hidden_ref.shape[1]
     part = min(units, 256)
+    loads = [
+        pltpu.make_async_copy(w_hbm, w_ref, load.at[0]),
+        pltpu.make_async_copy(wd_hbm, wd_ref, load.at[1]),
+    ]
+    for item in loads:
+        item.start()
     meet(line.greet())
     spread = Spread(line, x_ref, buf, send, recv)
     spread.begin()
     buf[line.own] = x_ref[...]
+    for item in loads:
+        item.wait()
 
     def kept(slot):
-        return pltpu.make_async_copy(buf.at[slot], g_ref.at[slot], keep.at[slot])
+        place = rows_at(slot, rows)
+        return [
+            pltpu.make_async_copy(buf.at[slot], g_ref.at[slot], keep.at[slot]),
+            pltpu.make_async_copy(hidden_ref.at[place], hidden_hbm.at[place], store.at[0, slot]),
+            pltpu.make_async_copy(d_ref.at[place], d_hbm.at[place], store.at[1, slot]),
+        ]
 
     def use(slot):
-        kept(slot).start()
         fetch = pltpu.make_async_copy(gd_ref.at[slot], d_buf, d_sem)
         fetch.start()
+        place = rows_at(slot, rows)
         fetch.wait()
-        place = rows_at(slot, rows)
 
         @pl.loop(0, units // part)
         def _(tile):
@@ -789,9 +811,16 @@
             d_ref[place, here] = to_half(d_hidden * up * sigma * (1.0 + gate * (1.0 - sigma)))
             d_ref[place, there] = to_half(d_hidden * swish)
 
+        for item in kept(slot):
+            item.start()
+
     spread.whole(use)
     spread.sent()
-    pl.loop(0, 2 * chips)(lambda slot: kept(slot).wait())
+
+    @pl.loop(0, 2 * chips)
+    def _(slot):
+        for item in kept(slot):
+            item.wait()
 
 
 def hidden_units(chips, x, w, wd, group_d, collective):
@@ -806,15 +835,21 @@
             jax.ShapeDtypeStruct((group * rows, units), half),
             jax.ShapeDtypeStruct((group * rows, 2 * units), half),
         ],
-        in_specs=[VMEM_SPEC, VMEM_SPEC, VMEM_SPEC, ANY_SPEC],
-        out_specs=[ANY_SPEC, VMEM_SPEC, VMEM_SPEC],
+        in_specs=[VMEM_SPEC, ANY_SPEC, ANY_SPEC, ANY_SPEC],
+        out_specs=[ANY_SPEC, ANY_SPEC, ANY_SPEC],
         scratch_shapes=[
             pltpu.VMEM((group, rows, width), half),
             pltpu.VMEM((rows, width), half),
+            pltpu.VMEM(w.shape, half),
+            pltpu.VMEM(wd.shape, half),
+            pltpu.VMEM((group * rows, units), half),
+            pltpu.VMEM((group * rows, 2 * units), half),
             sems(3, group),
             sems(group),
             sems(group),
             pltpu.SemaphoreType.DMA,
+            sems(2),
+            sems(2, group),
         ],
         compiler_params=comm_params(collective),
         cost_estimate=cost(
@@ -824,16 +859,161 @@
     )(x, w, wd, group_d)
 
 
+def units_back_kernel(
+    chips, a_hbm, w_hbm, b_hbm, v_ref, cot_ref, gain_ref, dm_ref, db_ref, gain_grad_ref, grad_hbm,
+    a_ref, w_ref, total, lefts, tiles, load, left_sem, tile_sem,
+    acc, cross_out, line_out, cross_in, line_in, sum_send, sum_recv,
+):
+    line = Line(chips)
+    rows, width = v_ref.shape
+    group = 2 * chips
+    part = lefts.shape[2]
+    loads = [
+        pltpu.make_async_copy(w_hbm, w_ref, load.at[0]),
+        pltpu.make_async_copy(a_hbm, a_ref, load.at[1]),
+    ]
+    for item in loads:
+        item.start()
+
+    def left(tile):
+        slot = lax.rem(tile, 2)
+        return pltpu.make_async_copy(
+            b_hbm.at[:, rows_at(tile, part)], lefts.at[slot], left_sem.at[slot]
+        )
+
+    def stored(tile):
+        slot = lax.rem(tile, 2)
+        return pltpu.make_async_copy(
+            tiles.at[slot], grad_hbm.at[rows_at(tile, part)], tile_sem.at[slot]
+        )
+
+    def weight_grad(tile):
+        left(tile).wait()
+        pl.when(tile + 1 < width // part)(lambda: left(tile + 1).start())
+        pl.when(tile >= 2)(lambda: stored(tile - 2).wait())
+        slot = lax.rem(tile, 2)
+        size = min(TILE, a_ref.shape[1])
+
+        @pl.loop(0, a_ref.shape[1] // size)
+        def _(column):
+            here = rows_at(column, size)
+            tiles[slot, :, here] = to_half(contract_rows(lefts[slot], a_ref[:, here]))
+
+        stored(tile).start()
+
+    def product(slot, tile):
+        return dot_nt(left_rows(a_ref, slot, rows), w_ref[rows_at(tile, TILE), :])
+
+    meet(line.greet())
+    left(0).start()
+    for item in loads:
+        item.wait()
+    reduce = Reduce(
+        line, product, total, acc, cross_out, line_out, cross_in, line_in, sum_send, sum_recv
+    )
+    count = width // part
+    per = -(-count // reduce.steps())
+
+    @pl.loop(0, reduce.steps())
+    def _(step):
+        reduce.step(step)
+
+        @pl.loop(0, per)
+        def _(turn):
+            tile = step * per + turn
+            pl.when(tile < count)(lambda: weight_grad(tile))
+
+    def put(here, d_values):
+        d_middle = cot_ref[here, :].astype(jnp.float32) + d_values
+        dm_ref[here, :] = d_middle
+        db_ref[here, :] = to_half(d_middle)
+
+    norm_back(rows, v_ref, total, gain_ref, gain_grad_ref, put)
+    reduce.sent()
+    stored(count - 2).wait()
+    stored(count - 1).wait()
+
+
+def units_back(chips, a, w, b, middle, cot, gain, collective):
+    rows, width = middle.shape
+    group = 2 * chips
+    half = jnp.bfloat16
+    part = 256 if a.shape[0] <= 2048 else 128
+    return pl.pallas_call(
+        functools.partial(units_back_kernel, chips),
+        out_shape=[
+            jax.ShapeDtypeStruct((rows, width), jnp.float32),
+            jax.ShapeDtypeStruct((rows, width), half),
+            jax.ShapeDtypeStruct((8, width), jnp.float32),
+            jax.ShapeDtypeStruct((width, a.shape[1]), half),
+        ],
+        in_specs=[ANY_SPEC] * 3 + [VMEM_SPEC] * 3,
+        out_specs=[VMEM_SPEC] * 3 + [ANY_SPEC],
+        scratch_shapes=[
+            pltpu.VMEM(a.shape, half),
+            pltpu.VMEM(w.shape, half),
+            pltpu.VMEM((rows, width), jnp.float32),
+            pltpu.VMEM((2, a.shape[0], part), half),
+            pltpu.VMEM((2, part, a.shape[1]), half),
+            sems(2),
+            sems(2),
+            sems(2),
+        ]
+        + Reduce.scratch(chips, rows, width),
+        compiler_params=comm_params(collective, 60),
+        cost_estimate=cost(
+            4 * group * rows * width * a.shape[1], 200 * MIB, group * rows * width * 2
+        ),
+        name="units_back",
+    )(a, w, b.reshape(group * rows, width), middle, cot, gain)
+
+
 def branch_back_kernel(
-    chips, batches, x_ref, w_ref, hidden_ref, wd_ref, g_ref, d_ref, out_ref,
-    acc, cross_out, line_out, cross_in, line_in, sum_send, sum_recv, buf, send, recv, keep,
+    chips, batches, x_ref, w_ref, att_ref, hidden_hbm, wd_hbm, gd_hbm,
+    d_ref, out_ref, out_grad_ref, down_hbm,
+    buf, hidden_ref, wd_ref, rights, tiles, grad_acc, send, recv, load, right_sem, tile_sem,
+    acc, cross_out, line_out, cross_in, line_in, sum_send, sum_recv,
 ):
     line = Line(chips)
     rows = x_ref.shape[0]
     piece = rows // batches
+    width = x_ref.shape[1]
+    part = rights.shape[2]
+    loads = [
+        pltpu.make_async_copy(hidden_hbm, hidden_ref, load.at[0]),
+        pltpu.make_async_copy(wd_hbm, wd_ref, load.at[1]),
+    ]
+    for item in loads:
+        item.start()
 
     def product(slot, tile):
         return dot_nn(left_rows(hidden_ref, slot, rows), wd_ref[:, rows_at(tile, TILE)])
+
+    def right(tile):
+        slot = lax.rem(tile, 2)
+        return pltpu.make_async_copy(
+            gd_hbm.at[:, rows_at(tile, part)], rights.at[slot], right_sem.at[slot]
+        )
+
+    def stored(tile):
+        slot = lax.rem(tile, 2)
+        return pltpu.make_async_copy(
+            tiles.at[slot], down_hbm.at[:, rows_at(tile, part)], tile_sem.at[slot]
+        )
+
+    def weight_grad(tile):
+        right(tile).wait()
+        pl.when(tile + 1 < width // part)(lambda: right(tile + 1).start())
+        pl.when(tile >= 2)(lambda: stored(tile - 2).wait())
+        slot = lax.rem(tile, 2)
+        size = min(256, hidden_ref.shape[1])
+
+        @pl.loop(0, hidden_ref.shape[1] // size)
+        def _(row):
+            here = rows_at(row, size)
+            tiles[slot, here, :] = to_half(contract_rows(hidden_ref[:, here], rights[slot]))
+
+        stored(tile).start()
 
     meet(line.greet())
     spread = Spread(line, x_ref, buf, send, recv)
@@ -841,21 +1021,25 @@
         line, product, out_ref, acc, cross_out, line_out, cross_in, line_in, sum_send, sum_recv
     )
     spread.begin()
+    right(0).start()
     buf[line.own] = x_ref[...]
-
-    def kept(slot, batch):
-        return pltpu.make_async_copy(
-            buf.at[slot, pl.ds(batch * piece, piece)],
-            g_ref.at[batch, rows_at(slot, piece)],
-            keep.at[slot, batch],
-        )
+    grad_acc[...] = jnp.zeros_like(grad_acc)
 
     def use(slot):
-        for batch in range(batches):
-            kept(slot, batch).start()
         got = to_half(dot_nt(buf[slot], w_ref[...]))
         for batch in range(batches):
             d_ref[batch, rows_at(slot, piece), :] = got[batch * piece : (batch + 1) * piece]
+        mixed = left_rows(att_ref, slot, rows)
+
+        @pl.loop(0, width // TILE)
+        def _(tile):
+            here = rows_at(tile, TILE)
+            grad_acc[:, here] += contract_rows(mixed, buf[slot, :, here])
+
+    for item in loads:
+        item.wait()
+    count = width // part
+    per = -(-count // reduce.steps())
 
     @pl.loop(0, reduce.steps())
     def _(step):
@@ -867,219 +1051,385 @@
             spread.relay(far)
             spread.each(far - 1, use)
 
+        @pl.loop(0, per)
+        def _(turn):
+            tile = step * per + turn
+            pl.when(tile < count)(lambda: weight_grad(tile))
+
     spread.each(chips - 1, use)
     spread.each(chips, use)
+    out_grad_ref[...] = to_half(grad_acc[...])
     spread.sent()
     reduce.sent()
-
-    @pl.loop(0, 2 * chips)
-    def _(slot):
-        for batch in range(batches):
-            kept(slot, batch).wait()
-
-
-def branch_back(chips, batches, x, w, hidden, wd, collective):
+    stored(count - 2).wait()
+    stored(count - 1).wait()
+
+
+def branch_back(chips, batches, x, w, attended, hidden, wd, group_d, collective):
     rows, width = x.shape
     group = 2 * chips
     length = group * rows // batches
     span = w.shape[0]
+    units = wd.shape[0]
     half = jnp.bfloat16
+    part = 256 if group * rows <= 2048 else 128
     return pl.pallas_call(
         functools.partial(branch_back_kernel, chips, batches),
         out_shape=[
-            jax.ShapeDtypeStruct((batches, length, width), half),
             jax.ShapeDtypeStruct((batches, length, span), half),
             jax.ShapeDtypeStruct((rows, width), jnp.float32),
+            jax.ShapeDtypeStruct((span, width), half),
+            jax.ShapeDtypeStruct((units, width), half),
         ],
-        in_specs=[VMEM_SPEC] * 4,
-        out_specs=[ANY_SPEC, VMEM_SPEC, VMEM_SPEC],
-        scratch_shapes=Reduce.scratch(chips, rows, width)
-        + [
+        in_specs=[VMEM_SPEC] * 3 + [ANY_SPEC] * 3,
+        out_specs=[VMEM_SPEC, VMEM_SPEC, VMEM_SPEC, ANY_SPEC],
+        scratch_shapes=[
             pltpu.VMEM((group, rows, width), half),
+            pltpu.VMEM(hidden.shape, half),
+            pltpu.VMEM(wd.shape, half),
+            pltpu.VMEM((2, group * rows, part), half),
+            pltpu.VMEM((2, units, part), half),
+            pltpu.VMEM((span, width), jnp.float32),
             sems(3, group),
             sems(group),
-            sems(group, batches),
-        ],
+            sems(2),
+            sems(2),
+            sems(2),
+        ]
+        + Reduce.scratch(chips, rows, width),
         compiler_params=comm_params(collective, 62),
         cost_estimate=cost(
-            2 * group * rows * width * (span + wd.shape[0]), 250 * MIB, 2 * group * rows * width * 2
+            2 * group * rows * width * (2 * span + 2 * units),
+            250 * MIB,
+            2 * group * rows * width * 2,
         ),
         name="branch_back",
-    )(x, w, hidden, wd)
-
-
-def sum_kernel(chips, a_ref, w_ref, out_ref, *scratch):
+    )(x, w, attended, hidden, wd, group_d.reshape(group * rows, width))
+
+
+def attend_back_kernel(
+    seqs, group, block, q_ref, pad_ref, low_ref, lse_ref, d_ref, sums_ref, heads_ref, cols_ref,
+    dk, dv, kt, back_out, back_in, halo_send, halo_recv, swap_send, swap_recv, swap_keep,
+):
+    seq = lax.axis_index("seq")
+    batches, length, span = q_ref.shape
+    has_left, has_right = seq > 0, seq < seqs - 1
+    pl.when(has_left)(lambda: signal_seq(seq - 1))
+    pl.when(has_right)(lambda: signal_seq(seq + 1))
+    meet(greet_group(group) + has_left.astype(jnp.int32) + has_right.astype(jnp.int32))
+    swap = Swap(group, sums_ref, cols_ref, swap_send, swap_recv, swap_keep)
+    swap.begin()
+    steps = length // block
+    scale = jnp.asarray(HEAD**-0.5, jnp.bfloat16)
+
+    def halo(batch, step, peer):
+        rows = rows_at(step, block)
+        return pltpu.make_async_remote_copy(
+            src_ref=back_out.at[batch, rows],
+            dst_ref=back_in.at[batch, rows],
+            send_sem=halo_send.at[batch, step],
+            recv_sem=halo_recv.at[batch, step],
+            device_id={"seq": peer},
+            device_id_type=MESH,
+        )
+
+    dk[...] = jnp.zeros_like(dk)
+    dv[...] = jnp.zeros_like(dv)
+    for batch in range(batches):
+        kt[...] = pad_ref[batch, :, :span].T * scale
+
+        @pl.loop(0, steps)
+        def _(step, batch=batch):
+            begin = pl.multiple_of(step * block, block)
+            keys = pl.ds(begin, block + WINDOW)
+            rows = pl.ds(begin, block)
+            low = low_ref[batch, :, rows]
+            for pair in range(span // PAIR):
+                lanes = slice(pair * PAIR, (pair + 1) * PAIR)
+                q_pair = q_ref[batch, rows, lanes] * scale
+                d_pair = d_ref[batch, rows, lanes]
+                k_rows = pad_ref[batch, keys, lanes]
+                v_rows = pad_ref[batch, keys, span + pair * PAIR : span + (pair + 1) * PAIR]
+                k_cols = kt[lanes, keys]
+                back = []
+                for half in range(2):
+                    row = pair * 2 + half
+                    q_head = head_lanes(q_pair, half)
+                    d_head = head_lanes(d_pair, half)
+                    scores = masked_scores(k_rows, q_head, low)
+                    probs = jnp.exp(scores - lse_ref[batch, row : row + 1, rows])
+                    d_probs = dot_nt(v_rows, d_head)
+                    along = jnp.sum(probs * d_probs, axis=0, keepdims=True)
+                    d_scores = to_half(probs * (d_probs - along))
+                    dv[batch, keys, lanes] += dot_nn(to_half(probs), d_head)
+                    dk[batch, keys, lanes] += dot_nn(d_scores, q_head)
+                    back.append(dot_nn(k_cols, d_scores))
+                at = lax.broadcasted_iota(jnp.int32, back[0].shape, 0)
+                heads_ref[batch, rows, lanes] = to_half(
+                    jnp.where(at < HEAD, back[0], back[1]).T
+                )
+
+            @pl.when(has_left & (step < WINDOW // block))
+            def _():
+                back_out[batch, rows, :span] = to_half(dk[batch, rows, :])
+                back_out[batch, rows, span:] = to_half(dv[batch, rows, :])
+                halo(batch, step, seq - 1).start()
+
+    first = length - WINDOW
+    for batch in range(batches):
+        if first:
+            heads_ref[batch, :first, span : 2 * span] = to_half(dk[batch, WINDOW:length, :])
+            heads_ref[batch, :first, 2 * span :] = to_half(dv[batch, WINDOW:length, :])
+
+        @pl.loop(0, WINDOW // block)
+        def _(step, batch=batch):
+            inner = pl.ds(pl.multiple_of(step * block + length, block), block)
+            rows = pl.ds(pl.multiple_of(step * block + first, block), block)
+
+            @pl.when(has_right)
+            def _():
+                halo(batch, step, seq).wait_recv()
+                got = back_in[batch, rows_at(step, block), :].astype(jnp.float32)
+                heads_ref[batch, rows, span : 2 * span] = to_half(
+                    dk[batch, inner, :] + got[:, :span]
+                )
+                heads_ref[batch, rows, 2 * span :] = to_half(dv[batch, inner, :] + got[:, span:])
+
+            @pl.when(jnp.logical_not(has_right))
+            def _():
+                heads_ref[batch, rows, span : 2 * span] = to_half(dk[batch, inner, :])
+                heads_ref[batch, rows, 2 * span :] = to_half(dv[batch, inner, :])
+
+            pl.when(has_left)(lambda: halo(batch, step, seq).wait_send())
+
+    swap.end()
+
+
+def attend_back(seqs, group, query, kv_pad, low, lse, d_att, block, sums, collective):
+    batches, length, span = query.shape
+    padded = kv_pad.shape[1]
+    half = jnp.bfloat16
+    return pl.pallas_call(
+        functools.partial(attend_back_kernel, seqs, group, block),
+        in_specs=[VMEM_SPEC] * 5 + [ANY_SPEC],
+        out_specs=[VMEM_SPEC, ANY_SPEC],
+        out_shape=[
+            jax.ShapeDtypeStruct((batches, length, 3 * span), half),
+            jax.ShapeDtypeStruct(sums.shape, half),
+        ],
+        scratch_shapes=[
+            pltpu.VMEM((batches, padded, span), jnp.float32),
+            pltpu.VMEM((batches, padded, span), jnp.float32),
+            pltpu.VMEM((span, padded), half),
+            pltpu.VMEM((batches, WINDOW, 2 * span), half),
+            pltpu.VMEM((batches, WINDOW, 2 * span), half),
+            sems(batches, WINDOW // block),
+            sems(batches, WINDOW // block),
+            sems(group),
+            sems(group),
+            pltpu.SemaphoreType.DMA,
+        ],
+        compiler_params=comm_params(collective),
+        cost_estimate=cost(
+            20 * batches * length * span * (WINDOW + block), 180 * MIB, sums.size * 2
+        ),
+        name="attend_back",
+    )(query, kv_pad, low, lse, d_att, sums)
+
+
+def heads_back_kernel(
+    seqs, chips, a_ref, w_ref, g_hbm, v_ref, dm_ref, gain_ref, mlp_gain_ref,
+    grad_ref, cols_ref, tile_ref,
+    total, gain_acc, lefts, parts, sums, cols, gain_out, gain_in, gain_sum, gain_back,
+    left_sem, part_send, part_recv, cols_send, cols_recv, cols_keep,
+    gain_send, gain_recv, back_send, back_recv,
+    acc, cross_out, line_out, cross_in, line_in, sum_send, sum_recv,
+):
     line = Line(chips)
-    rows = out_ref.shape[0]
+    group = 2 * chips
+    seq = lax.axis_index("seq")
+    own = line.own
+    rows, width = v_ref.shape
+    batches = a_ref.shape[0]
+    part = lefts.shape[3]
+    run = width // seqs
+    share = run // group
+    depth = a_ref.shape[2]
+
+    def left(tile):
+        slot = lax.rem(tile, 2)
+        return pltpu.make_async_copy(
+            g_hbm.at[:, :, rows_at(tile, part)], lefts.at[slot], left_sem.at[slot]
+        )
+
+    def weight_grad(tile):
+        left(tile).wait()
+        pl.when(tile + 1 < width // part)(lambda: left(tile + 1).start())
+        slot = lax.rem(tile, 2)
+        got = contract_rows(lefts[slot, 0], a_ref[0])
+        for batch in range(1, batches):
+            got = got + contract_rows(lefts[slot, batch], a_ref[batch])
+        parts[rows_at(tile, part), :] = to_half(got)
+
+    def to_seq(peer, place):
+        return pltpu.make_async_remote_copy(
+            src_ref=parts.at[rows_at(peer, run)],
+            dst_ref=sums.at[place],
+            send_sem=part_send.at[peer],
+            recv_sem=part_recv.at[place],
+            device_id={"seq": peer},
+            device_id_type=MESH,
+        )
+
+    def others(count, me, act):
+        pl.loop(1, count)(lambda ahead: act(lax.rem(me + ahead, count)))
 
     def product(slot, tile):
         return dot_nt(left_rows(a_ref, slot, rows), w_ref[rows_at(tile, TILE), :])
 
-    meet(line.greet())
-    reduce = Reduce(line, product, out_ref, *scratch)
-    pl.loop(0, reduce.steps())(reduce.step)
+    left(0).start()
+    meet(greet_group(group) + greet_seq(seqs))
+    reduce = Reduce(
+        line, product, total, acc, cross_out, line_out, cross_in, line_in, sum_send, sum_recv
+    )
+    count = width // part
+    per = -(-count // (2 * chips - 3))
+
+    @pl.loop(0, 2 * chips - 3)
+    def _(step):
+        reduce.step(step)
+
+        @pl.loop(0, per)
+        def _(turn):
+            tile = step * per + turn
+            pl.when(tile < count)(lambda: weight_grad(tile))
+
+    others(seqs, seq, lambda peer: to_seq(peer, seq).start())
+    pl.loop(2 * chips - 3, 2 * chips - 1)(reduce.step)
+
+    def put(here, d_values):
+        grad_ref[here, :] = dm_ref[here, :] + d_values
+
+    norm_back(rows, v_ref, total, gain_ref, gain_acc, put)
+    fold = 128 // share
+    near = group // fold
+    attn_row = jnp.sum(gain_acc[...], axis=0, keepdims=True)
+    mlp_row = jnp.sum(mlp_gain_ref[...], axis=0, keepdims=True)
+    gain_out[...] = jnp.zeros_like(gain_out)
+    for place in range(width // 128):
+        lanes = slice(place * 128, (place + 1) * 128)
+        gain_out[place % near, place // near, 0:1, :] = attn_row[:, lanes]
+        gain_out[place % near, place // near, 1:2, :] = mlp_row[:, lanes]
+
+    def gain_group(peer, member):
+        return pltpu.make_async_remote_copy(
+            src_ref=gain_out.at[peer // fold],
+            dst_ref=gain_in.at[member],
+            send_sem=gain_send.at[peer],
+            recv_sem=gain_recv.at[member],
+            device_id={"fsdp": peer},
+            device_id_type=MESH,
+        )
+
+    def gain_seq(peer, place):
+        return pltpu.make_async_remote_copy(
+            src_ref=gain_sum.at[peer],
+            dst_ref=gain_back.at[place],
+            send_sem=back_send.at[peer],
+            recv_sem=back_recv.at[place],
+            device_id={"seq": peer},
+            device_id_type=MESH,
+        )
+
+    def block_swap(peer, member):
+        return pltpu.make_async_remote_copy(
+            src_ref=parts.at[rows_at(seq * group + peer, share)],
+            dst_ref=cols.at[member],
+            send_sem=cols_send.at[peer],
+            recv_sem=cols_recv.at[member],
+            device_id={"fsdp": peer},
+            device_id_type=MESH,
+        )
+
+    others(group, own, lambda peer: gain_group(peer, own).start())
+    gain_in[own] = gain_out[own // fold]
+    others(seqs, seq, lambda peer: to_seq(peer, peer).wait_recv())
+
+    @pl.loop(0, run // 64)
+    def _(chunk):
+        here = rows_at(chunk, 64)
+        there = pl.ds(pl.multiple_of(seq * run + chunk * 64, 64), 64)
+        added = parts[there, :].astype(jnp.float32)
+        for place in range(seqs):
+            piece = sums[place, here, :].astype(jnp.float32)
+            added = added + jnp.where(place == seq, 0.0, piece)
+        parts[there, :] = to_half(added)
+
+    others(group, own, lambda peer: block_swap(peer, own).start())
+    cols[own] = parts[rows_at(seq * group + own, share), :]
+    others(group, own, lambda peer: gain_group(peer, peer).wait_recv())
+    gain_sum[...] = jnp.sum(gain_in[...], axis=0)
+    others(seqs, seq, lambda peer: gain_seq(peer, seq).start())
+    gain_back[seq] = gain_sum[seq]
+    others(seqs, seq, lambda peer: gain_seq(peer, peer).wait_recv())
+    tile_ref[...] = jnp.sum(gain_back[...], axis=0)
+    others(group, own, lambda peer: block_swap(peer, peer).wait_recv())
+    kept = pltpu.make_async_copy(cols, cols_ref, cols_keep)
+    kept.start()
     reduce.sent()
-
-
-def sum_products(chips, a, w, name, collective):
+    others(seqs, seq, lambda peer: to_seq(peer, seq).wait_send())
+    others(group, own, lambda peer: gain_group(peer, own).wait_send())
+    others(group, own, lambda peer: block_swap(peer, own).wait_send())
+    others(seqs, seq, lambda peer: gain_seq(peer, seq).wait_send())
+    kept.wait()
+
+
+def heads_back(seqs, chips, a, w, group_a, x, d_middle, gain, mlp_gain, collective):
+    rows, width = x.shape
+    batches, length, depth = a.shape
     group = 2 * chips
-    width, depth = w.shape
-    rows = a.size // depth // group
+    share = width // seqs // group
+    near = group // (128 // share)
+    half = jnp.bfloat16
+    part = 256 if batches * length <= 2048 else 128
     return pl.pallas_call(
-        functools.partial(sum_kernel, chips),
-        out_shape=jax.ShapeDtypeStruct((rows, width), jnp.float32),
-        in_specs=[VMEM_SPEC, VMEM_SPEC],
-        out_specs=VMEM_SPEC,
-        scratch_shapes=Reduce.scratch(chips, rows, width),
-        compiler_params=comm_params(collective),
-        cost_estimate=cost(2 * group * rows * width * depth, 200 * MIB, group * rows * width * 2),
-        name=name,
-    )(a, w)
-
-
-def swap_kernel(group, count, *refs):
-    sources, targets = refs[:count], refs[count : 2 * count]
-    send, recv, keep = refs[2 * count :]
-    meet(greet_group(group))
-    swaps = [
-        Swap(group, sources[item], targets[item], send.at[item], recv.at[item], keep.at[item])
-        for item in range(count)
-    ]
-    for item in swaps:
-        item.begin()
-    for item in swaps:
-        item.end()
-
-
-def swap_blocks(group, arrays, name, collective):
-    count = len(arrays)
-    return pl.pallas_call(
-        functools.partial(swap_kernel, group, count),
-        out_shape=[jax.ShapeDtypeStruct(item.shape, item.dtype) for item in arrays],
-        in_specs=[ANY_SPEC] * count,
-        out_specs=[ANY_SPEC] * count,
-        scratch_shapes=[sems(count, group), sems(count, group), sems(count)],
-        compiler_params=comm_params(collective, 16),
-        cost_estimate=cost(0, 150 * MIB, sum(item.size * 2 for item in arrays)),
-        name=name,
-    )(*arrays)
-
-
-def tiles_kernel(seqs, group, x_ref, out_ref, send, recv):
-    devices = seqs * group
-    own = lax.axis_index("seq") * group + lax.axis_index("fsdp")
-    barrier = pltpu.get_barrier_semaphore()
-
-    def place(peer):
-        return {"seq": peer // group, "fsdp": lax.rem(peer, group)}
-
-    @pl.loop(1, devices)
-    def _(ahead):
-        peer = lax.rem(own + ahead, devices)
-        pl.semaphore_signal(barrier, inc=1, device_id=place(peer), device_id_type=MESH)
-
-    meet(devices - 1)
-    out_ref[own] = x_ref[own]
-
-    def move(peer, source):
-        return pltpu.make_async_remote_copy(
-            src_ref=x_ref.at[peer],
-            dst_ref=out_ref.at[source],
-            send_sem=send.at[peer],
-            recv_sem=recv.at[source],
-            device_id=place(peer),
-            device_id_type=MESH,
-        )
-
-    pl.loop(1, devices)(lambda ahead: move(lax.rem(own + ahead, devices), own).start())
-
-    @pl.loop(1, devices)
-    def _(ahead):
-        peer = lax.rem(own + ahead, devices)
-        move(peer, peer).wait_recv()
-        move(peer, own).wait_send()
-
-
-def swap_tiles(seqs, group, x, name, collective):
-    devices = seqs * group
-    return pl.pallas_call(
-        functools.partial(tiles_kernel, seqs, group),
-        out_shape=jax.ShapeDtypeStruct((devices, 8, 128), jnp.float32),
-        in_specs=[VMEM_SPEC],
-        out_specs=VMEM_SPEC,
-        scratch_shapes=[sems(devices), sems(devices)],
-        compiler_params=comm_params(collective, 16),
-        name=name,
-    )(x)
-
-
-def attend_back_kernel(
-    block, q_ref, k_ref, v_ref, low_ref, lse_ref, d_ref, dq_ref, dk_ref, dv_ref, kt_ref
-):
-    step = pl.program_id(1)
-    span = q_ref.shape[2]
-    scale = jnp.asarray(HEAD**-0.5, jnp.bfloat16)
-
-    @pl.when(step == 0)
-    def _():
-        kt_ref[...] = k_ref[0].T * scale
-        dk_ref[...] = jnp.zeros_like(dk_ref)
-        dv_ref[...] = jnp.zeros_like(dv_ref)
-
-    begin = pl.multiple_of(step * block, block)
-    keys = pl.ds(begin, block + WINDOW)
-    low = low_ref[0]
-    for pair in range(span // PAIR):
-        lanes = slice(pair * PAIR, (pair + 1) * PAIR)
-        q_pair = q_ref[0, :, lanes] * scale
-        d_pair = d_ref[0, :, lanes]
-        k_rows = k_ref[0, keys, lanes]
-        v_rows = v_ref[0, keys, lanes]
-        kt = kt_ref[lanes, keys]
-        back = []
-        for half in range(2):
-            row = pair * 2 + half
-            q_head = head_lanes(q_pair, half)
-            d_head = head_lanes(d_pair, half)
-            scores = masked_scores(k_rows, q_head, low)
-            probs = jnp.exp(scores - lse_ref[0, row : row + 1, :])
-            d_probs = dot_nt(v_rows, d_head)
-            along = jnp.sum(probs * d_probs, axis=0, keepdims=True)
-            d_scores = (probs * (d_probs - along)).astype(jnp.bfloat16)
-            dv_ref[0, keys, lanes] += dot_nn(probs.astype(jnp.bfloat16), d_head)
-            dk_ref[0, keys, lanes] += dot_nn(d_scores, q_head)
-            back.append(dot_nn(kt, d_scores))
-        at = lax.broadcasted_iota(jnp.int32, back[0].shape, 0)
-        dq_ref[0, :, lanes] = jnp.where(at < HEAD, back[0], back[1]).T.astype(jnp.bfloat16)
-
-
-def attend_back(query, kv_pad, low, lse, d_att, block):
-    batches, length, span = query.shape
-    padded = kv_pad.shape[1]
-    heads = span // HEAD
-    rows = pl.BlockSpec((1, block, span), lambda b, i: (b, i, 0))
-    whole = pl.BlockSpec((1, padded, span), lambda b, i: (b, 0, 0))
-    return pl.pallas_call(
-        functools.partial(attend_back_kernel, block),
-        grid=(batches, length // block),
-        in_specs=[
-            rows,
-            whole,
-            pl.BlockSpec((1, padded, span), lambda b, i: (b, 0, 1)),
-            pl.BlockSpec((1, 1, block), lambda b, i: (b, 0, i)),
-            pl.BlockSpec((1, heads, block), lambda b, i: (b, 0, i)),
-            rows,
+        functools.partial(heads_back_kernel, seqs, chips),
+        out_shape=[
+            jax.ShapeDtypeStruct((rows, width), jnp.float32),
+            jax.ShapeDtypeStruct((group, share, depth), half),
+            jax.ShapeDtypeStruct((8, 128), jnp.float32),
         ],
-        out_specs=[rows, whole, whole],
-        out_shape=[
-            jax.ShapeDtypeStruct((batches, length, span), jnp.bfloat16),
-            jax.ShapeDtypeStruct((batches, padded, span), jnp.float32),
-            jax.ShapeDtypeStruct((batches, padded, span), jnp.float32),
-        ],
-        scratch_shapes=[pltpu.VMEM((span, padded), jnp.bfloat16)],
-        compiler_params=pltpu.CompilerParams(vmem_limit_bytes=48 * 2**20),
-        name="attend_back",
-    )(query, kv_pad, kv_pad, low, lse, d_att)
+        in_specs=[VMEM_SPEC, VMEM_SPEC, ANY_SPEC] + [VMEM_SPEC] * 4,
+        out_specs=[VMEM_SPEC, ANY_SPEC, VMEM_SPEC],
+        scratch_shapes=[
+            pltpu.VMEM((rows, width), jnp.float32),
+            pltpu.VMEM((8, width), jnp.float32),
+            pltpu.VMEM((2, batches, length, part), half),
+            pltpu.VMEM((width, depth), half),
+            pltpu.VMEM((seqs, width // seqs, depth), half),
+            pltpu.VMEM((group, share, depth), half),
+            pltpu.VMEM((near, seqs, 8, 128), jnp.float32),
+            pltpu.VMEM((group, seqs, 8, 128), jnp.float32),
+            pltpu.VMEM((seqs, 8, 128), jnp.float32),
+            pltpu.VMEM((seqs, 8, 128), jnp.float32),
+            sems(2),
+            sems(seqs),
+            sems(seqs),
+            sems(group),
+            sems(group),
+            pltpu.SemaphoreType.DMA,
+            sems(group),
+            sems(group),
+            sems(seqs),
+            sems(seqs),
+        ]
+        + Reduce.scratch(chips, rows, width),
+        compiler_params=comm_params(collective, 60),
+        cost_estimate=cost(
+            4 * group * rows * width * depth, 200 * MIB, 2 * group * rows * width * 2
+        ),
+        name="heads_back",
+    )(a, w, group_a, x, d_middle, gain, mlp_gain)
 
 
 def doc_starts(lengths, positions, batches, seq_len):
@@ -1117,8 +1467,6 @@
     share = w_query.shape[0]
     span = width // group
     length = group * piece
-    group_rows = group * rows
-    units = FF // group
     aligned = share == HEAD
     member = lax.axis_index("fsdp")
 
@@ -1135,7 +1483,6 @@
         return cols.reshape(group, share, seqs, part).transpose(1, 2, 0, 3).reshape(share, total)
 
     inputs = tokens.astype(jnp.float32).reshape(rows, width)
-    upstream = cotangent.astype(jnp.float32).reshape(rows, width)
     wd_part = lax.all_gather(w_down, "seq", axis=0, tiled=True)
     if aligned:
         wo_part = lax.all_gather(w_out, "seq", axis=0, tiled=True)
@@ -1177,69 +1524,36 @@
     middle = inputs + branch
     normed_b = to_half(normalize(middle, gain_two))
     group_b, hidden, d_units = hidden_units(chips, normed_b, w_units, wd_part, group_d, 4)
-    group_d = group_d.reshape(group_rows, width)
-    d_normed_b = sum_products(chips, d_units, w_units, "units_back", 5)
-    mlp_pull = jax.vjp(normalize, middle, gain_two)[1]
-    d_middle_norm, gain_two_grad = mlp_pull(d_normed_b)
-    d_middle = upstream + d_middle_norm
-    d_branch = to_half(d_middle)
+    d_middle, d_branch, mlp_gain_part, unit_part = units_back(
+        chips, d_units, w_units, group_b, middle, cotangent.reshape(rows, width), gain_two[None], 5
+    )
 
     def over_seq(values):
-        return lax.psum_scatter(to_half(values), "seq", scatter_dimension=0, tiled=True)
-
-    down_sum = over_seq(contract_rows(hidden, group_d))
-    unit_sums = over_seq(contract_rows(group_b.reshape(group_rows, width), d_units))
-
-    group_branch, d_attended, mlp_out = branch_back(
-        chips, batches, d_branch, wo_part, hidden, wd_part, 6
+        return lax.psum_scatter(values, "seq", scatter_dimension=0, tiled=True)
+
+    unit_sums = over_seq(unit_part).reshape(group, share, -1)
+    d_attended, mlp_out, out_grad, down_grad = branch_back(
+        chips, batches, d_branch, wo_part, attended, hidden, wd_part, group_d, 6
     )
     outputs = middle + mlp_out
-    d_query, d_key_pad, d_value_pad = attend_back(query, kv_pad, low, lse, d_attended, block)
-    behind = [(source + 1, source) for source in range(seqs - 1)]
-    back = lax.ppermute(
-        to_half(jnp.concatenate([d_key_pad[:, :WINDOW], d_value_pad[:, :WINDOW]], axis=2)),
-        "seq",
-        behind,
-    ).astype(jnp.float32)
-    back = jnp.pad(back, ((0, 0), (length - WINDOW, 0), (0, 0)))
-    d_heads = jnp.concatenate(
-        [
-            d_query,
-            to_half(d_key_pad[:, WINDOW:] + back[:, :, :span]),
-            to_half(d_value_pad[:, WINDOW:] + back[:, :, span:]),
-        ],
-        axis=2,
-    )
-    d_normed_a = sum_products(chips, d_heads, w_heads, "heads_back", 7)
-    flat_a = group_a.reshape(group_rows, width)
-    out_grad = contract_rows(
-        attended.reshape(group_rows, span), group_branch.reshape(group_rows, width)
+    down_sum = over_seq(down_grad)
+    d_heads, unit_cols = attend_back(
+        seqs, group, query, kv_pad, low, lse, d_attended, block, unit_sums, 7
     )
     if aligned:
         out_sum = over_seq(out_grad)
     else:
         whole = lax.dynamic_update_slice_in_dim(
-            jnp.zeros((width, width), jnp.bfloat16), to_half(out_grad), member * span, 0
+            jnp.zeros((width, width), jnp.bfloat16), out_grad, member * span, 0
         )
         out_sum = lax.psum_scatter(whole, ("seq", "fsdp"), scatter_dimension=0, tiled=True)
-    head_sums = over_seq(contract_rows(flat_a, d_heads.reshape(group_rows, 3 * span)))
-    head_cols, unit_cols = swap_blocks(
-        group,
-        [head_sums.reshape(group, share, -1), unit_sums.reshape(group, share, -1)],
-        "weight_grads",
-        8,
-    )
-
-    attn_pull = jax.vjp(normalize, inputs, gain_one)[1]
-    d_input_norm, gain_one_grad = attn_pull(d_normed_a)
-    input_grad = (d_middle + d_input_norm).reshape(batches, piece, width)
+    input_grad, head_cols, gain_tile = heads_back(
+        seqs, chips, d_heads, w_heads, group_a, tokens.reshape(rows, width), d_middle,
+        gain_one[None], mlp_gain_part, 8,
+    )
+    input_grad = input_grad.reshape(batches, piece, width)
     layer_out = to_half(outputs).reshape(batches, piece, width)
-
-    def lanes(values):
-        return jnp.pad(values.reshape(devices, 1, share), ((0, 0), (0, 7), (0, 64 - share)))
-
-    grad_tiles = jnp.concatenate([lanes(gain_one_grad), lanes(gain_two_grad)], axis=2)
-    grad_sums = jnp.sum(swap_tiles(seqs, group, grad_tiles, "gain_grads", 9)[:, 0], axis=0)
+    gain_grads = lax.dynamic_slice_in_dim(gain_tile[:2], lax.rem(device, fold) * share, share, 1)
 
     def whole_rows(cols, part, total):
         size = total // group
@@ -1248,12 +1562,12 @@
     return (
         layer_out,
         input_grad,
-        grad_sums[:share],
+        gain_grads[0],
         whole_rows(head_cols, 0, width),
         whole_rows(head_cols, 1, width),
         whole_rows(head_cols, 2, width),
         out_sum.astype(jnp.float32),
-        grad_sums[64 : 64 + share],
+        gain_grads[1],
         whole_rows(unit_cols, 0, FF),
         whole_rows(unit_cols, 1, FF),
         down_sum.astype(jnp.float32),

time: 1010 us -> 1010 us (level)
  waiting for transfers between devices: 60 us -> 168 us
  matrix products: 55 us -> 0 us
  Pallas kernels: 785 us -> 754 us
  local copies, waits for them, and re-layouts: 50.6 us -> 37 us
  other arithmetic: 35.2 us -> 21.8 us
    reduce_scatter x4 -> x3, waiting for transfers between devices: 0.03 us -> 165 us  [over_seq(): return lax.psum_scatter(values, 'seq', scatter_dimension=0, tiled=True)]
    ppermute x1 -> x0, waiting for transfers between devices: 58.6 us -> none  [body(): lax.ppermute(to_half(jnp.concatenate([d_key_pad[:, :WINDOW], d_value_pad[...]
    dot_general x4 -> x0, matrix products: 55 us -> none  [contract_rows(): lax.dot_general(left, right, (((0,), (0,)), ((), ())), preferred_element_...]
    pallas_call x5 -> x3, Pallas kernels: 316 us -> 293 us  [the longest x1 118 us: heads_back(): pl.pallas_call(functools.partial(heads_back_kernel, seqs, chips), out_sha...]
  transfers between devices with their start and end apart: 7 -> 5, of which waited for: 1 -> 3; matrix products, arithmetic and copies ran while one was open for 9% -> 3% of each run, Pallas kernels for 42% -> 28%
where the time goes in v3:
time: 1010 us; the launch traced here: 996 us
  Pallas kernels  754 us (75%)
  waiting for transfers between devices  168 us (17%)
  local copies, waits for them, and re-layouts  37 us (4%)
  other arithmetic  21.8 us (2%)
  between operations  14.7 us (1%)
    reduce_scatter x3, waiting for transfers between devices, over_seq(): return lax.psum_scatter(values, 'seq', scatter_dimension=0, tiled=True)  165 us
    pallas_call x1, Pallas kernels, branch_sum(): pl.pallas_call(functools.partial(branch_kernel, seqs, chips), out_shape=[...  119 us
    pallas_call x1, Pallas kernels, heads_back(): pl.pallas_call(functools.partial(heads_back_kernel, seqs, chips), out_sha...  118 us
    pallas_call x1, Pallas kernels, units_back(): pl.pallas_call(functools.partial(units_back_kernel, chips), out_shape=[ja...  115 us
    pallas_call x1, Pallas kernels, branch_back(): pl.pallas_call(functools.partial(branch_back_kernel, chips, batches), out...  107 us
    pallas_call x1, Pallas kernels, start(): pl.pallas_call(functools.partial(start_kernel, seqs, chips, batches), out...  99.3 us
    pallas_call x1, Pallas kernels, hidden_units(): pl.pallas_call(functools.partial(units_kernel, chips), out_shape=[jax.Sha...  74.5 us
    pallas_call x1, Pallas kernels, attend(): pl.pallas_call(functools.partial(attend_kernel, seqs, group, block), in_s...  61.5 us
  transfers between devices with their start and end apart: 5, of which 3 were waited for; matrix products, arithmetic and copies ran while one was open for 3% of the time, Pallas kernels for 28%

profile of v3, /device:TPU:9, one launch (start us, length us, event | category | flops | bytes accessed | tf_op | source)
XLA Modules:
  0.0 995.7 jit_solution(6791843870614010761)
XLA Ops:
  11.0 1.5 reshape.248
  13.8 1.0 reshape.251
  20.2 2.0 pad_maximum_fusion.1.blocks_ref
  22.2 99.3 %start.1 = (bf16[2,1024,2048]{2,1,0:T(8,128)(2,1)}, bf16[2,1024,256]{2,1,0:T(8,128)(2,1)}, bf16[2,1024,512]{2,1,0:T(8,128)(2,1)}, f32[8,4,8,128]{3,2,1,0:T(8,128)}, bf16[2048,768]{1,0:T(8,128)(2,1)}) custom-call(f32[1,8,128]{2,1,0:T(8,128)} %pad_bitcast_fusion.tile_ref, bf16[256,2048]{1,0:T(8,128)(2,1)} %bitcast.84, ...), custom_call_target="tpu_custom_call" | custom-call | flops 6442450944 | bytes 209715200 | tf_op jit(solution)/shard_map/start/pallas_call | solution.py:570
  123.2 1.5 pad_maximum_fusion.units_ref
  125.3 61.5 %attend.1 = (bf16[2,1024,256]{2,1,0:T(8,128)(2,1)}, f32[2,4,1024]{2,1,0:T(4,128)}, bf16[2,2048,512]{2,1,0:T(8,128)(2,1)}, bf16[8,64,2048]{2,1,0:T(8,128)(2,1)}) custom-call(bf16[2,1024,256]{2,1,0:T(8,128)(2,1)} %get-tuple-element.39.q_ref, bf16[2,1024,512]{2,1,0:T(8,128)(2,1)} %get-tuple-element.40.kv_ref, s32[2,1,1024]{2,1,0:T(1,128)} %maximum_subtract_fusion.low_ref, ...), custom_call_target="tpu_custom_call" | custom-call | flops 5368709120 | bytes 157286400 | tf_op jit(solution)/shard_map/attend/pallas_call | solution.py:679
  186.8 118.6 %branch_sum.1 = (f32[256,2048]{1,0:T(8,128)}, bf16[8,256,2048]{2,1,0:T(8,128)(2,1)}, bf16[4,512,2048]{2,1,0:T(8,128)(2,1)}) custom-call(bf16[2,1024,256]{2,1,0:T(8,128)(2,1)} %get-tuple-element.41.a_ref.att_ref, bf16[256,2048]{1,0:T(8,128)(2,1)} %all-gather.3.cloned.1.call-done.w_ref, bf16[256,2048]{1,0:T(8,128)(2,1)} %bitcast.92, bf16[512,2048]{1,0:T(8,128)(2,1)} %bitcast.98), custom_call_target="tpu_custom_call" | custom-call | flops 2147483648 | bytes 262144000 | tf_op jit(solution)/shard_map/branch_sum/pallas_call | solution.py:745
  305.4 1.9 multiply_reduce_fusion
  307.4 1.4 multiply_convert_fusion.x_ref
  308.8 74.5 %hidden_units.1 = (bf16[8,256,2048]{2,1,0:T(8,128)(2,1)}, bf16[2048,1024]{1,0:T(8,128)(2,1)}, bf16[2048,2048]{1,0:T(8,128)(2,1)}) custom-call(bf16[256,2048]{1,0:T(8,128)(2,1)} %multiply_convert_fusion.x_ref, bf16[2048,2048]{1,0:T(8,128)(2,1)} %bitcast.95, bf16[1024,2048]{1,0:T(8,128)(2,1)} %all-gather.5.cloned.1.call-done.wd_hbm, ...), custom_call_target="tpu_custom_call" | custom-call | flops 25769803776 | bytes 209715200 | tf_op jit(solution)/shard_map/hidden_units/pallas_call | solution.py:831
  383.4 115.2 %units_back.1 = (f32[256,2048]{1,0:T(8,128)}, bf16[256,2048]{1,0:T(8,128)(2,1)}, f32[8,2048]{1,0:T(8,128)}, bf16[2048,2048]{1,0:T(8,128)(2,1)}) custom-call(bf16[2048,2048]{1,0:T(8,128)(2,1)} %get-tuple-element.47.a_hbm, bf16[2048,2048]{1,0:T(8,128)(2,1)} %bitcast.96, bf16[2048,2048]{1,0:T(8,128)(2,1)} %bitcast.97, f32[256,2048]{1,0:T(8,128)} %copy-done, ...), custom_call_target="tpu_custom_call" | custom-call | flops 34359738368 | bytes 209715200 | tf_op jit(solution)/shard_map/units_back/pallas_call | solution.py:942
  498.5 107.0 %branch_back.1 = (bf16[2,1024,256]{2,1,0:T(8,128)(2,1)}, f32[256,2048]{1,0:T(8,128)}, bf16[256,2048]{1,0:T(8,128)(2,1)}, bf16[1024,2048]{1,0:T(8,128)(2,1)}) custom-call(bf16[256,2048]{1,0:T(8,128)(2,1)} %get-tuple-element.49.x_ref, bf16[256,2048]{1,0:T(8,128)(2,1)} %all-gather.3.cloned.1.call-done.w_ref, ...), custom_call_target="tpu_custom_call" | custom-call | flops 21474836480 | bytes 262144000 | tf_op jit(solution)/shard_map/branch_back/pallas_call | solution.py:1076
  607.8 2.8 add_convert_fusion
  610.6 24.8 %reduce-scatter.6.cloned.1.call-done = bf16[64,2048]{1,0:T(8,128)(2,1)} async-done(((bf16[256,2048]{1,0:T(8,128)(2,1)}), bf16[64,2048]{1,0:T(8,128)(2,1)}) %reduce-scatter.6.cloned.1.call-update) | async-done | bytes 262160 | tf_op jit(solution)/shard_map/reduce_scatter | solution.py:1532
  635.4 1.8 convert_element_type.97
  637.2 54.1 %reduce-scatter.8.cloned.1.call-done = bf16[256,2048]{1,0:T(8,128)(2,1)} async-done(((bf16[1024,2048]{1,0:T(8,128)(2,1)}), bf16[256,2048]{1,0:T(8,128)(2,1)}) %reduce-scatter.8.cloned.1.call-update) | async-done | bytes 1048592 | tf_op jit(solution)/shard_map/reduce_scatter | solution.py:1532
  691.2 2.8 convert_element_type.106
  694.0 86.5 %reduce-scatter.4.cloned.1.call-done = bf16[512,2048]{1,0:T(8,128)(2,1)} async-done(((bf16[2048,2048]{1,0:T(8,128)(2,1)}), bf16[512,2048]{1,0:T(8,128)(2,1)}) %reduce-scatter.4.cloned.1.call-update) | async-done | bytes 2097168 | tf_op jit(solution)/shard_map/reduce_scatter | solution.py:1532
  780.5 60.1 %attend_back.1 = (bf16[2,1024,768]{2,1,0:T(8,128)(2,1)}, bf16[8,64,2048]{2,1,0:T(8,128)(2,1)}) custom-call(bf16[2,1024,256]{2,1,0:T(8,128)(2,1)} %get-tuple-element.39.q_ref, bf16[2,2048,512]{2,1,0:T(8,128)(2,1)} %get-tuple-element.52.pad_ref, s32[2,1,1024]{2,1,0:T(1,128)} %maximum_subtract_fusion.low_ref, f32[2,4,1024]{2,1,0:T(4,128)} %get-tuple-element.53.lse_ref, ...), custom_call_target="tpu_custom_call" | custom-call | flops 13421772800 | bytes 188743680 | tf_op jit(solution)/shard_map/attend_back/pallas_call | solution.py:1212
  840.6 118.1 %heads_back.1 = (f32[256,2048]{1,0:T(8,128)}, bf16[8,64,768]{2,1,0:T(8,128)(2,1)}, f32[8,128]{1,0:T(8,128)}) custom-call(bf16[2,1024,768]{2,1,0:T(8,128)(2,1)} %get-tuple-element.56.a_ref, bf16[2048,768]{1,0:T(8,128)(2,1)} %get-tuple-element.57.w_ref, bf16[2,1024,2048]{2,1,0:T(8,128)(2,1)} %get-tuple-element.58.g_hbm, bf16[256,2048]{1,0:T(8,128)(2,1)} %bitcast.85, ...), custom_call_target="tpu_custom_call" | custom-call | flops 12884901888 | bytes 209715200 | tf_op jit(solution)/shard_map/heads_back/pallas_call | solution.py:1395
  960.0 1.3 slice_convert_fusion.2
  962.3 1.2 reshape.269
  964.6 1.2 reshape.268
  966.8 1.2 reshape.267
  967.9 3.3 slice_convert_fusion
  971.3 3.4 reshape.276
  974.7 2.8 copy.65
  977.5 2.5 copy.69
  980.0 2.0 reshape.275
  982.0 2.8 copy.64
  984.8 2.5 copy.68
  987.3 1.3 copy.81
  (67 shorter events, 19.3 us)
Async XLA Ops:
  7.2 5.9 copy-start.6
  7.2 179.6 %all-gather.3.cloned.1.call-start = ((), (), s32[]{:S(2)}) async-start(), calls=%async_computation.3 | async-start | bytes 1310720 | tf_op jit(solution)/shard_map/all_gather | solution.py:1488
  7.9 300.9 %all-gather.5.cloned.1.call-start = ((), (), s32[]{:S(2)}) async-start(), calls=%async_computation.4 | async-start | bytes 5242880 | tf_op jit(solution)/shard_map/all_gather | solution.py:1486
  8.7 626.7 %reduce-scatter.6.cloned.1.call-start = ((), (), s32[]{:S(2)}) async-start(), calls=%async_computation.6 | async-start | bytes 1310720 | tf_op jit(solution)/shard_map/reduce_scatter | solution.py:1532
  12.5 2.4 copy-start.7
  13.6 3.1 copy-start.3
  16.9 1.2 copy-start.4
  186.8 118.6 %copy-start.5 = (bf16[2,128,2048]{2,1,0:T(8,128)(2,1)S(1)}, bf16[2,128,2048]{2,1,0:T(8,128)(2,1)}, u32[]{:S(2)}) copy-start(bf16[2,128,2048]{2,1,0:T(8,128)(2,1)} %param.12) | copy-start | bytes 3145732
  307.4 76.0 %copy-start = (f32[256,2048]{1,0:T(8,128)}, f32[256,2048]{1,0:T(8,128)S(1)}, u32[]{:S(2)}) copy-start(f32[256,2048]{1,0:T(8,128)S(1)} %get-tuple-element.68.v_ref) | copy-start | bytes 6291460
  605.6 85.7 %reduce-scatter.8.cloned.1.call-start = ((), (), s32[]{:S(2)}) async-start(), calls=%async_computation.7 | async-start | bytes 5242880 | tf_op jit(solution)/shard_map/reduce_scatter | solution.py:1532
  606.1 174.4 %reduce-scatter.4.cloned.1.call-start = ((), (), s32[]{:S(2)}) async-start(), calls=%async_computation.5 | async-start | bytes 10485760 | tf_op jit(solution)/shard_map/reduce_scatter | solution.py:1532
  606.2 1.6 copy-start.1
  984.8 2.5 copy-start.2
Sparse Core Ops, SparseCore 0:
  9.9 31.5 all-gather.2
  43.3 69.6 all-gather.4
  605.7 29.6 reduce-scatter.5
  638.5 52.6 reduce-scatter.7
  694.1 86.3 reduce-scatter.3

commit v4 on v3

--- a/solution.py
+++ b/solution.py
@@ -369,6 +369,43 @@
             self.move(peer, self.own).wait_send()
 
 
+class ToSeq:
+    def __init__(self, seqs, source, target, send, recv):
+        self.seqs, self.source, self.target, self.send, self.recv = seqs, source, target, send, recv
+        self.own = lax.axis_index("seq")
+
+    def move(self, peer, place):
+        return pltpu.make_async_remote_copy(
+            src_ref=self.source.at[rows_at(peer, self.target.shape[1])],
+            dst_ref=self.target.at[place],
+            send_sem=self.send.at[peer],
+            recv_sem=self.recv.at[place],
+            device_id={"seq": peer},
+            device_id_type=MESH,
+        )
+
+    def begin(self):
+        pl.loop(1, self.seqs)(
+            lambda ahead: self.move(lax.rem(self.own + ahead, self.seqs), self.own).start()
+        )
+
+    def arrived(self):
+        @pl.loop(1, self.seqs)
+        def _(ahead):
+            peer = lax.rem(self.own + ahead, self.seqs)
+            self.move(peer, peer).wait_recv()
+
+    def sent(self):
+        @pl.loop(1, self.seqs)
+        def _(ahead):
+            peer = lax.rem(self.own + ahead, self.seqs)
+            self.move(peer, self.own).wait_send()
+
+    def end(self):
+        self.arrived()
+        self.sent()
+
+
 VMEM_SPEC = pl.BlockSpec(memory_space=pltpu.VMEM)
 ANY_SPEC = pl.BlockSpec(memory_space=pl.ANY)
 
@@ -416,8 +453,8 @@
 
 
 def start_kernel(
-    seqs, chips, batches, tile_ref, x_ref, blocks_ref, g_ref, q_ref, kv_ref, gains_ref, w_out_ref,
-    buf, normed, gain, gains, w, send, recv, keep, swap_send, share_send, w_recv,
+    seqs, chips, batches, tile_ref, x_ref, blocks_ref, g_ref, q_ref, pad_ref, gains_ref, w_out_ref,
+    buf, normed, kv_ref, zeros, halo_send, halo_recv, pad_keep, gain, gains, w, send, recv, keep, swap_send, share_send, w_recv,
     tile_send, tile_across, tile_recv, tile_back, w_keep, gain_keep,
 ):
     line = Line(chips)
@@ -429,6 +466,9 @@
     span = q_ref.shape[2]
     width = x_ref.shape[1]
     per = 128 * seqs * group // width
+    length = group * piece
+    first = length - WINDOW
+    has_left, has_right = seq > 0, seq < seqs - 1
     meet(greet_group(group) + greet_seq(seqs))
 
     def block_at(run, member):
@@ -506,6 +546,39 @@
             g_ref.at[batch, rows_at(slot, piece)],
             keep.at[slot, batch],
         )
+
+    def own_rows(slot, batch):
+        there = pl.ds(pl.multiple_of(slot * piece + WINDOW, piece), piece)
+        return pltpu.make_async_copy(
+            kv_ref.at[batch, rows_at(slot, piece)],
+            pad_ref.at[batch, there],
+            pad_keep.at[slot, batch],
+        )
+
+    def no_rows(place, batch):
+        return pltpu.make_async_copy(
+            zeros, pad_ref.at[batch, rows_at(place, piece)], halo_recv.at[place, batch]
+        )
+
+    def halo(slot, batch, peer):
+        there = pl.ds(pl.multiple_of(slot * piece - first, piece), piece)
+        return pltpu.make_async_remote_copy(
+            src_ref=kv_ref.at[batch, rows_at(slot, piece)],
+            dst_ref=pad_ref.at[batch, there],
+            send_sem=halo_send.at[slot, batch],
+            recv_sem=halo_recv.at[slot - first // piece, batch],
+            device_id={"seq": peer},
+            device_id_type=MESH,
+        )
+
+    @pl.when(jnp.logical_not(has_left))
+    def _():
+        zeros[...] = jnp.zeros_like(zeros)
+
+        @pl.loop(0, WINDOW // piece)
+        def _(place):
+            for batch in range(batches):
+                no_rows(place, batch).start()
 
     def use(slot):
         @pl.loop(0, x_ref.shape[0] // 16)
@@ -526,6 +599,13 @@
                     q_ref[batch, rows, :] = mine
                 else:
                     kv_ref[batch, rows, (part - 1) * span : part * span] = mine
+        for batch in range(batches):
+            own_rows(slot, batch).start()
+
+        @pl.when(has_right & (slot * piece >= first))
+        def _():
+            for batch in range(batches):
+                halo(slot, batch, seq + 1).start()
 
     pl.loop(1, chips - 1)(spread.relay)
 
@@ -558,6 +638,15 @@
     def _(slot):
         for batch in range(batches):
             kept(slot, batch).wait()
+            own_rows(slot, batch).wait()
+
+    @pl.loop(0, WINDOW // piece)
+    def _(place):
+        slot = place + first // piece
+        for batch in range(batches):
+            pl.when(has_right)(lambda batch=batch: halo(slot, batch, seq).wait_send())
+            pl.when(has_left)(lambda batch=batch: halo(slot, batch, seq).wait_recv())
+            pl.when(jnp.logical_not(has_left))(lambda batch=batch: no_rows(place, batch).wait())
 
 
 def start(seqs, chips, batches, tile, x, blocks, collective):
@@ -572,15 +661,20 @@
         out_shape=[
             jax.ShapeDtypeStruct((batches, length, width), half),
             jax.ShapeDtypeStruct((batches, length, span), half),
-            jax.ShapeDtypeStruct((batches, length, 2 * span), half),
+            jax.ShapeDtypeStruct((batches, length + WINDOW, 2 * span), half),
             jax.ShapeDtypeStruct((group, seqs, 8, 128), jnp.float32),
             jax.ShapeDtypeStruct((width, cols), half),
         ],
         in_specs=[VMEM_SPEC] * 3,
-        out_specs=[ANY_SPEC, VMEM_SPEC, VMEM_SPEC, ANY_SPEC, ANY_SPEC],
+        out_specs=[ANY_SPEC, VMEM_SPEC, ANY_SPEC, ANY_SPEC, ANY_SPEC],
         scratch_shapes=[
             pltpu.VMEM((group, rows, width), half),
             pltpu.VMEM((group, rows, width), half),
+            pltpu.VMEM((batches, length, 2 * span), half),
+            pltpu.VMEM((rows // batches, 2 * span), half),
+            sems(group, batches),
+            sems(WINDOW * group // length, batches),
+            sems(group, batches),
             pltpu.VMEM((8, width), jnp.float32),
             pltpu.VMEM((group, seqs, 8, 128), jnp.float32),
             pltpu.VMEM((width, cols), half),
@@ -604,42 +698,14 @@
 
 
 def attend_kernel(
-    seqs, group, block, q_ref, kv_ref, low_ref, units_ref, out_ref, lse_ref, pad_ref, own_units_ref,
-    pad, vt, halo_send, halo_recv, pad_keep, swap_send, swap_recv, swap_keep,
+    group, block, q_ref, pad, low_ref, units_ref, out_ref, lse_ref, own_units_ref,
+    vt, swap_send, swap_recv, swap_keep,
 ):
-    seq = lax.axis_index("seq")
     batches, length, span = q_ref.shape
-    has_left, has_right = seq > 0, seq < seqs - 1
-    pl.when(has_left)(lambda: signal_seq(seq - 1))
-    pl.when(has_right)(lambda: signal_seq(seq + 1))
-    meet(greet_group(group) + has_left.astype(jnp.int32) + has_right.astype(jnp.int32))
-
-    def halo(batch, peer):
-        return pltpu.make_async_remote_copy(
-            src_ref=kv_ref.at[batch, pl.ds(length - WINDOW, WINDOW)],
-            dst_ref=pad.at[batch, pl.ds(0, WINDOW)],
-            send_sem=halo_send.at[batch],
-            recv_sem=halo_recv.at[batch],
-            device_id={"seq": peer},
-            device_id_type=MESH,
-        )
-
-    for batch in range(batches):
-        pl.when(has_right)(lambda batch=batch: halo(batch, seq + 1).start())
+    meet(greet_group(group))
     swap = Swap(group, units_ref, own_units_ref, swap_send, swap_recv, swap_keep)
     swap.begin()
-    pad[:, WINDOW:, :] = kv_ref[...]
-
-    @pl.when(jnp.logical_not(has_left))
-    def _():
-        pad[:, :WINDOW, :] = jnp.zeros((batches, WINDOW, 2 * span), jnp.bfloat16)
-
-    def kept(batch):
-        return pltpu.make_async_copy(pad.at[batch], pad_ref.at[batch], pad_keep.at[batch])
-
     for batch in range(batches):
-        pl.when(has_left)(lambda batch=batch: halo(batch, seq).wait_recv())
-        kept(batch).start()
         vt[...] = pad[batch, :, span:].T
 
         @pl.loop(0, length // block)
@@ -665,33 +731,25 @@
                 lane = lax.broadcasted_iota(jnp.int32, mixed[0].shape, 0)
                 out_ref[batch, rows, lanes] = to_half(jnp.where(lane < HEAD, mixed[0], mixed[1]).T)
 
-    for batch in range(batches):
-        kept(batch).wait()
-        pl.when(has_right)(lambda batch=batch: halo(batch, seq + 1).wait_send())
     swap.end()
 
 
-def attend(seqs, group, query, key_value, low, block, units, collective):
+def attend(group, query, kv_pad, low, block, units, collective):
     batches, length, span = query.shape
-    padded = length + WINDOW
+    padded = kv_pad.shape[1]
     heads = span // HEAD
     half = jnp.bfloat16
     return pl.pallas_call(
-        functools.partial(attend_kernel, seqs, group, block),
+        functools.partial(attend_kernel, group, block),
         in_specs=[VMEM_SPEC, VMEM_SPEC, VMEM_SPEC, ANY_SPEC],
-        out_specs=[VMEM_SPEC, VMEM_SPEC, ANY_SPEC, ANY_SPEC],
+        out_specs=[VMEM_SPEC, VMEM_SPEC, ANY_SPEC],
         out_shape=[
             jax.ShapeDtypeStruct((batches, length, span), half),
             jax.ShapeDtypeStruct((batches, heads, length), jnp.float32),
-            jax.ShapeDtypeStruct((batches, padded, 2 * span), half),
             jax.ShapeDtypeStruct(units.shape, half),
         ],
         scratch_shapes=[
-            pltpu.VMEM((batches, padded, 2 * span), half),
             pltpu.VMEM((span, padded), half),
-            sems(batches),
-            sems(batches),
-            sems(batches),
             sems(group),
             sems(group),
             pltpu.SemaphoreType.DMA,
@@ -701,7 +759,7 @@
             8 * batches * length * span * (WINDOW + block), 150 * MIB, units.size * 2
         ),
         name="attend",
-    )(query, key_value, low, units)
+    )(query, kv_pad, low, units)
 
 
 def branch_kernel(
@@ -969,10 +1027,10 @@
 
 
 def branch_back_kernel(
-    chips, batches, x_ref, w_ref, att_ref, hidden_hbm, wd_hbm, gd_hbm,
-    d_ref, out_ref, out_grad_ref, down_hbm,
+    seqs, chips, batches, x_ref, w_ref, att_ref, hidden_hbm, wd_hbm, gd_hbm, units_hbm,
+    d_ref, out_ref, out_grad_ref, down_hbm, units_in,
     buf, hidden_ref, wd_ref, rights, tiles, grad_acc, send, recv, load, right_sem, tile_sem,
-    acc, cross_out, line_out, cross_in, line_in, sum_send, sum_recv,
+    part_send, part_recv, acc, cross_out, line_out, cross_in, line_in, sum_send, sum_recv,
 ):
     line = Line(chips)
     rows = x_ref.shape[0]
@@ -1015,12 +1073,14 @@
 
         stored(tile).start()
 
-    meet(line.greet())
+    meet(line.greet() + greet_seq(seqs))
+    sums = ToSeq(seqs, units_hbm, units_in, part_send, part_recv)
     spread = Spread(line, x_ref, buf, send, recv)
     reduce = Reduce(
         line, product, out_ref, acc, cross_out, line_out, cross_in, line_in, sum_send, sum_recv
     )
     spread.begin()
+    sums.begin()
     right(0).start()
     buf[line.own] = x_ref[...]
     grad_acc[...] = jnp.zeros_like(grad_acc)
@@ -1061,11 +1121,12 @@
     out_grad_ref[...] = to_half(grad_acc[...])
     spread.sent()
     reduce.sent()
+    sums.end()
     stored(count - 2).wait()
     stored(count - 1).wait()
 
 
-def branch_back(chips, batches, x, w, attended, hidden, wd, group_d, collective):
+def branch_back(seqs, chips, batches, x, w, attended, hidden, wd, group_d, unit_part, collective):
     rows, width = x.shape
     group = 2 * chips
     length = group * rows // batches
@@ -1074,15 +1135,16 @@
     half = jnp.bfloat16
     part = 256 if group * rows <= 2048 else 128
     return pl.pallas_call(
-        functools.partial(branch_back_kernel, chips, batches),
+        functools.partial(branch_back_kernel, seqs, chips, batches),
         out_shape=[
             jax.ShapeDtypeStruct((batches, length, span), half),
             jax.ShapeDtypeStruct((rows, width), jnp.float32),
             jax.ShapeDtypeStruct((span, width), half),
             jax.ShapeDtypeStruct((units, width), half),
+            jax.ShapeDtypeStruct((seqs, width // seqs, unit_part.shape[1]), half),
         ],
-        in_specs=[VMEM_SPEC] * 3 + [ANY_SPEC] * 3,
-        out_specs=[VMEM_SPEC, VMEM_SPEC, VMEM_SPEC, ANY_SPEC],
+        in_specs=[VMEM_SPEC] * 3 + [ANY_SPEC] * 4,
+        out_specs=[VMEM_SPEC, VMEM_SPEC, VMEM_SPEC, ANY_SPEC, ANY_SPEC],
         scratch_shapes=[
             pltpu.VMEM((group, rows, width), half),
             pltpu.VMEM(hidden.shape, half),
@@ -1095,6 +1157,8 @@
             sems(2),
             sems(2),
             sems(2),
+            sems(seqs),
+            sems(seqs),
         ]
         + Reduce.scratch(chips, rows, width),
         compiler_params=comm_params(collective, 62),
@@ -1104,19 +1168,44 @@
             2 * group * rows * width * 2,
         ),
         name="branch_back",
-    )(x, w, attended, hidden, wd, group_d.reshape(group * rows, width))
+    )(x, w, attended, hidden, wd, group_d.reshape(group * rows, width), unit_part)
 
 
 def attend_back_kernel(
-    seqs, group, block, q_ref, pad_ref, low_ref, lse_ref, d_ref, sums_ref, heads_ref, cols_ref,
+    seqs, group, block, q_ref, pad_ref, low_ref, lse_ref, d_ref, part_hbm, in_hbm, heads_ref, cols_ref,
     dk, dv, kt, back_out, back_in, halo_send, halo_recv, swap_send, swap_recv, swap_keep,
+    parts, sums_ref, load,
 ):
     seq = lax.axis_index("seq")
     batches, length, span = q_ref.shape
     has_left, has_right = seq > 0, seq < seqs - 1
+    run = parts.shape[1]
+
+    def loaded(place, own):
+        source = part_hbm.at[rows_at(seq, run)] if own else in_hbm.at[place]
+        return pltpu.make_async_copy(source, parts.at[place], load.at[place])
+
+    for place in range(seqs):
+        pl.when(place == seq)(lambda place=place: loaded(place, True).start())
+        pl.when(place != seq)(lambda place=place: loaded(place, False).start())
     pl.when(has_left)(lambda: signal_seq(seq - 1))
     pl.when(has_right)(lambda: signal_seq(seq + 1))
     meet(greet_group(group) + has_left.astype(jnp.int32) + has_right.astype(jnp.int32))
+    for place in range(seqs):
+        loaded(place, False).wait()
+
+    @pl.loop(0, group)
+    def _(member):
+        share = run // group
+
+        @pl.loop(0, share // 16)
+        def _(chunk):
+            here = pl.ds(pl.multiple_of(member * share + chunk * 16, 16), 16)
+            added = parts[0, here, :].astype(jnp.float32)
+            for place in range(1, seqs):
+                added = added + parts[place, here, :].astype(jnp.float32)
+            sums_ref[member, rows_at(chunk, 16), :] = to_half(added)
+
     swap = Swap(group, sums_ref, cols_ref, swap_send, swap_recv, swap_keep)
     swap.begin()
     steps = length // block
@@ -1205,17 +1294,19 @@
     swap.end()
 
 
-def attend_back(seqs, group, query, kv_pad, low, lse, d_att, block, sums, collective):
+def attend_back(seqs, group, query, kv_pad, low, lse, d_att, block, part, parts_in, collective):
     batches, length, span = query.shape
     padded = kv_pad.shape[1]
     half = jnp.bfloat16
+    share = part.shape[0] // seqs // group
+    sums = (group, share, part.shape[1])
     return pl.pallas_call(
         functools.partial(attend_back_kernel, seqs, group, block),
-        in_specs=[VMEM_SPEC] * 5 + [ANY_SPEC],
+        in_specs=[VMEM_SPEC] * 5 + [ANY_SPEC] * 2,
         out_specs=[VMEM_SPEC, ANY_SPEC],
         out_shape=[
             jax.ShapeDtypeStruct((batches, length, 3 * span), half),
-            jax.ShapeDtypeStruct(sums.shape, half),
+            jax.ShapeDtypeStruct(sums, half),
         ],
         scratch_shapes=[
             pltpu.VMEM((batches, padded, span), jnp.float32),
@@ -1228,19 +1319,21 @@
             sems(group),
             sems(group),
             pltpu.SemaphoreType.DMA,
+            pltpu.VMEM(parts_in.shape, half),
+            pltpu.VMEM(sums, half),
+            sems(seqs),
         ],
         compiler_params=comm_params(collective),
         cost_estimate=cost(
-            20 * batches * length * span * (WINDOW + block), 180 * MIB, sums.size * 2
+            20 * batches * length * span * (WINDOW + block), 180 * MIB, part.size // seqs * 2
         ),
         name="attend_back",
-    )(query, kv_pad, low, lse, d_att, sums)
+    )(query, kv_pad, low, lse, d_att, part, parts_in)
 
 
 def heads_back_kernel(
-    seqs, chips, a_ref, w_ref, g_hbm, v_ref, dm_ref, gain_ref, mlp_gain_ref,
-    grad_ref, cols_ref, tile_ref,
-    total, gain_acc, lefts, parts, sums, cols, gain_out, gain_in, gain_sum, gain_back,
+    seqs, chips, a_ref, w_ref, g_hbm, v_ref, dm_ref, gain_ref, mlp_gain_ref, units_hbm,
+    grad_ref, cols_ref, tile_ref, gate_ref, up_ref, units, unit_load, total, gain_acc, lefts, parts, sums, cols, gain_out, gain_in, gain_sum, gain_back,
     left_sem, part_send, part_recv, cols_send, cols_recv, cols_keep,
     gain_send, gain_recv, back_send, back_recv,
     acc, cross_out, line_out, cross_in, line_in, sum_send, sum_recv,
@@ -1287,15 +1380,17 @@
     def product(slot, tile):
         return dot_nt(left_rows(a_ref, slot, rows), w_ref[rows_at(tile, TILE), :])
 
+    units_in = pltpu.make_async_copy(units_hbm, units, unit_load)
+    units_in.start()
     left(0).start()
     meet(greet_group(group) + greet_seq(seqs))
     reduce = Reduce(
         line, product, total, acc, cross_out, line_out, cross_in, line_in, sum_send, sum_recv
     )
     count = width // part
-    per = -(-count // (2 * chips - 3))
-
-    @pl.loop(0, 2 * chips - 3)
+    per = -(-count // 2)
+
+    @pl.loop(0, 2)
     def _(step):
         reduce.step(step)
 
@@ -1305,7 +1400,42 @@
             pl.when(tile < count)(lambda: weight_grad(tile))
 
     others(seqs, seq, lambda peer: to_seq(peer, seq).start())
-    pl.loop(2 * chips - 3, 2 * chips - 1)(reduce.step)
+    units_in.wait()
+    block = units.shape[2] // 2 // seqs
+    for member in range(group):
+        for place in range(seqs):
+            column = (place * group + member) * block
+            for target, begin in ((gate_ref, 0), (up_ref, seqs * block)):
+                here = slice(begin + place * block, begin + (place + 1) * block)
+                target[:, column : column + block] = units[member, :, here].astype(jnp.float32)
+
+    pl.loop(2, 2 * chips - 2)(reduce.step)
+
+    def block_swap(peer, member):
+        return pltpu.make_async_remote_copy(
+            src_ref=parts.at[rows_at(seq * group + peer, share)],
+            dst_ref=cols.at[member],
+            send_sem=cols_send.at[peer],
+            recv_sem=cols_recv.at[member],
+            device_id={"fsdp": peer},
+            device_id_type=MESH,
+        )
+
+    others(seqs, seq, lambda peer: to_seq(peer, peer).wait_recv())
+
+    @pl.loop(0, run // 64)
+    def _(chunk):
+        here = rows_at(chunk, 64)
+        there = pl.ds(pl.multiple_of(seq * run + chunk * 64, 64), 64)
+        added = parts[there, :].astype(jnp.float32)
+        for place in range(seqs):
+            piece = sums[place, here, :].astype(jnp.float32)
+            added = added + jnp.where(place == seq, 0.0, piece)
+        parts[there, :] = to_half(added)
+
+    others(group, own, lambda peer: block_swap(peer, own).start())
+    cols[own] = parts[rows_at(seq * group + own, share), :]
+    reduce.step(2 * chips - 2)
 
     def put(here, d_values):
         grad_ref[here, :] = dm_ref[here, :] + d_values
@@ -1341,32 +1471,8 @@
             device_id_type=MESH,
         )
 
-    def block_swap(peer, member):
-        return pltpu.make_async_remote_copy(
-            src_ref=parts.at[rows_at(seq * group + peer, share)],
-            dst_ref=cols.at[member],
-            send_sem=cols_send.at[peer],
-            recv_sem=cols_recv.at[member],
-            device_id={"fsdp": peer},
-            device_id_type=MESH,
-        )
-
     others(group, own, lambda peer: gain_group(peer, own).start())
     gain_in[own] = gain_out[own // fold]
-    others(seqs, seq, lambda peer: to_seq(peer, peer).wait_recv())
-
-    @pl.loop(0, run // 64)
-    def _(chunk):
-        here = rows_at(chunk, 64)
-        there = pl.ds(pl.multiple_of(seq * run + chunk * 64, 64), 64)
-        added = parts[there, :].astype(jnp.float32)
-        for place in range(seqs):
-            piece = sums[place, here, :].astype(jnp.float32)
-            added = added + jnp.where(place == seq, 0.0, piece)
-        parts[there, :] = to_half(added)
-
-    others(group, own, lambda peer: block_swap(peer, own).start())
-    cols[own] = parts[rows_at(seq * group + own, share), :]
     others(group, own, lambda peer: gain_group(peer, peer).wait_recv())
     gain_sum[...] = jnp.sum(gain_in[...], axis=0)
     others(seqs, seq, lambda peer: gain_seq(peer, seq).start())
@@ -1384,7 +1490,7 @@
     kept.wait()
 
 
-def heads_back(seqs, chips, a, w, group_a, x, d_middle, gain, mlp_gain, collective):
+def heads_back(seqs, chips, a, w, group_a, x, d_middle, gain, mlp_gain, units, collective):
     rows, width = x.shape
     batches, length, depth = a.shape
     group = 2 * chips
@@ -1398,10 +1504,14 @@
             jax.ShapeDtypeStruct((rows, width), jnp.float32),
             jax.ShapeDtypeStruct((group, share, depth), half),
             jax.ShapeDtypeStruct((8, 128), jnp.float32),
+            jax.ShapeDtypeStruct((share, units.size // 2 // share), jnp.float32),
+            jax.ShapeDtypeStruct((share, units.size // 2 // share), jnp.float32),
         ],
-        in_specs=[VMEM_SPEC, VMEM_SPEC, ANY_SPEC] + [VMEM_SPEC] * 4,
-        out_specs=[VMEM_SPEC, ANY_SPEC, VMEM_SPEC],
+        in_specs=[VMEM_SPEC, VMEM_SPEC, ANY_SPEC] + [VMEM_SPEC] * 4 + [ANY_SPEC],
+        out_specs=[VMEM_SPEC, ANY_SPEC, VMEM_SPEC, VMEM_SPEC, VMEM_SPEC],
         scratch_shapes=[
+            pltpu.VMEM(units.shape, half),
+            pltpu.SemaphoreType.DMA,
             pltpu.VMEM((rows, width), jnp.float32),
             pltpu.VMEM((8, width), jnp.float32),
             pltpu.VMEM((2, batches, length, part), half),
@@ -1429,7 +1539,7 @@
             4 * group * rows * width * depth, 200 * MIB, 2 * group * rows * width * 2
         ),
         name="heads_back",
-    )(a, w, group_a, x, d_middle, gain, mlp_gain)
+    )(a, w, group_a, x, d_middle, gain, mlp_gain, units)
 
 
 def doc_starts(lengths, positions, batches, seq_len):
@@ -1507,15 +1617,13 @@
     both = jnp.stack([gain_attn, gain_mlp]).astype(jnp.float32)
     tile = jnp.where(here[None], jnp.tile(both, (1, fold)), 0.0)
     tile = jnp.pad(tile, ((0, 6), (0, 0)))[None]
-    group_a, query, key_value, gains, w_heads = start(
+    group_a, query, kv_pad, gains, w_heads = start(
         seqs, chips, batches, tile, tokens.reshape(rows, width), attn_blocks, 1
     )
     gains = gains.transpose(1, 0, 2, 3).reshape(devices // fold, fold, 8, 128).sum(axis=1)
     gain_one = gains[:, 0].reshape(width)
     gain_two = gains[:, 1].reshape(width)
-    attended, lse, kv_pad, unit_own = attend(
-        seqs, group, query, key_value, low, block, unit_blocks, 2
-    )
+    attended, lse, unit_own = attend(group, query, kv_pad, low, block, unit_blocks, 2)
     branch, group_d, w_units = branch_sum(
         seqs, chips, attended, wo_part, cotangent.reshape(rows, width),
         unit_own.reshape(group * share, -1), 3,
@@ -1531,14 +1639,13 @@
     def over_seq(values):
         return lax.psum_scatter(values, "seq", scatter_dimension=0, tiled=True)
 
-    unit_sums = over_seq(unit_part).reshape(group, share, -1)
-    d_attended, mlp_out, out_grad, down_grad = branch_back(
-        chips, batches, d_branch, wo_part, attended, hidden, wd_part, group_d, 6
+    d_attended, mlp_out, out_grad, down_grad, unit_in = branch_back(
+        seqs, chips, batches, d_branch, wo_part, attended, hidden, wd_part, group_d, unit_part, 6
     )
     outputs = middle + mlp_out
     down_sum = over_seq(down_grad)
     d_heads, unit_cols = attend_back(
-        seqs, group, query, kv_pad, low, lse, d_attended, block, unit_sums, 7
+        seqs, group, query, kv_pad, low, lse, d_attended, block, unit_part, unit_in, 7
     )
     if aligned:
         out_sum = over_seq(out_grad)
@@ -1547,9 +1654,9 @@
             jnp.zeros((width, width), jnp.bfloat16), out_grad, member * span, 0
         )
         out_sum = lax.psum_scatter(whole, ("seq", "fsdp"), scatter_dimension=0, tiled=True)
-    input_grad, head_cols, gain_tile = heads_back(
+    input_grad, head_cols, gain_tile, w_gate_grad, w_up_grad = heads_back(
         seqs, chips, d_heads, w_heads, group_a, tokens.reshape(rows, width), d_middle,
-        gain_one[None], mlp_gain_part, 8,
+        gain_one[None], mlp_gain_part, unit_cols, 8,
     )
     input_grad = input_grad.reshape(batches, piece, width)
     layer_out = to_half(outputs).reshape(batches, piece, width)
@@ -1568,8 +1675,8 @@
         whole_rows(head_cols, 2, width),
         out_sum.astype(jnp.float32),
         gain_grads[1],
-        whole_rows(unit_cols, 0, FF),
-        whole_rows(unit_cols, 1, FF),
+        w_gate_grad,
+        w_up_grad,
         down_sum.astype(jnp.float32),
     )
 

time: 1010 us -> 873 us (0.86)
  waiting for transfers between devices: 168 us -> 1.94 us
  Pallas kernels: 754 us -> 801 us
    reduce_scatter x3 -> x2, waiting for transfers between devices: 165 us -> 0.01 us  [over_seq(): return lax.psum_scatter(values, 'seq', scatter_dimension=0, tiled=True)]
    pallas_call x1, Pallas kernels: 99.3 us -> 136 us  [start(): pl.pallas_call(functools.partial(start_kernel, seqs, chips, batches), out...]
    pallas_call x1, Pallas kernels: 60.1 us -> 88.4 us  [attend_back(): pl.pallas_call(functools.partial(attend_back_kernel, seqs, group, block),...]
    pallas_call x1, Pallas kernels: 119 us -> 105 us  [branch_sum(): pl.pallas_call(functools.partial(branch_kernel, seqs, chips), out_shape=[...]
  transfers between devices with their start and end apart: 5 -> 4, of which waited for: 3 -> 0; matrix products, arithmetic and copies ran while one was open for 3% -> 4% of each run, Pallas kernels for 28% -> 58%
where the time goes in v4:
time: 873 us; the launch traced here: 865 us
  Pallas kernels  801 us (92%)
  local copies, waits for them, and re-layouts  27.8 us (3%)
  other arithmetic  19.4 us (2%)
  between operations  14.6 us (2%)
    pallas_call x1, Pallas kernels, start(): pl.pallas_call(functools.partial(start_kernel, seqs, chips, batches), out...  136 us
    pallas_call x1, Pallas kernels, heads_back(): pl.pallas_call(functools.partial(heads_back_kernel, seqs, chips), out_sha...  118 us
    pallas_call x1, Pallas kernels, units_back(): pl.pallas_call(functools.partial(units_back_kernel, chips), out_shape=[ja...  115 us
    pallas_call x1, Pallas kernels, branch_back(): pl.pallas_call(functools.partial(branch_back_kernel, seqs, chips, batches...  108 us
    pallas_call x1, Pallas kernels, branch_sum(): pl.pallas_call(functools.partial(branch_kernel, seqs, chips), out_shape=[...  105 us
    pallas_call x1, Pallas kernels, attend_back(): pl.pallas_call(functools.partial(attend_back_kernel, seqs, group, block),...  88.4 us
    pallas_call x1, Pallas kernels, hidden_units(): pl.pallas_call(functools.partial(units_kernel, chips), out_shape=[jax.Sha...  76.1 us
    pallas_call x1, Pallas kernels, attend(): pl.pallas_call(functools.partial(attend_kernel, group, block), in_specs=[...  52.9 us
  transfers between devices with their start and end apart: 4, of which 0 were waited for; matrix products, arithmetic and copies ran while one was open for 4% of the time, Pallas kernels for 58%

profile of v4, /device:TPU:9, one launch (start us, length us, event | category | flops | bytes accessed | tf_op | source)
XLA Modules:
  0.0 864.7 jit_solution(759466985631563228)
XLA Ops:
  9.5 0.8 reduce_window_sum.11
  11.0 1.5 reshape.233
  13.8 1.0 reshape.236
  15.6 1.0 reshape.238
  17.3 0.8 reshape.240
  20.2 2.0 pad_maximum_fusion.1.blocks_ref
  22.2 136.3 %start.1 = (bf16[2,1024,2048]{2,1,0:T(8,128)(2,1)}, bf16[2,1024,256]{2,1,0:T(8,128)(2,1)}, bf16[2,2048,512]{2,1,0:T(8,128)(2,1)}, f32[8,4,8,128]{3,2,1,0:T(8,128)}, bf16[2048,768]{1,0:T(8,128)(2,1)}) custom-call(f32[1,8,128]{2,1,0:T(8,128)} %pad_bitcast_fusion.tile_ref, bf16[256,2048]{1,0:T(8,128)(2,1)} %bitcast.69, ...), custom_call_target="tpu_custom_call" | custom-call | flops 6442450944 | bytes 209715200 | tf_op jit(solution)/shard_map/start/pallas_call | solution.py:659
  158.4 0.9 copy.54
  160.1 1.5 pad_maximum_fusion.units_ref
  162.3 52.9 %attend.1 = (bf16[2,1024,256]{2,1,0:T(8,128)(2,1)}, f32[2,4,1024]{2,1,0:T(4,128)}, bf16[8,64,2048]{2,1,0:T(8,128)(2,1)}) custom-call(bf16[2,1024,256]{2,1,0:T(8,128)(2,1)} %get-tuple-element.41.q_ref, bf16[2,2048,512]{2,1,0:T(8,128)(2,1)} %get-tuple-element.42.pad.pad_ref, s32[2,1,1024]{2,1,0:T(1,128)} %maximum_subtract_fusion.low_ref, ...), custom_call_target="tpu_custom_call" | custom-call | flops 5368709120 | bytes 157286400 | tf_op jit(solution)/shard_map/attend/pallas_call | solution.py:742
  215.2 105.4 %branch_sum.1 = (f32[256,2048]{1,0:T(8,128)}, bf16[8,256,2048]{2,1,0:T(8,128)(2,1)}, bf16[4,512,2048]{2,1,0:T(8,128)(2,1)}) custom-call(bf16[2,1024,256]{2,1,0:T(8,128)(2,1)} %get-tuple-element.43.a_ref.att_ref, bf16[256,2048]{1,0:T(8,128)(2,1)} %all-gather.3.cloned.1.call-done.w_ref, bf16[256,2048]{1,0:T(8,128)(2,1)} %bitcast.76, bf16[512,2048]{1,0:T(8,128)(2,1)} %bitcast.82), custom_call_target="tpu_custom_call" | custom-call | flops 2147483648 | bytes 262144000 | tf_op jit(solution)/shard_map/branch_sum/pallas_call | solution.py:803
  320.6 1.9 multiply_reduce_fusion
  322.6 1.4 multiply_convert_fusion.x_ref
  324.0 76.1 %hidden_units.1 = (bf16[8,256,2048]{2,1,0:T(8,128)(2,1)}, bf16[2048,1024]{1,0:T(8,128)(2,1)}, bf16[2048,2048]{1,0:T(8,128)(2,1)}) custom-call(bf16[256,2048]{1,0:T(8,128)(2,1)} %multiply_convert_fusion.x_ref, bf16[2048,2048]{1,0:T(8,128)(2,1)} %bitcast.79, bf16[1024,2048]{1,0:T(8,128)(2,1)} %all-gather.5.cloned.1.call-done.wd_hbm, ...), custom_call_target="tpu_custom_call" | custom-call | flops 25769803776 | bytes 209715200 | tf_op jit(solution)/shard_map/hidden_units/pallas_call | solution.py:889
  400.1 115.2 %units_back.1 = (f32[256,2048]{1,0:T(8,128)}, bf16[256,2048]{1,0:T(8,128)(2,1)}, f32[8,2048]{1,0:T(8,128)}, bf16[2048,2048]{1,0:T(8,128)(2,1)}) custom-call(bf16[2048,2048]{1,0:T(8,128)(2,1)} %get-tuple-element.49.a_hbm, bf16[2048,2048]{1,0:T(8,128)(2,1)} %bitcast.80, bf16[2048,2048]{1,0:T(8,128)(2,1)} %bitcast.81, f32[256,2048]{1,0:T(8,128)} %copy-done, ...), custom_call_target="tpu_custom_call" | custom-call | flops 34359738368 | bytes 209715200 | tf_op jit(solution)/shard_map/units_back/pallas_call | solution.py:1000
  515.3 108.0 %branch_back.1 = (bf16[2,1024,256]{2,1,0:T(8,128)(2,1)}, f32[256,2048]{1,0:T(8,128)}, bf16[256,2048]{1,0:T(8,128)(2,1)}, bf16[1024,2048]{1,0:T(8,128)(2,1)}, bf16[4,512,2048]{2,1,0:T(8,128)(2,1)}) custom-call(bf16[256,2048]{1,0:T(8,128)(2,1)} %get-tuple-element.51.x_ref, bf16[256,2048]{1,0:T(8,128)(2,1)} %all-gather.3.cloned.1.call-done.w_ref, ...), custom_call_target="tpu_custom_call" | custom-call | flops 21474836480 | bytes 262144000 | tf_op jit(solution)/shard_map/branch_back/pallas_call | solution.py:1137
  624.0 88.4 %attend_back.1 = (bf16[2,1024,768]{2,1,0:T(8,128)(2,1)}, bf16[8,64,2048]{2,1,0:T(8,128)(2,1)}) custom-call(bf16[2,1024,256]{2,1,0:T(8,128)(2,1)} %get-tuple-element.41.q_ref, bf16[2,2048,512]{2,1,0:T(8,128)(2,1)} %get-tuple-element.42.pad.pad_ref, s32[2,1,1024]{2,1,0:T(1,128)} %maximum_subtract_fusion.low_ref, f32[2,4,1024]{2,1,0:T(4,128)} %get-tuple-element.55.lse_ref, ...), custom_call_target="tpu_custom_call" | custom-call | flops 13421772800 | bytes 188743680 | tf_op jit(solution)/shard_map/attend_back/pallas_call | solution.py:1303
  712.4 118.5 %heads_back.1 = (f32[256,2048]{1,0:T(8,128)}, bf16[8,64,768]{2,1,0:T(8,128)(2,1)}, f32[8,128]{1,0:T(8,128)}, f32[64,8192]{1,0:T(8,128)}, f32[64,8192]{1,0:T(8,128)}) custom-call(bf16[2,1024,768]{2,1,0:T(8,128)(2,1)} %get-tuple-element.58.a_ref, bf16[2048,768]{1,0:T(8,128)(2,1)} %get-tuple-element.59.w_ref, bf16[2,1024,2048]{2,1,0:T(8,128)(2,1)} %get-tuple-element.60.g_hbm, ...), custom_call_target="tpu_custom_call" | custom-call | flops 12884901888 | bytes 209715200 | tf_op jit(solution)/shard_map/heads_back/pallas_call | solution.py:1501
  831.6 2.1 slice_convert_fusion
  834.8 1.2 reshape.253
  837.0 1.2 reshape.252
  838.1 1.5 reshape.254
  839.6 1.6 copy.55
  841.2 2.4 reshape.251
  844.2 2.8 add_convert_fusion
  847.0 1.9 convert_element_type.73
  848.9 2.8 convert_element_type.74
  851.7 1.3 copy.73
  853.0 1.0 copy-done.3
  854.1 1.3 copy.74
  855.4 1.0 copy-done.2
  856.4 1.3 copy.75
  (63 shorter events, 13.0 us)
Async XLA Ops:
  7.2 5.9 copy-start.8
  7.2 208.0 %all-gather.3.cloned.1.call-start = ((), (), s32[]{:S(2)}) async-start(), calls=%async_computation.2 | async-start | bytes 1310720 | tf_op jit(solution)/shard_map/all_gather | solution.py:1598
  7.9 316.1 %all-gather.5.cloned.1.call-start = ((), (), s32[]{:S(2)}) async-start(), calls=%async_computation.3 | async-start | bytes 5242880 | tf_op jit(solution)/shard_map/all_gather | solution.py:1596
  8.7 838.3 %reduce-scatter.3.cloned.1.call-start = ((), (), s32[]{:S(2)}) async-start(), calls=%async_computation.4 | async-start | bytes 1310720 | tf_op jit(solution)/shard_map/reduce_scatter | solution.py:1640
  12.5 2.4 copy-start.9
  13.6 3.1 copy-start.5
  16.9 1.2 copy-start.6
  215.2 105.4 %copy-start.7 = (bf16[2,128,2048]{2,1,0:T(8,128)(2,1)S(1)}, bf16[2,128,2048]{2,1,0:T(8,128)(2,1)}, u32[]{:S(2)}) copy-start(bf16[2,128,2048]{2,1,0:T(8,128)(2,1)} %param.12) | copy-start | bytes 3145732
  322.6 77.5 %copy-start = (f32[256,2048]{1,0:T(8,128)}, f32[256,2048]{1,0:T(8,128)S(1)}, u32[]{:S(2)}) copy-start(f32[256,2048]{1,0:T(8,128)S(1)} %get-tuple-element.72.v_ref) | copy-start | bytes 6291460
  623.4 225.5 %reduce-scatter.5.cloned.1.call-start = ((), (), s32[]{:S(2)}) async-start(), calls=%async_computation.5 | async-start | bytes 5242880 | tf_op jit(solution)/shard_map/reduce_scatter | solution.py:1640
  839.6 4.6 copy-start.1
  847.0 4.7 copy-start.4
  851.7 2.3 copy-start.3
  854.1 2.3 copy-start.2
Sparse Core Ops, SparseCore 0:
  9.9 31.5 all-gather.2
  43.3 81.3 all-gather.4
  623.5 32.9 reduce-scatter.2
  659.6 73.7 reduce-scatter.4

commit v5 on v4

--- a/solution.py
+++ b/solution.py
@@ -189,36 +189,39 @@
         self.line, self.product, self.out, self.acc = line, product, out, acc
         self.cross_out, self.line_out, self.cross_in, self.line_in = cross_out, line_out, cross_in, line_in
         self.send, self.recv = send, recv
+        self.tiles = line_out.shape[2] // TILE
 
     @staticmethod
     def scratch(chips, rows, width):
         part = pltpu.VMEM((chips, rows, width), jnp.bfloat16)
         return [
-            pltpu.VMEM((rows, width), jnp.float32),
+            pltpu.VMEM((rows, TILE), jnp.float32),
             pltpu.VMEM((rows, width), jnp.bfloat16),
             part,
             part,
             pltpu.VMEM((chips + 1, rows, width), jnp.bfloat16),
-            pltpu.SemaphoreType.DMA((2, chips)),
-            pltpu.SemaphoreType.DMA((2, chips + 1)),
+            pltpu.SemaphoreType.DMA((2, chips, width // TILE)),
+            pltpu.SemaphoreType.DMA((2, chips + 1, width // TILE)),
         ]
 
-    def cross(self, place):
+    def cross(self, place, tile):
+        here = rows_at(tile, TILE)
         return pltpu.make_async_remote_copy(
-            src_ref=self.cross_out,
-            dst_ref=self.cross_in.at[place],
-            send_sem=self.send.at[0, place],
-            recv_sem=self.recv.at[0, place],
+            src_ref=self.cross_out.at[:, here],
+            dst_ref=self.cross_in.at[place, :, here],
+            send_sem=self.send.at[0, place, tile],
+            recv_sem=self.recv.at[0, place, tile],
             device_id={"fsdp": self.line.other},
             device_id_type=MESH,
         )
 
-    def along(self, place, landing, peer):
+    def along(self, place, landing, tile, peer):
+        here = rows_at(tile, TILE)
         return pltpu.make_async_remote_copy(
-            src_ref=self.line_out.at[place],
-            dst_ref=self.line_in.at[landing],
-            send_sem=self.send.at[1, place],
-            recv_sem=self.recv.at[1, landing],
+            src_ref=self.line_out.at[place, :, here],
+            dst_ref=self.line_in.at[landing, :, here],
+            send_sem=self.send.at[1, place, tile],
+            recv_sem=self.recv.at[1, landing, tile],
             device_id={"fsdp": peer},
             device_id_type=MESH,
         )
@@ -228,75 +231,70 @@
 
     def step(self, step):
         line, acc = self.line, self.acc
-        tiles = acc.shape[1] // TILE
         away = line.chips - 1 - step // 2
-        side = lax.rem(step, 2)
-        place = line.chip + away * (1 - 2 * side)
+        rightward = lax.rem(step, 2) == 0
+        place = line.chip + jnp.where(rightward, away, -away)
+        upstream = (rightward & line.has_left) | (jnp.logical_not(rightward) & line.has_right)
 
         @pl.when((place >= 0) & (place < line.chips))
         def _():
-            @pl.loop(0, tiles)
+            @pl.loop(0, self.tiles)
             def _(tile):
                 got = self.product(place * 2 + 1 - line.core, tile)
                 self.cross_out[:, rows_at(tile, TILE)] = to_half(got)
-
-            self.cross(place).start()
-
-            @pl.loop(0, tiles)
+                self.cross(place, tile).start()
+
+            @pl.loop(0, self.tiles)
             def _(tile):
-                acc[:, rows_at(tile, TILE)] = self.product(place * 2 + line.core, tile)
-
-            self.cross(place).wait()
-
-            @pl.when(away > 0)
-            def _():
-                rightward = side == 0
-                upstream = (rightward & line.has_left) | (jnp.logical_not(rightward) & line.has_right)
-
-                @pl.when(upstream)
+                here = rows_at(tile, TILE)
+                acc[...] = self.product(place * 2 + line.core, tile)
+                self.cross(place, tile).wait()
+                acc[...] += self.cross_in[place, :, here].astype(jnp.float32)
+
+                @pl.when(away > 0)
                 def _():
-                    self.along(place, place, line.own).wait_recv()
-                    self.line_out[place] = to_half(
-                        acc[...]
-                        + self.cross_in[place].astype(jnp.float32)
-                        + self.line_in[place].astype(jnp.float32)
-                    )
-
-                @pl.when(jnp.logical_not(upstream))
+                    @pl.when(upstream)
+                    def _():
+                        self.along(place, place, tile, line.own).wait_recv()
+                        self.line_out[place, :, here] = to_half(
+                            acc[...] + self.line_in[place, :, here].astype(jnp.float32)
+                        )
+
+                    @pl.when(jnp.logical_not(upstream))
+                    def _():
+                        self.line_out[place, :, here] = to_half(acc[...])
+
+                    @pl.when(rightward)
+                    def _():
+                        self.along(place, place, tile, line.own + 2).start()
+
+                    @pl.when(jnp.logical_not(rightward))
+                    def _():
+                        landing = jnp.where(away == 1, line.chips, place)
+                        self.along(place, landing, tile, line.own - 2).start()
+
+                @pl.when(away == 0)
                 def _():
-                    self.line_out[place] = to_half(
-                        acc[...] + self.cross_in[place].astype(jnp.float32)
-                    )
-
-                @pl.when(rightward)
-                def _():
-                    self.along(place, place, line.own + 2).start()
-
-                @pl.when(jnp.logical_not(rightward))
-                def _():
-                    landing = jnp.where(away == 1, line.chips, place)
-                    self.along(place, landing, line.own - 2).start()
-
-            @pl.when(away == 0)
-            def _():
-                self.out[...] = acc[...] + self.cross_in[place].astype(jnp.float32)
-
-                @pl.when(line.has_left)
-                def _():
-                    self.along(place, place, line.own).wait_recv()
-                    self.out[...] += self.line_in[place].astype(jnp.float32)
-
-                @pl.when(line.has_right)
-                def _():
-                    self.along(place, line.chips, line.own).wait_recv()
-                    self.out[...] += self.line_in[line.chips].astype(jnp.float32)
+                    self.out[:, here] = acc[...]
+
+                    @pl.when(line.has_left)
+                    def _():
+                        self.along(place, place, tile, line.own).wait_recv()
+                        self.out[:, here] += self.line_in[place, :, here].astype(jnp.float32)
+
+                    @pl.when(line.has_right)
+                    def _():
+                        self.along(place, line.chips, tile, line.own).wait_recv()
+                        self.out[:, here] += self.line_in[line.chips, :, here].astype(jnp.float32)
 
     def sent(self):
         @pl.loop(0, self.line.chips)
         def _(place):
-            pl.when(place != self.line.chip)(
-                lambda: self.along(place, place, self.line.own).wait_send()
-            )
+            @pl.when(place != self.line.chip)
+            def _():
+                pl.loop(0, self.tiles)(
+                    lambda tile: self.along(place, place, tile, self.line.own).wait_send()
+                )
 
 
 class Swap:
@@ -438,9 +436,9 @@
 def norm_back(rows, v_ref, e_ref, gain_ref, gain_acc, put):
     gain_acc[...] = jnp.zeros_like(gain_acc)
 
-    @pl.loop(0, rows // 16)
+    @pl.loop(0, rows // 32)
     def _(chunk):
-        here = rows_at(chunk, 16)
+        here = rows_at(chunk, 32)
         values = v_ref[here, :].astype(jnp.float32)
         error = e_ref[here, :]
         rate = lax.rsqrt(jnp.mean(values * values, axis=-1, keepdims=True) + EPS)
@@ -448,13 +446,32 @@
         product = error * unit
         gain = gain_ref[0:1, :]
         mean = jnp.mean(product * gain, axis=-1, keepdims=True)
-        gain_acc[...] += product[0:8] + product[8:16]
+        gain_acc[...] += (product[0:8] + product[8:16]) + (product[16:24] + product[24:32])
         put(here, rate * (gain * error - unit * mean))
 
 
+def add_from_seq(seqs, own_rows, got, here):
+    seq = lax.axis_index("seq")
+    added = own_rows.astype(jnp.float32)
+    for place in range(seqs):
+        piece = got[place, here, :].astype(jnp.float32)
+        added = added + jnp.where(place == seq, 0.0, piece)
+    return added
+
+
+def column_parts(seqs, group, share, span):
+    size = HEAD if share == HEAD else span
+    parts = []
+    for member in range(group):
+        for run in range(span // size):
+            home = (run * group + member) * size
+            parts.append((member, run * size, home, size))
+    return parts
+
+
 def start_kernel(
-    seqs, chips, batches, tile_ref, x_ref, blocks_ref, g_ref, q_ref, pad_ref, gains_ref, w_out_ref,
-    buf, normed, kv_ref, zeros, halo_send, halo_recv, pad_keep, gain, gains, w, send, recv, keep, swap_send, share_send, w_recv,
+    seqs, chips, batches, tile_ref, x_ref, wq_ref, wk_ref, wv_ref, g_ref, q_ref, kv_ref, gains_ref, w_out_ref,
+    blocks_ref, buf, normed, gain, gains, w, send, recv, keep, swap_send, share_send, w_recv,
     tile_send, tile_across, tile_recv, tile_back, w_keep, gain_keep,
 ):
     line = Line(chips)
@@ -466,9 +483,10 @@
     span = q_ref.shape[2]
     width = x_ref.shape[1]
     per = 128 * seqs * group // width
-    length = group * piece
-    first = length - WINDOW
-    has_left, has_right = seq > 0, seq < seqs - 1
+    for index, source in enumerate((wq_ref, wk_ref, wv_ref)):
+        for member, first, home, size in column_parts(seqs, group, share, span):
+            first = first + index * span
+            blocks_ref[member, :, first : first + size] = source[:, home : home + size]
     meet(greet_group(group) + greet_seq(seqs))
 
     def block_at(run, member):
@@ -547,65 +565,21 @@
             keep.at[slot, batch],
         )
 
-    def own_rows(slot, batch):
-        there = pl.ds(pl.multiple_of(slot * piece + WINDOW, piece), piece)
-        return pltpu.make_async_copy(
-            kv_ref.at[batch, rows_at(slot, piece)],
-            pad_ref.at[batch, there],
-            pad_keep.at[slot, batch],
-        )
-
-    def no_rows(place, batch):
-        return pltpu.make_async_copy(
-            zeros, pad_ref.at[batch, rows_at(place, piece)], halo_recv.at[place, batch]
-        )
-
-    def halo(slot, batch, peer):
-        there = pl.ds(pl.multiple_of(slot * piece - first, piece), piece)
-        return pltpu.make_async_remote_copy(
-            src_ref=kv_ref.at[batch, rows_at(slot, piece)],
-            dst_ref=pad_ref.at[batch, there],
-            send_sem=halo_send.at[slot, batch],
-            recv_sem=halo_recv.at[slot - first // piece, batch],
-            device_id={"seq": peer},
-            device_id_type=MESH,
-        )
-
-    @pl.when(jnp.logical_not(has_left))
-    def _():
-        zeros[...] = jnp.zeros_like(zeros)
-
-        @pl.loop(0, WINDOW // piece)
-        def _(place):
-            for batch in range(batches):
-                no_rows(place, batch).start()
-
     def use(slot):
-        @pl.loop(0, x_ref.shape[0] // 16)
+        @pl.loop(0, x_ref.shape[0] // 64)
         def _(chunk):
-            rows = rows_at(chunk, 16)
+            rows = rows_at(chunk, 64)
             values = buf[slot, rows, :].astype(jnp.float32)
             normed[slot, rows, :] = to_half(normalize(values, gain[0:1, :]))
 
         for batch in range(batches):
             kept(slot, batch).start()
         rows = rows_at(slot, piece)
-        values = normed[slot]
-        for part in range(3):
-            got = to_half(dot_nn(values, w[:, part * span : (part + 1) * span]))
-            for batch in range(batches):
-                mine = got[batch * piece : (batch + 1) * piece]
-                if part == 0:
-                    q_ref[batch, rows, :] = mine
-                else:
-                    kv_ref[batch, rows, (part - 1) * span : part * span] = mine
+        got = to_half(dot_nn(normed[slot], w[...]))
         for batch in range(batches):
-            own_rows(slot, batch).start()
-
-        @pl.when(has_right & (slot * piece >= first))
-        def _():
-            for batch in range(batches):
-                halo(slot, batch, seq + 1).start()
+            mine = got[batch * piece : (batch + 1) * piece]
+            q_ref[batch, rows, :] = mine[:, :span]
+            kv_ref[batch, rows, :] = mine[:, span:]
 
     pl.loop(1, chips - 1)(spread.relay)
 
@@ -638,43 +612,31 @@
     def _(slot):
         for batch in range(batches):
             kept(slot, batch).wait()
-            own_rows(slot, batch).wait()
-
-    @pl.loop(0, WINDOW // piece)
-    def _(place):
-        slot = place + first // piece
-        for batch in range(batches):
-            pl.when(has_right)(lambda batch=batch: halo(slot, batch, seq).wait_send())
-            pl.when(has_left)(lambda batch=batch: halo(slot, batch, seq).wait_recv())
-            pl.when(jnp.logical_not(has_left))(lambda batch=batch: no_rows(place, batch).wait())
-
-
-def start(seqs, chips, batches, tile, x, blocks, collective):
+
+
+def start(seqs, chips, batches, tile, x, weights, collective):
     rows, width = x.shape
     group = 2 * chips
     length = group * rows // batches
-    share, cols = blocks.shape[1:]
-    span = cols // 3
+    share = weights[0].shape[0]
+    span = width // group
+    cols = 3 * span
     half = jnp.bfloat16
     return pl.pallas_call(
         functools.partial(start_kernel, seqs, chips, batches),
         out_shape=[
             jax.ShapeDtypeStruct((batches, length, width), half),
             jax.ShapeDtypeStruct((batches, length, span), half),
-            jax.ShapeDtypeStruct((batches, length + WINDOW, 2 * span), half),
+            jax.ShapeDtypeStruct((batches, length, 2 * span), half),
             jax.ShapeDtypeStruct((group, seqs, 8, 128), jnp.float32),
             jax.ShapeDtypeStruct((width, cols), half),
         ],
-        in_specs=[VMEM_SPEC] * 3,
-        out_specs=[ANY_SPEC, VMEM_SPEC, ANY_SPEC, ANY_SPEC, ANY_SPEC],
+        in_specs=[VMEM_SPEC] * 5,
+        out_specs=[ANY_SPEC, VMEM_SPEC, VMEM_SPEC, ANY_SPEC, ANY_SPEC],
         scratch_shapes=[
+            pltpu.VMEM((group, share, cols), half),
             pltpu.VMEM((group, rows, width), half),
             pltpu.VMEM((group, rows, width), half),
-            pltpu.VMEM((batches, length, 2 * span), half),
-            pltpu.VMEM((rows // batches, 2 * span), half),
-            sems(group, batches),
-            sems(WINDOW * group // length, batches),
-            sems(group, batches),
             pltpu.VMEM((8, width), jnp.float32),
             pltpu.VMEM((group, seqs, 8, 128), jnp.float32),
             pltpu.VMEM((width, cols), half),
@@ -694,22 +656,70 @@
         compiler_params=comm_params(collective),
         cost_estimate=cost(2 * group * rows * width * cols, 200 * MIB, group * rows * width * 2),
         name="start",
-    )(tile, x, blocks)
+    )(tile, x, *weights)
 
 
 def attend_kernel(
-    group, block, q_ref, pad, low_ref, units_ref, out_ref, lse_ref, own_units_ref,
-    vt, swap_send, swap_recv, swap_keep,
+    seqs, group, block, q_ref, kv_ref, low_ref, units_ref, out_ref, lse_ref, pad_ref, own_units_ref,
+    pad, vt_ref, halo_send, halo_recv, pad_keep, swap_send, swap_recv, swap_keep,
 ):
+    seq = lax.axis_index("seq")
     batches, length, span = q_ref.shape
-    meet(greet_group(group))
+    has_left, has_right = seq > 0, seq < seqs - 1
+    pl.when(has_left)(lambda: signal_seq(seq - 1))
+    pl.when(has_right)(lambda: signal_seq(seq + 1))
+    meet(greet_group(group) + has_left.astype(jnp.int32) + has_right.astype(jnp.int32))
+
+    steps, need = length // block, WINDOW // block
+
+    def halo(batch, step, peer):
+        return pltpu.make_async_remote_copy(
+            src_ref=kv_ref.at[batch, rows_at(step + steps - need, block)],
+            dst_ref=pad.at[batch, rows_at(step, block)],
+            send_sem=halo_send.at[batch, step],
+            recv_sem=halo_recv.at[batch, step],
+            device_id={"seq": peer},
+            device_id_type=MESH,
+        )
+
+    def send_halo(turn):
+        batch, step = turn // need, need - 1 - lax.rem(turn, need)
+        pl.when(has_right)(lambda: halo(batch, step, seq + 1).start())
+
+    def halo_sent(turn):
+        batch, step = turn // need, need - 1 - lax.rem(turn, need)
+        pl.when(has_right)(lambda: halo(batch, step, seq + 1).wait_send())
+
+    send_halo(0)
+    send_halo(1)
     swap = Swap(group, units_ref, own_units_ref, swap_send, swap_recv, swap_keep)
     swap.begin()
+    pad[:, WINDOW:, :] = kv_ref[...]
+
+    @pl.when(jnp.logical_not(has_left))
+    def _():
+        pad[:, :WINDOW, :] = jnp.zeros((batches, WINDOW, 2 * span), jnp.bfloat16)
+
+    def kept(batch):
+        return pltpu.make_async_copy(pad.at[batch], pad_ref.at[batch], pad_keep.at[batch])
+
+    vt = vt_ref
     for batch in range(batches):
-        vt[...] = pad[batch, :, span:].T
-
-        @pl.loop(0, length // block)
-        def _(step, batch=batch):
+        vt[:, WINDOW:] = pad[batch, WINDOW:, span:].T
+
+        @pl.loop(0, steps)
+        def _(turn, batch=batch):
+            step = steps - 1 - turn
+
+            @pl.when(step < need)
+            def _():
+                rows = rows_at(step, block)
+                pl.when(has_left)(lambda: halo(batch, step, seq).wait_recv())
+                vt[:, rows] = pad[batch, rows, span:].T
+                place = batch * need + need - 1 - step
+                halo_sent(place)
+                pl.when(place + 2 < batches * need)(lambda: send_halo(place + 2))
+
             begin = pl.multiple_of(step * block, block)
             keys = pl.ds(begin, block + WINDOW)
             rows = pl.ds(begin, block)
@@ -731,25 +741,34 @@
                 lane = lax.broadcasted_iota(jnp.int32, mixed[0].shape, 0)
                 out_ref[batch, rows, lanes] = to_half(jnp.where(lane < HEAD, mixed[0], mixed[1]).T)
 
+    for batch in range(batches):
+        kept(batch).start()
     swap.end()
-
-
-def attend(group, query, kv_pad, low, block, units, collective):
+    for batch in range(batches):
+        kept(batch).wait()
+
+
+def attend(seqs, group, query, key_value, low, block, units, collective):
     batches, length, span = query.shape
-    padded = kv_pad.shape[1]
+    padded = length + WINDOW
     heads = span // HEAD
     half = jnp.bfloat16
     return pl.pallas_call(
-        functools.partial(attend_kernel, group, block),
+        functools.partial(attend_kernel, seqs, group, block),
         in_specs=[VMEM_SPEC, VMEM_SPEC, VMEM_SPEC, ANY_SPEC],
-        out_specs=[VMEM_SPEC, VMEM_SPEC, ANY_SPEC],
+        out_specs=[VMEM_SPEC, VMEM_SPEC, ANY_SPEC, ANY_SPEC],
         out_shape=[
             jax.ShapeDtypeStruct((batches, length, span), half),
             jax.ShapeDtypeStruct((batches, heads, length), jnp.float32),
+            jax.ShapeDtypeStruct((batches, padded, 2 * span), half),
             jax.ShapeDtypeStruct(units.shape, half),
         ],
         scratch_shapes=[
+            pltpu.VMEM((batches, padded, 2 * span), half),
             pltpu.VMEM((span, padded), half),
+            sems(batches, WINDOW // block),
+            sems(batches, WINDOW // block),
+            sems(batches),
             sems(group),
             sems(group),
             pltpu.SemaphoreType.DMA,
@@ -759,12 +778,12 @@
             8 * batches * length * span * (WINDOW + block), 150 * MIB, units.size * 2
         ),
         name="attend",
-    )(query, kv_pad, low, units)
+    )(query, key_value, low, units)
 
 
 def branch_kernel(
-    seqs, chips, a_ref, w_ref, d_ref, units_ref, out_ref, gd_ref, w_units_ref,
-    acc, cross_out, line_out, cross_in, line_in, sum_send, sum_recv,
+    seqs, chips, a_ref, w_ref, d_ref, units_ref, x_ref, gain_ref, middle_ref, normed_ref, gd_ref, w_units_ref,
+    out_ref, acc, cross_out, line_out, cross_in, line_in, sum_send, sum_recv,
     send, recv, d_keep, share_send, share_recv, share_keep,
 ):
     line = Line(chips)
@@ -789,6 +808,13 @@
         reduce.step(step)
         pl.when(lax.rem(step, 2) == 1)(lambda: spread.relay((step + 1) // 2))
 
+    @pl.loop(0, rows // 32)
+    def _(chunk):
+        here = rows_at(chunk, 32)
+        middle = x_ref[here, :].astype(jnp.float32) + out_ref[here, :]
+        middle_ref[here, :] = middle
+        normed_ref[here, :] = to_half(normalize(middle, gain_ref[0:1, :]))
+
     spread.rest()
     spread.sent()
     reduce.sent()
@@ -796,7 +822,7 @@
     units.end()
 
 
-def branch_sum(seqs, chips, a, w, d_rows, units, collective):
+def branch_sum(seqs, chips, a, w, d_rows, units, x, gain, collective):
     rows, width = d_rows.shape
     group = 2 * chips
     half = jnp.bfloat16
@@ -804,12 +830,14 @@
         functools.partial(branch_kernel, seqs, chips),
         out_shape=[
             jax.ShapeDtypeStruct((rows, width), jnp.float32),
+            jax.ShapeDtypeStruct((rows, width), half),
             jax.ShapeDtypeStruct((group, rows, width), half),
             jax.ShapeDtypeStruct((seqs,) + units.shape, half),
         ],
-        in_specs=[VMEM_SPEC, VMEM_SPEC, ANY_SPEC, ANY_SPEC],
-        out_specs=[VMEM_SPEC, ANY_SPEC, ANY_SPEC],
-        scratch_shapes=Reduce.scratch(chips, rows, width)
+        in_specs=[VMEM_SPEC, VMEM_SPEC, ANY_SPEC, ANY_SPEC, VMEM_SPEC, VMEM_SPEC],
+        out_specs=[VMEM_SPEC, VMEM_SPEC, ANY_SPEC, ANY_SPEC],
+        scratch_shapes=[pltpu.VMEM((rows, width), jnp.float32)]
+        + Reduce.scratch(chips, rows, width)
         + [sems(3, group), sems(group), pltpu.SemaphoreType.DMA]
         + [sems(seqs), sems(seqs), pltpu.SemaphoreType.DMA],
         compiler_params=comm_params(collective),
@@ -817,17 +845,17 @@
             2 * group * rows * width * w.shape[0], 250 * MIB, 3 * group * rows * width * 2
         ),
         name="branch_sum",
-    )(a, w, d_rows, units)
+    )(a, w, d_rows, units, x, gain)
 
 
 def units_kernel(
-    chips, x_ref, w_hbm, wd_hbm, gd_ref, g_ref, hidden_hbm, d_hbm,
-    buf, d_buf, w_ref, wd_ref, hidden_ref, d_ref, send, recv, keep, d_sem, load, store,
+    chips, x_ref, w_hbm, wd_hbm, gd_ref, g_ref, hidden_hbm, d_hbm, down_hbm,
+    down, down_half, buf, d_buf, w_ref, wd_ref, hidden_ref, d_ref, send, recv, keep, d_sem, load, store, down_sem,
 ):
     line = Line(chips)
     rows = x_ref.shape[0]
     units = hidden_ref.shape[1]
-    part = min(units, 256)
+    part = min(units, TILE)
     loads = [
         pltpu.make_async_copy(w_hbm, w_ref, load.at[0]),
         pltpu.make_async_copy(wd_hbm, wd_ref, load.at[1]),
@@ -838,6 +866,7 @@
     spread = Spread(line, x_ref, buf, send, recv)
     spread.begin()
     buf[line.own] = x_ref[...]
+    down[...] = jnp.zeros_like(down)
     for item in loads:
         item.wait()
 
@@ -869,11 +898,25 @@
             d_ref[place, here] = to_half(d_hidden * up * sigma * (1.0 + gate * (1.0 - sigma)))
             d_ref[place, there] = to_half(d_hidden * swish)
 
+            @pl.loop(0, x_ref.shape[1] // TILE)
+            def _(column):
+                cols = rows_at(column, TILE)
+                down[here, cols] += contract_rows(hidden_ref[place, here], d_buf[:, cols])
+
         for item in kept(slot):
             item.start()
 
     spread.whole(use)
+
+    @pl.loop(0, units // 64)
+    def _(chunk):
+        here = rows_at(chunk, 64)
+        down_half[here, :] = to_half(down[here, :])
+
+    down_kept = pltpu.make_async_copy(down_half, down_hbm, down_sem)
+    down_kept.start()
     spread.sent()
+    down_kept.wait()
 
     @pl.loop(0, 2 * chips)
     def _(slot):
@@ -892,10 +935,13 @@
             jax.ShapeDtypeStruct((group, rows, width), half),
             jax.ShapeDtypeStruct((group * rows, units), half),
             jax.ShapeDtypeStruct((group * rows, 2 * units), half),
+            jax.ShapeDtypeStruct((units, width), half),
         ],
         in_specs=[VMEM_SPEC, ANY_SPEC, ANY_SPEC, ANY_SPEC],
-        out_specs=[ANY_SPEC, ANY_SPEC, ANY_SPEC],
+        out_specs=[ANY_SPEC] * 4,
         scratch_shapes=[
+            pltpu.VMEM((units, width), jnp.float32),
+            pltpu.VMEM((units, width), half),
             pltpu.VMEM((group, rows, width), half),
             pltpu.VMEM((rows, width), half),
             pltpu.VMEM(w.shape, half),
@@ -908,6 +954,7 @@
             pltpu.SemaphoreType.DMA,
             sems(2),
             sems(2, group),
+            pltpu.SemaphoreType.DMA,
         ],
         compiler_params=comm_params(collective),
         cost_estimate=cost(
@@ -918,8 +965,9 @@
 
 
 def units_back_kernel(
-    chips, a_hbm, w_hbm, b_hbm, v_ref, cot_ref, gain_ref, dm_ref, db_ref, gain_grad_ref, grad_hbm,
-    a_ref, w_ref, total, lefts, tiles, load, left_sem, tile_sem,
+    seqs, chips, a_hbm, w_hbm, b_hbm, down_hbm, v_ref, cot_ref, gain_ref,
+    dm_ref, db_ref, gain_grad_ref, grad_hbm, down_in,
+    a_ref, w_ref, total, lefts, tiles, load, left_sem, tile_sem, down_send, down_recv,
     acc, cross_out, line_out, cross_in, line_in, sum_send, sum_recv,
 ):
     line = Line(chips)
@@ -962,7 +1010,9 @@
     def product(slot, tile):
         return dot_nt(left_rows(a_ref, slot, rows), w_ref[rows_at(tile, TILE), :])
 
-    meet(line.greet())
+    meet(line.greet() + greet_seq(seqs))
+    down = ToSeq(seqs, down_hbm, down_in, down_send, down_recv)
+    down.begin()
     left(0).start()
     for item in loads:
         item.wait()
@@ -988,25 +1038,27 @@
 
     norm_back(rows, v_ref, total, gain_ref, gain_grad_ref, put)
     reduce.sent()
+    down.end()
     stored(count - 2).wait()
     stored(count - 1).wait()
 
 
-def units_back(chips, a, w, b, middle, cot, gain, collective):
+def units_back(seqs, chips, a, w, b, down, middle, cot, gain, collective):
     rows, width = middle.shape
     group = 2 * chips
     half = jnp.bfloat16
     part = 256 if a.shape[0] <= 2048 else 128
     return pl.pallas_call(
-        functools.partial(units_back_kernel, chips),
+        functools.partial(units_back_kernel, seqs, chips),
         out_shape=[
             jax.ShapeDtypeStruct((rows, width), jnp.float32),
             jax.ShapeDtypeStruct((rows, width), half),
             jax.ShapeDtypeStruct((8, width), jnp.float32),
             jax.ShapeDtypeStruct((width, a.shape[1]), half),
+            jax.ShapeDtypeStruct((seqs, down.shape[0] // seqs, width), half),
         ],
-        in_specs=[ANY_SPEC] * 3 + [VMEM_SPEC] * 3,
-        out_specs=[VMEM_SPEC] * 3 + [ANY_SPEC],
+        in_specs=[ANY_SPEC] * 4 + [VMEM_SPEC] * 3,
+        out_specs=[VMEM_SPEC] * 3 + [ANY_SPEC] * 2,
         scratch_shapes=[
             pltpu.VMEM(a.shape, half),
             pltpu.VMEM(w.shape, half),
@@ -1016,6 +1068,8 @@
             sems(2),
             sems(2),
             sems(2),
+            sems(seqs),
+            sems(seqs),
         ]
         + Reduce.scratch(chips, rows, width),
         compiler_params=comm_params(collective, 60),
@@ -1023,20 +1077,19 @@
             4 * group * rows * width * a.shape[1], 200 * MIB, group * rows * width * 2
         ),
         name="units_back",
-    )(a, w, b.reshape(group * rows, width), middle, cot, gain)
+    )(a, w, b.reshape(group * rows, width), down, middle, cot, gain)
 
 
 def branch_back_kernel(
-    seqs, chips, batches, x_ref, w_ref, att_ref, hidden_hbm, wd_hbm, gd_hbm, units_hbm,
-    d_ref, out_ref, out_grad_ref, down_hbm, units_in,
-    buf, hidden_ref, wd_ref, rights, tiles, grad_acc, send, recv, load, right_sem, tile_sem,
+    seqs, chips, batches, x_ref, w_ref, att_ref, middle_ref, hidden_hbm, wd_hbm, units_hbm,
+    d_ref, layer_ref, out_grad_ref, units_in,
+    out_ref, buf, hidden_ref, wd_ref, grad_acc, send, recv, load,
     part_send, part_recv, acc, cross_out, line_out, cross_in, line_in, sum_send, sum_recv,
 ):
     line = Line(chips)
     rows = x_ref.shape[0]
     piece = rows // batches
     width = x_ref.shape[1]
-    part = rights.shape[2]
     loads = [
         pltpu.make_async_copy(hidden_hbm, hidden_ref, load.at[0]),
         pltpu.make_async_copy(wd_hbm, wd_ref, load.at[1]),
@@ -1047,32 +1100,6 @@
     def product(slot, tile):
         return dot_nn(left_rows(hidden_ref, slot, rows), wd_ref[:, rows_at(tile, TILE)])
 
-    def right(tile):
-        slot = lax.rem(tile, 2)
-        return pltpu.make_async_copy(
-            gd_hbm.at[:, rows_at(tile, part)], rights.at[slot], right_sem.at[slot]
-        )
-
-    def stored(tile):
-        slot = lax.rem(tile, 2)
-        return pltpu.make_async_copy(
-            tiles.at[slot], down_hbm.at[:, rows_at(tile, part)], tile_sem.at[slot]
-        )
-
-    def weight_grad(tile):
-        right(tile).wait()
-        pl.when(tile + 1 < width // part)(lambda: right(tile + 1).start())
-        pl.when(tile >= 2)(lambda: stored(tile - 2).wait())
-        slot = lax.rem(tile, 2)
-        size = min(256, hidden_ref.shape[1])
-
-        @pl.loop(0, hidden_ref.shape[1] // size)
-        def _(row):
-            here = rows_at(row, size)
-            tiles[slot, here, :] = to_half(contract_rows(hidden_ref[:, here], rights[slot]))
-
-        stored(tile).start()
-
     meet(line.greet() + greet_seq(seqs))
     sums = ToSeq(seqs, units_hbm, units_in, part_send, part_recv)
     spread = Spread(line, x_ref, buf, send, recv)
@@ -1081,7 +1108,6 @@
     )
     spread.begin()
     sums.begin()
-    right(0).start()
     buf[line.own] = x_ref[...]
     grad_acc[...] = jnp.zeros_like(grad_acc)
 
@@ -1098,8 +1124,6 @@
 
     for item in loads:
         item.wait()
-    count = width // part
-    per = -(-count // reduce.steps())
 
     @pl.loop(0, reduce.steps())
     def _(step):
@@ -1111,51 +1135,44 @@
             spread.relay(far)
             spread.each(far - 1, use)
 
-        @pl.loop(0, per)
-        def _(turn):
-            tile = step * per + turn
-            pl.when(tile < count)(lambda: weight_grad(tile))
-
     spread.each(chips - 1, use)
     spread.each(chips, use)
+
+    @pl.loop(0, rows // 32)
+    def _(chunk):
+        here = rows_at(chunk, 32)
+        layer_ref[here, :] = to_half(middle_ref[here, :] + out_ref[here, :])
+
     out_grad_ref[...] = to_half(grad_acc[...])
     spread.sent()
     reduce.sent()
     sums.end()
-    stored(count - 2).wait()
-    stored(count - 1).wait()
-
-
-def branch_back(seqs, chips, batches, x, w, attended, hidden, wd, group_d, unit_part, collective):
+
+
+def branch_back(seqs, chips, batches, x, w, attended, middle, hidden, wd, unit_part, collective):
     rows, width = x.shape
     group = 2 * chips
     length = group * rows // batches
     span = w.shape[0]
-    units = wd.shape[0]
     half = jnp.bfloat16
-    part = 256 if group * rows <= 2048 else 128
     return pl.pallas_call(
         functools.partial(branch_back_kernel, seqs, chips, batches),
         out_shape=[
             jax.ShapeDtypeStruct((batches, length, span), half),
-            jax.ShapeDtypeStruct((rows, width), jnp.float32),
+            jax.ShapeDtypeStruct((rows, width), half),
             jax.ShapeDtypeStruct((span, width), half),
-            jax.ShapeDtypeStruct((units, width), half),
             jax.ShapeDtypeStruct((seqs, width // seqs, unit_part.shape[1]), half),
         ],
-        in_specs=[VMEM_SPEC] * 3 + [ANY_SPEC] * 4,
-        out_specs=[VMEM_SPEC, VMEM_SPEC, VMEM_SPEC, ANY_SPEC, ANY_SPEC],
+        in_specs=[VMEM_SPEC] * 4 + [ANY_SPEC] * 3,
+        out_specs=[VMEM_SPEC, VMEM_SPEC, VMEM_SPEC, ANY_SPEC],
         scratch_shapes=[
+            pltpu.VMEM((rows, width), jnp.float32),
             pltpu.VMEM((group, rows, width), half),
             pltpu.VMEM(hidden.shape, half),
             pltpu.VMEM(wd.shape, half),
-            pltpu.VMEM((2, group * rows, part), half),
-            pltpu.VMEM((2, units, part), half),
             pltpu.VMEM((span, width), jnp.float32),
             sems(3, group),
             sems(group),
-            sems(2),
-            sems(2),
             sems(2),
             sems(seqs),
             sems(seqs),
@@ -1163,12 +1180,12 @@
         + Reduce.scratch(chips, rows, width),
         compiler_params=comm_params(collective, 62),
         cost_estimate=cost(
-            2 * group * rows * width * (2 * span + 2 * units),
+            2 * group * rows * width * (2 * span + wd.shape[0]),
             250 * MIB,
             2 * group * rows * width * 2,
         ),
         name="branch_back",
-    )(x, w, attended, hidden, wd, group_d.reshape(group * rows, width), unit_part)
+    )(x, w, attended, middle, hidden, wd, unit_part)
 
 
 def attend_back_kernel(
@@ -1332,9 +1349,10 @@
 
 
 def heads_back_kernel(
-    seqs, chips, a_ref, w_ref, g_hbm, v_ref, dm_ref, gain_ref, mlp_gain_ref, units_hbm,
-    grad_ref, cols_ref, tile_ref, gate_ref, up_ref, units, unit_load, total, gain_acc, lefts, parts, sums, cols, gain_out, gain_in, gain_sum, gain_back,
-    left_sem, part_send, part_recv, cols_send, cols_recv, cols_keep,
+    seqs, chips, a_ref, w_ref, g_hbm, v_ref, dm_ref, gain_ref, mlp_gain_ref, units_hbm, out_ref,
+    grad_ref, q_ref, k_ref, v_out_ref, wo_ref, tile_ref, gate_ref, up_ref,
+    units, unit_load, out_in, out_send, out_recv, total, gain_acc, lefts, parts, sums, cols, gain_out, gain_in, gain_sum, gain_back,
+    left_sem, part_send, part_recv, cols_send, cols_recv,
     gain_send, gain_recv, back_send, back_recv,
     acc, cross_out, line_out, cross_in, line_in, sum_send, sum_recv,
 ):
@@ -1380,6 +1398,7 @@
     def product(slot, tile):
         return dot_nt(left_rows(a_ref, slot, rows), w_ref[rows_at(tile, TILE), :])
 
+    from_seq = ToSeq(seqs, out_ref, out_in, out_send, out_recv)
     units_in = pltpu.make_async_copy(units_hbm, units, unit_load)
     units_in.start()
     left(0).start()
@@ -1400,6 +1419,7 @@
             pl.when(tile < count)(lambda: weight_grad(tile))
 
     others(seqs, seq, lambda peer: to_seq(peer, seq).start())
+    from_seq.begin()
     units_in.wait()
     block = units.shape[2] // 2 // seqs
     for member in range(group):
@@ -1407,7 +1427,7 @@
             column = (place * group + member) * block
             for target, begin in ((gate_ref, 0), (up_ref, seqs * block)):
                 here = slice(begin + place * block, begin + (place + 1) * block)
-                target[:, column : column + block] = units[member, :, here].astype(jnp.float32)
+                target[:, column : column + block] = units[member, :, here]
 
     pl.loop(2, 2 * chips - 2)(reduce.step)
 
@@ -1427,14 +1447,13 @@
     def _(chunk):
         here = rows_at(chunk, 64)
         there = pl.ds(pl.multiple_of(seq * run + chunk * 64, 64), 64)
-        added = parts[there, :].astype(jnp.float32)
-        for place in range(seqs):
-            piece = sums[place, here, :].astype(jnp.float32)
-            added = added + jnp.where(place == seq, 0.0, piece)
-        parts[there, :] = to_half(added)
+        parts[there, :] = to_half(add_from_seq(seqs, parts[there, :], sums, here))
 
     others(group, own, lambda peer: block_swap(peer, own).start())
     cols[own] = parts[rows_at(seq * group + own, share), :]
+    from_seq.arrived()
+    size = out_in.shape[1]
+    wo_ref[...] = add_from_seq(seqs, out_ref[rows_at(seq, size), :], out_in, slice(None))
     reduce.step(2 * chips - 2)
 
     def put(here, d_values):
@@ -1480,17 +1499,20 @@
     others(seqs, seq, lambda peer: gain_seq(peer, peer).wait_recv())
     tile_ref[...] = jnp.sum(gain_back[...], axis=0)
     others(group, own, lambda peer: block_swap(peer, peer).wait_recv())
-    kept = pltpu.make_async_copy(cols, cols_ref, cols_keep)
-    kept.start()
+    span = depth // 3
+    for index, target in enumerate((q_ref, k_ref, v_out_ref)):
+        for member, first, home, size in column_parts(seqs, group, share, span):
+            first = first + index * span
+            target[:, home : home + size] = cols[member, :, first : first + size]
+    from_seq.sent()
     reduce.sent()
     others(seqs, seq, lambda peer: to_seq(peer, seq).wait_send())
     others(group, own, lambda peer: gain_group(peer, own).wait_send())
     others(group, own, lambda peer: block_swap(peer, own).wait_send())
     others(seqs, seq, lambda peer: gain_seq(peer, seq).wait_send())
-    kept.wait()
-
-
-def heads_back(seqs, chips, a, w, group_a, x, d_middle, gain, mlp_gain, units, collective):
+
+
+def heads_back(seqs, chips, a, w, group_a, x, d_middle, gain, mlp_gain, units, out_part, collective):
     rows, width = x.shape
     batches, length, depth = a.shape
     group = 2 * chips
@@ -1502,16 +1524,22 @@
         functools.partial(heads_back_kernel, seqs, chips),
         out_shape=[
             jax.ShapeDtypeStruct((rows, width), jnp.float32),
-            jax.ShapeDtypeStruct((group, share, depth), half),
+            jax.ShapeDtypeStruct((share, width), half),
+            jax.ShapeDtypeStruct((share, width), half),
+            jax.ShapeDtypeStruct((share, width), half),
+            jax.ShapeDtypeStruct((out_part.shape[0] // seqs, width), jnp.float32),
             jax.ShapeDtypeStruct((8, 128), jnp.float32),
-            jax.ShapeDtypeStruct((share, units.size // 2 // share), jnp.float32),
-            jax.ShapeDtypeStruct((share, units.size // 2 // share), jnp.float32),
+            jax.ShapeDtypeStruct((share, units.size // 2 // share), half),
+            jax.ShapeDtypeStruct((share, units.size // 2 // share), half),
         ],
-        in_specs=[VMEM_SPEC, VMEM_SPEC, ANY_SPEC] + [VMEM_SPEC] * 4 + [ANY_SPEC],
-        out_specs=[VMEM_SPEC, ANY_SPEC, VMEM_SPEC, VMEM_SPEC, VMEM_SPEC],
+        in_specs=[VMEM_SPEC, VMEM_SPEC, ANY_SPEC] + [VMEM_SPEC] * 4 + [ANY_SPEC, VMEM_SPEC],
+        out_specs=[VMEM_SPEC] * 8,
         scratch_shapes=[
             pltpu.VMEM(units.shape, half),
             pltpu.SemaphoreType.DMA,
+            pltpu.VMEM((seqs, out_part.shape[0] // seqs, width), half),
+            sems(seqs),
+            sems(seqs),
             pltpu.VMEM((rows, width), jnp.float32),
             pltpu.VMEM((8, width), jnp.float32),
             pltpu.VMEM((2, batches, length, part), half),
@@ -1527,7 +1555,6 @@
             sems(seqs),
             sems(group),
             sems(group),
-            pltpu.SemaphoreType.DMA,
             sems(group),
             sems(group),
             sems(seqs),
@@ -1539,7 +1566,7 @@
             4 * group * rows * width * depth, 200 * MIB, 2 * group * rows * width * 2
         ),
         name="heads_back",
-    )(a, w, group_a, x, d_middle, gain, mlp_gain, units)
+    )(a, w, group_a, x, d_middle, gain, mlp_gain, units, out_part)
 
 
 def doc_starts(lengths, positions, batches, seq_len):
@@ -1582,17 +1609,10 @@
 
     def blocks(weight):
         part = weight.shape[1] // devices
-        if part < HEAD:
-            return weight.reshape(share, group, -1).transpose(1, 0, 2)
         return weight.reshape(share, seqs, group, part).transpose(2, 0, 1, 3).reshape(group, share, -1)
 
-    def unblock(cols, total):
-        part = total // devices
-        if part < HEAD:
-            return cols.transpose(1, 0, 2).reshape(share, total)
-        return cols.reshape(group, share, seqs, part).transpose(1, 2, 0, 3).reshape(share, total)
-
-    inputs = tokens.astype(jnp.float32).reshape(rows, width)
+    x_rows = tokens.reshape(rows, width)
+    cot_rows = cotangent.reshape(rows, width)
     wd_part = lax.all_gather(w_down, "seq", axis=0, tiled=True)
     if aligned:
         wo_part = lax.all_gather(w_out, "seq", axis=0, tiled=True)
@@ -1600,8 +1620,18 @@
         wo_all = lax.all_gather(w_out, ("seq", "fsdp"), axis=0, tiled=True)
         wo_part = lax.dynamic_slice_in_dim(wo_all, member * span, span, 0)
 
-    attn_blocks = jnp.concatenate([blocks(w_query), blocks(w_key), blocks(w_value)], axis=2)
     unit_blocks = jnp.concatenate([blocks(w_gate), blocks(w_up)], axis=2)
+    lane = jnp.arange(128, dtype=jnp.int32)
+    device = lax.axis_index("seq") * group + member
+    fold = 128 // share
+    here = lane // share == lax.rem(device, fold)
+    both = jnp.stack([gain_attn, gain_mlp]).astype(jnp.float32)
+    tile = jnp.where(here[None], jnp.tile(both, (1, fold)), 0.0)
+    tile = jnp.pad(tile, ((0, 6), (0, 0)))[None]
+    group_a, query, key_value, gains, w_heads = start(
+        seqs, chips, batches, tile, x_rows, (w_query, w_key, w_value), 1
+    )
+    lengths, gains = lax.optimization_barrier((lengths, gains))
     group_start = lax.axis_index("seq") * length
     positions = group_start + jnp.arange(length, dtype=jnp.int32)
     begins = doc_starts(lengths, positions, batches, seq_len)
@@ -1610,74 +1640,57 @@
     low = jnp.maximum(begins - group_start + WINDOW, at[None, :] + 1) - (at // block * block)[None, :]
     low = low[:, None, :]
 
-    lane = jnp.arange(128, dtype=jnp.int32)
-    device = lax.axis_index("seq") * group + member
-    fold = 128 // share
-    here = lane // share == lax.rem(device, fold)
-    both = jnp.stack([gain_attn, gain_mlp]).astype(jnp.float32)
-    tile = jnp.where(here[None], jnp.tile(both, (1, fold)), 0.0)
-    tile = jnp.pad(tile, ((0, 6), (0, 0)))[None]
-    group_a, query, kv_pad, gains, w_heads = start(
-        seqs, chips, batches, tile, tokens.reshape(rows, width), attn_blocks, 1
-    )
     gains = gains.transpose(1, 0, 2, 3).reshape(devices // fold, fold, 8, 128).sum(axis=1)
     gain_one = gains[:, 0].reshape(width)
     gain_two = gains[:, 1].reshape(width)
-    attended, lse, unit_own = attend(group, query, kv_pad, low, block, unit_blocks, 2)
-    branch, group_d, w_units = branch_sum(
-        seqs, chips, attended, wo_part, cotangent.reshape(rows, width),
-        unit_own.reshape(group * share, -1), 3,
+    attended, lse, kv_pad, unit_own = attend(
+        seqs, group, query, key_value, low, block, unit_blocks, 2
+    )
+    middle, normed_b, group_d, w_units = branch_sum(
+        seqs, chips, attended, wo_part, cot_rows, unit_own.reshape(group * share, -1),
+        x_rows, gain_two[None], 3,
     )
     w_units = w_units.reshape(width, -1)
-    middle = inputs + branch
-    normed_b = to_half(normalize(middle, gain_two))
-    group_b, hidden, d_units = hidden_units(chips, normed_b, w_units, wd_part, group_d, 4)
-    d_middle, d_branch, mlp_gain_part, unit_part = units_back(
-        chips, d_units, w_units, group_b, middle, cotangent.reshape(rows, width), gain_two[None], 5
-    )
-
-    def over_seq(values):
-        return lax.psum_scatter(values, "seq", scatter_dimension=0, tiled=True)
-
-    d_attended, mlp_out, out_grad, down_grad, unit_in = branch_back(
-        seqs, chips, batches, d_branch, wo_part, attended, hidden, wd_part, group_d, unit_part, 6
-    )
-    outputs = middle + mlp_out
-    down_sum = over_seq(down_grad)
+    group_b, hidden, d_units, down_part = hidden_units(
+        chips, normed_b, w_units, wd_part, group_d, 4
+    )
+    d_middle, d_branch, mlp_gain_part, unit_part, down_in = units_back(
+        seqs, chips, d_units, w_units, group_b, down_part, middle, cot_rows, gain_two[None], 5
+    )
+    d_attended, layer_out, out_part, unit_in = branch_back(
+        seqs, chips, batches, d_branch, wo_part, attended, middle, hidden, wd_part, unit_part, 6
+    )
     d_heads, unit_cols = attend_back(
         seqs, group, query, kv_pad, low, lse, d_attended, block, unit_part, unit_in, 7
     )
-    if aligned:
-        out_sum = over_seq(out_grad)
-    else:
+    if not aligned:
         whole = lax.dynamic_update_slice_in_dim(
-            jnp.zeros((width, width), jnp.bfloat16), out_grad, member * span, 0
-        )
-        out_sum = lax.psum_scatter(whole, ("seq", "fsdp"), scatter_dimension=0, tiled=True)
-    input_grad, head_cols, gain_tile, w_gate_grad, w_up_grad = heads_back(
-        seqs, chips, d_heads, w_heads, group_a, tokens.reshape(rows, width), d_middle,
-        gain_one[None], mlp_gain_part, unit_cols, 8,
-    )
-    input_grad = input_grad.reshape(batches, piece, width)
-    layer_out = to_half(outputs).reshape(batches, piece, width)
+            jnp.zeros((width, width), jnp.bfloat16), out_part, member * span, 0
+        )
+        out_part = lax.psum(whole, "fsdp").reshape(seqs, group, share, width)
+        out_part = lax.dynamic_slice_in_dim(out_part, member, 1, 1).reshape(seqs * share, width)
+    input_grad, wq_grad, wk_grad, wv_grad, wo_grad, gain_tile, gate_grad, up_grad = heads_back(
+        seqs, chips, d_heads, w_heads, group_a, x_rows, d_middle, gain_one[None], mlp_gain_part,
+        unit_cols, out_part, 8,
+    )
+    run = lax.axis_index("seq")
+    down_own = lax.dynamic_slice_in_dim(down_part, run * w_down.shape[0], w_down.shape[0], 0)
+    others = jnp.arange(seqs)[:, None, None] != run
+    down_sum = jnp.sum(jnp.where(others, down_in.astype(jnp.float32), 0.0), axis=0)
     gain_grads = lax.dynamic_slice_in_dim(gain_tile[:2], lax.rem(device, fold) * share, share, 1)
-
-    def whole_rows(cols, part, total):
-        size = total // group
-        return unblock(cols[:, :, part * size : (part + 1) * size], total).astype(jnp.float32)
-
+    wide = jnp.float32
     return (
-        layer_out,
-        input_grad,
+        layer_out.reshape(batches, piece, width),
+        input_grad.reshape(batches, piece, width),
         gain_grads[0],
-        whole_rows(head_cols, 0, width),
-        whole_rows(head_cols, 1, width),
-        whole_rows(head_cols, 2, width),
-        out_sum.astype(jnp.float32),
+        wq_grad.astype(wide),
+        wk_grad.astype(wide),
+        wv_grad.astype(wide),
+        wo_grad,
         gain_grads[1],
-        w_gate_grad,
-        w_up_grad,
-        down_sum.astype(jnp.float32),
+        gate_grad.astype(wide),
+        up_grad.astype(wide),
+        down_sum + down_own.astype(wide),
     )
 
 

time: 873 us -> 786 us (0.900)
  Pallas kernels: 801 us -> 736 us
  local copies, waits for them, and re-layouts: 27.8 us -> 8.56 us
    pallas_call x1, Pallas kernels: 136 us -> 98.4 us  [start(): pl.pallas_call(functools.partial(start_kernel, seqs, chips, batches), out...]
    pallas_call x1, Pallas kernels: 88.4 us -> 60.7 us  [attend_back(): pl.pallas_call(functools.partial(attend_back_kernel, seqs, group, block),...]
    pallas_call x1, Pallas kernels: 118 us -> 106 us  [heads_back(): pl.pallas_call(functools.partial(heads_back_kernel, seqs, chips), out_sha...]
    pallas_call x1, Pallas kernels: 76.1 us -> 87.7 us  [hidden_units(): pl.pallas_call(functools.partial(units_kernel, chips), out_shape=[jax.Sha...]
    convert_element_type x9 -> x0, local copies, waits for them, and re-layouts: 9.86 us -> none  [whole_rows(): unblock(cols[:, :, part * size:(part + 1) * size], total)]
  transfers between devices with their start and end apart: 4 -> 2, of which waited for: 0 -> 0; matrix products, arithmetic and copies ran while one was open for 4% -> 1% of each run, Pallas kernels for 58% -> 35%
where the time goes in v5:
time: 786 us; the launch traced here: 775 us
  Pallas kernels  736 us (94%)
  between operations  14.8 us (2%)
  other arithmetic  13.9 us (2%)
  local copies, waits for them, and re-layouts  8.56 us (1%)
    pallas_call x1, Pallas kernels, branch_back(): pl.pallas_call(functools.partial(branch_back_kernel, seqs, chips, batches...  112 us
    pallas_call x1, Pallas kernels, branch_sum(): pl.pallas_call(functools.partial(branch_kernel, seqs, chips), out_shape=[...  109 us
    pallas_call x1, Pallas kernels, heads_back(): pl.pallas_call(functools.partial(heads_back_kernel, seqs, chips), out_sha...  106 us
    pallas_call x1, Pallas kernels, units_back(): pl.pallas_call(functools.partial(units_back_kernel, seqs, chips), out_sha...  101 us
    pallas_call x1, Pallas kernels, start(): pl.pallas_call(functools.partial(start_kernel, seqs, chips, batches), out...  98.4 us
    pallas_call x1, Pallas kernels, hidden_units(): pl.pallas_call(functools.partial(units_kernel, chips), out_shape=[jax.Sha...  87.7 us
    pallas_call x1, Pallas kernels, attend(): pl.pallas_call(functools.partial(attend_kernel, seqs, group, block), in_s...  61.1 us
    pallas_call x1, Pallas kernels, attend_back(): pl.pallas_call(functools.partial(attend_back_kernel, seqs, group, block),...  60.7 us
  transfers between devices with their start and end apart: 2, of which 0 were waited for; matrix products, arithmetic and copies ran while one was open for 1% of the time, Pallas kernels for 35%

profile of v5, /device:TPU:9, one launch (start us, length us, event | category | flops | bytes accessed | tf_op | source)
XLA Modules:
  0.0 774.8 jit_solution(383701259863314619)
XLA Ops:
  7.2 0.7 all-gather.3.cloned.1.call-update
  8.0 0.7 all-gather.5.cloned.1.call-update
  8.7 0.7 maximum_convert_fusion
  9.5 0.6 pad_bitcast_fusion.tile_ref
  10.1 98.4 %start.1 = (bf16[2,1024,2048]{2,1,0:T(8,128)(2,1)}, bf16[2,1024,256]{2,1,0:T(8,128)(2,1)}, bf16[2,1024,512]{2,1,0:T(8,128)(2,1)}, f32[8,4,8,128]{3,2,1,0:T(8,128)}, bf16[2048,768]{1,0:T(8,128)(2,1)}) custom-call(f32[1,8,128]{2,1,0:T(8,128)} %pad_bitcast_fusion.tile_ref, bf16[256,2048]{1,0:T(8,128)(2,1)} %bitcast.47, bf16[64,2048]{1,0:T(8,128)(2,1)} %wq_ref.1, ...), custom_call_target="tpu_custom_call" | custom-call | flops 6442450944 | bytes 209715200 | tf_op jit(solution)/shard_map/start/pallas_call | solution.py:625
  108.9 0.4 copy.39
  109.3 0.8 reshape.184
  110.1 0.3 copy.35
  110.4 0.4 copy.38
  110.8 0.8 reshape.186
  111.8 0.6 maximum_subtract_fusion.low_ref
  112.4 1.5 pad_maximum_fusion.units_ref
  113.9 0.6 slice_bitcast_fusion
  114.5 61.1 %attend.1 = (bf16[2,1024,256]{2,1,0:T(8,128)(2,1)}, f32[2,4,1024]{2,1,0:T(4,128)}, bf16[2,2048,512]{2,1,0:T(8,128)(2,1)}, bf16[8,64,2048]{2,1,0:T(8,128)(2,1)}) custom-call(bf16[2,1024,256]{2,1,0:T(8,128)(2,1)} %get-tuple-element.49.q_ref, bf16[2,1024,512]{2,1,0:T(8,128)(2,1)} %get-tuple-element.50.kv_ref, s32[2,1,1024]{2,1,0:T(1,128)} %maximum_subtract_fusion.low_ref, ...), custom_call_target="tpu_custom_call" | custom-call | flops 5368709120 | bytes 157286400 | tf_op jit(solution)/shard_map/attend/pallas_call | solution.py:756
  175.6 109.2 %branch_sum.1 = (f32[256,2048]{1,0:T(8,128)}, bf16[256,2048]{1,0:T(8,128)(2,1)}, bf16[8,256,2048]{2,1,0:T(8,128)(2,1)}, bf16[4,512,2048]{2,1,0:T(8,128)(2,1)}) custom-call(bf16[2,1024,256]{2,1,0:T(8,128)(2,1)} %get-tuple-element.53.a_ref.att_ref, bf16[256,2048]{1,0:T(8,128)(2,1)} %all-gather.3.cloned.1.call-done.w_ref, bf16[256,2048]{1,0:T(8,128)(2,1)} %bitcast.45, ...), custom_call_target="tpu_custom_call" | custom-call | flops 2147483648 | bytes 262144000 | tf_op jit(solution)/shard_map/branch_sum/pallas_call | solution.py:829
  284.8 87.7 %hidden_units.1 = (bf16[8,256,2048]{2,1,0:T(8,128)(2,1)}, bf16[2048,1024]{1,0:T(8,128)(2,1)}, bf16[2048,2048]{1,0:T(8,128)(2,1)}, bf16[1024,2048]{1,0:T(8,128)(2,1)}) custom-call(bf16[256,2048]{1,0:T(8,128)(2,1)} %get-tuple-element.56.x_ref, bf16[2048,2048]{1,0:T(8,128)(2,1)} %bitcast.50, bf16[1024,2048]{1,0:T(8,128)(2,1)} %all-gather.5.cloned.1.call-done.wd_hbm, ...), custom_call_target="tpu_custom_call" | custom-call | flops 25769803776 | bytes 209715200 | tf_op jit(solution)/shard_map/hidden_units/pallas_call | solution.py:932
  372.6 101.1 %units_back.1 = (f32[256,2048]{1,0:T(8,128)}, bf16[256,2048]{1,0:T(8,128)(2,1)}, f32[8,2048]{1,0:T(8,128)}, bf16[2048,2048]{1,0:T(8,128)(2,1)}, bf16[4,256,2048]{2,1,0:T(8,128)(2,1)}) custom-call(bf16[2048,2048]{1,0:T(8,128)(2,1)} %get-tuple-element.59.a_hbm, bf16[2048,2048]{1,0:T(8,128)(2,1)} %bitcast.51, bf16[2048,2048]{1,0:T(8,128)(2,1)} %bitcast.52, ...), custom_call_target="tpu_custom_call" | custom-call | flops 34359738368 | bytes 209715200 | tf_op jit(solution)/shard_map/units_back/pallas_call | solution.py:1051
  473.7 112.0 %branch_back.1 = (bf16[2,1024,256]{2,1,0:T(8,128)(2,1)}, bf16[256,2048]{1,0:T(8,128)(2,1)}, bf16[256,2048]{1,0:T(8,128)(2,1)}, bf16[4,512,2048]{2,1,0:T(8,128)(2,1)}) custom-call(bf16[256,2048]{1,0:T(8,128)(2,1)} %get-tuple-element.63.x_ref, bf16[256,2048]{1,0:T(8,128)(2,1)} %all-gather.3.cloned.1.call-done.w_ref, ...), custom_call_target="tpu_custom_call" | custom-call | flops 12884901888 | bytes 262144000 | tf_op jit(solution)/shard_map/branch_back/pallas_call | solution.py:1158
  585.7 60.7 %attend_back.1 = (bf16[2,1024,768]{2,1,0:T(8,128)(2,1)}, bf16[8,64,2048]{2,1,0:T(8,128)(2,1)}) custom-call(bf16[2,1024,256]{2,1,0:T(8,128)(2,1)} %get-tuple-element.49.q_ref, bf16[2,2048,512]{2,1,0:T(8,128)(2,1)} %get-tuple-element.67.pad_ref, s32[2,1,1024]{2,1,0:T(1,128)} %maximum_subtract_fusion.low_ref, f32[2,4,1024]{2,1,0:T(4,128)} %get-tuple-element.68.lse_ref, ...), custom_call_target="tpu_custom_call" | custom-call | flops 13421772800 | bytes 188743680 | tf_op jit(solution)/shard_map/attend_back/pallas_call | solution.py:1320
  646.4 105.8 %heads_back.1 = (f32[256,2048]{1,0:T(8,128)}, bf16[64,2048]{1,0:T(8,128)(2,1)}, bf16[64,2048]{1,0:T(8,128)(2,1)}, bf16[64,2048]{1,0:T(8,128)(2,1)}, f32[64,2048]...) custom-call(bf16[2,1024,768]{2,1,0:T(8,128)(2,1)} %get-tuple-element.71.a_ref, ...), custom_call_target="tpu_custom_call" | custom-call | flops 12884901888 | bytes 209715200 | tf_op jit(solution)/shard_map/heads_back/pallas_call | solution.py:1523
  752.3 2.8 convert_element_type.34
  755.1 1.5 convert_element_type.35
  756.6 0.8 convert_element_type.31
  757.4 0.8 convert_element_type.32
  758.2 0.8 convert_element_type.33
  759.1 0.7 slice.17
  759.8 0.5 slice_bitcast_fusion.2
  760.3 1.0 select_reduce_fusion
  761.4 3.0 convert_add_fusion
  764.4 1.0 copy.43
  765.4 1.3 copy.44
  766.7 0.8 copy.45
  (43 shorter events, 0.9 us)
Async XLA Ops:
  7.2 168.4 %all-gather.3.cloned.1.call-start = ((), (), s32[]{:S(2)}) async-start(), calls=%async_computation | async-start | bytes 1310720 | tf_op jit(solution)/shard_map/all_gather | solution.py:1618
  7.9 276.9 %all-gather.5.cloned.1.call-start = ((), (), s32[]{:S(2)}) async-start(), calls=%async_computation.1 | async-start | bytes 5242880 | tf_op jit(solution)/shard_map/all_gather | solution.py:1616
  10.1 98.4 %copy-start.11 = (s32[2,4]{1,0:T(2,128)S(1)}, s32[2,4]{1,0:T(2,128)}, u32[]{:S(2)}) copy-start(s32[2,4]{1,0:T(2,128)} %param.14) | copy-start | bytes 100
  10.1 98.6 %copy-start.3 = (bf16[64,8192]{1,0:T(8,128)(2,1)S(1)}, bf16[64,8192]{1,0:T(8,128)(2,1)}, u32[]{:S(2)}) copy-start(bf16[64,8192]{1,0:T(8,128)(2,1)} %param.21) | copy-start | bytes 3145732
  108.6 1.4 copy-start.4
  110.1 1.5 copy-start.10
  752.3 2.8 copy-start.2
  752.3 4.3 copy-start.9
  752.3 5.1 copy-start.8
  755.1 3.1 copy-start.7
  755.1 5.2 copy-start
  761.4 3.1 copy-start.5
  761.4 4.0 copy-start.1
  764.4 2.3 copy-start.6
Sparse Core Ops, SparseCore 0:
  9.9 36.4 all-gather.2
  48.2 57.8 all-gather.4

commit v6 on v5

--- a/solution.py
+++ b/solution.py
@@ -368,14 +368,16 @@
 
 
 class ToSeq:
-    def __init__(self, seqs, source, target, send, recv):
+    def __init__(self, seqs, source, target, send, recv, first=0, count=None):
         self.seqs, self.source, self.target, self.send, self.recv = seqs, source, target, send, recv
         self.own = lax.axis_index("seq")
+        self.first, self.count = first, target.shape[1] if count is None else count
 
     def move(self, peer, place):
+        begin = pl.multiple_of(peer * self.target.shape[1] + self.first, 16)
         return pltpu.make_async_remote_copy(
-            src_ref=self.source.at[rows_at(peer, self.target.shape[1])],
-            dst_ref=self.target.at[place],
+            src_ref=self.source.at[pl.ds(begin, self.count)],
+            dst_ref=self.target.at[place, pl.ds(self.first, self.count)],
             send_sem=self.send.at[peer],
             recv_sem=self.recv.at[place],
             device_id={"seq": peer},
@@ -434,8 +436,6 @@
 
 
 def norm_back(rows, v_ref, e_ref, gain_ref, gain_acc, put):
-    gain_acc[...] = jnp.zeros_like(gain_acc)
-
     @pl.loop(0, rows // 32)
     def _(chunk):
         here = rows_at(chunk, 32)
@@ -848,14 +848,140 @@
     )(a, w, d_rows, units, x, gain)
 
 
-def units_kernel(
-    chips, x_ref, w_hbm, wd_hbm, gd_ref, g_ref, hidden_hbm, d_hbm, down_hbm,
-    down, down_half, buf, d_buf, w_ref, wd_ref, hidden_ref, d_ref, send, recv, keep, d_sem, load, store, down_sem,
+class PairReduce:
+    def __init__(self, line, product, out, acc, keep, cross_out, cross_in, line_out, line_in, send, recv):
+        self.line, self.product, self.out, self.acc, self.keep = line, product, out, acc, keep
+        self.cross_out, self.cross_in, self.line_out, self.line_in = cross_out, cross_in, line_out, line_in
+        self.send, self.recv = send, recv
+        self.tiles = keep.shape[1] // TILE
+
+    @staticmethod
+    def scratch(chips, piece, width):
+        half = jnp.bfloat16
+        return [
+            pltpu.VMEM((piece, width), half),
+            pltpu.VMEM((2, piece, width), half),
+            pltpu.VMEM((2, piece, width), half),
+            pltpu.VMEM((chips + 1, piece, width), half),
+            pltpu.SemaphoreType.DMA((3, width // TILE)),
+            pltpu.SemaphoreType.DMA((chips + 3, width // TILE)),
+        ]
+
+    def cross(self, parity, tile):
+        here = rows_at(tile, TILE)
+        return pltpu.make_async_remote_copy(
+            src_ref=self.cross_out.at[:, here],
+            dst_ref=self.cross_in.at[parity, :, here],
+            send_sem=self.send.at[0, tile],
+            recv_sem=self.recv.at[self.line.chips + 1 + parity, tile],
+            device_id={"fsdp": self.line.other},
+            device_id_type=MESH,
+        )
+
+    def along(self, parity, landing, tile, peer):
+        here = rows_at(tile, TILE)
+        return pltpu.make_async_remote_copy(
+            src_ref=self.line_out.at[parity, :, here],
+            dst_ref=self.line_in.at[landing, :, here],
+            send_sem=self.send.at[1 + parity, tile],
+            recv_sem=self.recv.at[landing, tile],
+            device_id={"fsdp": peer},
+            device_id_type=MESH,
+        )
+
+    def steps(self):
+        return 2 * self.line.chips - 1
+
+    def step(self, step):
+        line, keep = self.line, self.keep
+        piece = keep.shape[0]
+        right_side = line.chips - 1 - line.chip
+        away = line.chips - 1 - step // 2
+        second = lax.rem(step, 2)
+        rightward = (right_side >= line.chip) == (second == 0)
+        place = line.chip + jnp.where(rightward, away, -away)
+        longer = jnp.maximum(right_side, line.chip)
+        shorter = jnp.minimum(right_side, line.chip)
+        count = longer - away + jnp.maximum(shorter - away, 0) + second
+        parity = lax.rem(count + 2 * line.chips, 2)
+        upstream = (rightward & line.has_left) | (jnp.logical_not(rightward) & line.has_right)
+
+        @pl.when((place >= 0) & (place < line.chips))
+        def _():
+            @pl.loop(0, self.tiles)
+            def _(tile):
+                here = rows_at(tile, TILE)
+                self.acc[...] = self.product(place, tile)
+                self.cross_out[:, here] = to_half(self.acc[rows_at(1 - line.core, piece), :])
+                keep[:, here] = self.acc[rows_at(line.core, piece), :]
+                self.cross(parity, tile).start()
+
+            @pl.loop(0, self.tiles)
+            def _(tile):
+                here = rows_at(tile, TILE)
+                self.cross(parity, tile).wait()
+                keep[:, here] += self.cross_in[parity, :, here].astype(jnp.float32)
+
+                @pl.when(away > 0)
+                def _():
+                    pl.when(count >= 2)(
+                        lambda: self.along(parity, place, tile, line.own).wait_send()
+                    )
+
+                    @pl.when(upstream)
+                    def _():
+                        self.along(parity, place, tile, line.own).wait_recv()
+                        self.line_out[parity, :, here] = to_half(
+                            keep[:, here] + self.line_in[place, :, here].astype(jnp.float32)
+                        )
+
+                    @pl.when(jnp.logical_not(upstream))
+                    def _():
+                        self.line_out[parity, :, here] = to_half(keep[:, here])
+
+                    @pl.when(rightward)
+                    def _():
+                        self.along(parity, place, tile, line.own + 2).start()
+
+                    @pl.when(jnp.logical_not(rightward))
+                    def _():
+                        landing = jnp.where(away == 1, line.chips, place)
+                        self.along(parity, landing, tile, line.own - 2).start()
+
+                @pl.when(away == 0)
+                def _():
+                    self.out[:, here] = keep[:, here]
+
+                    @pl.when(line.has_left)
+                    def _():
+                        self.along(parity, place, tile, line.own).wait_recv()
+                        self.out[:, here] += self.line_in[place, :, here].astype(jnp.float32)
+
+                    @pl.when(line.has_right)
+                    def _():
+                        self.along(parity, line.chips, tile, line.own).wait_recv()
+                        self.out[:, here] += self.line_in[line.chips, :, here].astype(jnp.float32)
+
+    def sent(self):
+        for count in range(max(self.line.chips - 3, 0), self.line.chips - 1):
+            pl.loop(0, self.tiles)(
+                lambda tile, parity=count % 2: self.along(parity, 0, tile, self.line.own).wait_send()
+            )
+
+
+def feed_kernel(
+    chips, batches, x_ref, w_hbm, wd_hbm, gd_hbm, v_ref, cot_ref, gain_ref,
+    dm_ref, db_ref, gain_grad_ref, hidden_hbm, grad_hbm,
+    buf, d_buf, h_buf, w_ref, wd_ref, d_ref, tiles, totals, acc, keep,
+    load, d_sem, h_sem, tile_sem, send, recv, *sums,
 ):
     line = Line(chips)
-    rows = x_ref.shape[0]
-    units = hidden_ref.shape[1]
+    rows, width = x_ref.shape
+    piece = rows // batches
+    pair = 2 * piece
+    units = wd_ref.shape[0]
     part = min(units, TILE)
+    block = tiles.shape[1]
     loads = [
         pltpu.make_async_copy(w_hbm, w_ref, load.at[0]),
         pltpu.make_async_copy(wd_hbm, wd_ref, load.at[1]),
@@ -863,227 +989,236 @@
     for item in loads:
         item.start()
     meet(line.greet())
-    spread = Spread(line, x_ref, buf, send, recv)
-    spread.begin()
-    buf[line.own] = x_ref[...]
-    down[...] = jnp.zeros_like(down)
+    spreads = [
+        Spread(
+            line,
+            x_ref.at[pl.ds(batch * piece, piece)],
+            buf.at[batch],
+            send.at[batch],
+            recv.at[batch],
+        )
+        for batch in range(batches)
+    ]
+    spreads[0].begin()
+    for batch in range(batches):
+        buf[batch, line.own] = x_ref[batch * piece : (batch + 1) * piece, :]
+
+    def fetch(batch, place, side):
+        return [
+            pltpu.make_async_copy(
+                gd_hbm.at[place * 2 + core, pl.ds(batch * piece, piece)],
+                d_buf.at[side, pl.ds(core * piece, piece)],
+                d_sem.at[side, core],
+            )
+            for core in range(2)
+        ]
+
+    def stored(batch, place):
+        return [
+            pltpu.make_async_copy(
+                h_buf.at[pl.ds(core * piece, piece)],
+                hidden_hbm.at[
+                    pl.ds(pl.multiple_of((place * 2 + core) * rows + batch * piece, piece), piece)
+                ],
+                h_sem.at[core],
+            )
+            for core in range(2)
+        ]
+
+    def sides(far, act):
+        @pl.loop(0, 2)
+        def _(side):
+            place = line.chip + far * (2 * side - 1)
+            valid = (place >= 0) & (place < chips) & ((side == 0) | (far > 0))
+            pl.when(valid)(lambda: act(place, side))
+
+    def take(batch, far):
+        def begin(place, side):
+            for item in fetch(batch, place, side):
+                item.start()
+
+        sides(far, begin)
+        pl.when(far > 0)(lambda: spreads[batch].relay(far))
+
+    def compute(batch, far):
+        def act(place, side):
+            spreads[batch].move(place * 2 + 1 - line.core, 2, line.own).wait_recv()
+            for item in fetch(batch, place, side):
+                item.wait()
+
+            def free():
+                for item in stored(batch, place):
+                    item.wait()
+
+            if batch:
+                free()
+            else:
+                pl.when((far > 0) | (side > 0))(free)
+            there = rows_at(place, pair)
+
+            @pl.loop(0, units // part)
+            def _(tile):
+                first = rows_at(tile, part)
+                second = rows_at(units // part + tile, part)
+                values = buf[batch, pl.ds(place * 2, 2), :, :].reshape(pair, width)
+                gate = dot_nn(values, w_ref[:, first])
+                up = dot_nn(values, w_ref[:, second])
+                d_hidden = dot_nt(d_buf[side], wd_ref[first, :])
+                sigma = jax.nn.sigmoid(gate)
+                swish = gate * sigma
+                h_buf[:, first] = to_half(swish * up)
+                slope = sigma * (1.0 + gate * (1.0 - sigma))
+                d_ref[batch, there, first] = to_half(d_hidden * up * slope)
+                d_ref[batch, there, second] = to_half(d_hidden * swish)
+
+            for item in stored(batch, place):
+                item.start()
+
+        sides(far, act)
+
+    def product(batch):
+        def get(place, tile):
+            return dot_nt(d_ref[batch, rows_at(place, pair), :], w_ref[rows_at(tile, TILE), :])
+
+        return get
+
+    reduces = [
+        PairReduce(line, product(batch), totals.at[batch], acc, keep, *sums[6 * batch : 6 * batch + 6])
+        for batch in range(batches)
+    ]
+
+    def grad_stored(tile):
+        slot = lax.rem(tile, 2)
+        return pltpu.make_async_copy(
+            tiles.at[slot], grad_hbm.at[rows_at(tile, block)], tile_sem.at[slot]
+        )
+
+    count = width // block
+
+    def weight_grad(tile):
+        pl.when(tile >= 2)(lambda: grad_stored(tile - 2).wait())
+        slot = lax.rem(tile, 2)
+        size = min(TILE, 2 * units)
+
+        @pl.loop(0, 2 * units // size)
+        def _(column):
+            here = rows_at(column, size)
+            got = 0.0
+            for batch in range(batches):
+                left = buf[batch, :, :, rows_at(tile, block)].reshape(2 * chips * piece, block)
+                got = got + contract_rows(left, d_ref[batch, :, here])
+            tiles[slot, :, here] = to_half(got)
+
+        grad_stored(tile).start()
+
+    def norm_batch(batch):
+        own = pl.ds(batch * piece, piece)
+
+        def put(here, d_values):
+            there = pl.ds(pl.multiple_of(here.start + batch * piece, here.size), here.size)
+            d_middle = cot_ref[there, :].astype(jnp.float32) + d_values
+            dm_ref[there, :] = d_middle
+            db_ref[there, :] = to_half(d_middle)
+
+        norm_back(piece, v_ref.at[own], totals.at[batch], gain_ref, gain_grad_ref, put)
+
+    gain_grad_ref[...] = jnp.zeros_like(gain_grad_ref)
     for item in loads:
         item.wait()
-
-    def kept(slot):
-        place = rows_at(slot, rows)
-        return [
-            pltpu.make_async_copy(buf.at[slot], g_ref.at[slot], keep.at[slot]),
-            pltpu.make_async_copy(hidden_ref.at[place], hidden_hbm.at[place], store.at[0, slot]),
-            pltpu.make_async_copy(d_ref.at[place], d_hbm.at[place], store.at[1, slot]),
-        ]
-
-    def use(slot):
-        fetch = pltpu.make_async_copy(gd_ref.at[slot], d_buf, d_sem)
-        fetch.start()
-        place = rows_at(slot, rows)
-        fetch.wait()
-
-        @pl.loop(0, units // part)
-        def _(tile):
-            here = rows_at(tile, part)
-            there = rows_at(units // part + tile, part)
-            values = buf[slot]
-            gate = dot_nn(values, w_ref[:, here])
-            up = dot_nn(values, w_ref[:, there])
-            d_hidden = dot_nt(d_buf[...], wd_ref[here, :])
-            sigma = jax.nn.sigmoid(gate)
-            swish = gate * sigma
-            hidden_ref[place, here] = to_half(swish * up)
-            d_ref[place, here] = to_half(d_hidden * up * sigma * (1.0 + gate * (1.0 - sigma)))
-            d_ref[place, there] = to_half(d_hidden * swish)
-
-            @pl.loop(0, x_ref.shape[1] // TILE)
-            def _(column):
-                cols = rows_at(column, TILE)
-                down[here, cols] += contract_rows(hidden_ref[place, here], d_buf[:, cols])
-
-        for item in kept(slot):
-            item.start()
-
-    spread.whole(use)
-
-    @pl.loop(0, units // 64)
-    def _(chunk):
-        here = rows_at(chunk, 64)
-        down_half[here, :] = to_half(down[here, :])
-
-    down_kept = pltpu.make_async_copy(down_half, down_hbm, down_sem)
-    down_kept.start()
-    spread.sent()
-    down_kept.wait()
-
-    @pl.loop(0, 2 * chips)
-    def _(slot):
-        for item in kept(slot):
-            item.wait()
-
-
-def hidden_units(chips, x, w, wd, group_d, collective):
+    last = 2 * chips - 2
+
+    @pl.loop(0, chips)
+    def _(far):
+        take(0, far)
+        pl.when(far == chips - 2)(spreads[1].begin)
+        compute(0, far)
+
+    @pl.loop(0, chips - 1)
+    def _(far):
+        take(1, far)
+        reduces[0].step(2 * far)
+        reduces[0].step(2 * far + 1)
+        compute(1, far)
+
+    take(1, chips - 1)
+    compute(1, chips - 1)
+
+    @pl.loop(0, 2)
+    def _(step):
+        reduces[1].step(step)
+        weight_grad(step)
+
+    reduces[0].step(last)
+    norm_batch(0)
+
+    @pl.loop(2, last)
+    def _(step):
+        reduces[1].step(step)
+        pl.when(step < count)(lambda: weight_grad(step))
+
+    @pl.loop(last, max(count, last))
+    def _(tile):
+        weight_grad(tile)
+
+    reduces[1].step(last)
+    norm_batch(1)
+    for batch in range(batches):
+        spreads[batch].sent()
+        reduces[batch].sent()
+    for item in stored(1, 0):
+        item.wait()
+    grad_stored(count - 2).wait()
+    grad_stored(count - 1).wait()
+
+
+def feed_forward(chips, batches, x, w, wd, group_d, middle, cot, gain, collective):
     rows, width = x.shape
     group = 2 * chips
     units = wd.shape[0]
+    piece = rows // batches
     half = jnp.bfloat16
     return pl.pallas_call(
-        functools.partial(units_kernel, chips),
-        out_shape=[
-            jax.ShapeDtypeStruct((group, rows, width), half),
-            jax.ShapeDtypeStruct((group * rows, units), half),
-            jax.ShapeDtypeStruct((group * rows, 2 * units), half),
-            jax.ShapeDtypeStruct((units, width), half),
-        ],
-        in_specs=[VMEM_SPEC, ANY_SPEC, ANY_SPEC, ANY_SPEC],
-        out_specs=[ANY_SPEC] * 4,
-        scratch_shapes=[
-            pltpu.VMEM((units, width), jnp.float32),
-            pltpu.VMEM((units, width), half),
-            pltpu.VMEM((group, rows, width), half),
-            pltpu.VMEM((rows, width), half),
-            pltpu.VMEM(w.shape, half),
-            pltpu.VMEM(wd.shape, half),
-            pltpu.VMEM((group * rows, units), half),
-            pltpu.VMEM((group * rows, 2 * units), half),
-            sems(3, group),
-            sems(group),
-            sems(group),
-            pltpu.SemaphoreType.DMA,
-            sems(2),
-            sems(2, group),
-            pltpu.SemaphoreType.DMA,
-        ],
-        compiler_params=comm_params(collective),
-        cost_estimate=cost(
-            6 * group * rows * width * units, 200 * MIB, group * rows * width * 2
-        ),
-        name="hidden_units",
-    )(x, w, wd, group_d)
-
-
-def units_back_kernel(
-    seqs, chips, a_hbm, w_hbm, b_hbm, down_hbm, v_ref, cot_ref, gain_ref,
-    dm_ref, db_ref, gain_grad_ref, grad_hbm, down_in,
-    a_ref, w_ref, total, lefts, tiles, load, left_sem, tile_sem, down_send, down_recv,
-    acc, cross_out, line_out, cross_in, line_in, sum_send, sum_recv,
-):
-    line = Line(chips)
-    rows, width = v_ref.shape
-    group = 2 * chips
-    part = lefts.shape[2]
-    loads = [
-        pltpu.make_async_copy(w_hbm, w_ref, load.at[0]),
-        pltpu.make_async_copy(a_hbm, a_ref, load.at[1]),
-    ]
-    for item in loads:
-        item.start()
-
-    def left(tile):
-        slot = lax.rem(tile, 2)
-        return pltpu.make_async_copy(
-            b_hbm.at[:, rows_at(tile, part)], lefts.at[slot], left_sem.at[slot]
-        )
-
-    def stored(tile):
-        slot = lax.rem(tile, 2)
-        return pltpu.make_async_copy(
-            tiles.at[slot], grad_hbm.at[rows_at(tile, part)], tile_sem.at[slot]
-        )
-
-    def weight_grad(tile):
-        left(tile).wait()
-        pl.when(tile + 1 < width // part)(lambda: left(tile + 1).start())
-        pl.when(tile >= 2)(lambda: stored(tile - 2).wait())
-        slot = lax.rem(tile, 2)
-        size = min(TILE, a_ref.shape[1])
-
-        @pl.loop(0, a_ref.shape[1] // size)
-        def _(column):
-            here = rows_at(column, size)
-            tiles[slot, :, here] = to_half(contract_rows(lefts[slot], a_ref[:, here]))
-
-        stored(tile).start()
-
-    def product(slot, tile):
-        return dot_nt(left_rows(a_ref, slot, rows), w_ref[rows_at(tile, TILE), :])
-
-    meet(line.greet() + greet_seq(seqs))
-    down = ToSeq(seqs, down_hbm, down_in, down_send, down_recv)
-    down.begin()
-    left(0).start()
-    for item in loads:
-        item.wait()
-    reduce = Reduce(
-        line, product, total, acc, cross_out, line_out, cross_in, line_in, sum_send, sum_recv
-    )
-    count = width // part
-    per = -(-count // reduce.steps())
-
-    @pl.loop(0, reduce.steps())
-    def _(step):
-        reduce.step(step)
-
-        @pl.loop(0, per)
-        def _(turn):
-            tile = step * per + turn
-            pl.when(tile < count)(lambda: weight_grad(tile))
-
-    def put(here, d_values):
-        d_middle = cot_ref[here, :].astype(jnp.float32) + d_values
-        dm_ref[here, :] = d_middle
-        db_ref[here, :] = to_half(d_middle)
-
-    norm_back(rows, v_ref, total, gain_ref, gain_grad_ref, put)
-    reduce.sent()
-    down.end()
-    stored(count - 2).wait()
-    stored(count - 1).wait()
-
-
-def units_back(seqs, chips, a, w, b, down, middle, cot, gain, collective):
-    rows, width = middle.shape
-    group = 2 * chips
-    half = jnp.bfloat16
-    part = 256 if a.shape[0] <= 2048 else 128
-    return pl.pallas_call(
-        functools.partial(units_back_kernel, seqs, chips),
+        functools.partial(feed_kernel, chips, batches),
         out_shape=[
             jax.ShapeDtypeStruct((rows, width), jnp.float32),
             jax.ShapeDtypeStruct((rows, width), half),
             jax.ShapeDtypeStruct((8, width), jnp.float32),
-            jax.ShapeDtypeStruct((width, a.shape[1]), half),
-            jax.ShapeDtypeStruct((seqs, down.shape[0] // seqs, width), half),
+            jax.ShapeDtypeStruct((group * rows, units), half),
+            jax.ShapeDtypeStruct((width, 2 * units), half),
         ],
-        in_specs=[ANY_SPEC] * 4 + [VMEM_SPEC] * 3,
+        in_specs=[VMEM_SPEC] + [ANY_SPEC] * 3 + [VMEM_SPEC] * 3,
         out_specs=[VMEM_SPEC] * 3 + [ANY_SPEC] * 2,
         scratch_shapes=[
-            pltpu.VMEM(a.shape, half),
+            pltpu.VMEM((batches, group, piece, width), half),
+            pltpu.VMEM((2, 2 * piece, width), half),
+            pltpu.VMEM((2 * piece, units), half),
             pltpu.VMEM(w.shape, half),
-            pltpu.VMEM((rows, width), jnp.float32),
-            pltpu.VMEM((2, a.shape[0], part), half),
-            pltpu.VMEM((2, part, a.shape[1]), half),
+            pltpu.VMEM(wd.shape, half),
+            pltpu.VMEM((batches, group * piece, 2 * units), half),
+            pltpu.VMEM((2, 256, 2 * units), half),
+            pltpu.VMEM((batches, piece, width), jnp.float32),
+            pltpu.VMEM((2 * piece, TILE), jnp.float32),
+            pltpu.VMEM((piece, width), jnp.float32),
+            sems(2),
+            sems(2, 2),
             sems(2),
             sems(2),
-            sems(2),
-            sems(seqs),
-            sems(seqs),
+            sems(batches, 3, group),
+            sems(batches, group),
         ]
-        + Reduce.scratch(chips, rows, width),
-        compiler_params=comm_params(collective, 60),
+        + PairReduce.scratch(chips, piece, width) * batches,
+        compiler_params=comm_params(collective, 63),
         cost_estimate=cost(
-            4 * group * rows * width * a.shape[1], 200 * MIB, group * rows * width * 2
+            14 * group * rows * width * units, 400 * MIB, 2 * group * rows * width * 2
         ),
-        name="units_back",
-    )(a, w, b.reshape(group * rows, width), down, middle, cot, gain)
+        name="feed_forward",
+    )(x, w, wd, group_d, middle, cot, gain)
 
 
 def branch_back_kernel(
-    seqs, chips, batches, x_ref, w_ref, att_ref, middle_ref, hidden_hbm, wd_hbm, units_hbm,
-    d_ref, layer_ref, out_grad_ref, units_in,
-    out_ref, buf, hidden_ref, wd_ref, grad_acc, send, recv, load,
+    seqs, chips, batches, x_ref, w_ref, att_ref, middle_ref, hidden_hbm, wd_hbm, units_hbm, gd_hbm,
+    d_ref, layer_ref, out_grad_ref, units_in, down_hbm,
+    out_ref, buf, hidden_ref, wd_ref, grad_acc, rights, tiles, send, recv, load, right_sem, tile_sem,
     part_send, part_recv, acc, cross_out, line_out, cross_in, line_in, sum_send, sum_recv,
 ):
     line = Line(chips)
@@ -1100,6 +1235,36 @@
     def product(slot, tile):
         return dot_nn(left_rows(hidden_ref, slot, rows), wd_ref[:, rows_at(tile, TILE)])
 
+    part = rights.shape[2]
+    count = width // part
+
+    def right(tile):
+        slot = lax.rem(tile, 2)
+        return pltpu.make_async_copy(
+            gd_hbm.at[:, rows_at(tile, part)], rights.at[slot], right_sem.at[slot]
+        )
+
+    def stored(tile):
+        slot = lax.rem(tile, 2)
+        return pltpu.make_async_copy(
+            tiles.at[slot], down_hbm.at[:, rows_at(tile, part)], tile_sem.at[slot]
+        )
+
+    def weight_grad(tile):
+        right(tile).wait()
+        pl.when(tile + 1 < count)(lambda: right(tile + 1).start())
+        pl.when(tile >= 2)(lambda: stored(tile - 2).wait())
+        slot = lax.rem(tile, 2)
+        size = min(TILE, hidden_ref.shape[1])
+
+        @pl.loop(0, hidden_ref.shape[1] // size)
+        def _(row):
+            here = rows_at(row, size)
+            tiles[slot, here, :] = to_half(contract_rows(hidden_ref[:, here], rights[slot]))
+
+        stored(tile).start()
+
+    right(0).start()
     meet(line.greet() + greet_seq(seqs))
     sums = ToSeq(seqs, units_hbm, units_in, part_send, part_recv)
     spread = Spread(line, x_ref, buf, send, recv)
@@ -1125,6 +1290,8 @@
     for item in loads:
         item.wait()
 
+    per = -(-count // reduce.steps())
+
     @pl.loop(0, reduce.steps())
     def _(step):
         reduce.step(step)
@@ -1135,6 +1302,11 @@
             spread.relay(far)
             spread.each(far - 1, use)
 
+        @pl.loop(0, per)
+        def _(turn):
+            tile = step * per + turn
+            pl.when(tile < count)(lambda: weight_grad(tile))
+
     spread.each(chips - 1, use)
     spread.each(chips, use)
 
@@ -1147,14 +1319,17 @@
     spread.sent()
     reduce.sent()
     sums.end()
-
-
-def branch_back(seqs, chips, batches, x, w, attended, middle, hidden, wd, unit_part, collective):
+    stored(count - 2).wait()
+    stored(count - 1).wait()
+
+
+def branch_back(seqs, chips, batches, x, w, attended, middle, hidden, wd, unit_part, group_d, collective):
     rows, width = x.shape
     group = 2 * chips
     length = group * rows // batches
     span = w.shape[0]
     half = jnp.bfloat16
+    part = 256 if group * rows <= 2048 else 128
     return pl.pallas_call(
         functools.partial(branch_back_kernel, seqs, chips, batches),
         out_shape=[
@@ -1162,17 +1337,22 @@
             jax.ShapeDtypeStruct((rows, width), half),
             jax.ShapeDtypeStruct((span, width), half),
             jax.ShapeDtypeStruct((seqs, width // seqs, unit_part.shape[1]), half),
+            jax.ShapeDtypeStruct((wd.shape[0], width), half),
         ],
-        in_specs=[VMEM_SPEC] * 4 + [ANY_SPEC] * 3,
-        out_specs=[VMEM_SPEC, VMEM_SPEC, VMEM_SPEC, ANY_SPEC],
+        in_specs=[VMEM_SPEC] * 4 + [ANY_SPEC] * 4,
+        out_specs=[VMEM_SPEC, VMEM_SPEC, VMEM_SPEC, ANY_SPEC, ANY_SPEC],
         scratch_shapes=[
             pltpu.VMEM((rows, width), jnp.float32),
             pltpu.VMEM((group, rows, width), half),
             pltpu.VMEM(hidden.shape, half),
             pltpu.VMEM(wd.shape, half),
             pltpu.VMEM((span, width), jnp.float32),
+            pltpu.VMEM((2, group * rows, part), half),
+            pltpu.VMEM((2, wd.shape[0], part), half),
             sems(3, group),
             sems(group),
+            sems(2),
+            sems(2),
             sems(2),
             sems(seqs),
             sems(seqs),
@@ -1180,12 +1360,12 @@
         + Reduce.scratch(chips, rows, width),
         compiler_params=comm_params(collective, 62),
         cost_estimate=cost(
-            2 * group * rows * width * (2 * span + wd.shape[0]),
+            2 * group * rows * width * (2 * span + 2 * wd.shape[0]),
             250 * MIB,
             2 * group * rows * width * 2,
         ),
         name="branch_back",
-    )(x, w, attended, middle, hidden, wd, unit_part)
+    )(x, w, attended, middle, hidden, wd, unit_part, group_d.reshape(group * rows, width))
 
 
 def attend_back_kernel(
@@ -1349,9 +1529,9 @@
 
 
 def heads_back_kernel(
-    seqs, chips, a_ref, w_ref, g_hbm, v_ref, dm_ref, gain_ref, mlp_gain_ref, units_hbm, out_ref,
-    grad_ref, q_ref, k_ref, v_out_ref, wo_ref, tile_ref, gate_ref, up_ref,
-    units, unit_load, out_in, out_send, out_recv, total, gain_acc, lefts, parts, sums, cols, gain_out, gain_in, gain_sum, gain_back,
+    seqs, chips, a_ref, w_ref, g_hbm, v_ref, dm_ref, gain_ref, mlp_gain_ref, units_hbm, out_ref, down_hbm,
+    grad_ref, q_ref, k_ref, v_out_ref, wo_ref, tile_ref, gate_ref, up_ref, down_in,
+    down_send, down_recv,     units, unit_load, out_in, out_send, out_recv, total, gain_acc, lefts, parts, sums, cols, gain_out, gain_in, gain_sum, gain_back,
     left_sem, part_send, part_recv, cols_send, cols_recv,
     gain_send, gain_recv, back_send, back_recv,
     acc, cross_out, line_out, cross_in, line_in, sum_send, sum_recv,
@@ -1398,11 +1578,18 @@
     def product(slot, tile):
         return dot_nt(left_rows(a_ref, slot, rows), w_ref[rows_at(tile, TILE), :])
 
+    size = down_in.shape[1]
+    cut = size // 16 * 3 // 8 * 16
+    downs = [
+        ToSeq(seqs, down_hbm, down_in, down_send.at[0], down_recv.at[0], 0, cut),
+        ToSeq(seqs, down_hbm, down_in, down_send.at[1], down_recv.at[1], cut, size - cut),
+    ]
     from_seq = ToSeq(seqs, out_ref, out_in, out_send, out_recv)
     units_in = pltpu.make_async_copy(units_hbm, units, unit_load)
     units_in.start()
     left(0).start()
     meet(greet_group(group) + greet_seq(seqs))
+    downs[0].begin()
     reduce = Reduce(
         line, product, total, acc, cross_out, line_out, cross_in, line_in, sum_send, sum_recv
     )
@@ -1442,6 +1629,7 @@
         )
 
     others(seqs, seq, lambda peer: to_seq(peer, peer).wait_recv())
+    downs[1].begin()
 
     @pl.loop(0, run // 64)
     def _(chunk):
@@ -1459,6 +1647,7 @@
     def put(here, d_values):
         grad_ref[here, :] = dm_ref[here, :] + d_values
 
+    gain_acc[...] = jnp.zeros_like(gain_acc)
     norm_back(rows, v_ref, total, gain_ref, gain_acc, put)
     fold = 128 // share
     near = group // fold
@@ -1505,6 +1694,8 @@
             first = first + index * span
             target[:, home : home + size] = cols[member, :, first : first + size]
     from_seq.sent()
+    for item in downs:
+        item.end()
     reduce.sent()
     others(seqs, seq, lambda peer: to_seq(peer, seq).wait_send())
     others(group, own, lambda peer: gain_group(peer, own).wait_send())
@@ -1512,7 +1703,7 @@
     others(seqs, seq, lambda peer: gain_seq(peer, seq).wait_send())
 
 
-def heads_back(seqs, chips, a, w, group_a, x, d_middle, gain, mlp_gain, units, out_part, collective):
+def heads_back(seqs, chips, a, w, group_a, x, d_middle, gain, mlp_gain, units, out_part, down, collective):
     rows, width = x.shape
     batches, length, depth = a.shape
     group = 2 * chips
@@ -1531,10 +1722,13 @@
             jax.ShapeDtypeStruct((8, 128), jnp.float32),
             jax.ShapeDtypeStruct((share, units.size // 2 // share), half),
             jax.ShapeDtypeStruct((share, units.size // 2 // share), half),
+            jax.ShapeDtypeStruct((seqs, down.shape[0] // seqs, width), half),
         ],
-        in_specs=[VMEM_SPEC, VMEM_SPEC, ANY_SPEC] + [VMEM_SPEC] * 4 + [ANY_SPEC, VMEM_SPEC],
-        out_specs=[VMEM_SPEC] * 8,
+        in_specs=[VMEM_SPEC, VMEM_SPEC, ANY_SPEC] + [VMEM_SPEC] * 4 + [ANY_SPEC, VMEM_SPEC, ANY_SPEC],
+        out_specs=[VMEM_SPEC] * 8 + [ANY_SPEC],
         scratch_shapes=[
+            sems(2, seqs),
+            sems(2, seqs),
             pltpu.VMEM(units.shape, half),
             pltpu.SemaphoreType.DMA,
             pltpu.VMEM((seqs, out_part.shape[0] // seqs, width), half),
@@ -1566,7 +1760,7 @@
             4 * group * rows * width * depth, 200 * MIB, 2 * group * rows * width * 2
         ),
         name="heads_back",
-    )(a, w, group_a, x, d_middle, gain, mlp_gain, units, out_part)
+    )(a, w, group_a, x, d_middle, gain, mlp_gain, units, out_part, down)
 
 
 def doc_starts(lengths, positions, batches, seq_len):
@@ -1651,17 +1845,15 @@
         x_rows, gain_two[None], 3,
     )
     w_units = w_units.reshape(width, -1)
-    group_b, hidden, d_units, down_part = hidden_units(
-        chips, normed_b, w_units, wd_part, group_d, 4
+    d_middle, d_branch, mlp_gain_part, hidden, unit_part = feed_forward(
+        chips, batches, normed_b, w_units, wd_part, group_d, middle, cot_rows, gain_two[None], 4
     )
-    d_middle, d_branch, mlp_gain_part, unit_part, down_in = units_back(
-        seqs, chips, d_units, w_units, group_b, down_part, middle, cot_rows, gain_two[None], 5
-    )
-    d_attended, layer_out, out_part, unit_in = branch_back(
-        seqs, chips, batches, d_branch, wo_part, attended, middle, hidden, wd_part, unit_part, 6
+    d_attended, layer_out, out_part, unit_in, down_part = branch_back(
+        seqs, chips, batches, d_branch, wo_part, attended, middle, hidden, wd_part, unit_part,
+        group_d, 5,
     )
     d_heads, unit_cols = attend_back(
-        seqs, group, query, kv_pad, low, lse, d_attended, block, unit_part, unit_in, 7
+        seqs, group, query, kv_pad, low, lse, d_attended, block, unit_part, unit_in, 6
     )
     if not aligned:
         whole = lax.dynamic_update_slice_in_dim(
@@ -1669,9 +1861,9 @@
         )
         out_part = lax.psum(whole, "fsdp").reshape(seqs, group, share, width)
         out_part = lax.dynamic_slice_in_dim(out_part, member, 1, 1).reshape(seqs * share, width)
-    input_grad, wq_grad, wk_grad, wv_grad, wo_grad, gain_tile, gate_grad, up_grad = heads_back(
+    input_grad, wq_grad, wk_grad, wv_grad, wo_grad, gain_tile, gate_grad, up_grad, down_in = heads_back(
         seqs, chips, d_heads, w_heads, group_a, x_rows, d_middle, gain_one[None], mlp_gain_part,
-        unit_cols, out_part, 8,
+        unit_cols, out_part, down_part, 7,
     )
     run = lax.axis_index("seq")
     down_own = lax.dynamic_slice_in_dim(down_part, run * w_down.shape[0], w_down.shape[0], 0)

time: 786 us -> 738 us (0.939)
  Pallas kernels: 736 us -> 692 us
    pallas_call x2 -> x1, Pallas kernels: 189 us -> 150 us  [feed_forward(): pl.pallas_call(functools.partial(feed_kernel, chips, batches), out_shape=...]
  transfers between devices with their start and end apart: 2 -> 2, of which waited for: 0 -> 0; matrix products, arithmetic and copies ran while one was open for 1% -> 1% of each run, Pallas kernels for 35% -> 37%
where the time goes in v6:
time: 738 us; the launch traced here: 731 us
  Pallas kernels  692 us (94%)
  between operations  14.6 us (2%)
  other arithmetic  13.9 us (2%)
  local copies, waits for them, and re-layouts  8.55 us (1%)
    pallas_call x1, Pallas kernels, feed_forward(): pl.pallas_call(functools.partial(feed_kernel, chips, batches), out_shape=...  150 us
    pallas_call x1, Pallas kernels, branch_sum(): pl.pallas_call(functools.partial(branch_kernel, seqs, chips), out_shape=[...  109 us
    pallas_call x1, Pallas kernels, branch_back(): pl.pallas_call(functools.partial(branch_back_kernel, seqs, chips, batches...  107 us
    pallas_call x1, Pallas kernels, heads_back(): pl.pallas_call(functools.partial(heads_back_kernel, seqs, chips), out_sha...  105 us
    pallas_call x1, Pallas kernels, start(): pl.pallas_call(functools.partial(start_kernel, seqs, chips, batches), out...  98.3 us
    pallas_call x1, Pallas kernels, attend_back(): pl.pallas_call(functools.partial(attend_back_kernel, seqs, group, block),...  61.4 us
    pallas_call x1, Pallas kernels, attend(): pl.pallas_call(functools.partial(attend_kernel, seqs, group, block), in_s...  61.1 us
  transfers between devices with their start and end apart: 2, of which 0 were waited for; matrix products, arithmetic and copies ran while one was open for 1% of the time, Pallas kernels for 37%

profile of v6, /device:TPU:9, one launch (start us, length us, event | category | flops | bytes accessed | tf_op | source)
XLA Modules:
  0.0 730.5 jit_solution(17997007436010754527)
XLA Ops:
  7.2 0.7 all-gather.3.cloned.1.call-update
  8.0 0.7 all-gather.5.cloned.1.call-update
  8.7 0.7 maximum_convert_fusion
  9.5 0.6 pad_bitcast_fusion.tile_ref
  10.1 98.3 %start.1 = (bf16[2,1024,2048]{2,1,0:T(8,128)(2,1)}, bf16[2,1024,256]{2,1,0:T(8,128)(2,1)}, bf16[2,1024,512]{2,1,0:T(8,128)(2,1)}, f32[8,4,8,128]{3,2,1,0:T(8,128)}, bf16[2048,768]{1,0:T(8,128)(2,1)}) custom-call(f32[1,8,128]{2,1,0:T(8,128)} %pad_bitcast_fusion.tile_ref, bf16[256,2048]{1,0:T(8,128)(2,1)} %bitcast.47, bf16[64,2048]{1,0:T(8,128)(2,1)} %wq_ref.1, ...), custom_call_target="tpu_custom_call" | custom-call | flops 6442450944 | bytes 209715200 | tf_op jit(solution)/shard_map/start/pallas_call | solution.py:625
  108.6 0.3 copy.34
  108.9 0.4 copy.39
  109.3 0.8 reshape.184
  110.1 0.3 copy.35
  110.3 0.4 copy.38
  110.7 0.8 reshape.186
  111.7 0.6 maximum_subtract_fusion.low_ref
  112.3 1.5 pad_maximum_fusion.units_ref
  113.8 0.6 slice_bitcast_fusion
  114.5 61.1 %attend.1 = (bf16[2,1024,256]{2,1,0:T(8,128)(2,1)}, f32[2,4,1024]{2,1,0:T(4,128)}, bf16[2,2048,512]{2,1,0:T(8,128)(2,1)}, bf16[8,64,2048]{2,1,0:T(8,128)(2,1)}) custom-call(bf16[2,1024,256]{2,1,0:T(8,128)(2,1)} %get-tuple-element.47.q_ref, bf16[2,1024,512]{2,1,0:T(8,128)(2,1)} %get-tuple-element.48.kv_ref, s32[2,1,1024]{2,1,0:T(1,128)} %maximum_subtract_fusion.low_ref, ...), custom_call_target="tpu_custom_call" | custom-call | flops 5368709120 | bytes 157286400 | tf_op jit(solution)/shard_map/attend/pallas_call | solution.py:756
  175.5 109.2 %branch_sum.1 = (f32[256,2048]{1,0:T(8,128)}, bf16[256,2048]{1,0:T(8,128)(2,1)}, bf16[8,256,2048]{2,1,0:T(8,128)(2,1)}, bf16[4,512,2048]{2,1,0:T(8,128)(2,1)}) custom-call(bf16[2,1024,256]{2,1,0:T(8,128)(2,1)} %get-tuple-element.51.a_ref.att_ref, bf16[256,2048]{1,0:T(8,128)(2,1)} %all-gather.3.cloned.1.call-done.w_ref, bf16[256,2048]{1,0:T(8,128)(2,1)} %bitcast.45, ...), custom_call_target="tpu_custom_call" | custom-call | flops 2147483648 | bytes 262144000 | tf_op jit(solution)/shard_map/branch_sum/pallas_call | solution.py:829
  284.8 149.9 %feed_forward.1 = (f32[256,2048]{1,0:T(8,128)}, bf16[256,2048]{1,0:T(8,128)(2,1)}, f32[8,2048]{1,0:T(8,128)}, bf16[2048,1024]{1,0:T(8,128)(2,1)}, bf16[2048,2048]{1,0:T(8,128)(2,1)}) custom-call(bf16[256,2048]{1,0:T(8,128)(2,1)} %get-tuple-element.54.x_ref, bf16[2048,2048]{1,0:T(8,128)(2,1)} %bitcast.51, ...), custom_call_target="tpu_custom_call" | custom-call | flops 60129542144 | bytes 419430400 | tf_op jit(solution)/shard_map/feed_forward/pallas_call | solution.py:1180
  434.8 106.8 %branch_back.1 = (bf16[2,1024,256]{2,1,0:T(8,128)(2,1)}, bf16[256,2048]{1,0:T(8,128)(2,1)}, bf16[256,2048]{1,0:T(8,128)(2,1)}, bf16[4,512,2048]{2,1,0:T(8,128)(2,1)}, bf16[1024,2048]{1,0:T(8,128)(2,1)}) custom-call(bf16[256,2048]{1,0:T(8,128)(2,1)} %get-tuple-element.58.x_ref, bf16[256,2048]{1,0:T(8,128)(2,1)} %all-gather.3.cloned.1.call-done.w_ref, ...), custom_call_target="tpu_custom_call" | custom-call | flops 21474836480 | bytes 262144000 | tf_op jit(solution)/shard_map/branch_back/pallas_call | solution.py:1333
  541.6 61.4 %attend_back.1 = (bf16[2,1024,768]{2,1,0:T(8,128)(2,1)}, bf16[8,64,2048]{2,1,0:T(8,128)(2,1)}) custom-call(bf16[2,1024,256]{2,1,0:T(8,128)(2,1)} %get-tuple-element.47.q_ref, bf16[2,2048,512]{2,1,0:T(8,128)(2,1)} %get-tuple-element.62.pad_ref, s32[2,1,1024]{2,1,0:T(1,128)} %maximum_subtract_fusion.low_ref, f32[2,4,1024]{2,1,0:T(4,128)} %get-tuple-element.63.lse_ref, ...), custom_call_target="tpu_custom_call" | custom-call | flops 13421772800 | bytes 188743680 | tf_op jit(solution)/shard_map/attend_back/pallas_call | solution.py:1500
  603.0 105.2 %heads_back.1 = (f32[256,2048]{1,0:T(8,128)}, bf16[64,2048]{1,0:T(8,128)(2,1)}, bf16[64,2048]{1,0:T(8,128)(2,1)}, bf16[64,2048]{1,0:T(8,128)(2,1)}, f32[64,2048]...) custom-call(bf16[2,1024,768]{2,1,0:T(8,128)(2,1)} %get-tuple-element, ...), custom_call_target="tpu_custom_call" | custom-call | flops 12884901888 | bytes 209715200 | tf_op jit(solution)/shard_map/heads_back/pallas_call | solution.py:1714
  708.3 2.8 convert_element_type.34
  711.1 1.5 convert_element_type.35
  712.5 0.8 convert_element_type.31
  713.4 0.8 convert_element_type.32
  714.2 0.8 convert_element_type.33
  715.0 0.7 slice.17
  715.8 0.5 slice_bitcast_fusion.2
  716.3 1.0 select_reduce_fusion
  717.3 3.0 convert_add_fusion
  720.4 1.0 copy.43
  721.3 1.3 copy.44
  722.7 0.8 copy.45
  (42 shorter events, 0.7 us)
Async XLA Ops:
  7.2 168.4 %all-gather.3.cloned.1.call-start = ((), (), s32[]{:S(2)}) async-start(), calls=%async_computation | async-start | bytes 1310720 | tf_op jit(solution)/shard_map/all_gather | solution.py:1812
  7.9 276.9 %all-gather.5.cloned.1.call-start = ((), (), s32[]{:S(2)}) async-start(), calls=%async_computation.1 | async-start | bytes 5242880 | tf_op jit(solution)/shard_map/all_gather | solution.py:1810
  10.1 98.3 %copy-start.11 = (s32[2,4]{1,0:T(2,128)S(1)}, s32[2,4]{1,0:T(2,128)}, u32[]{:S(2)}) copy-start(s32[2,4]{1,0:T(2,128)} %param.14) | copy-start | bytes 100
  10.1 98.5 %copy-start.3 = (bf16[64,8192]{1,0:T(8,128)(2,1)S(1)}, bf16[64,8192]{1,0:T(8,128)(2,1)}, u32[]{:S(2)}) copy-start(bf16[64,8192]{1,0:T(8,128)(2,1)} %param.21) | copy-start | bytes 3145732
  108.6 1.4 copy-start.4
  110.0 1.5 copy-start.10
  708.2 2.8 copy-start.2
  708.2 4.3 copy-start.9
  708.2 5.1 copy-start.8
  711.1 3.1 copy-start.7
  711.1 5.2 copy-start
  717.3 3.1 copy-start.5
  717.3 4.0 copy-start.1
  720.4 2.3 copy-start.6
Sparse Core Ops, SparseCore 0:
  9.9 36.4 all-gather.2
  48.2 57.8 all-gather.4

commit v7 on v6

--- a/solution.py
+++ b/solution.py
@@ -1368,199 +1368,188 @@
     )(x, w, attended, middle, hidden, wd, unit_part, group_d.reshape(group * rows, width))
 
 
-def attend_back_kernel(
-    seqs, group, block, q_ref, pad_ref, low_ref, lse_ref, d_ref, part_hbm, in_hbm, heads_ref, cols_ref,
-    dk, dv, kt, back_out, back_in, halo_send, halo_recv, swap_send, swap_recv, swap_keep,
-    parts, sums_ref, load,
-):
-    seq = lax.axis_index("seq")
-    batches, length, span = q_ref.shape
-    has_left, has_right = seq > 0, seq < seqs - 1
-    run = parts.shape[1]
-
-    def loaded(place, own):
-        source = part_hbm.at[rows_at(seq, run)] if own else in_hbm.at[place]
-        return pltpu.make_async_copy(source, parts.at[place], load.at[place])
-
-    for place in range(seqs):
-        pl.when(place == seq)(lambda place=place: loaded(place, True).start())
-        pl.when(place != seq)(lambda place=place: loaded(place, False).start())
-    pl.when(has_left)(lambda: signal_seq(seq - 1))
-    pl.when(has_right)(lambda: signal_seq(seq + 1))
-    meet(greet_group(group) + has_left.astype(jnp.int32) + has_right.astype(jnp.int32))
-    for place in range(seqs):
-        loaded(place, False).wait()
-
-    @pl.loop(0, group)
-    def _(member):
-        share = run // group
-
-        @pl.loop(0, share // 16)
-        def _(chunk):
-            here = pl.ds(pl.multiple_of(member * share + chunk * 16, 16), 16)
-            added = parts[0, here, :].astype(jnp.float32)
-            for place in range(1, seqs):
-                added = added + parts[place, here, :].astype(jnp.float32)
-            sums_ref[member, rows_at(chunk, 16), :] = to_half(added)
-
-    swap = Swap(group, sums_ref, cols_ref, swap_send, swap_recv, swap_keep)
-    swap.begin()
-    steps = length // block
-    scale = jnp.asarray(HEAD**-0.5, jnp.bfloat16)
-
-    def halo(batch, step, peer):
-        rows = rows_at(step, block)
-        return pltpu.make_async_remote_copy(
-            src_ref=back_out.at[batch, rows],
-            dst_ref=back_in.at[batch, rows],
-            send_sem=halo_send.at[batch, step],
-            recv_sem=halo_recv.at[batch, step],
-            device_id={"seq": peer},
-            device_id_type=MESH,
-        )
-
-    dk[...] = jnp.zeros_like(dk)
-    dv[...] = jnp.zeros_like(dv)
-    for batch in range(batches):
-        kt[...] = pad_ref[batch, :, :span].T * scale
-
-        @pl.loop(0, steps)
-        def _(step, batch=batch):
-            begin = pl.multiple_of(step * block, block)
-            keys = pl.ds(begin, block + WINDOW)
-            rows = pl.ds(begin, block)
-            low = low_ref[batch, :, rows]
-            for pair in range(span // PAIR):
-                lanes = slice(pair * PAIR, (pair + 1) * PAIR)
-                q_pair = q_ref[batch, rows, lanes] * scale
-                d_pair = d_ref[batch, rows, lanes]
-                k_rows = pad_ref[batch, keys, lanes]
-                v_rows = pad_ref[batch, keys, span + pair * PAIR : span + (pair + 1) * PAIR]
-                k_cols = kt[lanes, keys]
-                back = []
-                for half in range(2):
-                    row = pair * 2 + half
-                    q_head = head_lanes(q_pair, half)
-                    d_head = head_lanes(d_pair, half)
-                    scores = masked_scores(k_rows, q_head, low)
-                    probs = jnp.exp(scores - lse_ref[batch, row : row + 1, rows])
-                    d_probs = dot_nt(v_rows, d_head)
-                    along = jnp.sum(probs * d_probs, axis=0, keepdims=True)
-                    d_scores = to_half(probs * (d_probs - along))
-                    dv[batch, keys, lanes] += dot_nn(to_half(probs), d_head)
-                    dk[batch, keys, lanes] += dot_nn(d_scores, q_head)
-                    back.append(dot_nn(k_cols, d_scores))
-                at = lax.broadcasted_iota(jnp.int32, back[0].shape, 0)
-                heads_ref[batch, rows, lanes] = to_half(
-                    jnp.where(at < HEAD, back[0], back[1]).T
-                )
-
-            @pl.when(has_left & (step < WINDOW // block))
-            def _():
-                back_out[batch, rows, :span] = to_half(dk[batch, rows, :])
-                back_out[batch, rows, span:] = to_half(dv[batch, rows, :])
-                halo(batch, step, seq - 1).start()
-
-    first = length - WINDOW
-    for batch in range(batches):
-        if first:
-            heads_ref[batch, :first, span : 2 * span] = to_half(dk[batch, WINDOW:length, :])
-            heads_ref[batch, :first, 2 * span :] = to_half(dv[batch, WINDOW:length, :])
-
-        @pl.loop(0, WINDOW // block)
-        def _(step, batch=batch):
-            inner = pl.ds(pl.multiple_of(step * block + length, block), block)
-            rows = pl.ds(pl.multiple_of(step * block + first, block), block)
-
-            @pl.when(has_right)
-            def _():
-                halo(batch, step, seq).wait_recv()
-                got = back_in[batch, rows_at(step, block), :].astype(jnp.float32)
-                heads_ref[batch, rows, span : 2 * span] = to_half(
-                    dk[batch, inner, :] + got[:, :span]
-                )
-                heads_ref[batch, rows, 2 * span :] = to_half(dv[batch, inner, :] + got[:, span:])
-
-            @pl.when(jnp.logical_not(has_right))
-            def _():
-                heads_ref[batch, rows, span : 2 * span] = to_half(dk[batch, inner, :])
-                heads_ref[batch, rows, 2 * span :] = to_half(dv[batch, inner, :])
-
-            pl.when(has_left)(lambda: halo(batch, step, seq).wait_send())
-
-    swap.end()
-
-
-def attend_back(seqs, group, query, kv_pad, low, lse, d_att, block, part, parts_in, collective):
-    batches, length, span = query.shape
-    padded = kv_pad.shape[1]
-    half = jnp.bfloat16
-    share = part.shape[0] // seqs // group
-    sums = (group, share, part.shape[1])
-    return pl.pallas_call(
-        functools.partial(attend_back_kernel, seqs, group, block),
-        in_specs=[VMEM_SPEC] * 5 + [ANY_SPEC] * 2,
-        out_specs=[VMEM_SPEC, ANY_SPEC],
-        out_shape=[
-            jax.ShapeDtypeStruct((batches, length, 3 * span), half),
-            jax.ShapeDtypeStruct(sums, half),
-        ],
-        scratch_shapes=[
-            pltpu.VMEM((batches, padded, span), jnp.float32),
-            pltpu.VMEM((batches, padded, span), jnp.float32),
-            pltpu.VMEM((span, padded), half),
-            pltpu.VMEM((batches, WINDOW, 2 * span), half),
-            pltpu.VMEM((batches, WINDOW, 2 * span), half),
-            sems(batches, WINDOW // block),
-            sems(batches, WINDOW // block),
-            sems(group),
-            sems(group),
-            pltpu.SemaphoreType.DMA,
-            pltpu.VMEM(parts_in.shape, half),
-            pltpu.VMEM(sums, half),
-            sems(seqs),
-        ],
-        compiler_params=comm_params(collective),
-        cost_estimate=cost(
-            20 * batches * length * span * (WINDOW + block), 180 * MIB, part.size // seqs * 2
-        ),
-        name="attend_back",
-    )(query, kv_pad, low, lse, d_att, part, parts_in)
-
-
-def heads_back_kernel(
-    seqs, chips, a_ref, w_ref, g_hbm, v_ref, dm_ref, gain_ref, mlp_gain_ref, units_hbm, out_ref, down_hbm,
-    grad_ref, q_ref, k_ref, v_out_ref, wo_ref, tile_ref, gate_ref, up_ref, down_in,
-    down_send, down_recv,     units, unit_load, out_in, out_send, out_recv, total, gain_acc, lefts, parts, sums, cols, gain_out, gain_in, gain_sum, gain_back,
-    left_sem, part_send, part_recv, cols_send, cols_recv,
-    gain_send, gain_recv, back_send, back_recv,
-    acc, cross_out, line_out, cross_in, line_in, sum_send, sum_recv,
+def attention_back_kernel(
+    seqs, chips, block, q_ref, pad_ref, low_ref, lse_ref, d_ref, part_hbm, in_hbm,
+    w_ref, g_hbm, v_ref, dm_hbm, gain_ref, mlp_gain_ref, out_ref, down_hbm,
+    grad_ref, wq_ref, wk_ref, wv_ref, wo_ref, tile_ref, gate_ref, up_ref, down_in,
+    dk, dv, kt, heads, back_out, back_in, unit_parts, unit_sums, units, lefts, parts, sums, cols, out_in,
+    totals, gain_acc, gain_out, gain_in, gain_sum, gain_back, acc, keep,
+    halo_send, halo_recv, unit_load, unit_send, unit_recv, unit_keep, dm_load, left_sem,
+    part_send, part_recv, cols_send, cols_recv, out_send, out_recv, down_send, down_recv,
+    gain_send, gain_recv, back_send, back_recv, *line_sums,
 ):
     line = Line(chips)
     group = 2 * chips
     seq = lax.axis_index("seq")
     own = line.own
+    batches, length, span = q_ref.shape
     rows, width = v_ref.shape
-    batches = a_ref.shape[0]
-    part = lefts.shape[3]
+    piece = rows // batches
+    pair_rows = 2 * piece
+    depth = 3 * span
     run = width // seqs
     share = run // group
-    depth = a_ref.shape[2]
+    part = lefts.shape[3]
+    steps, need = length // block, WINDOW // block
+    first = length - WINDOW
+    has_left, has_right = seq > 0, seq < seqs - 1
+    scale = jnp.asarray(HEAD**-0.5, jnp.bfloat16)
+
+    def others(count, me, act):
+        pl.loop(1, count)(lambda ahead: act(lax.rem(me + ahead, count)))
+
+    def unit_loaded(turn, place, mine):
+        member = lax.rem(own + turn, group)
+        slot = lax.rem(turn, 2)
+        if mine:
+            source = part_hbm.at[rows_at(seq * group + member, share)]
+        else:
+            source = in_hbm.at[place, rows_at(member, share)]
+        return pltpu.make_async_copy(source, unit_parts.at[slot, place], unit_load.at[slot, place])
+
+    def load_units(turn):
+        for place in range(seqs):
+            pl.when(place == seq)(lambda place=place: unit_loaded(turn, place, True).start())
+            pl.when(place != seq)(lambda place=place: unit_loaded(turn, place, False).start())
+
+    load_units(1)
+    dm_loaded = pltpu.make_async_copy(dm_hbm, grad_ref, dm_load)
+    dm_loaded.start()
+    meet(greet_group(group) + greet_seq(seqs))
+    size = down_in.shape[1]
+    cut = size // 16 * 3 // 8 * 16
+    downs = [
+        ToSeq(seqs, down_hbm, down_in, down_send.at[0], down_recv.at[0], 0, cut),
+        ToSeq(seqs, down_hbm, down_in, down_send.at[1], down_recv.at[1], cut, size - cut),
+    ]
+    downs[0].begin()
+    swap = Swap(group, unit_sums, units, unit_send, unit_recv, unit_keep)
+
+    @pl.loop(1, group + 1)
+    def _(turn):
+        member = lax.rem(own + turn, group)
+        slot = lax.rem(turn, 2)
+        pl.when(turn < group)(lambda: load_units(turn + 1))
+        for place in range(seqs):
+            unit_loaded(turn, place, False).wait()
+
+        @pl.loop(0, share // 16)
+        def _(chunk):
+            here = rows_at(chunk, 16)
+            added = unit_parts[slot, 0, here, :].astype(jnp.float32)
+            for place in range(1, seqs):
+                added = added + unit_parts[slot, place, here, :].astype(jnp.float32)
+            unit_sums[member, here, :] = to_half(added)
+
+        pl.when(turn < group)(lambda: swap.move(member, own).start())
+        pl.when(turn == group)(lambda: swap.kept().start())
+
+    def halo(batch, step, peer):
+        here = rows_at(step, block)
+        return pltpu.make_async_remote_copy(
+            src_ref=back_out.at[batch, here],
+            dst_ref=back_in.at[batch, here],
+            send_sem=halo_send.at[batch, step],
+            recv_sem=halo_recv.at[batch, step],
+            device_id={"seq": peer},
+            device_id_type=MESH,
+        )
+
+    def attend_block(batch, step):
+        begin = pl.multiple_of(step * block, block)
+        keys = pl.ds(begin, block + WINDOW)
+        rows = pl.ds(begin, block)
+        low = low_ref[batch, :, rows]
+        for pair in range(span // PAIR):
+            lanes = slice(pair * PAIR, (pair + 1) * PAIR)
+            q_pair = q_ref[batch, rows, lanes] * scale
+            d_pair = d_ref[batch, rows, lanes]
+            k_rows = pad_ref[batch, keys, lanes]
+            v_rows = pad_ref[batch, keys, span + pair * PAIR : span + (pair + 1) * PAIR]
+            k_cols = kt[lanes, keys]
+            back = []
+            for half in range(2):
+                row = pair * 2 + half
+                q_head = head_lanes(q_pair, half)
+                d_head = head_lanes(d_pair, half)
+                scores = masked_scores(k_rows, q_head, low)
+                probs = jnp.exp(scores - lse_ref[batch, row : row + 1, rows])
+                d_probs = dot_nt(v_rows, d_head)
+                along = jnp.sum(probs * d_probs, axis=0, keepdims=True)
+                d_scores = to_half(probs * (d_probs - along))
+                dv[keys, lanes] += dot_nn(to_half(probs), d_head)
+                dk[keys, lanes] += dot_nn(d_scores, q_head)
+                back.append(dot_nn(k_cols, d_scores))
+            at = lax.broadcasted_iota(jnp.int32, back[0].shape, 0)
+            heads[batch, rows, lanes] = to_half(
+                jnp.where(at < HEAD, back[0], back[1]).T
+            )
+
+
+        @pl.when(has_left & (step < need))
+        def _():
+            back_out[batch, rows, :span] = to_half(dk[rows, :])
+            back_out[batch, rows, span:] = to_half(dv[rows, :])
+            halo(batch, step, seq - 1).start()
+
+        @pl.when(step == steps - 1)
+        def _():
+            heads[batch, :, span : 2 * span] = to_half(dk[WINDOW:, :])
+            heads[batch, :, 2 * span :] = to_half(dv[WINDOW:, :])
+
+    def add_halo(batch):
+        @pl.when(has_right)
+        def _():
+            @pl.loop(0, need)
+            def _(step):
+                there = pl.ds(pl.multiple_of(step * block + first, block), block)
+                halo(batch, step, seq).wait_recv()
+                got = back_in[batch, rows_at(step, block), :].astype(jnp.float32)
+                mine = heads[batch, there, span:].astype(jnp.float32)
+                heads[batch, there, span:] = to_half(mine + got)
+
+    def product(batch):
+        def get(place, tile):
+            return dot_nt(heads[batch, rows_at(place, pair_rows), :], w_ref[rows_at(tile, TILE), :])
+
+        return get
+
+    reduces = [
+        PairReduce(
+            line, product(batch), totals.at[batch], acc, keep, *line_sums[6 * batch : 6 * batch + 6]
+        )
+        for batch in range(batches)
+    ]
+    last = 2 * chips - 2
+
+    @pl.loop(0, 2 * steps)
+    def _(turn):
+        batch, step = turn // steps, lax.rem(turn, steps)
+
+        @pl.when(step == 0)
+        def _():
+            kt[...] = pad_ref[batch, :, :span].T * scale
+            dk[...] = jnp.zeros_like(dk)
+            dv[...] = jnp.zeros_like(dv)
+
+        attend_block(batch, step)
+        after = turn - steps - 1
+        pl.when(after == 0)(lambda: add_halo(0))
+
+        @pl.when((after >= 0) & (2 * after < last))
+        def _():
+            reduces[0].step(2 * after)
+            reduces[0].step(2 * after + 1)
+
+    for after in range(steps - 1, chips - 1):
+        reduces[0].step(2 * after)
+        reduces[0].step(2 * after + 1)
 
     def left(tile):
         slot = lax.rem(tile, 2)
         return pltpu.make_async_copy(
             g_hbm.at[:, :, rows_at(tile, part)], lefts.at[slot], left_sem.at[slot]
         )
-
-    def weight_grad(tile):
-        left(tile).wait()
-        pl.when(tile + 1 < width // part)(lambda: left(tile + 1).start())
-        slot = lax.rem(tile, 2)
-        got = contract_rows(lefts[slot, 0], a_ref[0])
-        for batch in range(1, batches):
-            got = got + contract_rows(lefts[slot, batch], a_ref[batch])
-        parts[rows_at(tile, part), :] = to_half(got)
 
     def to_seq(peer, place):
         return pltpu.make_async_remote_copy(
@@ -1572,51 +1561,46 @@
             device_id_type=MESH,
         )
 
-    def others(count, me, act):
-        pl.loop(1, count)(lambda ahead: act(lax.rem(me + ahead, count)))
-
-    def product(slot, tile):
-        return dot_nt(left_rows(a_ref, slot, rows), w_ref[rows_at(tile, TILE), :])
-
-    size = down_in.shape[1]
-    cut = size // 16 * 3 // 8 * 16
-    downs = [
-        ToSeq(seqs, down_hbm, down_in, down_send.at[0], down_recv.at[0], 0, cut),
-        ToSeq(seqs, down_hbm, down_in, down_send.at[1], down_recv.at[1], cut, size - cut),
-    ]
+    left(0).start()
+    add_halo(1)
+
+    @pl.loop(0, width // part)
+    def _(tile):
+        left(tile).wait()
+        pl.when(tile + 1 < width // part)(lambda: left(tile + 1).start())
+        slot = lax.rem(tile, 2)
+        got = contract_rows(lefts[slot, 0], heads[0])
+        for batch in range(1, batches):
+            got = got + contract_rows(lefts[slot, batch], heads[batch])
+        parts[rows_at(tile, part), :] = to_half(got)
+
+    others(seqs, seq, lambda peer: to_seq(peer, seq).start())
     from_seq = ToSeq(seqs, out_ref, out_in, out_send, out_recv)
-    units_in = pltpu.make_async_copy(units_hbm, units, unit_load)
-    units_in.start()
-    left(0).start()
-    meet(greet_group(group) + greet_seq(seqs))
-    downs[0].begin()
-    reduce = Reduce(
-        line, product, total, acc, cross_out, line_out, cross_in, line_in, sum_send, sum_recv
-    )
-    count = width // part
-    per = -(-count // 2)
-
-    @pl.loop(0, 2)
-    def _(step):
-        reduce.step(step)
-
-        @pl.loop(0, per)
-        def _(turn):
-            tile = step * per + turn
-            pl.when(tile < count)(lambda: weight_grad(tile))
-
-    others(seqs, seq, lambda peer: to_seq(peer, seq).start())
     from_seq.begin()
-    units_in.wait()
-    block = units.shape[2] // 2 // seqs
+    gain_acc[...] = jnp.zeros_like(gain_acc)
+    dm_loaded.wait()
+
+    def norm_batch(batch):
+        mine = pl.ds(batch * piece, piece)
+
+        def put(here, d_values):
+            there = pl.ds(pl.multiple_of(here.start + batch * piece, here.size), here.size)
+            grad_ref[there, :] += d_values
+
+        norm_back(piece, v_ref.at[mine], totals.at[batch], gain_ref, gain_acc, put)
+
+    pl.loop(0, 2)(reduces[1].step)
+    reduces[0].step(last)
+    norm_batch(0)
+    pl.loop(2, last)(reduces[1].step)
+    swap.end()
+    cell = units.shape[2] // 2 // seqs
     for member in range(group):
         for place in range(seqs):
-            column = (place * group + member) * block
-            for target, begin in ((gate_ref, 0), (up_ref, seqs * block)):
-                here = slice(begin + place * block, begin + (place + 1) * block)
-                target[:, column : column + block] = units[member, :, here]
-
-    pl.loop(2, 2 * chips - 2)(reduce.step)
+            column = (place * group + member) * cell
+            for target, begin in ((gate_ref, 0), (up_ref, seqs * cell)):
+                here = slice(begin + place * cell, begin + (place + 1) * cell)
+                target[:, column : column + cell] = units[member, :, here]
 
     def block_swap(peer, member):
         return pltpu.make_async_remote_copy(
@@ -1640,15 +1624,10 @@
     others(group, own, lambda peer: block_swap(peer, own).start())
     cols[own] = parts[rows_at(seq * group + own, share), :]
     from_seq.arrived()
-    size = out_in.shape[1]
-    wo_ref[...] = add_from_seq(seqs, out_ref[rows_at(seq, size), :], out_in, slice(None))
-    reduce.step(2 * chips - 2)
-
-    def put(here, d_values):
-        grad_ref[here, :] = dm_ref[here, :] + d_values
-
-    gain_acc[...] = jnp.zeros_like(gain_acc)
-    norm_back(rows, v_ref, total, gain_ref, gain_acc, put)
+    out_rows = out_in.shape[1]
+    wo_ref[...] = add_from_seq(seqs, out_ref[rows_at(seq, out_rows), :], out_in, slice(None))
+    reduces[1].step(last)
+    norm_batch(1)
     fold = 128 // share
     near = group // fold
     attn_row = jnp.sum(gain_acc[...], axis=0, keepdims=True)
@@ -1688,79 +1667,118 @@
     others(seqs, seq, lambda peer: gain_seq(peer, peer).wait_recv())
     tile_ref[...] = jnp.sum(gain_back[...], axis=0)
     others(group, own, lambda peer: block_swap(peer, peer).wait_recv())
-    span = depth // 3
-    for index, target in enumerate((q_ref, k_ref, v_out_ref)):
+    for index, target in enumerate((wq_ref, wk_ref, wv_ref)):
         for member, first, home, size in column_parts(seqs, group, share, span):
             first = first + index * span
             target[:, home : home + size] = cols[member, :, first : first + size]
     from_seq.sent()
     for item in downs:
         item.end()
-    reduce.sent()
+    for batch in range(batches):
+        reduces[batch].sent()
+
+        @pl.when(has_left)
+        def _(batch=batch):
+            pl.loop(0, need)(lambda step: halo(batch, step, seq).wait_send())
+
     others(seqs, seq, lambda peer: to_seq(peer, seq).wait_send())
     others(group, own, lambda peer: gain_group(peer, own).wait_send())
     others(group, own, lambda peer: block_swap(peer, own).wait_send())
     others(seqs, seq, lambda peer: gain_seq(peer, seq).wait_send())
 
 
-def heads_back(seqs, chips, a, w, group_a, x, d_middle, gain, mlp_gain, units, out_part, down, collective):
+def attention_back(
+    seqs, chips, block, query, kv_pad, low, lse, d_att, part_own, parts_in, w, group_a, x, d_middle,
+    gain, mlp_gain, out_part, down, collective,
+):
+    batches, length, span = query.shape
+    padded = kv_pad.shape[1]
     rows, width = x.shape
-    batches, length, depth = a.shape
+    piece = rows // batches
     group = 2 * chips
-    share = width // seqs // group
+    depth = w.shape[1]
+    run = width // seqs
+    share = run // group
     near = group // (128 // share)
-    half = jnp.bfloat16
+    cells = part_own.shape[1]
+    out_rows = out_part.shape[0] // seqs
+    half, wide = jnp.bfloat16, jnp.float32
     part = 256 if batches * length <= 2048 else 128
     return pl.pallas_call(
-        functools.partial(heads_back_kernel, seqs, chips),
+        functools.partial(attention_back_kernel, seqs, chips, block),
         out_shape=[
-            jax.ShapeDtypeStruct((rows, width), jnp.float32),
+            jax.ShapeDtypeStruct((rows, width), wide),
             jax.ShapeDtypeStruct((share, width), half),
             jax.ShapeDtypeStruct((share, width), half),
             jax.ShapeDtypeStruct((share, width), half),
-            jax.ShapeDtypeStruct((out_part.shape[0] // seqs, width), jnp.float32),
-            jax.ShapeDtypeStruct((8, 128), jnp.float32),
-            jax.ShapeDtypeStruct((share, units.size // 2 // share), half),
-            jax.ShapeDtypeStruct((share, units.size // 2 // share), half),
+            jax.ShapeDtypeStruct((out_rows, width), wide),
+            jax.ShapeDtypeStruct((8, 128), wide),
+            jax.ShapeDtypeStruct((share, cells // 2 * group), half),
+            jax.ShapeDtypeStruct((share, cells // 2 * group), half),
             jax.ShapeDtypeStruct((seqs, down.shape[0] // seqs, width), half),
         ],
-        in_specs=[VMEM_SPEC, VMEM_SPEC, ANY_SPEC] + [VMEM_SPEC] * 4 + [ANY_SPEC, VMEM_SPEC, ANY_SPEC],
+        in_specs=[VMEM_SPEC] * 5
+        + [ANY_SPEC] * 2
+        + [VMEM_SPEC, ANY_SPEC, VMEM_SPEC, ANY_SPEC]
+        + [VMEM_SPEC] * 3
+        + [ANY_SPEC],
         out_specs=[VMEM_SPEC] * 8 + [ANY_SPEC],
         scratch_shapes=[
-            sems(2, seqs),
-            sems(2, seqs),
-            pltpu.VMEM(units.shape, half),
-            pltpu.SemaphoreType.DMA,
-            pltpu.VMEM((seqs, out_part.shape[0] // seqs, width), half),
-            sems(seqs),
-            sems(seqs),
-            pltpu.VMEM((rows, width), jnp.float32),
-            pltpu.VMEM((8, width), jnp.float32),
+            pltpu.VMEM((padded, span), wide),
+            pltpu.VMEM((padded, span), wide),
+            pltpu.VMEM((span, padded), half),
+            pltpu.VMEM((batches, length, depth), half),
+            pltpu.VMEM((batches, WINDOW, 2 * span), half),
+            pltpu.VMEM((batches, WINDOW, 2 * span), half),
+            pltpu.VMEM((2, seqs, share, cells), half),
+            pltpu.VMEM((group, share, cells), half),
+            pltpu.VMEM((group, share, cells), half),
             pltpu.VMEM((2, batches, length, part), half),
             pltpu.VMEM((width, depth), half),
-            pltpu.VMEM((seqs, width // seqs, depth), half),
+            pltpu.VMEM((seqs, run, depth), half),
             pltpu.VMEM((group, share, depth), half),
-            pltpu.VMEM((near, seqs, 8, 128), jnp.float32),
-            pltpu.VMEM((group, seqs, 8, 128), jnp.float32),
-            pltpu.VMEM((seqs, 8, 128), jnp.float32),
-            pltpu.VMEM((seqs, 8, 128), jnp.float32),
+            pltpu.VMEM((seqs, out_rows, width), half),
+            pltpu.VMEM((batches, piece, width), wide),
+            pltpu.VMEM((8, width), wide),
+            pltpu.VMEM((near, seqs, 8, 128), wide),
+            pltpu.VMEM((group, seqs, 8, 128), wide),
+            pltpu.VMEM((seqs, 8, 128), wide),
+            pltpu.VMEM((seqs, 8, 128), wide),
+            pltpu.VMEM((2 * piece, TILE), wide),
+            pltpu.VMEM((piece, width), wide),
+            sems(batches, WINDOW // block),
+            sems(batches, WINDOW // block),
+            sems(2, seqs),
+            sems(group),
+            sems(group),
+            pltpu.SemaphoreType.DMA,
+            pltpu.SemaphoreType.DMA,
             sems(2),
             sems(seqs),
             sems(seqs),
             sems(group),
             sems(group),
+            sems(seqs),
+            sems(seqs),
+            sems(2, seqs),
+            sems(2, seqs),
             sems(group),
             sems(group),
             sems(seqs),
             sems(seqs),
         ]
-        + Reduce.scratch(chips, rows, width),
-        compiler_params=comm_params(collective, 60),
+        + PairReduce.scratch(chips, piece, width) * batches,
+        compiler_params=comm_params(collective, 63),
         cost_estimate=cost(
-            4 * group * rows * width * depth, 200 * MIB, 2 * group * rows * width * 2
+            20 * batches * length * span * (WINDOW + block) + 4 * group * rows * width * depth,
+            400 * MIB,
+            3 * group * rows * width * 2,
         ),
-        name="heads_back",
-    )(a, w, group_a, x, d_middle, gain, mlp_gain, units, out_part, down)
+        name="attention_back",
+    )(
+        query, kv_pad, low, lse, d_att, part_own, parts_in, w, group_a, x, d_middle, gain, mlp_gain,
+        out_part, down,
+    )
 
 
 def doc_starts(lengths, positions, batches, seq_len):
@@ -1852,18 +1870,17 @@
         seqs, chips, batches, d_branch, wo_part, attended, middle, hidden, wd_part, unit_part,
         group_d, 5,
     )
-    d_heads, unit_cols = attend_back(
-        seqs, group, query, kv_pad, low, lse, d_attended, block, unit_part, unit_in, 6
-    )
     if not aligned:
         whole = lax.dynamic_update_slice_in_dim(
             jnp.zeros((width, width), jnp.bfloat16), out_part, member * span, 0
         )
         out_part = lax.psum(whole, "fsdp").reshape(seqs, group, share, width)
         out_part = lax.dynamic_slice_in_dim(out_part, member, 1, 1).reshape(seqs * share, width)
-    input_grad, wq_grad, wk_grad, wv_grad, wo_grad, gain_tile, gate_grad, up_grad, down_in = heads_back(
-        seqs, chips, d_heads, w_heads, group_a, x_rows, d_middle, gain_one[None], mlp_gain_part,
-        unit_cols, out_part, down_part, 7,
+    input_grad, wq_grad, wk_grad, wv_grad, wo_grad, gain_tile, gate_grad, up_grad, down_in = (
+        attention_back(
+            seqs, chips, block, query, kv_pad, low, lse, d_attended, unit_part, unit_in, w_heads,
+            group_a, x_rows, d_middle, gain_one[None], mlp_gain_part, out_part, down_part, 6,
+        )
     )
     run = lax.axis_index("seq")
     down_own = lax.dynamic_slice_in_dim(down_part, run * w_down.shape[0], w_down.shape[0], 0)

time: 738 us -> 741 us (level)
    pallas_call x2 -> x1, Pallas kernels: 167 us -> 171 us  [attention_back(): pl.pallas_call(functools.partial(attention_back_kernel, seqs, chips, bloc...]
  transfers between devices with their start and end apart: 2 -> 2, of which waited for: 0 -> 0; matrix products, arithmetic and copies ran while one was open for 1% -> 1% of each run, Pallas kernels for 37% -> 36%
where the time goes in v7:
time: 741 us; the launch traced here: 736 us
  Pallas kernels  697 us (94%)
  between operations  14.8 us (2%)
  other arithmetic  13.9 us (2%)
  local copies, waits for them, and re-layouts  8.55 us (1%)
    pallas_call x1, Pallas kernels, attention_back(): pl.pallas_call(functools.partial(attention_back_kernel, seqs, chips, bloc...  171 us
    pallas_call x1, Pallas kernels, feed_forward(): pl.pallas_call(functools.partial(feed_kernel, chips, batches), out_shape=...  150 us
    pallas_call x1, Pallas kernels, branch_sum(): pl.pallas_call(functools.partial(branch_kernel, seqs, chips), out_shape=[...  109 us
    pallas_call x1, Pallas kernels, branch_back(): pl.pallas_call(functools.partial(branch_back_kernel, seqs, chips, batches...  107 us
    pallas_call x1, Pallas kernels, start(): pl.pallas_call(functools.partial(start_kernel, seqs, chips, batches), out...  98.3 us
    pallas_call x1, Pallas kernels, attend(): pl.pallas_call(functools.partial(attend_kernel, seqs, group, block), in_s...  61.1 us
  transfers between devices with their start and end apart: 2, of which 0 were waited for; matrix products, arithmetic and copies ran while one was open for 1% of the time, Pallas kernels for 36%

profile of v7, /device:TPU:9, one launch (start us, length us, event | category | flops | bytes accessed | tf_op | source)
XLA Modules:
  0.0 735.9 jit_solution(16199900055736623326)
XLA Ops:
  7.2 0.7 all-gather.3.cloned.1.call-update
  8.0 0.7 all-gather.5.cloned.1.call-update
  8.7 0.7 maximum_convert_fusion
  9.5 0.6 pad_bitcast_fusion.tile_ref
  10.1 98.3 %start.1 = (bf16[2,1024,2048]{2,1,0:T(8,128)(2,1)}, bf16[2,1024,256]{2,1,0:T(8,128)(2,1)}, bf16[2,1024,512]{2,1,0:T(8,128)(2,1)}, f32[8,4,8,128]{3,2,1,0:T(8,128)}, bf16[2048,768]{1,0:T(8,128)(2,1)}) custom-call(f32[1,8,128]{2,1,0:T(8,128)} %pad_bitcast_fusion.tile_ref, bf16[256,2048]{1,0:T(8,128)(2,1)} %bitcast.47, bf16[64,2048]{1,0:T(8,128)(2,1)} %wq_ref.1, ...), custom_call_target="tpu_custom_call" | custom-call | flops 6442450944 | bytes 209715200 | tf_op jit(solution)/shard_map/start/pallas_call | solution.py:625
  108.4 0.2 reduce_window_sum.11
  108.6 0.3 copy.34
  108.8 0.4 copy.39
  109.2 0.8 reshape.184
  110.0 0.3 copy.35
  110.3 0.4 copy.38
  110.7 0.8 reshape.186
  111.7 0.6 maximum_subtract_fusion.low_ref
  112.3 1.5 pad_maximum_fusion.units_ref
  113.8 0.6 slice_bitcast_fusion
  114.4 61.1 %attend.1 = (bf16[2,1024,256]{2,1,0:T(8,128)(2,1)}, f32[2,4,1024]{2,1,0:T(4,128)}, bf16[2,2048,512]{2,1,0:T(8,128)(2,1)}, bf16[8,64,2048]{2,1,0:T(8,128)(2,1)}) custom-call(bf16[2,1024,256]{2,1,0:T(8,128)(2,1)} %get-tuple-element.45.q_ref, bf16[2,1024,512]{2,1,0:T(8,128)(2,1)} %get-tuple-element.46.kv_ref, s32[2,1,1024]{2,1,0:T(1,128)} %maximum_subtract_fusion.low_ref, ...), custom_call_target="tpu_custom_call" | custom-call | flops 5368709120 | bytes 157286400 | tf_op jit(solution)/shard_map/attend/pallas_call | solution.py:756
  175.5 109.2 %branch_sum.1 = (f32[256,2048]{1,0:T(8,128)}, bf16[256,2048]{1,0:T(8,128)(2,1)}, bf16[8,256,2048]{2,1,0:T(8,128)(2,1)}, bf16[4,512,2048]{2,1,0:T(8,128)(2,1)}) custom-call(bf16[2,1024,256]{2,1,0:T(8,128)(2,1)} %get-tuple-element.49.a_ref.att_ref, bf16[256,2048]{1,0:T(8,128)(2,1)} %all-gather.3.cloned.1.call-done.w_ref, bf16[256,2048]{1,0:T(8,128)(2,1)} %bitcast.45, ...), custom_call_target="tpu_custom_call" | custom-call | flops 2147483648 | bytes 262144000 | tf_op jit(solution)/shard_map/branch_sum/pallas_call | solution.py:829
  284.8 150.3 %feed_forward.1 = (f32[256,2048]{1,0:T(8,128)}, bf16[256,2048]{1,0:T(8,128)(2,1)}, f32[8,2048]{1,0:T(8,128)}, bf16[2048,1024]{1,0:T(8,128)(2,1)}, bf16[2048,2048]{1,0:T(8,128)(2,1)}) custom-call(bf16[256,2048]{1,0:T(8,128)(2,1)} %get-tuple-element.52.x_ref, bf16[2048,2048]{1,0:T(8,128)(2,1)} %bitcast.51, ...), custom_call_target="tpu_custom_call" | custom-call | flops 60129542144 | bytes 419430400 | tf_op jit(solution)/shard_map/feed_forward/pallas_call | solution.py:1180
  435.2 106.8 %branch_back.1 = (bf16[2,1024,256]{2,1,0:T(8,128)(2,1)}, bf16[256,2048]{1,0:T(8,128)(2,1)}, bf16[256,2048]{1,0:T(8,128)(2,1)}, bf16[4,512,2048]{2,1,0:T(8,128)(2,1)}, bf16[1024,2048]{1,0:T(8,128)(2,1)}) custom-call(bf16[256,2048]{1,0:T(8,128)(2,1)} %get-tuple-element.56.x_ref, bf16[256,2048]{1,0:T(8,128)(2,1)} %all-gather.3.cloned.1.call-done.w_ref, ...), custom_call_target="tpu_custom_call" | custom-call | flops 21474836480 | bytes 262144000 | tf_op jit(solution)/shard_map/branch_back/pallas_call | solution.py:1333
  541.9 171.4 %attention_back.1 = (f32[256,2048]{1,0:T(8,128)}, bf16[64,2048]{1,0:T(8,128)(2,1)}, bf16[64,2048]{1,0:T(8,128)(2,1)}, bf16[64,2048]{1,0:T(8,128)(2,1)}, f32[64,2...) custom-call(bf16[2,1024,256]{2,1,0:T(8,128)(2,1)} %get-tuple-element, ...), custom_call_target="tpu_custom_call" | custom-call | flops 26306674688 | bytes 419430400 | tf_op jit(solution)/shard_map/attention_back/pallas_call | solution.py:1707
  713.4 2.8 convert_element_type.34
  716.2 1.5 convert_element_type.35
  717.6 0.8 convert_element_type.31
  718.5 0.8 convert_element_type.32
  719.3 0.8 convert_element_type.33
  720.1 0.7 slice.17
  720.9 0.5 slice_bitcast_fusion.2
  721.4 1.0 select_reduce_fusion
  722.4 3.0 convert_add_fusion
  725.5 1.0 copy.43
  726.5 1.3 copy.44
  727.8 0.8 copy.45
  (41 shorter events, 0.5 us)
Async XLA Ops:
  7.2 168.3 %all-gather.3.cloned.1.call-start = ((), (), s32[]{:S(2)}) async-start(), calls=%async_computation | async-start | bytes 1310720 | tf_op jit(solution)/shard_map/all_gather | solution.py:1830
  7.9 276.9 %all-gather.5.cloned.1.call-start = ((), (), s32[]{:S(2)}) async-start(), calls=%async_computation.1 | async-start | bytes 5242880 | tf_op jit(solution)/shard_map/all_gather | solution.py:1828
  10.1 98.3 %copy-start.11 = (s32[2,4]{1,0:T(2,128)S(1)}, s32[2,4]{1,0:T(2,128)}, u32[]{:S(2)}) copy-start(s32[2,4]{1,0:T(2,128)} %param.14) | copy-start | bytes 100
  10.1 98.5 %copy-start.3 = (bf16[64,8192]{1,0:T(8,128)(2,1)S(1)}, bf16[64,8192]{1,0:T(8,128)(2,1)}, u32[]{:S(2)}) copy-start(bf16[64,8192]{1,0:T(8,128)(2,1)} %param.21) | copy-start | bytes 3145732
  108.5 1.4 copy-start.4
  110.0 1.5 copy-start.10
  713.3 2.8 copy-start.2
  713.4 4.3 copy-start.9
  713.4 5.1 copy-start.8
  716.2 3.1 copy-start.7
  716.2 5.2 copy-start
  722.4 3.1 copy-start.5
  722.4 4.0 copy-start.1
  725.5 2.3 copy-start.6
Sparse Core Ops, SparseCore 0:
  9.9 36.4 all-gather.2
  48.2 57.8 all-gather.4

commit v8 on v7

--- a/solution.py
+++ b/solution.py
@@ -12,6 +12,7 @@
 WINDOW = 1024
 PAIR = 128
 TILE = 512
+PARTS = 4
 LOW = -1e30
 EPS = 1e-05
 MESH = pl.DeviceIdType.MESH
@@ -106,39 +107,55 @@
 class Spread:
     def __init__(self, line, first, buf, send, recv):
         self.line, self.first, self.buf, self.send, self.recv = line, first, buf, send, recv
-
-    def move(self, slot, way, peer, source=None):
+        self.parts = recv.shape[1]
+        self.size = first.shape[0] // self.parts
+
+    def move(self, slot, part, way, peer, source=None):
+        here = rows_at(part, self.size)
         return pltpu.make_async_remote_copy(
-            src_ref=self.buf.at[slot] if source is None else source,
-            dst_ref=self.buf.at[slot],
-            send_sem=self.send.at[way, slot],
-            recv_sem=self.recv.at[slot],
+            src_ref=self.buf.at[slot, here] if source is None else source.at[here],
+            dst_ref=self.buf.at[slot, here],
+            send_sem=self.send.at[way, slot, part],
+            recv_sem=self.recv.at[slot, part],
             device_id={"fsdp": peer},
             device_id_type=MESH,
         )
 
     def begin(self):
         line = self.line
-        pl.when(line.has_right)(lambda: self.move(line.own, 1, line.own + 2, self.first).start())
-        pl.when(line.has_left)(lambda: self.move(line.own, 0, line.own - 2, self.first).start())
-        self.move(line.own, 2, line.other, self.first).start()
-
-    def relay(self, far):
+
+        @pl.loop(0, self.parts)
+        def _(part):
+            pl.when(line.has_right)(
+                lambda: self.move(line.own, part, 1, line.own + 2, self.first).start()
+            )
+            pl.when(line.has_left)(
+                lambda: self.move(line.own, part, 0, line.own - 2, self.first).start()
+            )
+            self.move(line.own, part, 2, line.other, self.first).start()
+
+    def relay_part(self, far, part):
         line = self.line
 
         @pl.when(line.chip - far >= 0)
         def _():
             slot = (line.chip - far) * 2 + line.core
-            self.move(slot, 1, line.own).wait_recv()
-            pl.when(line.has_right)(lambda: self.move(slot, 1, line.own + 2).start())
-            self.move(slot, 2, line.other).start()
+            self.move(slot, part, 1, line.own).wait_recv()
+            pl.when(line.has_right)(lambda: self.move(slot, part, 1, line.own + 2).start())
+            self.move(slot, part, 2, line.other).start()
 
         @pl.when(line.chip + far < line.chips)
         def _():
             slot = (line.chip + far) * 2 + line.core
-            self.move(slot, 0, line.own).wait_recv()
-            pl.when(line.has_left)(lambda: self.move(slot, 0, line.own - 2).start())
-            self.move(slot, 2, line.other).start()
+            self.move(slot, part, 0, line.own).wait_recv()
+            pl.when(line.has_left)(lambda: self.move(slot, part, 0, line.own - 2).start())
+            self.move(slot, part, 2, line.other).start()
+
+    def relay(self, far):
+        pl.loop(0, self.parts)(lambda part: self.relay_part(far, part))
+
+    def across(self, slot):
+        pl.loop(0, self.parts)(lambda part: self.move(slot, part, 2, self.line.own).wait_recv())
 
     def each(self, far, use):
         line = self.line
@@ -146,28 +163,20 @@
         @pl.loop(0, 4)
         def _(turn):
             side = lax.rem(turn, 2)
-            across = turn // 2
-            away = far - across
+            over = turn // 2
+            away = far - over
             source = line.chip + away * (2 * side - 1)
             valid = (away >= 0) & (away < line.chips) & (source >= 0) & (source < line.chips)
             valid = valid & ((side == 0) | (away > 0))
 
             @pl.when(valid)
             def _():
-                slot = source * 2 + line.core + across * (1 - 2 * line.core)
-                pl.when(across == 1)(lambda: self.move(slot, 2, line.own).wait_recv())
+                slot = source * 2 + line.core + over * (1 - 2 * line.core)
+                pl.when(over == 1)(lambda: self.across(slot))
                 use(slot)
 
-    def whole(self, use):
-        @pl.loop(0, self.line.chips + 1)
-        def _(far):
-            pl.when(far > 0)(lambda: self.relay(far))
-            self.each(far, use)
-
     def rest(self):
-        pl.loop(0, self.line.chips)(
-            lambda place: self.move(place * 2 + 1 - self.line.core, 2, self.line.own).wait_recv()
-        )
+        pl.loop(0, self.line.chips)(lambda place: self.across(place * 2 + 1 - self.line.core))
 
     def sent(self):
         line = self.line
@@ -175,13 +184,16 @@
         @pl.loop(0, line.chips)
         def _(place):
             slot = place * 2 + line.core
-            self.move(slot, 2, line.other).wait_send()
-            pl.when(line.has_right & (place <= line.chip))(
-                lambda: self.move(slot, 1, line.own + 2).wait_send()
-            )
-            pl.when(line.has_left & (place >= line.chip))(
-                lambda: self.move(slot, 0, line.own - 2).wait_send()
-            )
+
+            @pl.loop(0, self.parts)
+            def _(part):
+                self.move(slot, part, 2, line.other).wait_send()
+                pl.when(line.has_right & (place <= line.chip))(
+                    lambda: self.move(slot, part, 1, line.own + 2).wait_send()
+                )
+                pl.when(line.has_left & (place >= line.chip))(
+                    lambda: self.move(slot, part, 0, line.own - 2).wait_send()
+                )
 
 
 class Reduce:
@@ -196,7 +208,7 @@
         part = pltpu.VMEM((chips, rows, width), jnp.bfloat16)
         return [
             pltpu.VMEM((rows, TILE), jnp.float32),
-            pltpu.VMEM((rows, width), jnp.bfloat16),
+            pltpu.VMEM((2, rows, width), jnp.bfloat16),
             part,
             part,
             pltpu.VMEM((chips + 1, rows, width), jnp.bfloat16),
@@ -204,10 +216,10 @@
             pltpu.SemaphoreType.DMA((2, chips + 1, width // TILE)),
         ]
 
-    def cross(self, place, tile):
+    def cross(self, side, place, tile):
         here = rows_at(tile, TILE)
         return pltpu.make_async_remote_copy(
-            src_ref=self.cross_out.at[:, here],
+            src_ref=self.cross_out.at[side, :, here],
             dst_ref=self.cross_in.at[place, :, here],
             send_sem=self.send.at[0, place, tile],
             recv_sem=self.recv.at[0, place, tile],
@@ -226,66 +238,78 @@
             device_id_type=MESH,
         )
 
-    def steps(self):
-        return 2 * self.line.chips - 1
-
-    def step(self, step):
+    def where(self, away, side):
+        line = self.line
+        rightward = (line.chips - 1 - line.chip >= line.chip) == (side == 0)
+        place = line.chip + jnp.where(rightward, away, -away)
+        valid = (place >= 0) & (place < line.chips) & ((away > 0) | (side == 0))
+        return valid, place, rightward
+
+    def level(self, away, also):
+        @pl.loop(0, 2)
+        def _(side):
+            valid, place, _ = self.where(away, side)
+
+            @pl.when(valid)
+            def _():
+                @pl.loop(0, self.tiles)
+                def _(tile):
+                    got = self.product(place * 2 + 1 - self.line.core, tile)
+                    self.cross_out[side, :, rows_at(tile, TILE)] = to_half(got)
+                    self.cross(side, place, tile).start()
+
+        @pl.loop(0, self.tiles)
+        def _(tile):
+            @pl.loop(0, 2)
+            def _(side):
+                valid, place, rightward = self.where(away, side)
+                pl.when(valid)(lambda: self.close(away, side, place, rightward, tile))
+
+            also(tile)
+
+    def close(self, away, side, place, rightward, tile):
         line, acc = self.line, self.acc
-        away = line.chips - 1 - step // 2
-        rightward = lax.rem(step, 2) == 0
-        place = line.chip + jnp.where(rightward, away, -away)
+        here = rows_at(tile, TILE)
         upstream = (rightward & line.has_left) | (jnp.logical_not(rightward) & line.has_right)
-
-        @pl.when((place >= 0) & (place < line.chips))
+        acc[...] = self.product(place * 2 + line.core, tile)
+        self.cross(side, place, tile).wait()
+        acc[...] += self.cross_in[place, :, here].astype(jnp.float32)
+
+        @pl.when(away > 0)
         def _():
-            @pl.loop(0, self.tiles)
-            def _(tile):
-                got = self.product(place * 2 + 1 - line.core, tile)
-                self.cross_out[:, rows_at(tile, TILE)] = to_half(got)
-                self.cross(place, tile).start()
-
-            @pl.loop(0, self.tiles)
-            def _(tile):
-                here = rows_at(tile, TILE)
-                acc[...] = self.product(place * 2 + line.core, tile)
-                self.cross(place, tile).wait()
-                acc[...] += self.cross_in[place, :, here].astype(jnp.float32)
-
-                @pl.when(away > 0)
-                def _():
-                    @pl.when(upstream)
-                    def _():
-                        self.along(place, place, tile, line.own).wait_recv()
-                        self.line_out[place, :, here] = to_half(
-                            acc[...] + self.line_in[place, :, here].astype(jnp.float32)
-                        )
-
-                    @pl.when(jnp.logical_not(upstream))
-                    def _():
-                        self.line_out[place, :, here] = to_half(acc[...])
-
-                    @pl.when(rightward)
-                    def _():
-                        self.along(place, place, tile, line.own + 2).start()
-
-                    @pl.when(jnp.logical_not(rightward))
-                    def _():
-                        landing = jnp.where(away == 1, line.chips, place)
-                        self.along(place, landing, tile, line.own - 2).start()
-
-                @pl.when(away == 0)
-                def _():
-                    self.out[:, here] = acc[...]
-
-                    @pl.when(line.has_left)
-                    def _():
-                        self.along(place, place, tile, line.own).wait_recv()
-                        self.out[:, here] += self.line_in[place, :, here].astype(jnp.float32)
-
-                    @pl.when(line.has_right)
-                    def _():
-                        self.along(place, line.chips, tile, line.own).wait_recv()
-                        self.out[:, here] += self.line_in[line.chips, :, here].astype(jnp.float32)
+            @pl.when(upstream)
+            def _():
+                self.along(place, place, tile, line.own).wait_recv()
+                self.line_out[place, :, here] = to_half(
+                    acc[...] + self.line_in[place, :, here].astype(jnp.float32)
+                )
+
+            @pl.when(jnp.logical_not(upstream))
+            def _():
+                self.line_out[place, :, here] = to_half(acc[...])
+
+            @pl.when(rightward)
+            def _():
+                self.along(place, place, tile, line.own + 2).start()
+
+            @pl.when(jnp.logical_not(rightward))
+            def _():
+                landing = jnp.where(away == 1, line.chips, place)
+                self.along(place, landing, tile, line.own - 2).start()
+
+        @pl.when(away == 0)
+        def _():
+            self.out[:, here] = acc[...]
+
+            @pl.when(line.has_left)
+            def _():
+                self.along(place, place, tile, line.own).wait_recv()
+                self.out[:, here] += self.line_in[place, :, here].astype(jnp.float32)
+
+            @pl.when(line.has_right)
+            def _():
+                self.along(place, line.chips, tile, line.own).wait_recv()
+                self.out[:, here] += self.line_in[line.chips, :, here].astype(jnp.float32)
 
     def sent(self):
         @pl.loop(0, self.line.chips)
@@ -337,47 +361,87 @@
         self.seqs, self.source, self.target = seqs, source, target
         self.send, self.recv, self.keep = send, recv, keep
         self.own = lax.axis_index("seq")
+        self.half = source.shape[0] // 2
 
     def move(self, peer, place):
         return pltpu.make_async_remote_copy(
             src_ref=self.source,
             dst_ref=self.target.at[place],
-            send_sem=self.send.at[peer],
-            recv_sem=self.recv.at[place],
+            send_sem=self.send.at[peer, 0],
+            recv_sem=self.recv.at[place, 0],
             device_id={"seq": peer},
             device_id_type=MESH,
         )
 
+    def relay(self, peer, place, part):
+        here = pl.ds(part * self.half, self.half)
+        return pltpu.make_async_remote_copy(
+            src_ref=self.target.at[place, here],
+            dst_ref=self.target.at[place, here],
+            send_sem=self.send.at[peer, 1],
+            recv_sem=self.recv.at[place, part],
+            device_id={"seq": peer},
+            device_id_type=MESH,
+        )
+
+    def near(self):
+        one = self.own + 1 - 2 * lax.rem(self.own, 2)
+        two = lax.rem(self.own + 2, 4)
+        return one, two, lax.rem(one + 2, 4)
+
     def kept(self):
         return pltpu.make_async_copy(self.source, self.target.at[self.own], self.keep)
 
     def begin(self):
         self.kept().start()
-        pl.loop(1, self.seqs)(
-            lambda ahead: self.move(lax.rem(self.own + ahead, self.seqs), self.own).start()
-        )
+        if self.seqs == 4:
+            one, two, _ = self.near()
+            self.move(one, self.own).start()
+            self.move(two, self.own).start()
+        else:
+            pl.loop(1, self.seqs)(
+                lambda ahead: self.move(lax.rem(self.own + ahead, self.seqs), self.own).start()
+            )
+
+    def pass_on(self):
+        if self.seqs == 4:
+            one, two, _ = self.near()
+            self.move(one, one).wait_recv()
+            self.relay(two, one, 0).start()
+            self.move(two, two).wait_recv()
+            self.relay(one, two, 1).start()
 
     def end(self):
         self.kept().wait()
-
-        @pl.loop(1, self.seqs)
-        def _(ahead):
-            peer = lax.rem(self.own + ahead, self.seqs)
-            self.move(peer, peer).wait_recv()
-            self.move(peer, self.own).wait_send()
+        if self.seqs == 4:
+            one, two, far = self.near()
+            self.relay(two, far, 0).wait_recv()
+            self.relay(one, far, 1).wait_recv()
+            self.move(one, self.own).wait_send()
+            self.move(two, self.own).wait_send()
+            self.relay(two, one, 0).wait_send()
+            self.relay(one, two, 1).wait_send()
+        else:
+
+            @pl.loop(1, self.seqs)
+            def _(ahead):
+                peer = lax.rem(self.own + ahead, self.seqs)
+                self.move(peer, peer).wait_recv()
+                self.move(peer, self.own).wait_send()
 
 
 class ToSeq:
-    def __init__(self, seqs, source, target, send, recv, first=0, count=None):
+    def __init__(self, seqs, source, target, send, recv, first=0):
         self.seqs, self.source, self.target, self.send, self.recv = seqs, source, target, send, recv
         self.own = lax.axis_index("seq")
-        self.first, self.count = first, target.shape[1] if count is None else count
+        self.first = first
 
     def move(self, peer, place):
-        begin = pl.multiple_of(peer * self.target.shape[1] + self.first, 16)
+        run = self.source.shape[0] // self.seqs
+        begin = pl.multiple_of(peer * run + self.first, 16)
         return pltpu.make_async_remote_copy(
-            src_ref=self.source.at[pl.ds(begin, self.count)],
-            dst_ref=self.target.at[place, pl.ds(self.first, self.count)],
+            src_ref=self.source.at[pl.ds(begin, self.target.shape[1])],
+            dst_ref=self.target.at[place],
             send_sem=self.send.at[peer],
             recv_sem=self.recv.at[place],
             device_id={"seq": peer},
@@ -470,7 +534,9 @@
 
 
 def start_kernel(
-    seqs, chips, batches, tile_ref, x_ref, wq_ref, wk_ref, wv_ref, g_ref, q_ref, kv_ref, gains_ref, w_out_ref,
+    seqs, chips, batches, tile_ref, x_ref, wq_ref, wk_ref, wv_ref, gate_hbm, up_hbm,
+    g_ref, q_ref, kv_ref, gains_ref, w_out_ref, units_ref,
+    gate, up, units, unit_sem,
     blocks_ref, buf, normed, gain, gains, w, send, recv, keep, swap_send, share_send, w_recv,
     tile_send, tile_across, tile_recv, tile_back, w_keep, gain_keep,
 ):
@@ -483,6 +549,12 @@
     span = q_ref.shape[2]
     width = x_ref.shape[1]
     per = 128 * seqs * group // width
+    unit_loads = [
+        pltpu.make_async_copy(gate_hbm, gate, unit_sem.at[0]),
+        pltpu.make_async_copy(up_hbm, up, unit_sem.at[1]),
+    ]
+    for item in unit_loads:
+        item.start()
     for index, source in enumerate((wq_ref, wk_ref, wv_ref)):
         for member, first, home, size in column_parts(seqs, group, share, span):
             first = first + index * span
@@ -545,6 +617,17 @@
     buf[own] = x_ref[...]
     others(seqs, seq, lambda peer: tile_to_seq(peer, peer).wait_recv())
     others(group, own, lambda peer: tiles_to_group(peer, own).start())
+    for item in unit_loads:
+        item.wait()
+    cell = units.shape[2] // 2 // seqs
+    for member in range(group):
+        for run in range(seqs):
+            home = (run * group + member) * cell
+            for index, source in enumerate((gate, up)):
+                first = (index * seqs + run) * cell
+                units[member, :, first : first + cell] = source[:, home : home + cell]
+    units_kept = pltpu.make_async_copy(units, units_ref, unit_sem.at[2])
+    units_kept.start()
 
     def pass_block(member):
         block_swap(member, member).wait_recv()
@@ -607,6 +690,7 @@
     )
     w_kept.wait()
     gains_kept.wait()
+    units_kept.wait()
 
     @pl.loop(0, group)
     def _(slot):
@@ -614,13 +698,14 @@
             kept(slot, batch).wait()
 
 
-def start(seqs, chips, batches, tile, x, weights, collective):
+def start(seqs, chips, batches, tile, x, weights, unit_weights, collective):
     rows, width = x.shape
     group = 2 * chips
     length = group * rows // batches
     share = weights[0].shape[0]
     span = width // group
     cols = 3 * span
+    wide = unit_weights[0].shape[1]
     half = jnp.bfloat16
     return pl.pallas_call(
         functools.partial(start_kernel, seqs, chips, batches),
@@ -630,18 +715,23 @@
             jax.ShapeDtypeStruct((batches, length, 2 * span), half),
             jax.ShapeDtypeStruct((group, seqs, 8, 128), jnp.float32),
             jax.ShapeDtypeStruct((width, cols), half),
+            jax.ShapeDtypeStruct((group, share, 2 * wide // group), half),
         ],
-        in_specs=[VMEM_SPEC] * 5,
-        out_specs=[ANY_SPEC, VMEM_SPEC, VMEM_SPEC, ANY_SPEC, ANY_SPEC],
+        in_specs=[VMEM_SPEC] * 5 + [ANY_SPEC] * 2,
+        out_specs=[ANY_SPEC, VMEM_SPEC, VMEM_SPEC, ANY_SPEC, ANY_SPEC, ANY_SPEC],
         scratch_shapes=[
+            pltpu.VMEM((share, wide), half),
+            pltpu.VMEM((share, wide), half),
+            pltpu.VMEM((group, share, 2 * wide // group), half),
+            sems(3),
             pltpu.VMEM((group, share, cols), half),
             pltpu.VMEM((group, rows, width), half),
             pltpu.VMEM((group, rows, width), half),
             pltpu.VMEM((8, width), jnp.float32),
             pltpu.VMEM((group, seqs, 8, 128), jnp.float32),
             pltpu.VMEM((width, cols), half),
-            sems(3, group),
-            sems(group),
+            sems(3, group, PARTS),
+            sems(group, PARTS),
             sems(group, batches),
             sems(group),
             sems(seqs, group),
@@ -656,7 +746,7 @@
         compiler_params=comm_params(collective),
         cost_estimate=cost(2 * group * rows * width * cols, 200 * MIB, group * rows * width * 2),
         name="start",
-    )(tile, x, *weights)
+    )(tile, x, *weights, *unit_weights)
 
 
 def attend_kernel(
@@ -803,10 +893,13 @@
     spread.begin()
     d_kept.start()
 
-    @pl.loop(0, reduce.steps())
+    @pl.loop(0, chips)
     def _(step):
-        reduce.step(step)
-        pl.when(lax.rem(step, 2) == 1)(lambda: spread.relay((step + 1) // 2))
+        def also(tile):
+            pl.when(step < chips - 1)(lambda: spread.relay_part(step + 1, tile))
+
+        reduce.level(chips - 1 - step, also)
+        pl.when(step == chips - 2)(units.pass_on)
 
     @pl.loop(0, rows // 32)
     def _(chunk):
@@ -838,8 +931,8 @@
         out_specs=[VMEM_SPEC, VMEM_SPEC, ANY_SPEC, ANY_SPEC],
         scratch_shapes=[pltpu.VMEM((rows, width), jnp.float32)]
         + Reduce.scratch(chips, rows, width)
-        + [sems(3, group), sems(group), pltpu.SemaphoreType.DMA]
-        + [sems(seqs), sems(seqs), pltpu.SemaphoreType.DMA],
+        + [sems(3, group, PARTS), sems(group, PARTS), pltpu.SemaphoreType.DMA]
+        + [sems(seqs, 2), sems(seqs, 2), pltpu.SemaphoreType.DMA],
         compiler_params=comm_params(collective),
         cost_estimate=cost(
             2 * group * rows * width * w.shape[0], 250 * MIB, 3 * group * rows * width * 2
@@ -970,10 +1063,10 @@
 
 
 def feed_kernel(
-    chips, batches, x_ref, w_hbm, wd_hbm, gd_hbm, v_ref, cot_ref, gain_ref,
-    dm_ref, db_ref, gain_grad_ref, hidden_hbm, grad_hbm,
+    seqs, chips, batches, x_ref, w_hbm, wd_hbm, gd_hbm, v_ref, cot_ref, gain_ref,
+    dm_ref, db_ref, gain_grad_ref, hidden_hbm, grad_hbm, grad_in,
     buf, d_buf, h_buf, w_ref, wd_ref, d_ref, tiles, totals, acc, keep,
-    load, d_sem, h_sem, tile_sem, send, recv, *sums,
+    load, d_sem, h_sem, tile_sem, send, recv, part_send, part_recv, *sums,
 ):
     line = Line(chips)
     rows, width = x_ref.shape
@@ -988,7 +1081,7 @@
     ]
     for item in loads:
         item.start()
-    meet(line.greet())
+    meet(line.greet() + greet_seq(seqs))
     spreads = [
         Spread(
             line,
@@ -1042,7 +1135,7 @@
 
     def compute(batch, far):
         def act(place, side):
-            spreads[batch].move(place * 2 + 1 - line.core, 2, line.own).wait_recv()
+            spreads[batch].across(place * 2 + 1 - line.core)
             for item in fetch(batch, place, side):
                 item.wait()
 
@@ -1087,18 +1180,31 @@
         for batch in range(batches)
     ]
 
-    def grad_stored(tile):
-        slot = lax.rem(tile, 2)
+    count = width // block
+    seq = lax.axis_index("seq")
+
+    def tile_at(turn):
+        early = turn < seqs - 1
+        late = turn - (seqs - 1)
+        dest = lax.rem(seq + jnp.where(early, turn + 1, late), seqs)
+        return dest, dest * 2 + jnp.where(early | (late == 0), 0, 1)
+
+    def grad_stored(turn):
+        slot = lax.rem(turn, 2)
         return pltpu.make_async_copy(
-            tiles.at[slot], grad_hbm.at[rows_at(tile, block)], tile_sem.at[slot]
-        )
-
-    count = width // block
-
-    def weight_grad(tile):
-        pl.when(tile >= 2)(lambda: grad_stored(tile - 2).wait())
-        slot = lax.rem(tile, 2)
+            tiles.at[slot], grad_hbm.at[rows_at(tile_at(turn)[1], block)], tile_sem.at[slot]
+        )
+
+    parts = ToSeq(seqs, grad_hbm, grad_in, part_send, part_recv)
+
+    def leave(turn):
+        grad_stored(turn).wait()
+        pl.when(turn < seqs - 1)(lambda: parts.move(tile_at(turn)[0], seq).start())
+
+    def weight_grad(turn):
+        slot = lax.rem(turn, 2)
         size = min(TILE, 2 * units)
+        tile = tile_at(turn)[1]
 
         @pl.loop(0, 2 * units // size)
         def _(column):
@@ -1109,7 +1215,8 @@
                 got = got + contract_rows(left, d_ref[batch, :, here])
             tiles[slot, :, here] = to_half(got)
 
-        grad_stored(tile).start()
+        pl.when(turn > 0)(lambda: leave(turn - 1))
+        grad_stored(turn).start()
 
     def norm_batch(batch):
         own = pl.ds(batch * piece, piece)
@@ -1167,27 +1274,29 @@
         reduces[batch].sent()
     for item in stored(1, 0):
         item.wait()
-    grad_stored(count - 2).wait()
-    grad_stored(count - 1).wait()
-
-
-def feed_forward(chips, batches, x, w, wd, group_d, middle, cot, gain, collective):
+    leave(count - 1)
+    parts.end()
+
+
+def feed_forward(seqs, chips, batches, x, w, wd, group_d, middle, cot, gain, collective):
     rows, width = x.shape
     group = 2 * chips
     units = wd.shape[0]
     piece = rows // batches
+    block = width // seqs // 2
     half = jnp.bfloat16
     return pl.pallas_call(
-        functools.partial(feed_kernel, chips, batches),
+        functools.partial(feed_kernel, seqs, chips, batches),
         out_shape=[
             jax.ShapeDtypeStruct((rows, width), jnp.float32),
             jax.ShapeDtypeStruct((rows, width), half),
             jax.ShapeDtypeStruct((8, width), jnp.float32),
             jax.ShapeDtypeStruct((group * rows, units), half),
             jax.ShapeDtypeStruct((width, 2 * units), half),
+            jax.ShapeDtypeStruct((seqs, block, 2 * units), half),
         ],
         in_specs=[VMEM_SPEC] + [ANY_SPEC] * 3 + [VMEM_SPEC] * 3,
-        out_specs=[VMEM_SPEC] * 3 + [ANY_SPEC] * 2,
+        out_specs=[VMEM_SPEC] * 3 + [ANY_SPEC] * 3,
         scratch_shapes=[
             pltpu.VMEM((batches, group, piece, width), half),
             pltpu.VMEM((2, 2 * piece, width), half),
@@ -1195,7 +1304,7 @@
             pltpu.VMEM(w.shape, half),
             pltpu.VMEM(wd.shape, half),
             pltpu.VMEM((batches, group * piece, 2 * units), half),
-            pltpu.VMEM((2, 256, 2 * units), half),
+            pltpu.VMEM((2, block, 2 * units), half),
             pltpu.VMEM((batches, piece, width), jnp.float32),
             pltpu.VMEM((2 * piece, TILE), jnp.float32),
             pltpu.VMEM((piece, width), jnp.float32),
@@ -1203,8 +1312,10 @@
             sems(2, 2),
             sems(2),
             sems(2),
-            sems(batches, 3, group),
-            sems(batches, group),
+            sems(batches, 3, group, PARTS // 2),
+            sems(batches, group, PARTS // 2),
+            sems(seqs),
+            sems(seqs),
         ]
         + PairReduce.scratch(chips, piece, width) * batches,
         compiler_params=comm_params(collective, 63),
@@ -1217,9 +1328,9 @@
 
 def branch_back_kernel(
     seqs, chips, batches, x_ref, w_ref, att_ref, middle_ref, hidden_hbm, wd_hbm, units_hbm, gd_hbm,
-    d_ref, layer_ref, out_grad_ref, units_in, down_hbm,
+    d_ref, layer_ref, out_grad_ref, units_in, down_hbm, down_in,
     out_ref, buf, hidden_ref, wd_ref, grad_acc, rights, tiles, send, recv, load, right_sem, tile_sem,
-    part_send, part_recv, acc, cross_out, line_out, cross_in, line_in, sum_send, sum_recv,
+    part_send, part_recv, down_send, down_recv, down_keep, acc, cross_out, line_out, cross_in, line_in, sum_send, sum_recv,
 ):
     line = Line(chips)
     rows = x_ref.shape[0]
@@ -1266,7 +1377,12 @@
 
     right(0).start()
     meet(line.greet() + greet_seq(seqs))
-    sums = ToSeq(seqs, units_hbm, units_in, part_send, part_recv)
+    sums = ToSeq(seqs, units_hbm, units_in, part_send, part_recv, units_in.shape[1])
+    down = ToSeq(seqs, down_hbm, down_in, down_send, down_recv)
+    down_rows = down_in.shape[1]
+    down_kept = pltpu.make_async_copy(
+        down_hbm.at[rows_at(down.own, down_rows)], down_in.at[down.own], down_keep
+    )
     spread = Spread(line, x_ref, buf, send, recv)
     reduce = Reduce(
         line, product, out_ref, acc, cross_out, line_out, cross_in, line_in, sum_send, sum_recv
@@ -1290,24 +1406,30 @@
     for item in loads:
         item.wait()
 
-    per = -(-count // reduce.steps())
-
-    @pl.loop(0, reduce.steps())
+    per = -(-count // 2)
+
+    @pl.loop(0, chips)
     def _(step):
-        reduce.step(step)
-
-        @pl.when(lax.rem(step, 2) == 1)
+        def also(tile):
+            pl.when(step < chips - 1)(lambda: spread.relay_part(step + 1, tile))
+
+        reduce.level(chips - 1 - step, also)
+        spread.each(step, use)
+
+        @pl.when(step < 2)
         def _():
-            far = (step + 1) // 2
-            spread.relay(far)
-            spread.each(far - 1, use)
-
-        @pl.loop(0, per)
-        def _(turn):
-            tile = step * per + turn
-            pl.when(tile < count)(lambda: weight_grad(tile))
-
-    spread.each(chips - 1, use)
+            @pl.loop(0, per)
+            def _(turn):
+                tile = step * per + turn
+                pl.when(tile < count)(lambda: weight_grad(tile))
+
+        @pl.when(step == 1)
+        def _():
+            stored(count - 2).wait()
+            stored(count - 1).wait()
+            down.begin()
+            down_kept.start()
+
     spread.each(chips, use)
 
     @pl.loop(0, rows // 32)
@@ -1319,8 +1441,8 @@
     spread.sent()
     reduce.sent()
     sums.end()
-    stored(count - 2).wait()
-    stored(count - 1).wait()
+    down.end()
+    down_kept.wait()
 
 
 def branch_back(seqs, chips, batches, x, w, attended, middle, hidden, wd, unit_part, group_d, collective):
@@ -1336,11 +1458,12 @@
             jax.ShapeDtypeStruct((batches, length, span), half),
             jax.ShapeDtypeStruct((rows, width), half),
             jax.ShapeDtypeStruct((span, width), half),
-            jax.ShapeDtypeStruct((seqs, width // seqs, unit_part.shape[1]), half),
+            jax.ShapeDtypeStruct((seqs, width // seqs // 2, unit_part.shape[1]), half),
             jax.ShapeDtypeStruct((wd.shape[0], width), half),
+            jax.ShapeDtypeStruct((seqs, wd.shape[0] // seqs, width), half),
         ],
         in_specs=[VMEM_SPEC] * 4 + [ANY_SPEC] * 4,
-        out_specs=[VMEM_SPEC, VMEM_SPEC, VMEM_SPEC, ANY_SPEC, ANY_SPEC],
+        out_specs=[VMEM_SPEC, VMEM_SPEC, VMEM_SPEC, ANY_SPEC, ANY_SPEC, ANY_SPEC],
         scratch_shapes=[
             pltpu.VMEM((rows, width), jnp.float32),
             pltpu.VMEM((group, rows, width), half),
@@ -1349,13 +1472,16 @@
             pltpu.VMEM((span, width), jnp.float32),
             pltpu.VMEM((2, group * rows, part), half),
             pltpu.VMEM((2, wd.shape[0], part), half),
-            sems(3, group),
-            sems(group),
+            sems(3, group, PARTS),
+            sems(group, PARTS),
             sems(2),
             sems(2),
             sems(2),
             sems(seqs),
             sems(seqs),
+            sems(seqs),
+            sems(seqs),
+            pltpu.SemaphoreType.DMA,
         ]
         + Reduce.scratch(chips, rows, width),
         compiler_params=comm_params(collective, 62),
@@ -1369,13 +1495,13 @@
 
 
 def attention_back_kernel(
-    seqs, chips, block, q_ref, pad_ref, low_ref, lse_ref, d_ref, part_hbm, in_hbm,
-    w_ref, g_hbm, v_ref, dm_hbm, gain_ref, mlp_gain_ref, out_ref, down_hbm,
-    grad_ref, wq_ref, wk_ref, wv_ref, wo_ref, tile_ref, gate_ref, up_ref, down_in,
+    seqs, chips, block, q_ref, pad_ref, low_ref, lse_ref, d_ref, part_hbm, in_one, in_two,
+    w_ref, g_hbm, v_ref, dm_hbm, gain_ref, mlp_gain_ref, out_ref,
+    grad_ref, wq_ref, wk_ref, wv_ref, wo_ref, tile_ref, gate_ref, up_ref,
     dk, dv, kt, heads, back_out, back_in, unit_parts, unit_sums, units, lefts, parts, sums, cols, out_in,
     totals, gain_acc, gain_out, gain_in, gain_sum, gain_back, acc, keep,
     halo_send, halo_recv, unit_load, unit_send, unit_recv, unit_keep, dm_load, left_sem,
-    part_send, part_recv, cols_send, cols_recv, out_send, out_recv, down_send, down_recv,
+    part_send, part_recv, cols_send, cols_recv, out_send, out_recv,
     gain_send, gain_recv, back_send, back_recv, *line_sums,
 ):
     line = Line(chips)
@@ -1398,31 +1524,32 @@
     def others(count, me, act):
         pl.loop(1, count)(lambda ahead: act(lax.rem(me + ahead, count)))
 
-    def unit_loaded(turn, place, mine):
+    def unit_loaded(turn, place, source):
+        slot = lax.rem(turn, 2)
+        return pltpu.make_async_copy(source, unit_parts.at[slot, place], unit_load.at[slot, place])
+
+    def load_units(turn):
         member = lax.rem(own + turn, group)
-        slot = lax.rem(turn, 2)
-        if mine:
-            source = part_hbm.at[rows_at(seq * group + member, share)]
-        else:
-            source = in_hbm.at[place, rows_at(member, share)]
-        return pltpu.make_async_copy(source, unit_parts.at[slot, place], unit_load.at[slot, place])
-
-    def load_units(turn):
+        mine = part_hbm.at[rows_at(seq * group + member, share)]
         for place in range(seqs):
-            pl.when(place == seq)(lambda place=place: unit_loaded(turn, place, True).start())
-            pl.when(place != seq)(lambda place=place: unit_loaded(turn, place, False).start())
+
+            def fetch(source, place=place):
+                unit_loaded(turn, place, source).start()
+
+            pl.when(place == seq)(lambda: fetch(mine))
+
+            @pl.when((place != seq) & (member < chips))
+            def _(place=place):
+                fetch(in_one.at[place, rows_at(member, share)])
+
+            @pl.when((place != seq) & (member >= chips))
+            def _(place=place):
+                fetch(in_two.at[place, rows_at(member - chips, share)])
 
     load_units(1)
     dm_loaded = pltpu.make_async_copy(dm_hbm, grad_ref, dm_load)
     dm_loaded.start()
     meet(greet_group(group) + greet_seq(seqs))
-    size = down_in.shape[1]
-    cut = size // 16 * 3 // 8 * 16
-    downs = [
-        ToSeq(seqs, down_hbm, down_in, down_send.at[0], down_recv.at[0], 0, cut),
-        ToSeq(seqs, down_hbm, down_in, down_send.at[1], down_recv.at[1], cut, size - cut),
-    ]
-    downs[0].begin()
     swap = Swap(group, unit_sums, units, unit_send, unit_recv, unit_keep)
 
     @pl.loop(1, group + 1)
@@ -1431,7 +1558,7 @@
         slot = lax.rem(turn, 2)
         pl.when(turn < group)(lambda: load_units(turn + 1))
         for place in range(seqs):
-            unit_loaded(turn, place, False).wait()
+            unit_loaded(turn, place, part_hbm.at[rows_at(0, share)]).wait()
 
         @pl.loop(0, share // 16)
         def _(chunk):
@@ -1613,7 +1740,6 @@
         )
 
     others(seqs, seq, lambda peer: to_seq(peer, peer).wait_recv())
-    downs[1].begin()
 
     @pl.loop(0, run // 64)
     def _(chunk):
@@ -1672,8 +1798,6 @@
             first = first + index * span
             target[:, home : home + size] = cols[member, :, first : first + size]
     from_seq.sent()
-    for item in downs:
-        item.end()
     for batch in range(batches):
         reduces[batch].sent()
 
@@ -1688,8 +1812,8 @@
 
 
 def attention_back(
-    seqs, chips, block, query, kv_pad, low, lse, d_att, part_own, parts_in, w, group_a, x, d_middle,
-    gain, mlp_gain, out_part, down, collective,
+    seqs, chips, block, query, kv_pad, low, lse, d_att, part_own, parts_one, parts_two, w, group_a, x,
+    d_middle, gain, mlp_gain, out_part, collective,
 ):
     batches, length, span = query.shape
     padded = kv_pad.shape[1]
@@ -1715,14 +1839,12 @@
             jax.ShapeDtypeStruct((8, 128), wide),
             jax.ShapeDtypeStruct((share, cells // 2 * group), half),
             jax.ShapeDtypeStruct((share, cells // 2 * group), half),
-            jax.ShapeDtypeStruct((seqs, down.shape[0] // seqs, width), half),
         ],
         in_specs=[VMEM_SPEC] * 5
-        + [ANY_SPEC] * 2
+        + [ANY_SPEC] * 3
         + [VMEM_SPEC, ANY_SPEC, VMEM_SPEC, ANY_SPEC]
-        + [VMEM_SPEC] * 3
-        + [ANY_SPEC],
-        out_specs=[VMEM_SPEC] * 8 + [ANY_SPEC],
+        + [VMEM_SPEC] * 3,
+        out_specs=[VMEM_SPEC] * 8,
         scratch_shapes=[
             pltpu.VMEM((padded, span), wide),
             pltpu.VMEM((padded, span), wide),
@@ -1760,8 +1882,6 @@
             sems(group),
             sems(seqs),
             sems(seqs),
-            sems(2, seqs),
-            sems(2, seqs),
             sems(group),
             sems(group),
             sems(seqs),
@@ -1776,8 +1896,8 @@
         ),
         name="attention_back",
     )(
-        query, kv_pad, low, lse, d_att, part_own, parts_in, w, group_a, x, d_middle, gain, mlp_gain,
-        out_part, down,
+        query, kv_pad, low, lse, d_att, part_own, parts_one, parts_two, w, group_a, x, d_middle,
+        gain, mlp_gain, out_part,
     )
 
 
@@ -1819,10 +1939,6 @@
     aligned = share == HEAD
     member = lax.axis_index("fsdp")
 
-    def blocks(weight):
-        part = weight.shape[1] // devices
-        return weight.reshape(share, seqs, group, part).transpose(2, 0, 1, 3).reshape(group, share, -1)
-
     x_rows = tokens.reshape(rows, width)
     cot_rows = cotangent.reshape(rows, width)
     wd_part = lax.all_gather(w_down, "seq", axis=0, tiled=True)
@@ -1832,7 +1948,6 @@
         wo_all = lax.all_gather(w_out, ("seq", "fsdp"), axis=0, tiled=True)
         wo_part = lax.dynamic_slice_in_dim(wo_all, member * span, span, 0)
 
-    unit_blocks = jnp.concatenate([blocks(w_gate), blocks(w_up)], axis=2)
     lane = jnp.arange(128, dtype=jnp.int32)
     device = lax.axis_index("seq") * group + member
     fold = 128 // share
@@ -1840,8 +1955,8 @@
     both = jnp.stack([gain_attn, gain_mlp]).astype(jnp.float32)
     tile = jnp.where(here[None], jnp.tile(both, (1, fold)), 0.0)
     tile = jnp.pad(tile, ((0, 6), (0, 0)))[None]
-    group_a, query, key_value, gains, w_heads = start(
-        seqs, chips, batches, tile, x_rows, (w_query, w_key, w_value), 1
+    group_a, query, key_value, gains, w_heads, unit_blocks = start(
+        seqs, chips, batches, tile, x_rows, (w_query, w_key, w_value), (w_gate, w_up), 1
     )
     lengths, gains = lax.optimization_barrier((lengths, gains))
     group_start = lax.axis_index("seq") * length
@@ -1863,10 +1978,11 @@
         x_rows, gain_two[None], 3,
     )
     w_units = w_units.reshape(width, -1)
-    d_middle, d_branch, mlp_gain_part, hidden, unit_part = feed_forward(
-        chips, batches, normed_b, w_units, wd_part, group_d, middle, cot_rows, gain_two[None], 4
+    d_middle, d_branch, mlp_gain_part, hidden, unit_part, unit_one = feed_forward(
+        seqs, chips, batches, normed_b, w_units, wd_part, group_d, middle, cot_rows,
+        gain_two[None], 4,
     )
-    d_attended, layer_out, out_part, unit_in, down_part = branch_back(
+    d_attended, layer_out, out_part, unit_two, _, down_in = branch_back(
         seqs, chips, batches, d_branch, wo_part, attended, middle, hidden, wd_part, unit_part,
         group_d, 5,
     )
@@ -1876,16 +1992,11 @@
         )
         out_part = lax.psum(whole, "fsdp").reshape(seqs, group, share, width)
         out_part = lax.dynamic_slice_in_dim(out_part, member, 1, 1).reshape(seqs * share, width)
-    input_grad, wq_grad, wk_grad, wv_grad, wo_grad, gain_tile, gate_grad, up_grad, down_in = (
-        attention_back(
-            seqs, chips, block, query, kv_pad, low, lse, d_attended, unit_part, unit_in, w_heads,
-            group_a, x_rows, d_middle, gain_one[None], mlp_gain_part, out_part, down_part, 6,
-        )
+    input_grad, wq_grad, wk_grad, wv_grad, wo_grad, gain_tile, gate_grad, up_grad = attention_back(
+        seqs, chips, block, query, kv_pad, low, lse, d_attended, unit_part, unit_one, unit_two,
+        w_heads, group_a, x_rows, d_middle, gain_one[None], mlp_gain_part, out_part, 6,
     )
-    run = lax.axis_index("seq")
-    down_own = lax.dynamic_slice_in_dim(down_part, run * w_down.shape[0], w_down.shape[0], 0)
-    others = jnp.arange(seqs)[:, None, None] != run
-    down_sum = jnp.sum(jnp.where(others, down_in.astype(jnp.float32), 0.0), axis=0)
+    down_grad = jnp.sum(down_in.astype(jnp.float32), axis=0)
     gain_grads = lax.dynamic_slice_in_dim(gain_tile[:2], lax.rem(device, fold) * share, share, 1)
     wide = jnp.float32
     return (
@@ -1899,7 +2010,7 @@
         gain_grads[1],
         gate_grad.astype(wide),
         up_grad.astype(wide),
-        down_sum + down_own.astype(wide),
+        down_grad,
     )
 
 

time: 741 us -> 730 us (0.985)
  Pallas kernels: 697 us -> 683 us
    pallas_call x1, Pallas kernels: 171 us -> 146 us  [attention_back(): pl.pallas_call(functools.partial(attention_back_kernel, seqs, chips, bloc...]
    pallas_call x1, Pallas kernels: 107 us -> 126 us  [branch_back(): pl.pallas_call(functools.partial(branch_back_kernel, seqs, chips, batches...]
  transfers between devices with their start and end apart: 2 -> 2, of which waited for: 0 -> 0; matrix products, arithmetic and copies ran while one was open for 1% -> 1% of each run, Pallas kernels for 36% -> 37%
where the time goes in v8:
time: 730 us; the launch traced here: 719 us
  Pallas kernels  683 us (94%)
  between operations  14.6 us (2%)
  other arithmetic  13.4 us (2%)
    pallas_call x1, Pallas kernels, feed_forward(): pl.pallas_call(functools.partial(feed_kernel, seqs, chips, batches), out_...  147 us
    pallas_call x1, Pallas kernels, attention_back(): pl.pallas_call(functools.partial(attention_back_kernel, seqs, chips, bloc...  146 us
    pallas_call x1, Pallas kernels, branch_back(): pl.pallas_call(functools.partial(branch_back_kernel, seqs, chips, batches...  126 us
    pallas_call x1, Pallas kernels, branch_sum(): pl.pallas_call(functools.partial(branch_kernel, seqs, chips), out_shape=[...  105 us
    pallas_call x1, Pallas kernels, start(): pl.pallas_call(functools.partial(start_kernel, seqs, chips, batches), out...  98.4 us
    pallas_call x1, Pallas kernels, attend(): pl.pallas_call(functools.partial(attend_kernel, seqs, group, block), in_s...  60 us
  transfers between devices with their start and end apart: 2, of which 0 were waited for; matrix products, arithmetic and copies ran while one was open for 1% of the time, Pallas kernels for 37%

profile of v8, /device:TPU:9, one launch (start us, length us, event | category | flops | bytes accessed | tf_op | source)
XLA Modules:
  0.0 719.3 jit_solution(17363184581187208911)
XLA Ops:
  7.2 0.0 all-gather.3.cloned.1.call-start
  7.2 0.7 all-gather.3.cloned.1.call-update
  7.9 0.0 all-gather.5.cloned.1.call-start
  8.0 0.7 all-gather.5.cloned.1.call-update
  8.7 0.7 maximum_convert_fusion
  9.4 0.1 tile.10
  9.5 0.6 pad_bitcast_fusion.tile_ref
  10.1 98.4 %start.1 = (bf16[2,1024,2048]{2,1,0:T(8,128)(2,1)}, bf16[2,1024,256]{2,1,0:T(8,128)(2,1)}, bf16[2,1024,512]{2,1,0:T(8,128)(2,1)}, f32[8,4,8,128]{3,2,1,0:T(8,128...) custom-call(f32[1,8,128]{2,1,0:T(8,128)} %pad_bitcast_fusion.tile_ref, bf16[256,2048]{1,0:T(8,128)(2,1)} %bitcast.29, ...), custom_call_target="tpu_custom_call" | custom-call | flops 6442450944 | bytes 209715200 | tf_op jit(solution)/shard_map/start/pallas_call | solution.py:710
  108.5 0.9 copy.25
  109.4 0.2 reduce_window_sum.11
  109.6 0.1 select_reduce_fusion
  109.7 0.6 maximum_subtract_fusion.low_ref
  110.3 0.6 slice_bitcast_fusion
  111.0 60.0 %attend.1 = (bf16[2,1024,256]{2,1,0:T(8,128)(2,1)}, f32[2,4,1024]{2,1,0:T(4,128)}, bf16[2,2048,512]{2,1,0:T(8,128)(2,1)}, bf16[8,64,2048]{2,1,0:T(8,128)(2,1)}) custom-call(bf16[2,1024,256]{2,1,0:T(8,128)(2,1)} %get-tuple-element.46.q_ref, bf16[2,1024,512]{2,1,0:T(8,128)(2,1)} %get-tuple-element.47.kv_ref, s32[2,1,1024]{2,1,0:T(1,128)} %maximum_subtract_fusion.low_ref, ...), custom_call_target="tpu_custom_call" | custom-call | flops 5368709120 | bytes 157286400 | tf_op jit(solution)/shard_map/attend/pallas_call | solution.py:846
  171.0 0.0 all-gather.3.cloned.1.call-done.w_ref
  171.0 105.3 %branch_sum.1 = (f32[256,2048]{1,0:T(8,128)}, bf16[256,2048]{1,0:T(8,128)(2,1)}, bf16[8,256,2048]{2,1,0:T(8,128)(2,1)}, bf16[4,512,2048]{2,1,0:T(8,128)(2,1)}) custom-call(bf16[2,1024,256]{2,1,0:T(8,128)(2,1)} %get-tuple-element.51.a_ref.att_ref, bf16[256,2048]{1,0:T(8,128)(2,1)} %all-gather.3.cloned.1.call-done.w_ref, bf16[256,2048]{1,0:T(8,128)(2,1)} %bitcast.27, ...), custom_call_target="tpu_custom_call" | custom-call | flops 2147483648 | bytes 262144000 | tf_op jit(solution)/shard_map/branch_sum/pallas_call | solution.py:922
  276.4 0.0 all-gather.5.cloned.1.call-done.wd_hbm
  276.4 147.5 %feed_forward.1 = (f32[256,2048]{1,0:T(8,128)}, bf16[256,2048]{1,0:T(8,128)(2,1)}, f32[8,2048]{1,0:T(8,128)}, bf16[2048,1024]{1,0:T(8,128)(2,1)}, bf16[2048,2048...) custom-call(bf16[256,2048]{1,0:T(8,128)(2,1)} %get-tuple-element.54.x_ref, bf16[2048,2048]{1,0:T(8,128)(2,1)} %bitcast.33, ...), custom_call_target="tpu_custom_call" | custom-call | flops 60129542144 | bytes 419430400 | tf_op jit(solution)/shard_map/feed_forward/pallas_call | solution.py:1288
  423.9 125.6 %branch_back.1 = (bf16[2,1024,256]{2,1,0:T(8,128)(2,1)}, bf16[256,2048]{1,0:T(8,128)(2,1)}, bf16[256,2048]{1,0:T(8,128)(2,1)}, bf16[4,256,2048]{2,1,0:T(8,128)(2...) custom-call(bf16[256,2048]{1,0:T(8,128)(2,1)} %get-tuple-element.58.x_ref, ...), custom_call_target="tpu_custom_call" | custom-call | flops 21474836480 | bytes 262144000 | tf_op jit(solution)/shard_map/branch_back/pallas_call | solution.py:1455
  549.5 146.3 %attention_back.1 = (f32[256,2048]{1,0:T(8,128)}, bf16[64,2048]{1,0:T(8,128)(2,1)}, bf16[64,2048]{1,0:T(8,128)(2,1)}, bf16[64,2048]{1,0:T(8,128)(2,1)}, f32[64,2...) custom-call(bf16[2,1024,256]{2,1,0:T(8,128)(2,1)} %get-tuple-element.46.q_ref, ...), custom_call_target="tpu_custom_call" | custom-call | flops 26306674688 | bytes 419430400 | tf_op jit(solution)/shard_map/attention_back/pallas_call | solution.py:1831
  695.8 0.8 slice.17
  696.6 0.1 constant_dynamic-slice_fusion
  696.7 0.5 slice_bitcast_fusion.2
  697.2 1.9 convert_element_type.28
  699.1 1.8 convert_element_type.29
  700.9 1.8 convert_element_type.30
  702.7 2.7 convert_element_type.31
  705.3 1.5 convert_element_type.32
  706.8 2.1 convert_reduce_fusion
  708.9 1.0 copy.29
  709.9 1.3 copy.30
  711.2 0.8 copy.31
  (20 shorter events, 0.1 us)
Async XLA Ops:
  7.2 163.9 %all-gather.3.cloned.1.call-start = ((), (), s32[]{:S(2)}) async-start(), calls=%async_computation | async-start | bytes 1310720 | tf_op jit(solution)/shard_map/all_gather | solution.py:1946
  7.9 268.5 %all-gather.5.cloned.1.call-start = ((), (), s32[]{:S(2)}) async-start(), calls=%async_computation.1 | async-start | bytes 5242880 | tf_op jit(solution)/shard_map/all_gather | solution.py:1944
  10.1 99.3 %copy-start.5 = (s32[2,4]{1,0:T(2,128)S(1)}, s32[2,4]{1,0:T(2,128)}, u32[]{:S(2)}) copy-start(s32[2,4]{1,0:T(2,128)} %param.14) | copy-start | bytes 100
  695.8 9.5 %copy-start.2 = (bf16[64,8192]{1,0:T(8,128)(2,1)S(1)}, bf16[64,8192]{1,0:T(8,128)(2,1)}, u32[]{:S(2)}) copy-start(bf16[64,8192]{1,0:T(8,128)(2,1)} %get-tuple-element.79) | copy-start | bytes 3145732
  697.2 9.6 %copy-start = (bf16[4,256,2048]{2,1,0:T(8,128)(2,1)S(1)}, bf16[4,256,2048]{2,1,0:T(8,128)(2,1)}, u32[]{:S(2)}) copy-start(bf16[4,256,2048]{2,1,0:T(8,128)(2,1)} %get-tuple-element.80) | copy-start | bytes 12582916
  705.3 3.6 copy-start.3
  706.8 3.1 copy-start.1
  708.9 2.3 copy-start.4
Sparse Core Ops, SparseCore 0:
  9.9 36.3 all-gather.2
  48.1 57.9 all-gather.4

commit v9 on v8

--- a/solution.py
+++ b/solution.py
@@ -1001,13 +1001,16 @@
 
         @pl.when((place >= 0) & (place < line.chips))
         def _():
-            @pl.loop(0, self.tiles)
+            wide = self.acc.shape[1]
+
+            @pl.loop(0, keep.shape[1] // wide)
             def _(tile):
-                here = rows_at(tile, TILE)
-                self.acc[...] = self.product(place, tile)
+                here = rows_at(tile, wide)
+                self.acc[...] = self.product(place, here)
                 self.cross_out[:, here] = to_half(self.acc[rows_at(1 - line.core, piece), :])
                 keep[:, here] = self.acc[rows_at(line.core, piece), :]
-                self.cross(parity, tile).start()
+                for piece_of in range(wide // TILE):
+                    self.cross(parity, tile * (wide // TILE) + piece_of).start()
 
             @pl.loop(0, self.tiles)
             def _(tile):
@@ -1064,16 +1067,17 @@
 
 def feed_kernel(
     seqs, chips, batches, x_ref, w_hbm, wd_hbm, gd_hbm, v_ref, cot_ref, gain_ref,
-    dm_ref, db_ref, gain_grad_ref, hidden_hbm, grad_hbm, grad_in,
+    dm_ref, db_ref, gain_grad_ref, hidden_hbm, grad_hbm, grad_in, branch_hbm,
     buf, d_buf, h_buf, w_ref, wd_ref, d_ref, tiles, totals, acc, keep,
-    load, d_sem, h_sem, tile_sem, send, recv, part_send, part_recv, *sums,
+    load, d_sem, h_sem, tile_sem, send, recv, part_send, part_recv,
+    branch_send, branch_recv, branch_keep, *sums,
 ):
     line = Line(chips)
     rows, width = x_ref.shape
     piece = rows // batches
     pair = 2 * piece
     units = wd_ref.shape[0]
-    part = min(units, TILE)
+    part = min(units, 2 * TILE)
     block = tiles.shape[1]
     loads = [
         pltpu.make_async_copy(w_hbm, w_ref, load.at[0]),
@@ -1170,8 +1174,8 @@
         sides(far, act)
 
     def product(batch):
-        def get(place, tile):
-            return dot_nt(d_ref[batch, rows_at(place, pair), :], w_ref[rows_at(tile, TILE), :])
+        def get(place, here):
+            return dot_nt(d_ref[batch, rows_at(place, pair), :], w_ref[here, :])
 
         return get
 
@@ -1203,7 +1207,7 @@
 
     def weight_grad(turn):
         slot = lax.rem(turn, 2)
-        size = min(TILE, 2 * units)
+        size = min(4 * TILE, 2 * units)
         tile = tile_at(turn)[1]
 
         @pl.loop(0, 2 * units // size)
@@ -1257,16 +1261,23 @@
 
     reduces[0].step(last)
     norm_batch(0)
+    first = db_ref.at[pl.ds(0, piece)]
+    branch = Spread(line, first, branch_hbm, branch_send, branch_recv)
+    branch_kept = pltpu.make_async_copy(first, branch_hbm.at[line.own], branch_keep)
+    branch.begin()
+    branch_kept.start()
 
     @pl.loop(2, last)
     def _(step):
         reduces[1].step(step)
         pl.when(step < count)(lambda: weight_grad(step))
+        pl.when(lax.rem(step, 2) == 1)(lambda: branch.relay((step - 1) // 2))
 
     @pl.loop(last, max(count, last))
     def _(tile):
         weight_grad(tile)
 
+    branch.relay(chips - 1)
     reduces[1].step(last)
     norm_batch(1)
     for batch in range(batches):
@@ -1276,6 +1287,9 @@
         item.wait()
     leave(count - 1)
     parts.end()
+    branch.rest()
+    branch.sent()
+    branch_kept.wait()
 
 
 def feed_forward(seqs, chips, batches, x, w, wd, group_d, middle, cot, gain, collective):
@@ -1294,9 +1308,10 @@
             jax.ShapeDtypeStruct((group * rows, units), half),
             jax.ShapeDtypeStruct((width, 2 * units), half),
             jax.ShapeDtypeStruct((seqs, block, 2 * units), half),
+            jax.ShapeDtypeStruct((group, piece, width), half),
         ],
         in_specs=[VMEM_SPEC] + [ANY_SPEC] * 3 + [VMEM_SPEC] * 3,
-        out_specs=[VMEM_SPEC] * 3 + [ANY_SPEC] * 3,
+        out_specs=[VMEM_SPEC] * 3 + [ANY_SPEC] * 4,
         scratch_shapes=[
             pltpu.VMEM((batches, group, piece, width), half),
             pltpu.VMEM((2, 2 * piece, width), half),
@@ -1306,7 +1321,7 @@
             pltpu.VMEM((batches, group * piece, 2 * units), half),
             pltpu.VMEM((2, block, 2 * units), half),
             pltpu.VMEM((batches, piece, width), jnp.float32),
-            pltpu.VMEM((2 * piece, TILE), jnp.float32),
+            pltpu.VMEM((2 * piece, 2 * TILE), jnp.float32),
             pltpu.VMEM((piece, width), jnp.float32),
             sems(2),
             sems(2, 2),
@@ -1316,6 +1331,9 @@
             sems(batches, group, PARTS // 2),
             sems(seqs),
             sems(seqs),
+            sems(3, group, PARTS // 2),
+            sems(group, PARTS // 2),
+            pltpu.SemaphoreType.DMA,
         ]
         + PairReduce.scratch(chips, piece, width) * batches,
         compiler_params=comm_params(collective, 63),
@@ -1327,9 +1345,9 @@
 
 
 def branch_back_kernel(
-    seqs, chips, batches, x_ref, w_ref, att_ref, middle_ref, hidden_hbm, wd_hbm, units_hbm, gd_hbm,
+    seqs, chips, batches, x_ref, b_hbm, w_ref, att_ref, middle_ref, hidden_hbm, wd_hbm, units_hbm, gd_hbm,
     d_ref, layer_ref, out_grad_ref, units_in, down_hbm, down_in,
-    out_ref, buf, hidden_ref, wd_ref, grad_acc, rights, tiles, send, recv, load, right_sem, tile_sem,
+    out_ref, early, buf, hidden_ref, wd_ref, grad_acc, rights, tiles, send, recv, load, right_sem, tile_sem,
     part_send, part_recv, down_send, down_recv, down_keep, acc, cross_out, line_out, cross_in, line_in, sum_send, sum_recv,
 ):
     line = Line(chips)
@@ -1339,6 +1357,7 @@
     loads = [
         pltpu.make_async_copy(hidden_hbm, hidden_ref, load.at[0]),
         pltpu.make_async_copy(wd_hbm, wd_ref, load.at[1]),
+        pltpu.make_async_copy(b_hbm, early, load.at[2]),
     ]
     for item in loads:
         item.start()
@@ -1383,17 +1402,19 @@
     down_kept = pltpu.make_async_copy(
         down_hbm.at[rows_at(down.own, down_rows)], down_in.at[down.own], down_keep
     )
-    spread = Spread(line, x_ref, buf, send, recv)
+    late = x_ref.at[pl.ds(piece, piece)]
+    spread = Spread(line, late, buf, send, recv)
     reduce = Reduce(
         line, product, out_ref, acc, cross_out, line_out, cross_in, line_in, sum_send, sum_recv
     )
     spread.begin()
     sums.begin()
-    buf[line.own] = x_ref[...]
+    buf[line.own] = late[...]
     grad_acc[...] = jnp.zeros_like(grad_acc)
 
     def use(slot):
-        got = to_half(dot_nt(buf[slot], w_ref[...]))
+        both = jnp.concatenate([early[slot], buf[slot]], axis=0)
+        got = to_half(dot_nt(both, w_ref[...]))
         for batch in range(batches):
             d_ref[batch, rows_at(slot, piece), :] = got[batch * piece : (batch + 1) * piece]
         mixed = left_rows(att_ref, slot, rows)
@@ -1401,34 +1422,30 @@
         @pl.loop(0, width // TILE)
         def _(tile):
             here = rows_at(tile, TILE)
-            grad_acc[:, here] += contract_rows(mixed, buf[slot, :, here])
+            right = jnp.concatenate([early[slot, :, here], buf[slot, :, here]], axis=0)
+            grad_acc[:, here] += contract_rows(mixed, right)
 
     for item in loads:
         item.wait()
 
-    per = -(-count // 2)
-
-    @pl.loop(0, chips)
+    reduce.level(chips - 1, lambda tile: None)
+    pl.loop(0, count)(weight_grad)
+    stored(count - 2).wait()
+    stored(count - 1).wait()
+    down.begin()
+    down_kept.start()
+    spread.relay(1)
+    spread.each(0, use)
+
+    @pl.loop(1, chips)
     def _(step):
         def also(tile):
-            pl.when(step < chips - 1)(lambda: spread.relay_part(step + 1, tile))
+            pl.when((step < chips - 1) & (tile < spread.parts))(
+                lambda: spread.relay_part(step + 1, tile)
+            )
 
         reduce.level(chips - 1 - step, also)
         spread.each(step, use)
-
-        @pl.when(step < 2)
-        def _():
-            @pl.loop(0, per)
-            def _(turn):
-                tile = step * per + turn
-                pl.when(tile < count)(lambda: weight_grad(tile))
-
-        @pl.when(step == 1)
-        def _():
-            stored(count - 2).wait()
-            stored(count - 1).wait()
-            down.begin()
-            down_kept.start()
 
     spread.each(chips, use)
 
@@ -1445,7 +1462,7 @@
     down_kept.wait()
 
 
-def branch_back(seqs, chips, batches, x, w, attended, middle, hidden, wd, unit_part, group_d, collective):
+def branch_back(seqs, chips, batches, x, early, w, attended, middle, hidden, wd, unit_part, group_d, collective):
     rows, width = x.shape
     group = 2 * chips
     length = group * rows // batches
@@ -1462,19 +1479,20 @@
             jax.ShapeDtypeStruct((wd.shape[0], width), half),
             jax.ShapeDtypeStruct((seqs, wd.shape[0] // seqs, width), half),
         ],
-        in_specs=[VMEM_SPEC] * 4 + [ANY_SPEC] * 4,
+        in_specs=[VMEM_SPEC, ANY_SPEC] + [VMEM_SPEC] * 3 + [ANY_SPEC] * 4,
         out_specs=[VMEM_SPEC, VMEM_SPEC, VMEM_SPEC, ANY_SPEC, ANY_SPEC, ANY_SPEC],
         scratch_shapes=[
             pltpu.VMEM((rows, width), jnp.float32),
-            pltpu.VMEM((group, rows, width), half),
+            pltpu.VMEM((group, rows // batches, width), half),
+            pltpu.VMEM((group, rows // batches, width), half),
             pltpu.VMEM(hidden.shape, half),
             pltpu.VMEM(wd.shape, half),
             pltpu.VMEM((span, width), jnp.float32),
             pltpu.VMEM((2, group * rows, part), half),
             pltpu.VMEM((2, wd.shape[0], part), half),
-            sems(3, group, PARTS),
-            sems(group, PARTS),
-            sems(2),
+            sems(3, group, PARTS // 2),
+            sems(group, PARTS // 2),
+            sems(3),
             sems(2),
             sems(2),
             sems(seqs),
@@ -1491,7 +1509,7 @@
             2 * group * rows * width * 2,
         ),
         name="branch_back",
-    )(x, w, attended, middle, hidden, wd, unit_part, group_d.reshape(group * rows, width))
+    )(x, early, w, attended, middle, hidden, wd, unit_part, group_d.reshape(group * rows, width))
 
 
 def attention_back_kernel(
@@ -1636,8 +1654,8 @@
                 heads[batch, there, span:] = to_half(mine + got)
 
     def product(batch):
-        def get(place, tile):
-            return dot_nt(heads[batch, rows_at(place, pair_rows), :], w_ref[rows_at(tile, TILE), :])
+        def get(place, here):
+            return dot_nt(heads[batch, rows_at(place, pair_rows), :], w_ref[here, :])
 
         return get
 
@@ -1901,6 +1919,37 @@
     )
 
 
+def finish_kernel(*refs):
+    half = len(refs) // 2
+    for source, target in zip(refs[:half], refs[half:]):
+        if len(source.shape) == len(target.shape):
+            target[...] = source[...].astype(target.dtype)
+        else:
+            target[...] = jnp.sum(source[...].astype(jnp.float32), axis=0)
+
+
+def finish(steps, arrays, kinds):
+    in_specs, out_specs, out_shape = [], [], []
+    for item, kind in zip(arrays, kinds):
+        rows, width = item.shape[-2:]
+        block = (rows // steps, width)
+        out_specs.append(pl.BlockSpec(block, lambda i: (i, 0)))
+        out_shape.append(jax.ShapeDtypeStruct((rows, width), kind))
+        if item.ndim == 3:
+            in_specs.append(pl.BlockSpec((item.shape[0],) + block, lambda i: (0, i, 0)))
+        else:
+            in_specs.append(out_specs[-1])
+    return pl.pallas_call(
+        finish_kernel,
+        grid=(steps,),
+        in_specs=in_specs,
+        out_specs=out_specs,
+        out_shape=out_shape,
+        compiler_params=pltpu.CompilerParams(vmem_limit_bytes=48 * MIB),
+        name="finish",
+    )(*arrays)
+
+
 def doc_starts(lengths, positions, batches, seq_len):
     table = lengths.reshape(batches, -1, lengths.shape[1])
     starts = jnp.cumsum(table, axis=2) - table
@@ -1978,12 +2027,12 @@
         x_rows, gain_two[None], 3,
     )
     w_units = w_units.reshape(width, -1)
-    d_middle, d_branch, mlp_gain_part, hidden, unit_part, unit_one = feed_forward(
+    d_middle, d_branch, mlp_gain_part, hidden, unit_part, unit_one, early = feed_forward(
         seqs, chips, batches, normed_b, w_units, wd_part, group_d, middle, cot_rows,
         gain_two[None], 4,
     )
     d_attended, layer_out, out_part, unit_two, _, down_in = branch_back(
-        seqs, chips, batches, d_branch, wo_part, attended, middle, hidden, wd_part, unit_part,
+        seqs, chips, batches, d_branch, early, wo_part, attended, middle, hidden, wd_part, unit_part,
         group_d, 5,
     )
     if not aligned:
@@ -1996,20 +2045,24 @@
         seqs, chips, block, query, kv_pad, low, lse, d_attended, unit_part, unit_one, unit_two,
         w_heads, group_a, x_rows, d_middle, gain_one[None], mlp_gain_part, out_part, 6,
     )
-    down_grad = jnp.sum(down_in.astype(jnp.float32), axis=0)
     gain_grads = lax.dynamic_slice_in_dim(gain_tile[:2], lax.rem(device, fold) * share, share, 1)
     wide = jnp.float32
+    (layer_out, input_grad, wq_grad, wk_grad, wv_grad, wo_grad, gate_grad, up_grad, down_grad) = finish(
+        share // 16,
+        [layer_out, input_grad, wq_grad, wk_grad, wv_grad, wo_grad, gate_grad, up_grad, down_in],
+        [jnp.bfloat16] + [wide] * 8,
+    )
     return (
         layer_out.reshape(batches, piece, width),
         input_grad.reshape(batches, piece, width),
         gain_grads[0],
-        wq_grad.astype(wide),
-        wk_grad.astype(wide),
-        wv_grad.astype(wide),
+        wq_grad,
+        wk_grad,
+        wv_grad,
         wo_grad,
         gain_grads[1],
-        gate_grad.astype(wide),
-        up_grad.astype(wide),
+        gate_grad,
+        up_grad,
         down_grad,
     )
 

time: 730 us -> 724 us (level)
  other arithmetic: 13.4 us -> 1.63 us
    pallas_call x1, Pallas kernels: 126 us -> 107 us  [branch_back(): pl.pallas_call(functools.partial(branch_back_kernel, seqs, chips, batches...]
    pallas_call x1, Pallas kernels: 147 us -> 158 us  [feed_forward(): pl.pallas_call(functools.partial(feed_kernel, seqs, chips, batches), out_...]
    convert_element_type x5 -> x0, other arithmetic: 9.62 us -> none  [the longest x1 2.68 us: body(): gate_grad.astype(wide)]
    pallas_call x0 -> x1, Pallas kernels: none -> 7.46 us  [finish(): pl.pallas_call(finish_kernel, grid=(steps,), in_specs=in_specs, out_specs...]
where the time goes in v9:
time: 724 us; the launch traced here: 712 us
  Pallas kernels  683 us (94%)
  between operations  14.6 us (2%)
  local copies, waits for them, and re-layouts  11 us (2%)
    pallas_call x1, Pallas kernels, feed_forward(): pl.pallas_call(functools.partial(feed_kernel, seqs, chips, batches), out_...  158 us
    pallas_call x1, Pallas kernels, attention_back(): pl.pallas_call(functools.partial(attention_back_kernel, seqs, chips, bloc...  147 us
    pallas_call x1, Pallas kernels, branch_back(): pl.pallas_call(functools.partial(branch_back_kernel, seqs, chips, batches...  107 us
    pallas_call x1, Pallas kernels, branch_sum(): pl.pallas_call(functools.partial(branch_kernel, seqs, chips), out_shape=[...  106 us
    pallas_call x1, Pallas kernels, start(): pl.pallas_call(functools.partial(start_kernel, seqs, chips, batches), out...  98.4 us
    pallas_call x1, Pallas kernels, attend(): pl.pallas_call(functools.partial(attend_kernel, seqs, group, block), in_s...  60.1 us
  transfers between devices with their start and end apart: 2, of which 0 were waited for; matrix products, arithmetic and copies ran while one was open for 1% of the time, Pallas kernels for 37%

profile of v9, /device:TPU:9, one launch (start us, length us, event | category | flops | bytes accessed | tf_op | source)
XLA Modules:
  0.0 712.2 jit_solution(419227072564074214)
XLA Ops:
  7.2 0.0 all-gather.3.cloned.1.call-start
  7.2 0.7 all-gather.3.cloned.1.call-update
  7.9 0.0 all-gather.5.cloned.1.call-start
  8.0 0.7 all-gather.5.cloned.1.call-update
  8.7 0.7 maximum_convert_fusion
  9.4 0.1 tile.10
  9.5 0.6 pad_bitcast_fusion.tile_ref
  10.1 98.4 %start.1 = (bf16[2,1024,2048]{2,1,0:T(8,128)(2,1)}, bf16[2,1024,256]{2,1,0:T(8,128)(2,1)}, bf16[2,1024,512]{2,1,0:T(8,128)(2,1)}, f32[8,4,8,128]{3,2,1,0:T(8,128...) custom-call(f32[1,8,128]{2,1,0:T(8,128)} %pad_bitcast_fusion.tile_ref, bf16[256,2048]{1,0:T(8,128)(2,1)} %bitcast.28, ...), custom_call_target="tpu_custom_call" | custom-call | flops 6442450944 | bytes 209715200 | tf_op jit(solution)/shard_map/start/pallas_call | solution.py:710
  108.5 0.9 copy.25
  109.4 0.0 copy-done.7
  109.4 0.2 reduce_window_sum.11
  109.6 0.1 select_reduce_fusion
  109.8 0.6 maximum_subtract_fusion.low_ref
  110.4 0.6 slice_bitcast_fusion
  111.0 60.1 %attend.1 = (bf16[2,1024,256]{2,1,0:T(8,128)(2,1)}, f32[2,4,1024]{2,1,0:T(4,128)}, bf16[2,2048,512]{2,1,0:T(8,128)(2,1)}, bf16[8,64,2048]{2,1,0:T(8,128)(2,1)}) custom-call(bf16[2,1024,256]{2,1,0:T(8,128)(2,1)} %get-tuple-element.56.q_ref, bf16[2,1024,512]{2,1,0:T(8,128)(2,1)} %get-tuple-element.57.kv_ref, s32[2,1,1024]{2,1,0:T(1,128)} %maximum_subtract_fusion.low_ref, ...), custom_call_target="tpu_custom_call" | custom-call | flops 5368709120 | bytes 157286400 | tf_op jit(solution)/shard_map/attend/pallas_call | solution.py:846
  171.1 0.0 all-gather.3.cloned.1.call-done.w_ref
  171.1 105.6 %branch_sum.1 = (f32[256,2048]{1,0:T(8,128)}, bf16[256,2048]{1,0:T(8,128)(2,1)}, bf16[8,256,2048]{2,1,0:T(8,128)(2,1)}, bf16[4,512,2048]{2,1,0:T(8,128)(2,1)}) custom-call(bf16[2,1024,256]{2,1,0:T(8,128)(2,1)} %get-tuple-element.61.a_ref.att_ref, bf16[256,2048]{1,0:T(8,128)(2,1)} %all-gather.3.cloned.1.call-done.w_ref, bf16[256,2048]{1,0:T(8,128)(2,1)} %bitcast.26, ...), custom_call_target="tpu_custom_call" | custom-call | flops 2147483648 | bytes 262144000 | tf_op jit(solution)/shard_map/branch_sum/pallas_call | solution.py:922
  276.7 0.0 all-gather.5.cloned.1.call-done.wd_hbm
  276.8 157.8 %feed_forward.1 = (f32[256,2048]{1,0:T(8,128)}, bf16[256,2048]{1,0:T(8,128)(2,1)}, f32[8,2048]{1,0:T(8,128)}, bf16[2048,1024]{1,0:T(8,128)(2,1)}, bf16[2048,2048...) custom-call(bf16[256,2048]{1,0:T(8,128)(2,1)} %get-tuple-element.64.x_ref, ...), custom_call_target="tpu_custom_call" | custom-call | flops 60129542144 | bytes 419430400 | tf_op jit(solution)/shard_map/feed_forward/pallas_call | solution.py:1302
  434.6 107.3 %branch_back.1 = (bf16[2,1024,256]{2,1,0:T(8,128)(2,1)}, bf16[256,2048]{1,0:T(8,128)(2,1)}, bf16[256,2048]{1,0:T(8,128)(2,1)}, bf16[4,256,2048]{2,1,0:T(8,128)(2...) custom-call(bf16[256,2048]{1,0:T(8,128)(2,1)} %get-tuple-element.68.x_ref, ...), custom_call_target="tpu_custom_call" | custom-call | flops 21474836480 | bytes 262144000 | tf_op jit(solution)/shard_map/branch_back/pallas_call | solution.py:1472
  541.9 146.7 %attention_back.1 = (f32[256,2048]{1,0:T(8,128)}, bf16[64,2048]{1,0:T(8,128)(2,1)}, bf16[64,2048]{1,0:T(8,128)(2,1)}, bf16[64,2048]{1,0:T(8,128)(2,1)}, f32[64,2...) custom-call(bf16[2,1024,256]{2,1,0:T(8,128)(2,1)} %get-tuple-element.56.q_ref, ...), custom_call_target="tpu_custom_call" | custom-call | flops 26306674688 | bytes 419430400 | tf_op jit(solution)/shard_map/attention_back/pallas_call | solution.py:1849
  688.6 0.7 slice.17
  689.3 0.1 constant_dynamic-slice_fusion
  689.4 0.5 slice_bitcast_fusion.2
  689.9 1.2 copy-done
  691.1 1.2 copy-done.1
  692.3 1.2 copy-done.2
  693.6 1.0 copy-done.3
  694.6 0.9 copy-done.4
  695.5 0.9 copy-done.5
  696.5 0.9 copy-done.6
  697.4 7.5 %finish.1 = (bf16[256,2048]{1,0:T(8,128)(2,1)}, f32[256,2048]{1,0:T(8,128)}, f32[64,2048]{1,0:T(8,128)}, f32[64,2048]{1,0:T(8,128)}, f32[64,2048]{1,0:T(8,128)},...) custom-call(bf16[256,2048]{1,0:T(8,128)(2,1)S(1)} %copy-done, ...), custom_call_target="tpu_custom_call" | custom-call | tf_op jit(solution)/shard_map/finish/pallas_call | solution.py:1942
  (16 shorter events, 0.1 us)
Async XLA Ops:
  7.2 163.9 %all-gather.3.cloned.1.call-start = ((), (), s32[]{:S(2)}) async-start(), calls=%async_computation | async-start | bytes 1310720 | tf_op jit(solution)/shard_map/all_gather | solution.py:1995
  7.9 268.8 %all-gather.5.cloned.1.call-start = ((), (), s32[]{:S(2)}) async-start(), calls=%async_computation.1 | async-start | bytes 5242880 | tf_op jit(solution)/shard_map/all_gather | solution.py:1993
  10.1 99.4 %copy-start.7 = (s32[2,4]{1,0:T(2,128)S(1)}, s32[2,4]{1,0:T(2,128)}, u32[]{:S(2)}) copy-start(s32[2,4]{1,0:T(2,128)} %param.14) | copy-start | bytes 100
  689.9 1.2 copy-start
  691.1 1.2 copy-start.1
  692.3 1.2 copy-start.2
  693.6 1.0 copy-start.3
  694.6 0.9 copy-start.4
  695.5 0.9 copy-start.5
  696.5 0.9 copy-start.6
Sparse Core Ops, SparseCore 0:
  9.9 36.3 all-gather.2
  48.1 57.9 all-gather.4

commit v10 on v9

--- a/solution.py
+++ b/solution.py
@@ -430,40 +430,46 @@
                 self.move(peer, self.own).wait_send()
 
 
-class ToSeq:
-    def __init__(self, seqs, source, target, send, recv, first=0):
-        self.seqs, self.source, self.target, self.send, self.recv = seqs, source, target, send, recv
-        self.own = lax.axis_index("seq")
-        self.first = first
-
-    def move(self, peer, place):
-        run = self.source.shape[0] // self.seqs
-        begin = pl.multiple_of(peer * run + self.first, 16)
+def seq_peers(seqs):
+    own = lax.axis_index("seq")
+    if seqs == 4:
+        one = own + 1 - 2 * lax.rem(own, 2)
+        return [one, lax.rem(own + 2, 4)], [lax.rem(one + 2, 4)]
+    ahead = [lax.rem(own + step, seqs) for step in range(1, seqs)]
+    return ahead[:1], ahead[1:]
+
+
+def near_count(seqs):
+    return 2 if seqs == 4 else 1
+
+
+class ToPeers:
+    def __init__(self, seqs, peers, source, target, send, recv, first=0):
+        self.peers, self.source, self.target, self.send, self.recv = peers, source, target, send, recv
+        self.run, self.first = source.shape[0] // seqs, first
+
+    def move(self, index):
+        begin = pl.multiple_of(self.peers[index] * self.run + self.first, 16)
         return pltpu.make_async_remote_copy(
             src_ref=self.source.at[pl.ds(begin, self.target.shape[1])],
-            dst_ref=self.target.at[place],
-            send_sem=self.send.at[peer],
-            recv_sem=self.recv.at[place],
-            device_id={"seq": peer},
+            dst_ref=self.target.at[index],
+            send_sem=self.send.at[index],
+            recv_sem=self.recv.at[index],
+            device_id={"seq": self.peers[index]},
             device_id_type=MESH,
         )
 
     def begin(self):
-        pl.loop(1, self.seqs)(
-            lambda ahead: self.move(lax.rem(self.own + ahead, self.seqs), self.own).start()
-        )
+        for index in range(len(self.peers)):
+            self.move(index).start()
 
     def arrived(self):
-        @pl.loop(1, self.seqs)
-        def _(ahead):
-            peer = lax.rem(self.own + ahead, self.seqs)
-            self.move(peer, peer).wait_recv()
+        for index in range(len(self.peers)):
+            self.move(index).wait_recv()
 
     def sent(self):
-        @pl.loop(1, self.seqs)
-        def _(ahead):
-            peer = lax.rem(self.own + ahead, self.seqs)
-            self.move(peer, self.own).wait_send()
+        for index in range(len(self.peers)):
+            self.move(index).wait_send()
 
     def end(self):
         self.arrived()
@@ -514,12 +520,10 @@
         put(here, rate * (gain * error - unit * mean))
 
 
-def add_from_seq(seqs, own_rows, got, here):
-    seq = lax.axis_index("seq")
+def add_from_seq(own_rows, got, here):
     added = own_rows.astype(jnp.float32)
-    for place in range(seqs):
-        piece = got[place, here, :].astype(jnp.float32)
-        added = added + jnp.where(place == seq, 0.0, piece)
+    for index in range(got.shape[0]):
+        added = added + got[index, here, :].astype(jnp.float32)
     return added
 
 
@@ -1067,10 +1071,9 @@
 
 def feed_kernel(
     seqs, chips, batches, x_ref, w_hbm, wd_hbm, gd_hbm, v_ref, cot_ref, gain_ref,
-    dm_ref, db_ref, gain_grad_ref, hidden_hbm, grad_hbm, grad_in, branch_hbm,
+    dm_ref, db_ref, gain_grad_ref, hidden_hbm, grad_hbm, grad_in,
     buf, d_buf, h_buf, w_ref, wd_ref, d_ref, tiles, totals, acc, keep,
-    load, d_sem, h_sem, tile_sem, send, recv, part_send, part_recv,
-    branch_send, branch_recv, branch_keep, *sums,
+    load, d_sem, h_sem, tile_sem, send, recv, part_send, part_recv, *sums,
 ):
     line = Line(chips)
     rows, width = x_ref.shape
@@ -1187,28 +1190,34 @@
     count = width // block
     seq = lax.axis_index("seq")
 
+    near, far_off = seq_peers(seqs)
+    soon = len(near)
+    order = [peer * 2 for peer in near] + [peer * 2 for peer in far_off] + [seq * 2]
+    order = order + [peer * 2 + 1 for peer in near] + [peer * 2 + 1 for peer in far_off] + [seq * 2 + 1]
+
     def tile_at(turn):
-        early = turn < seqs - 1
-        late = turn - (seqs - 1)
-        dest = lax.rem(seq + jnp.where(early, turn + 1, late), seqs)
-        return dest, dest * 2 + jnp.where(early | (late == 0), 0, 1)
+        tile = order[-1]
+        for index in range(len(order) - 1):
+            tile = jnp.where(turn == index, order[index], tile)
+        return tile
 
     def grad_stored(turn):
         slot = lax.rem(turn, 2)
         return pltpu.make_async_copy(
-            tiles.at[slot], grad_hbm.at[rows_at(tile_at(turn)[1], block)], tile_sem.at[slot]
-        )
-
-    parts = ToSeq(seqs, grad_hbm, grad_in, part_send, part_recv)
+            tiles.at[slot], grad_hbm.at[rows_at(tile_at(turn), block)], tile_sem.at[slot]
+        )
+
+    parts = ToPeers(seqs, near, grad_hbm, grad_in, part_send, part_recv)
 
     def leave(turn):
         grad_stored(turn).wait()
-        pl.when(turn < seqs - 1)(lambda: parts.move(tile_at(turn)[0], seq).start())
+        for index in range(soon):
+            pl.when(turn == index)(lambda index=index: parts.move(index).start())
 
     def weight_grad(turn):
         slot = lax.rem(turn, 2)
         size = min(4 * TILE, 2 * units)
-        tile = tile_at(turn)[1]
+        tile = tile_at(turn)
 
         @pl.loop(0, 2 * units // size)
         def _(column):
@@ -1261,23 +1270,16 @@
 
     reduces[0].step(last)
     norm_batch(0)
-    first = db_ref.at[pl.ds(0, piece)]
-    branch = Spread(line, first, branch_hbm, branch_send, branch_recv)
-    branch_kept = pltpu.make_async_copy(first, branch_hbm.at[line.own], branch_keep)
-    branch.begin()
-    branch_kept.start()
 
     @pl.loop(2, last)
     def _(step):
         reduces[1].step(step)
         pl.when(step < count)(lambda: weight_grad(step))
-        pl.when(lax.rem(step, 2) == 1)(lambda: branch.relay((step - 1) // 2))
 
     @pl.loop(last, max(count, last))
     def _(tile):
         weight_grad(tile)
 
-    branch.relay(chips - 1)
     reduces[1].step(last)
     norm_batch(1)
     for batch in range(batches):
@@ -1287,9 +1289,6 @@
         item.wait()
     leave(count - 1)
     parts.end()
-    branch.rest()
-    branch.sent()
-    branch_kept.wait()
 
 
 def feed_forward(seqs, chips, batches, x, w, wd, group_d, middle, cot, gain, collective):
@@ -1307,11 +1306,10 @@
             jax.ShapeDtypeStruct((8, width), jnp.float32),
             jax.ShapeDtypeStruct((group * rows, units), half),
             jax.ShapeDtypeStruct((width, 2 * units), half),
-            jax.ShapeDtypeStruct((seqs, block, 2 * units), half),
-            jax.ShapeDtypeStruct((group, piece, width), half),
+            jax.ShapeDtypeStruct((near_count(seqs), block, 2 * units), half),
         ],
         in_specs=[VMEM_SPEC] + [ANY_SPEC] * 3 + [VMEM_SPEC] * 3,
-        out_specs=[VMEM_SPEC] * 3 + [ANY_SPEC] * 4,
+        out_specs=[VMEM_SPEC] * 3 + [ANY_SPEC] * 3,
         scratch_shapes=[
             pltpu.VMEM((batches, group, piece, width), half),
             pltpu.VMEM((2, 2 * piece, width), half),
@@ -1331,9 +1329,6 @@
             sems(batches, group, PARTS // 2),
             sems(seqs),
             sems(seqs),
-            sems(3, group, PARTS // 2),
-            sems(group, PARTS // 2),
-            pltpu.SemaphoreType.DMA,
         ]
         + PairReduce.scratch(chips, piece, width) * batches,
         compiler_params=comm_params(collective, 63),
@@ -1345,9 +1340,9 @@
 
 
 def branch_back_kernel(
-    seqs, chips, batches, x_ref, b_hbm, w_ref, att_ref, middle_ref, hidden_hbm, wd_hbm, units_hbm, gd_hbm,
-    d_ref, layer_ref, out_grad_ref, units_in, down_hbm, down_in,
-    out_ref, early, buf, hidden_ref, wd_ref, grad_acc, rights, tiles, send, recv, load, right_sem, tile_sem,
+    seqs, chips, batches, x_ref, w_ref, att_ref, middle_ref, hidden_hbm, wd_hbm, units_hbm, gd_hbm,
+    d_ref, layer_ref, out_grad_ref, half_in, whole_in, down_hbm, down_in,
+    out_ref, buf, hidden_ref, wd_ref, grad_acc, rights, tiles, send, recv, load, right_sem, tile_sem,
     part_send, part_recv, down_send, down_recv, down_keep, acc, cross_out, line_out, cross_in, line_in, sum_send, sum_recv,
 ):
     line = Line(chips)
@@ -1357,7 +1352,6 @@
     loads = [
         pltpu.make_async_copy(hidden_hbm, hidden_ref, load.at[0]),
         pltpu.make_async_copy(wd_hbm, wd_ref, load.at[1]),
-        pltpu.make_async_copy(b_hbm, early, load.at[2]),
     ]
     for item in loads:
         item.start()
@@ -1396,25 +1390,30 @@
 
     right(0).start()
     meet(line.greet() + greet_seq(seqs))
-    sums = ToSeq(seqs, units_hbm, units_in, part_send, part_recv, units_in.shape[1])
-    down = ToSeq(seqs, down_hbm, down_in, down_send, down_recv)
-    down_rows = down_in.shape[1]
+    near, far_off = seq_peers(seqs)
+    soon = len(near)
+    halves = ToPeers(
+        seqs, near, units_hbm, half_in, part_send.at[0], part_recv.at[0], half_in.shape[1]
+    )
+    wholes = ToPeers(seqs, far_off, units_hbm, whole_in, part_send.at[1], part_recv.at[1])
+    down = ToPeers(
+        seqs, near, down_hbm, down_in.at[pl.ds(0, soon)], down_send, down_recv
+    )
     down_kept = pltpu.make_async_copy(
-        down_hbm.at[rows_at(down.own, down_rows)], down_in.at[down.own], down_keep
+        down_hbm.at[rows_at(lax.axis_index("seq"), down_in.shape[1])], down_in.at[soon], down_keep
     )
-    late = x_ref.at[pl.ds(piece, piece)]
-    spread = Spread(line, late, buf, send, recv)
+    spread = Spread(line, x_ref, buf, send, recv)
     reduce = Reduce(
         line, product, out_ref, acc, cross_out, line_out, cross_in, line_in, sum_send, sum_recv
     )
     spread.begin()
-    sums.begin()
-    buf[line.own] = late[...]
+    halves.begin()
+    wholes.begin()
+    buf[line.own] = x_ref[...]
     grad_acc[...] = jnp.zeros_like(grad_acc)
 
     def use(slot):
-        both = jnp.concatenate([early[slot], buf[slot]], axis=0)
-        got = to_half(dot_nt(both, w_ref[...]))
+        got = to_half(dot_nt(buf[slot], w_ref[...]))
         for batch in range(batches):
             d_ref[batch, rows_at(slot, piece), :] = got[batch * piece : (batch + 1) * piece]
         mixed = left_rows(att_ref, slot, rows)
@@ -1422,8 +1421,7 @@
         @pl.loop(0, width // TILE)
         def _(tile):
             here = rows_at(tile, TILE)
-            right = jnp.concatenate([early[slot, :, here], buf[slot, :, here]], axis=0)
-            grad_acc[:, here] += contract_rows(mixed, right)
+            grad_acc[:, here] += contract_rows(mixed, buf[slot, :, here])
 
     for item in loads:
         item.wait()
@@ -1440,9 +1438,7 @@
     @pl.loop(1, chips)
     def _(step):
         def also(tile):
-            pl.when((step < chips - 1) & (tile < spread.parts))(
-                lambda: spread.relay_part(step + 1, tile)
-            )
+            pl.when(step < chips - 1)(lambda: spread.relay_part(step + 1, tile))
 
         reduce.level(chips - 1 - step, also)
         spread.each(step, use)
@@ -1457,46 +1453,48 @@
     out_grad_ref[...] = to_half(grad_acc[...])
     spread.sent()
     reduce.sent()
-    sums.end()
+    halves.end()
+    wholes.end()
     down.end()
     down_kept.wait()
 
 
-def branch_back(seqs, chips, batches, x, early, w, attended, middle, hidden, wd, unit_part, group_d, collective):
+def branch_back(seqs, chips, batches, x, w, attended, middle, hidden, wd, unit_part, group_d, collective):
     rows, width = x.shape
     group = 2 * chips
     length = group * rows // batches
     span = w.shape[0]
     half = jnp.bfloat16
     part = 256 if group * rows <= 2048 else 128
+    near, run = near_count(seqs), width // seqs
     return pl.pallas_call(
         functools.partial(branch_back_kernel, seqs, chips, batches),
         out_shape=[
             jax.ShapeDtypeStruct((batches, length, span), half),
             jax.ShapeDtypeStruct((rows, width), half),
             jax.ShapeDtypeStruct((span, width), half),
-            jax.ShapeDtypeStruct((seqs, width // seqs // 2, unit_part.shape[1]), half),
+            jax.ShapeDtypeStruct((near, run // 2, unit_part.shape[1]), half),
+            jax.ShapeDtypeStruct((seqs - 1 - near, run, unit_part.shape[1]), half),
             jax.ShapeDtypeStruct((wd.shape[0], width), half),
-            jax.ShapeDtypeStruct((seqs, wd.shape[0] // seqs, width), half),
+            jax.ShapeDtypeStruct((near + 1, wd.shape[0] // seqs, width), half),
         ],
-        in_specs=[VMEM_SPEC, ANY_SPEC] + [VMEM_SPEC] * 3 + [ANY_SPEC] * 4,
-        out_specs=[VMEM_SPEC, VMEM_SPEC, VMEM_SPEC, ANY_SPEC, ANY_SPEC, ANY_SPEC],
+        in_specs=[VMEM_SPEC] * 4 + [ANY_SPEC] * 4,
+        out_specs=[VMEM_SPEC, VMEM_SPEC, VMEM_SPEC, ANY_SPEC, ANY_SPEC, ANY_SPEC, ANY_SPEC],
         scratch_shapes=[
             pltpu.VMEM((rows, width), jnp.float32),
-            pltpu.VMEM((group, rows // batches, width), half),
-            pltpu.VMEM((group, rows // batches, width), half),
+            pltpu.VMEM((group, rows, width), half),
             pltpu.VMEM(hidden.shape, half),
             pltpu.VMEM(wd.shape, half),
             pltpu.VMEM((span, width), jnp.float32),
             pltpu.VMEM((2, group * rows, part), half),
             pltpu.VMEM((2, wd.shape[0], part), half),
-            sems(3, group, PARTS // 2),
-            sems(group, PARTS // 2),
-            sems(3),
+            sems(3, group, PARTS),
+            sems(group, PARTS),
             sems(2),
             sems(2),
-            sems(seqs),
-            sems(seqs),
+            sems(2),
+            sems(2, seqs),
+            sems(2, seqs),
             sems(seqs),
             sems(seqs),
             pltpu.SemaphoreType.DMA,
@@ -1509,13 +1507,14 @@
             2 * group * rows * width * 2,
         ),
         name="branch_back",
-    )(x, early, w, attended, middle, hidden, wd, unit_part, group_d.reshape(group * rows, width))
+    )(x, w, attended, middle, hidden, wd, unit_part, group_d.reshape(group * rows, width))
 
 
 def attention_back_kernel(
-    seqs, chips, block, q_ref, pad_ref, low_ref, lse_ref, d_ref, part_hbm, in_one, in_two,
-    w_ref, g_hbm, v_ref, dm_hbm, gain_ref, mlp_gain_ref, out_ref,
-    grad_ref, wq_ref, wk_ref, wv_ref, wo_ref, tile_ref, gate_ref, up_ref,
+    seqs, chips, block, q_ref, pad_ref, low_ref, lse_ref, d_ref, part_hbm, in_one, in_two, in_far,
+    w_ref, g_hbm, v_ref, dm_hbm, gain_ref, mlp_gain_ref, out_ref, down_hbm,
+    grad_hbm, wq_ref, wk_ref, wv_ref, wo_hbm, tile_ref, gate_hbm, up_hbm, down_in,
+    grad_ref, wo_ref, gate_ref, up_ref, result_sem, down_send, down_recv,
     dk, dv, kt, heads, back_out, back_in, unit_parts, unit_sums, units, lefts, parts, sums, cols, out_in,
     totals, gain_acc, gain_out, gain_in, gain_sum, gain_back, acc, keep,
     halo_send, halo_recv, unit_load, unit_send, unit_recv, unit_keep, dm_load, left_sem,
@@ -1548,26 +1547,33 @@
 
     def load_units(turn):
         member = lax.rem(own + turn, group)
-        mine = part_hbm.at[rows_at(seq * group + member, share)]
-        for place in range(seqs):
-
-            def fetch(source, place=place):
-                unit_loaded(turn, place, source).start()
-
-            pl.when(place == seq)(lambda: fetch(mine))
-
-            @pl.when((place != seq) & (member < chips))
-            def _(place=place):
-                fetch(in_one.at[place, rows_at(member, share)])
-
-            @pl.when((place != seq) & (member >= chips))
-            def _(place=place):
-                fetch(in_two.at[place, rows_at(member - chips, share)])
+        unit_loaded(turn, 0, part_hbm.at[rows_at(seq * group + member, share)]).start()
+        soon = in_one.shape[0]
+        for index in range(seqs - 1):
+
+            def fetch(source, index=index):
+                unit_loaded(turn, index + 1, source).start()
+
+            if index < soon:
+
+                @pl.when(member < chips)
+                def _(index=index, fetch=fetch):
+                    fetch(in_one.at[index, rows_at(member, share)])
+
+                @pl.when(member >= chips)
+                def _(index=index, fetch=fetch):
+                    fetch(in_two.at[index, rows_at(member - chips, share)])
+
+            else:
+                fetch(in_far.at[index - soon, rows_at(member, share)])
 
     load_units(1)
     dm_loaded = pltpu.make_async_copy(dm_hbm, grad_ref, dm_load)
     dm_loaded.start()
     meet(greet_group(group) + greet_seq(seqs))
+    near, far_off = seq_peers(seqs)
+    down = ToPeers(seqs, far_off, down_hbm, down_in, down_send, down_recv)
+    down.begin()
     swap = Swap(group, unit_sums, units, unit_send, unit_recv, unit_keep)
 
     @pl.loop(1, group + 1)
@@ -1696,16 +1702,7 @@
             g_hbm.at[:, :, rows_at(tile, part)], lefts.at[slot], left_sem.at[slot]
         )
 
-    def to_seq(peer, place):
-        return pltpu.make_async_remote_copy(
-            src_ref=parts.at[rows_at(peer, run)],
-            dst_ref=sums.at[place],
-            send_sem=part_send.at[peer],
-            recv_sem=part_recv.at[place],
-            device_id={"seq": peer},
-            device_id_type=MESH,
-        )
-
+    heads_near = ToPeers(seqs, near + far_off, parts, sums, part_send, part_recv)
     left(0).start()
     add_halo(1)
 
@@ -1719,8 +1716,8 @@
             got = got + contract_rows(lefts[slot, batch], heads[batch])
         parts[rows_at(tile, part), :] = to_half(got)
 
-    others(seqs, seq, lambda peer: to_seq(peer, seq).start())
-    from_seq = ToSeq(seqs, out_ref, out_in, out_send, out_recv)
+    heads_near.begin()
+    from_seq = ToPeers(seqs, near + far_off, out_ref, out_in, out_send, out_recv)
     from_seq.begin()
     gain_acc[...] = jnp.zeros_like(gain_acc)
     dm_loaded.wait()
@@ -1747,6 +1744,15 @@
                 here = slice(begin + place * cell, begin + (place + 1) * cell)
                 target[:, column : column + cell] = units[member, :, here]
 
+    results = [
+        pltpu.make_async_copy(source, target, result_sem.at[index])
+        for index, (source, target) in enumerate(
+            ((gate_ref, gate_hbm), (up_ref, up_hbm), (wo_ref, wo_hbm), (grad_ref, grad_hbm))
+        )
+    ]
+    results[0].start()
+    results[1].start()
+
     def block_swap(peer, member):
         return pltpu.make_async_remote_copy(
             src_ref=parts.at[rows_at(seq * group + peer, share)],
@@ -1757,21 +1763,23 @@
             device_id_type=MESH,
         )
 
-    others(seqs, seq, lambda peer: to_seq(peer, peer).wait_recv())
+    heads_near.arrived()
 
     @pl.loop(0, run // 64)
     def _(chunk):
         here = rows_at(chunk, 64)
         there = pl.ds(pl.multiple_of(seq * run + chunk * 64, 64), 64)
-        parts[there, :] = to_half(add_from_seq(seqs, parts[there, :], sums, here))
+        parts[there, :] = to_half(add_from_seq(parts[there, :], sums, here))
 
     others(group, own, lambda peer: block_swap(peer, own).start())
     cols[own] = parts[rows_at(seq * group + own, share), :]
     from_seq.arrived()
     out_rows = out_in.shape[1]
-    wo_ref[...] = add_from_seq(seqs, out_ref[rows_at(seq, out_rows), :], out_in, slice(None))
+    wo_ref[...] = add_from_seq(out_ref[rows_at(seq, out_rows), :], out_in, slice(None))
+    results[2].start()
     reduces[1].step(last)
     norm_batch(1)
+    results[3].start()
     fold = 128 // share
     near = group // fold
     attn_row = jnp.sum(gain_acc[...], axis=0, keepdims=True)
@@ -1816,6 +1824,8 @@
             first = first + index * span
             target[:, home : home + size] = cols[member, :, first : first + size]
     from_seq.sent()
+    for item in results:
+        item.wait()
     for batch in range(batches):
         reduces[batch].sent()
 
@@ -1823,15 +1833,16 @@
         def _(batch=batch):
             pl.loop(0, need)(lambda step: halo(batch, step, seq).wait_send())
 
-    others(seqs, seq, lambda peer: to_seq(peer, seq).wait_send())
+    heads_near.sent()
+    down.end()
     others(group, own, lambda peer: gain_group(peer, own).wait_send())
     others(group, own, lambda peer: block_swap(peer, own).wait_send())
     others(seqs, seq, lambda peer: gain_seq(peer, seq).wait_send())
 
 
 def attention_back(
-    seqs, chips, block, query, kv_pad, low, lse, d_att, part_own, parts_one, parts_two, w, group_a, x,
-    d_middle, gain, mlp_gain, out_part, collective,
+    seqs, chips, block, query, kv_pad, low, lse, d_att, part_own, parts_one, parts_two, parts_far, w, group_a,
+    x, d_middle, gain, mlp_gain, out_part, down, collective,
 ):
     batches, length, span = query.shape
     padded = kv_pad.shape[1]
@@ -1857,13 +1868,23 @@
             jax.ShapeDtypeStruct((8, 128), wide),
             jax.ShapeDtypeStruct((share, cells // 2 * group), half),
             jax.ShapeDtypeStruct((share, cells // 2 * group), half),
+            jax.ShapeDtypeStruct((seqs - 1 - near_count(seqs), down.shape[0] // seqs, width), half),
         ],
         in_specs=[VMEM_SPEC] * 5
-        + [ANY_SPEC] * 3
+        + [ANY_SPEC] * 4
         + [VMEM_SPEC, ANY_SPEC, VMEM_SPEC, ANY_SPEC]
-        + [VMEM_SPEC] * 3,
-        out_specs=[VMEM_SPEC] * 8,
+        + [VMEM_SPEC] * 3
+        + [ANY_SPEC],
+        out_specs=[ANY_SPEC, VMEM_SPEC, VMEM_SPEC, VMEM_SPEC, ANY_SPEC, VMEM_SPEC]
+        + [ANY_SPEC] * 3,
         scratch_shapes=[
+            pltpu.VMEM((rows, width), wide),
+            pltpu.VMEM((out_rows, width), wide),
+            pltpu.VMEM((share, cells // 2 * group), half),
+            pltpu.VMEM((share, cells // 2 * group), half),
+            sems(4),
+            sems(seqs),
+            sems(seqs),
             pltpu.VMEM((padded, span), wide),
             pltpu.VMEM((padded, span), wide),
             pltpu.VMEM((span, padded), half),
@@ -1875,9 +1896,9 @@
             pltpu.VMEM((group, share, cells), half),
             pltpu.VMEM((2, batches, length, part), half),
             pltpu.VMEM((width, depth), half),
-            pltpu.VMEM((seqs, run, depth), half),
+            pltpu.VMEM((seqs - 1, run, depth), half),
             pltpu.VMEM((group, share, depth), half),
-            pltpu.VMEM((seqs, out_rows, width), half),
+            pltpu.VMEM((seqs - 1, out_rows, width), half),
             pltpu.VMEM((batches, piece, width), wide),
             pltpu.VMEM((8, width), wide),
             pltpu.VMEM((near, seqs, 8, 128), wide),
@@ -1914,40 +1935,41 @@
         ),
         name="attention_back",
     )(
-        query, kv_pad, low, lse, d_att, part_own, parts_one, parts_two, w, group_a, x, d_middle,
-        gain, mlp_gain, out_part,
+        query, kv_pad, low, lse, d_att, part_own, parts_one, parts_two, parts_far, w, group_a, x,
+        d_middle, gain, mlp_gain, out_part, down,
     )
 
 
-def finish_kernel(*refs):
-    half = len(refs) // 2
-    for source, target in zip(refs[:half], refs[half:]):
-        if len(source.shape) == len(target.shape):
-            target[...] = source[...].astype(target.dtype)
-        else:
-            target[...] = jnp.sum(source[...].astype(jnp.float32), axis=0)
-
-
-def finish(steps, arrays, kinds):
+def finish_kernel(count, *refs):
+    sources, targets = refs[:-count], refs[-count:]
+    for source, target in zip(sources, targets[:-1]):
+        target[...] = source[...].astype(target.dtype)
+    added = 0.0
+    for source in sources[count - 1 :]:
+        added = added + jnp.sum(source[...].astype(jnp.float32), axis=0)
+    targets[-1][...] = added
+
+
+def finish(steps, arrays, parts, kinds):
     in_specs, out_specs, out_shape = [], [], []
-    for item, kind in zip(arrays, kinds):
+    for item, kind in zip(arrays + parts[:1], kinds):
         rows, width = item.shape[-2:]
         block = (rows // steps, width)
         out_specs.append(pl.BlockSpec(block, lambda i: (i, 0)))
         out_shape.append(jax.ShapeDtypeStruct((rows, width), kind))
-        if item.ndim == 3:
-            in_specs.append(pl.BlockSpec((item.shape[0],) + block, lambda i: (0, i, 0)))
-        else:
+        if item.ndim == 2:
             in_specs.append(out_specs[-1])
+    for item in parts:
+        in_specs.append(pl.BlockSpec((item.shape[0],) + block, lambda i: (0, i, 0)))
     return pl.pallas_call(
-        finish_kernel,
+        functools.partial(finish_kernel, len(kinds)),
         grid=(steps,),
         in_specs=in_specs,
         out_specs=out_specs,
         out_shape=out_shape,
         compiler_params=pltpu.CompilerParams(vmem_limit_bytes=48 * MIB),
         name="finish",
-    )(*arrays)
+    )(*arrays, *parts)
 
 
 def doc_starts(lengths, positions, batches, seq_len):
@@ -2027,12 +2049,12 @@
         x_rows, gain_two[None], 3,
     )
     w_units = w_units.reshape(width, -1)
-    d_middle, d_branch, mlp_gain_part, hidden, unit_part, unit_one, early = feed_forward(
+    d_middle, d_branch, mlp_gain_part, hidden, unit_part, unit_one = feed_forward(
         seqs, chips, batches, normed_b, w_units, wd_part, group_d, middle, cot_rows,
         gain_two[None], 4,
     )
-    d_attended, layer_out, out_part, unit_two, _, down_in = branch_back(
-        seqs, chips, batches, d_branch, early, wo_part, attended, middle, hidden, wd_part, unit_part,
+    d_attended, layer_out, out_part, unit_two, unit_far, down_part, down_near = branch_back(
+        seqs, chips, batches, d_branch, wo_part, attended, middle, hidden, wd_part, unit_part,
         group_d, 5,
     )
     if not aligned:
@@ -2041,15 +2063,19 @@
         )
         out_part = lax.psum(whole, "fsdp").reshape(seqs, group, share, width)
         out_part = lax.dynamic_slice_in_dim(out_part, member, 1, 1).reshape(seqs * share, width)
-    input_grad, wq_grad, wk_grad, wv_grad, wo_grad, gain_tile, gate_grad, up_grad = attention_back(
+    (
+        input_grad, wq_grad, wk_grad, wv_grad, wo_grad, gain_tile, gate_grad, up_grad, down_far,
+    ) = attention_back(
         seqs, chips, block, query, kv_pad, low, lse, d_attended, unit_part, unit_one, unit_two,
-        w_heads, group_a, x_rows, d_middle, gain_one[None], mlp_gain_part, out_part, 6,
+        unit_far, w_heads, group_a, x_rows, d_middle, gain_one[None], mlp_gain_part, out_part,
+        down_part, 6,
     )
     gain_grads = lax.dynamic_slice_in_dim(gain_tile[:2], lax.rem(device, fold) * share, share, 1)
     wide = jnp.float32
     (layer_out, input_grad, wq_grad, wk_grad, wv_grad, wo_grad, gate_grad, up_grad, down_grad) = finish(
         share // 16,
-        [layer_out, input_grad, wq_grad, wk_grad, wv_grad, wo_grad, gate_grad, up_grad, down_in],
+        [layer_out, input_grad, wq_grad, wk_grad, wv_grad, wo_grad, gate_grad, up_grad],
+        [down_near, down_far],
         [jnp.bfloat16] + [wide] * 8,
     )
     return (

time: 724 us -> 716 us (0.989)
  Pallas kernels: 683 us -> 674 us
    pallas_call x1, Pallas kernels: 158 us -> 141 us  [feed_forward(): pl.pallas_call(functools.partial(feed_kernel, seqs, chips, batches), out_...]
    pallas_call x1, Pallas kernels: 147 us -> 159 us  [attention_back(): pl.pallas_call(functools.partial(attention_back_kernel, seqs, chips, bloc...]
  transfers between devices with their start and end apart: 2 -> 2, of which waited for: 0 -> 0; matrix products, arithmetic and copies ran while one was open for 1% -> 1% of each run, Pallas kernels for 37% -> 38%
where the time goes in v10:
time: 716 us; the launch traced here: 704 us
  Pallas kernels  674 us (94%)
  between operations  14.6 us (2%)
  local copies, waits for them, and re-layouts  12.3 us (2%)
    pallas_call x1, Pallas kernels, attention_back(): pl.pallas_call(functools.partial(attention_back_kernel, seqs, chips, bloc...  159 us
    pallas_call x1, Pallas kernels, feed_forward(): pl.pallas_call(functools.partial(feed_kernel, seqs, chips, batches), out_...  141 us
    pallas_call x1, Pallas kernels, branch_sum(): pl.pallas_call(functools.partial(branch_kernel, seqs, chips), out_shape=[...  106 us
    pallas_call x1, Pallas kernels, branch_back(): pl.pallas_call(functools.partial(branch_back_kernel, seqs, chips, batches...  102 us
    pallas_call x1, Pallas kernels, start(): pl.pallas_call(functools.partial(start_kernel, seqs, chips, batches), out...  98.5 us
    pallas_call x1, Pallas kernels, attend(): pl.pallas_call(functools.partial(attend_kernel, seqs, group, block), in_s...  60.1 us
  transfers between devices with their start and end apart: 2, of which 0 were waited for; matrix products, arithmetic and copies ran while one was open for 1% of the time, Pallas kernels for 38%

profile of v10, /device:TPU:9, one launch (start us, length us, event | category | flops | bytes accessed | tf_op | source)
XLA Modules:
  0.0 704.1 jit_solution(2000949594165610627)
XLA Ops:
  7.2 0.0 all-gather.3.cloned.1.call-start
  7.2 0.7 all-gather.3.cloned.1.call-update
  7.9 0.0 all-gather.5.cloned.1.call-start
  8.0 0.7 all-gather.5.cloned.1.call-update
  8.7 0.7 maximum_convert_fusion
  9.4 0.1 tile.10
  9.5 0.6 pad_bitcast_fusion.tile_ref
  10.1 98.5 %start.1 = (bf16[2,1024,2048]{2,1,0:T(8,128)(2,1)}, bf16[2,1024,256]{2,1,0:T(8,128)(2,1)}, bf16[2,1024,512]{2,1,0:T(8,128)(2,1)}, f32[8,4,8,128]{3,2,1,0:T(8,128...) custom-call(f32[1,8,128]{2,1,0:T(8,128)} %pad_bitcast_fusion.tile_ref, bf16[256,2048]{1,0:T(8,128)(2,1)} %bitcast.28, ...), custom_call_target="tpu_custom_call" | custom-call | flops 6442450944 | bytes 209715200 | tf_op jit(solution)/shard_map/start/pallas_call | solution.py:714
  108.6 0.9 copy.25
  109.5 0.2 reduce_window_sum.11
  109.7 0.1 select_reduce_fusion
  109.8 0.6 maximum_subtract_fusion.low_ref
  110.4 0.6 slice_bitcast_fusion
  111.1 60.1 %attend.1 = (bf16[2,1024,256]{2,1,0:T(8,128)(2,1)}, f32[2,4,1024]{2,1,0:T(4,128)}, bf16[2,2048,512]{2,1,0:T(8,128)(2,1)}, bf16[8,64,2048]{2,1,0:T(8,128)(2,1)}) custom-call(bf16[2,1024,256]{2,1,0:T(8,128)(2,1)} %get-tuple-element.58.q_ref, bf16[2,1024,512]{2,1,0:T(8,128)(2,1)} %get-tuple-element.59.kv_ref, s32[2,1,1024]{2,1,0:T(1,128)} %maximum_subtract_fusion.low_ref, ...), custom_call_target="tpu_custom_call" | custom-call | flops 5368709120 | bytes 157286400 | tf_op jit(solution)/shard_map/attend/pallas_call | solution.py:850
  171.2 0.0 all-gather.3.cloned.1.call-done.w_ref
  171.2 105.6 %branch_sum.1 = (f32[256,2048]{1,0:T(8,128)}, bf16[256,2048]{1,0:T(8,128)(2,1)}, bf16[8,256,2048]{2,1,0:T(8,128)(2,1)}, bf16[4,512,2048]{2,1,0:T(8,128)(2,1)}) custom-call(bf16[2,1024,256]{2,1,0:T(8,128)(2,1)} %get-tuple-element.63.a_ref.att_ref, bf16[256,2048]{1,0:T(8,128)(2,1)} %all-gather.3.cloned.1.call-done.w_ref, bf16[256,2048]{1,0:T(8,128)(2,1)} %bitcast.26, ...), custom_call_target="tpu_custom_call" | custom-call | flops 2147483648 | bytes 262144000 | tf_op jit(solution)/shard_map/branch_sum/pallas_call | solution.py:926
  276.8 0.0 all-gather.5.cloned.1.call-done.wd_hbm
  276.8 141.0 %feed_forward.1 = (f32[256,2048]{1,0:T(8,128)}, bf16[256,2048]{1,0:T(8,128)(2,1)}, f32[8,2048]{1,0:T(8,128)}, bf16[2048,1024]{1,0:T(8,128)(2,1)}, bf16[2048,2048...) custom-call(bf16[256,2048]{1,0:T(8,128)(2,1)} %get-tuple-element.66.x_ref, bf16[2048,2048]{1,0:T(8,128)(2,1)} %bitcast.33, ...), custom_call_target="tpu_custom_call" | custom-call | flops 60129542144 | bytes 419430400 | tf_op jit(solution)/shard_map/feed_forward/pallas_call | solution.py:1301
  417.8 102.5 %branch_back.1 = (bf16[2,1024,256]{2,1,0:T(8,128)(2,1)}, bf16[256,2048]{1,0:T(8,128)(2,1)}, bf16[256,2048]{1,0:T(8,128)(2,1)}, bf16[2,256,2048]{2,1,0:T(8,128)(2...) custom-call(bf16[256,2048]{1,0:T(8,128)(2,1)} %get-tuple-element.70.x_ref, ...), custom_call_target="tpu_custom_call" | custom-call | flops 21474836480 | bytes 262144000 | tf_op jit(solution)/shard_map/branch_back/pallas_call | solution.py:1470
  520.3 159.3 %attention_back.1 = (f32[256,2048]{1,0:T(8,128)}, bf16[64,2048]{1,0:T(8,128)(2,1)}, bf16[64,2048]{1,0:T(8,128)(2,1)}, bf16[64,2048]{1,0:T(8,128)(2,1)}, f32[64,2...) custom-call(bf16[2,1024,256]{2,1,0:T(8,128)(2,1)} %get-tuple-element, ...), custom_call_target="tpu_custom_call" | custom-call | flops 26306674688 | bytes 419430400 | tf_op jit(solution)/shard_map/attention_back/pallas_call | solution.py:1860
  679.7 0.7 slice.17
  680.3 0.1 constant_dynamic-slice_fusion
  680.4 0.5 slice_bitcast_fusion.2
  680.9 1.2 copy-done
  682.2 1.2 copy-done.1
  683.4 1.2 copy-done.2
  684.6 1.2 copy-done.3
  685.8 1.0 copy-done.4
  686.9 0.9 copy-done.5
  687.8 0.9 copy-done.6
  688.8 0.9 copy-done.7
  689.7 7.1 %finish.1 = (bf16[256,2048]{1,0:T(8,128)(2,1)}, f32[256,2048]{1,0:T(8,128)}, f32[64,2048]{1,0:T(8,128)}, f32[64,2048]{1,0:T(8,128)}, f32[64,2048]{1,0:T(8,128)},...) custom-call(bf16[256,2048]{1,0:T(8,128)(2,1)S(1)} %copy-done, ...), custom_call_target="tpu_custom_call" | custom-call | tf_op jit(solution)/shard_map/finish/pallas_call | solution.py:1964
  (18 shorter events, 0.1 us)
Async XLA Ops:
  7.2 164.0 %all-gather.3.cloned.1.call-start = ((), (), s32[]{:S(2)}) async-start(), calls=%async_computation | async-start | bytes 1310720 | tf_op jit(solution)/shard_map/all_gather | solution.py:2017
  7.9 268.9 %all-gather.5.cloned.1.call-start = ((), (), s32[]{:S(2)}) async-start(), calls=%async_computation.1 | async-start | bytes 5242880 | tf_op jit(solution)/shard_map/all_gather | solution.py:2015
  10.1 99.4 %copy-start.8 = (s32[2,4]{1,0:T(2,128)S(1)}, s32[2,4]{1,0:T(2,128)}, u32[]{:S(2)}) copy-start(s32[2,4]{1,0:T(2,128)} %param.14) | copy-start | bytes 100
  680.9 1.2 copy-start
  682.2 1.2 copy-start.1
  683.4 1.2 copy-start.2
  684.6 1.2 copy-start.3
  685.8 1.0 copy-start.4
  686.9 0.9 copy-start.5
  687.8 0.9 copy-start.6
  688.8 0.9 copy-start.7
Sparse Core Ops, SparseCore 0:
  9.9 36.3 all-gather.2
  48.1 57.9 all-gather.4

commit v11 on v10

--- a/solution.py
+++ b/solution.py
@@ -538,21 +538,24 @@
 
 
 def start_kernel(
-    seqs, chips, batches, tile_ref, x_ref, wq_ref, wk_ref, wv_ref, gate_hbm, up_hbm,
-    g_ref, q_ref, kv_ref, gains_ref, w_out_ref, units_ref,
-    gate, up, units, unit_sem,
-    blocks_ref, buf, normed, gain, gains, w, send, recv, keep, swap_send, share_send, w_recv,
+    seqs, chips, batches, block, tile_ref, x_ref, wq_ref, wk_ref, wv_ref, gate_hbm, up_hbm, low_ref,
+    g_ref, q_ref, out_ref, lse_ref, pad_ref, gains_ref, w_out_ref, own_units_ref,
+    gate, up, units, blocks_ref, buf, normed, pad, vt, gain, gains, w,
+    unit_sem, send, recv, keep, swap_send, share_send, w_recv,
     tile_send, tile_across, tile_recv, tile_back, w_keep, gain_keep,
+    halo_send, halo_recv, pad_keep, unit_send, unit_recv, unit_keep,
 ):
     line = Line(chips)
     group = 2 * chips
     seq = lax.axis_index("seq")
     own = line.own
     share = blocks_ref.shape[1]
-    piece = x_ref.shape[0] // batches
-    span = q_ref.shape[2]
-    width = x_ref.shape[1]
+    rows, width = x_ref.shape
+    piece = rows // batches
+    length, span = q_ref.shape[1:]
     per = 128 * seqs * group // width
+    steps, need = length // block, WINDOW // block
+    has_left, has_right = seq > 0, seq < seqs - 1
     unit_loads = [
         pltpu.make_async_copy(gate_hbm, gate, unit_sem.at[0]),
         pltpu.make_async_copy(up_hbm, up, unit_sem.at[1]),
@@ -613,12 +616,16 @@
 
     others(seqs, seq, lambda peer: tile_to_seq(peer, seq).start())
     others(group, own, lambda peer: block_swap(peer, own).start())
-    spread = Spread(line, x_ref, buf, send, recv)
-    spread.begin()
+    spreads = [
+        Spread(line, x_ref.at[pl.ds(batch * piece, piece)], buf.at[batch], send.at[batch], recv.at[batch])
+        for batch in range(batches)
+    ]
+    spreads[0].begin()
     gains[own, seq] = tile_ref[0]
     w[rows_at(seq * group + own, share), :] = blocks_ref[own]
     others(seqs, seq, lambda peer: block_share(seq, own, peer).start())
-    buf[own] = x_ref[...]
+    for batch in range(batches):
+        buf[batch, own] = x_ref[batch * piece : (batch + 1) * piece, :]
     others(seqs, seq, lambda peer: tile_to_seq(peer, peer).wait_recv())
     others(group, own, lambda peer: tiles_to_group(peer, own).start())
     for item in unit_loads:
@@ -630,8 +637,11 @@
             for index, source in enumerate((gate, up)):
                 first = (index * seqs + run) * cell
                 units[member, :, first : first + cell] = source[:, home : home + cell]
-    units_kept = pltpu.make_async_copy(units, units_ref, unit_sem.at[2])
-    units_kept.start()
+    unit_swap = Swap(group, units, own_units_ref, unit_send, unit_recv, unit_keep)
+
+    @pl.when(jnp.logical_not(has_left))
+    def _():
+        pad[:, :WINDOW, :] = jnp.zeros((batches, WINDOW, 2 * span), jnp.bfloat16)
 
     def pass_block(member):
         block_swap(member, member).wait_recv()
@@ -645,30 +655,60 @@
             total = total + gains[place % group, place // group, 0:1, :]
         gain[0:1, column * 128 : (column + 1) * 128] = total
 
-    def kept(slot, batch):
+    def sides(far, act):
+        @pl.loop(0, 2)
+        def _(side):
+            place = line.chip + far * (2 * side - 1)
+            valid = (place >= 0) & (place < chips) & ((side == 0) | (far > 0))
+            pl.when(valid)(lambda: act(place))
+
+    def kept(batch, place):
+        here = rows_at(place, block)
         return pltpu.make_async_copy(
-            normed.at[slot, pl.ds(batch * piece, piece)],
-            g_ref.at[batch, rows_at(slot, piece)],
-            keep.at[slot, batch],
-        )
-
-    def use(slot):
-        @pl.loop(0, x_ref.shape[0] // 64)
-        def _(chunk):
-            rows = rows_at(chunk, 64)
-            values = buf[slot, rows, :].astype(jnp.float32)
-            normed[slot, rows, :] = to_half(normalize(values, gain[0:1, :]))
-
-        for batch in range(batches):
-            kept(slot, batch).start()
-        rows = rows_at(slot, piece)
-        got = to_half(dot_nn(normed[slot], w[...]))
-        for batch in range(batches):
-            mine = got[batch * piece : (batch + 1) * piece]
-            q_ref[batch, rows, :] = mine[:, :span]
-            kv_ref[batch, rows, :] = mine[:, span:]
-
-    pl.loop(1, chips - 1)(spread.relay)
+            normed.at[batch, here], g_ref.at[batch, here], keep.at[batch, place]
+        )
+
+    def norm_pair(batch, place):
+        spreads[batch].across(place * 2 + 1 - line.core)
+
+        @pl.loop(0, 2)
+        def _(member):
+            @pl.loop(0, piece // 64)
+            def _(chunk):
+                values = buf[batch, place * 2 + member, rows_at(chunk, 64), :].astype(jnp.float32)
+                there = pl.multiple_of(place * block + member * piece + chunk * 64, 64)
+                normed[batch, pl.ds(there, 64), :] = to_half(normalize(values, gain[0:1, :]))
+
+        kept(batch, place).start()
+
+    def halo(batch, step, peer):
+        there = pl.multiple_of(WINDOW + (step + steps - need) * block, block)
+        return pltpu.make_async_remote_copy(
+            src_ref=pad.at[batch, pl.ds(there, block)],
+            dst_ref=pad.at[batch, rows_at(step, block)],
+            send_sem=halo_send.at[batch, step],
+            recv_sem=halo_recv.at[batch, step],
+            device_id={"seq": peer},
+            device_id_type=MESH,
+        )
+
+    def project(batch, place):
+        here = rows_at(place, block)
+        got = to_half(dot_nn(normed[batch, here, :], w[...]))
+        q_ref[batch, here, :] = got[:, :span]
+        pad[batch, pl.ds(pl.multiple_of(WINDOW + place * block, block), block), :] = got[:, span:]
+
+        @pl.when(has_right & (place >= steps - need))
+        def _():
+            halo(batch, place - (steps - need), seq + 1).start()
+
+    @pl.loop(0, chips)
+    def _(far):
+        pl.when(far > 0)(lambda: spreads[0].relay(far))
+        pl.when(far == chips - 2)(spreads[1].begin)
+        sides(far, lambda place: norm_pair(0, place))
+
+    spreads[1].relay(1)
 
     def have_block(run, member):
         block_share(run, member, seq).wait_recv()
@@ -678,126 +718,22 @@
     w_kept.start()
     gains_kept = pltpu.make_async_copy(gains, gains_ref, gain_keep)
     gains_kept.start()
-
-    pl.loop(0, chips - 1)(lambda far: spread.each(far, use))
-    spread.relay(chips - 1)
-    spread.each(chips - 1, use)
-    spread.each(chips, use)
-    spread.sent()
-    others(seqs, seq, lambda peer: tile_to_seq(peer, seq).wait_send())
-    others(group, own, lambda peer: block_swap(peer, own).wait_send())
-    others(group, own, lambda peer: tiles_to_group(peer, own).wait_send())
-    others(
-        seqs,
-        seq,
-        lambda peer: pl.loop(0, group)(lambda member: block_share(seq, member, peer).wait_send()),
-    )
-    w_kept.wait()
-    gains_kept.wait()
-    units_kept.wait()
-
-    @pl.loop(0, group)
-    def _(slot):
-        for batch in range(batches):
-            kept(slot, batch).wait()
-
-
-def start(seqs, chips, batches, tile, x, weights, unit_weights, collective):
-    rows, width = x.shape
-    group = 2 * chips
-    length = group * rows // batches
-    share = weights[0].shape[0]
-    span = width // group
-    cols = 3 * span
-    wide = unit_weights[0].shape[1]
-    half = jnp.bfloat16
-    return pl.pallas_call(
-        functools.partial(start_kernel, seqs, chips, batches),
-        out_shape=[
-            jax.ShapeDtypeStruct((batches, length, width), half),
-            jax.ShapeDtypeStruct((batches, length, span), half),
-            jax.ShapeDtypeStruct((batches, length, 2 * span), half),
-            jax.ShapeDtypeStruct((group, seqs, 8, 128), jnp.float32),
-            jax.ShapeDtypeStruct((width, cols), half),
-            jax.ShapeDtypeStruct((group, share, 2 * wide // group), half),
-        ],
-        in_specs=[VMEM_SPEC] * 5 + [ANY_SPEC] * 2,
-        out_specs=[ANY_SPEC, VMEM_SPEC, VMEM_SPEC, ANY_SPEC, ANY_SPEC, ANY_SPEC],
-        scratch_shapes=[
-            pltpu.VMEM((share, wide), half),
-            pltpu.VMEM((share, wide), half),
-            pltpu.VMEM((group, share, 2 * wide // group), half),
-            sems(3),
-            pltpu.VMEM((group, share, cols), half),
-            pltpu.VMEM((group, rows, width), half),
-            pltpu.VMEM((group, rows, width), half),
-            pltpu.VMEM((8, width), jnp.float32),
-            pltpu.VMEM((group, seqs, 8, 128), jnp.float32),
-            pltpu.VMEM((width, cols), half),
-            sems(3, group, PARTS),
-            sems(group, PARTS),
-            sems(group, batches),
-            sems(group),
-            sems(seqs, group),
-            sems(seqs, group),
-            sems(seqs),
-            sems(group),
-            sems(seqs),
-            sems(group),
-            pltpu.SemaphoreType.DMA,
-            pltpu.SemaphoreType.DMA,
-        ],
-        compiler_params=comm_params(collective),
-        cost_estimate=cost(2 * group * rows * width * cols, 200 * MIB, group * rows * width * 2),
-        name="start",
-    )(tile, x, *weights, *unit_weights)
-
-
-def attend_kernel(
-    seqs, group, block, q_ref, kv_ref, low_ref, units_ref, out_ref, lse_ref, pad_ref, own_units_ref,
-    pad, vt_ref, halo_send, halo_recv, pad_keep, swap_send, swap_recv, swap_keep,
-):
-    seq = lax.axis_index("seq")
-    batches, length, span = q_ref.shape
-    has_left, has_right = seq > 0, seq < seqs - 1
-    pl.when(has_left)(lambda: signal_seq(seq - 1))
-    pl.when(has_right)(lambda: signal_seq(seq + 1))
-    meet(greet_group(group) + has_left.astype(jnp.int32) + has_right.astype(jnp.int32))
-
-    steps, need = length // block, WINDOW // block
-
-    def halo(batch, step, peer):
-        return pltpu.make_async_remote_copy(
-            src_ref=kv_ref.at[batch, rows_at(step + steps - need, block)],
-            dst_ref=pad.at[batch, rows_at(step, block)],
-            send_sem=halo_send.at[batch, step],
-            recv_sem=halo_recv.at[batch, step],
-            device_id={"seq": peer},
-            device_id_type=MESH,
-        )
-
-    def send_halo(turn):
-        batch, step = turn // need, need - 1 - lax.rem(turn, need)
-        pl.when(has_right)(lambda: halo(batch, step, seq + 1).start())
-
-    def halo_sent(turn):
-        batch, step = turn // need, need - 1 - lax.rem(turn, need)
-        pl.when(has_right)(lambda: halo(batch, step, seq + 1).wait_send())
-
-    send_halo(0)
-    send_halo(1)
-    swap = Swap(group, units_ref, own_units_ref, swap_send, swap_recv, swap_keep)
-    swap.begin()
-    pad[:, WINDOW:, :] = kv_ref[...]
-
-    @pl.when(jnp.logical_not(has_left))
-    def _():
-        pad[:, :WINDOW, :] = jnp.zeros((batches, WINDOW, 2 * span), jnp.bfloat16)
-
-    def kept(batch):
+    pl.loop(0, steps)(lambda place: project(0, place))
+
+    @pl.loop(2, chips)
+    def _(far):
+        spreads[1].relay(far)
+
+    unit_swap.begin()
+
+    @pl.loop(0, chips)
+    def _(far):
+        sides(far, lambda place: norm_pair(1, place))
+        sides(far, lambda place: project(1, place))
+
+    def pad_kept(batch):
         return pltpu.make_async_copy(pad.at[batch], pad_ref.at[batch], pad_keep.at[batch])
 
-    vt = vt_ref
     for batch in range(batches):
         vt[:, WINDOW:] = pad[batch, WINDOW:, span:].T
 
@@ -807,12 +743,9 @@
 
             @pl.when(step < need)
             def _():
-                rows = rows_at(step, block)
+                arrived = rows_at(step, block)
                 pl.when(has_left)(lambda: halo(batch, step, seq).wait_recv())
-                vt[:, rows] = pad[batch, rows, span:].T
-                place = batch * need + need - 1 - step
-                halo_sent(place)
-                pl.when(place + 2 < batches * need)(lambda: send_halo(place + 2))
+                vt[:, arrived] = pad[batch, arrived, span:].T
 
             begin = pl.multiple_of(step * block, block)
             keys = pl.ds(begin, block + WINDOW)
@@ -835,44 +768,102 @@
                 lane = lax.broadcasted_iota(jnp.int32, mixed[0].shape, 0)
                 out_ref[batch, rows, lanes] = to_half(jnp.where(lane < HEAD, mixed[0], mixed[1]).T)
 
+        pad_kept(batch).start()
+
     for batch in range(batches):
-        kept(batch).start()
-    swap.end()
+        spreads[batch].sent()
+    others(seqs, seq, lambda peer: tile_to_seq(peer, seq).wait_send())
+    others(group, own, lambda peer: block_swap(peer, own).wait_send())
+    others(group, own, lambda peer: tiles_to_group(peer, own).wait_send())
+    others(
+        seqs,
+        seq,
+        lambda peer: pl.loop(0, group)(lambda member: block_share(seq, member, peer).wait_send()),
+    )
+
+    @pl.loop(0, need)
+    def _(step):
+        for batch in range(batches):
+            pl.when(has_right)(lambda batch=batch: halo(batch, step, seq).wait_send())
+
+    w_kept.wait()
+    gains_kept.wait()
+    unit_swap.end()
     for batch in range(batches):
-        kept(batch).wait()
-
-
-def attend(seqs, group, query, key_value, low, block, units, collective):
-    batches, length, span = query.shape
+        pad_kept(batch).wait()
+
+        @pl.loop(0, steps)
+        def _(place, batch=batch):
+            kept(batch, place).wait()
+
+
+def start(seqs, chips, batches, block, tile, x, weights, unit_weights, low, collective):
+    rows, width = x.shape
+    group = 2 * chips
+    length = group * rows // batches
+    share = weights[0].shape[0]
+    span = width // group
+    cols = 3 * span
+    wide = unit_weights[0].shape[1]
+    cells = 2 * wide // group
+    piece = rows // batches
     padded = length + WINDOW
-    heads = span // HEAD
     half = jnp.bfloat16
+    need = WINDOW // block
     return pl.pallas_call(
-        functools.partial(attend_kernel, seqs, group, block),
-        in_specs=[VMEM_SPEC, VMEM_SPEC, VMEM_SPEC, ANY_SPEC],
-        out_specs=[VMEM_SPEC, VMEM_SPEC, ANY_SPEC, ANY_SPEC],
+        functools.partial(start_kernel, seqs, chips, batches, block),
         out_shape=[
+            jax.ShapeDtypeStruct((batches, length, width), half),
             jax.ShapeDtypeStruct((batches, length, span), half),
-            jax.ShapeDtypeStruct((batches, heads, length), jnp.float32),
+            jax.ShapeDtypeStruct((batches, length, span), half),
+            jax.ShapeDtypeStruct((batches, span // HEAD, length), jnp.float32),
             jax.ShapeDtypeStruct((batches, padded, 2 * span), half),
-            jax.ShapeDtypeStruct(units.shape, half),
+            jax.ShapeDtypeStruct((group, seqs, 8, 128), jnp.float32),
+            jax.ShapeDtypeStruct((width, cols), half),
+            jax.ShapeDtypeStruct((group, share, cells), half),
         ],
+        in_specs=[VMEM_SPEC] * 5 + [ANY_SPEC] * 2 + [VMEM_SPEC],
+        out_specs=[ANY_SPEC] + [VMEM_SPEC] * 3 + [ANY_SPEC] * 4,
         scratch_shapes=[
+            pltpu.VMEM((share, wide), half),
+            pltpu.VMEM((share, wide), half),
+            pltpu.VMEM((group, share, cells), half),
+            pltpu.VMEM((group, share, cols), half),
+            pltpu.VMEM((batches, group, piece, width), half),
+            pltpu.VMEM((batches, length, width), half),
             pltpu.VMEM((batches, padded, 2 * span), half),
             pltpu.VMEM((span, padded), half),
-            sems(batches, WINDOW // block),
-            sems(batches, WINDOW // block),
+            pltpu.VMEM((8, width), jnp.float32),
+            pltpu.VMEM((group, seqs, 8, 128), jnp.float32),
+            pltpu.VMEM((width, cols), half),
+            sems(2),
+            sems(batches, 3, group, PARTS // 2),
+            sems(batches, group, PARTS // 2),
+            sems(batches, chips),
+            sems(group),
+            sems(seqs, group),
+            sems(seqs, group),
+            sems(seqs),
+            sems(group),
+            sems(seqs),
+            sems(group),
+            pltpu.SemaphoreType.DMA,
+            pltpu.SemaphoreType.DMA,
+            sems(batches, need),
+            sems(batches, need),
             sems(batches),
             sems(group),
             sems(group),
             pltpu.SemaphoreType.DMA,
         ],
-        compiler_params=comm_params(collective),
+        compiler_params=comm_params(collective, 62),
         cost_estimate=cost(
-            8 * batches * length * span * (WINDOW + block), 150 * MIB, units.size * 2
+            2 * group * rows * width * cols + 8 * batches * length * span * (WINDOW + block),
+            300 * MIB,
+            2 * group * rows * width * 2,
         ),
-        name="attend",
-    )(query, key_value, low, units)
+        name="start",
+    )(tile, x, *weights, *unit_weights, low)
 
 
 def branch_kernel(
@@ -1573,7 +1564,6 @@
     meet(greet_group(group) + greet_seq(seqs))
     near, far_off = seq_peers(seqs)
     down = ToPeers(seqs, far_off, down_hbm, down_in, down_send, down_recv)
-    down.begin()
     swap = Swap(group, unit_sums, units, unit_send, unit_recv, unit_keep)
 
     @pl.loop(1, group + 1)
@@ -1764,6 +1754,7 @@
         )
 
     heads_near.arrived()
+    down.begin()
 
     @pl.loop(0, run // 64)
     def _(chunk):
@@ -1967,7 +1958,7 @@
         in_specs=in_specs,
         out_specs=out_specs,
         out_shape=out_shape,
-        compiler_params=pltpu.CompilerParams(vmem_limit_bytes=48 * MIB),
+        compiler_params=pltpu.CompilerParams(vmem_limit_bytes=63 * MIB),
         name="finish",
     )(*arrays, *parts)
 
@@ -2026,10 +2017,6 @@
     both = jnp.stack([gain_attn, gain_mlp]).astype(jnp.float32)
     tile = jnp.where(here[None], jnp.tile(both, (1, fold)), 0.0)
     tile = jnp.pad(tile, ((0, 6), (0, 0)))[None]
-    group_a, query, key_value, gains, w_heads, unit_blocks = start(
-        seqs, chips, batches, tile, x_rows, (w_query, w_key, w_value), (w_gate, w_up), 1
-    )
-    lengths, gains = lax.optimization_barrier((lengths, gains))
     group_start = lax.axis_index("seq") * length
     positions = group_start + jnp.arange(length, dtype=jnp.int32)
     begins = doc_starts(lengths, positions, batches, seq_len)
@@ -2037,13 +2024,12 @@
     block = min(256, length)
     low = jnp.maximum(begins - group_start + WINDOW, at[None, :] + 1) - (at // block * block)[None, :]
     low = low[:, None, :]
-
+    group_a, query, attended, lse, kv_pad, gains, w_heads, unit_own = start(
+        seqs, chips, batches, block, tile, x_rows, (w_query, w_key, w_value), (w_gate, w_up), low, 1
+    )
     gains = gains.transpose(1, 0, 2, 3).reshape(devices // fold, fold, 8, 128).sum(axis=1)
     gain_one = gains[:, 0].reshape(width)
     gain_two = gains[:, 1].reshape(width)
-    attended, lse, kv_pad, unit_own = attend(
-        seqs, group, query, key_value, low, block, unit_blocks, 2
-    )
     middle, normed_b, group_d, w_units = branch_sum(
         seqs, chips, attended, wo_part, cot_rows, unit_own.reshape(group * share, -1),
         x_rows, gain_two[None], 3,

time: 716 us -> 717 us (level)
  local copies, waits for them, and re-layouts: 12.3 us -> 3.49 us
    pallas_call x2 -> x1, Pallas kernels: 159 us -> 137 us  [start(): pl.pallas_call(functools.partial(start_kernel, seqs, chips, batches, bloc...]
    pallas_call x1, Pallas kernels: 106 us -> 121 us  [branch_sum(): pl.pallas_call(functools.partial(branch_kernel, seqs, chips), out_shape=[...]
    unnamed x18 -> x0, local copies, waits for them, and re-layouts: 8.79 us -> none
    pallas_call x1, Pallas kernels: 159 us -> 168 us  [attention_back(): pl.pallas_call(functools.partial(attention_back_kernel, seqs, chips, bloc...]
  transfers between devices with their start and end apart: 2 -> 2, of which waited for: 0 -> 0; matrix products, arithmetic and copies ran while one was open for 1% -> 1% of each run, Pallas kernels for 38% -> 37%
where the time goes in v11:
time: 717 us; the launch traced here: 704 us
  Pallas kernels  681 us (95%)
  between operations  14.6 us (2%)
    pallas_call x1, Pallas kernels, attention_back(): pl.pallas_call(functools.partial(attention_back_kernel, seqs, chips, bloc...  168 us
    pallas_call x1, Pallas kernels, feed_forward(): pl.pallas_call(functools.partial(feed_kernel, seqs, chips, batches), out_...  145 us
    pallas_call x1, Pallas kernels, start(): pl.pallas_call(functools.partial(start_kernel, seqs, chips, batches, bloc...  137 us
    pallas_call x1, Pallas kernels, branch_sum(): pl.pallas_call(functools.partial(branch_kernel, seqs, chips), out_shape=[...  121 us
    pallas_call x1, Pallas kernels, branch_back(): pl.pallas_call(functools.partial(branch_back_kernel, seqs, chips, batches...  102 us
  transfers between devices with their start and end apart: 2, of which 0 were waited for; matrix products, arithmetic and copies ran while one was open for 1% of the time, Pallas kernels for 37%

profile of v11, /device:TPU:9, one launch (start us, length us, event | category | flops | bytes accessed | tf_op | source)
XLA Modules:
  0.0 704.0 jit_solution(13511870133470279540)
XLA Ops:
  7.2 0.0 all-gather.3.cloned.1.call-start
  7.2 0.7 all-gather.3.cloned.1.call-update
  7.9 0.0 all-gather.5.cloned.1.call-start
  8.0 0.7 all-gather.5.cloned.1.call-update
  8.7 0.7 maximum_convert_fusion
  9.4 0.1 tile.10
  9.4 0.8 reduce_window_sum.11
  10.3 0.7 sub.46
  11.0 0.6 pad_bitcast_fusion.tile_ref
  11.6 0.1 select_reduce_fusion
  11.7 0.6 maximum_subtract_fusion.low_ref
  12.3 137.0 %start.1 = (bf16[2,1024,2048]{2,1,0:T(8,128)(2,1)}, bf16[2,1024,256]{2,1,0:T(8,128)(2,1)}, bf16[2,1024,256]{2,1,0:T(8,128)(2,1)}, f32[2,4,1024]{2,1,0:T(4,128)},...) custom-call(f32[1,8,128]{2,1,0:T(8,128)} %pad_bitcast_fusion.tile_re, ...), custom_call_target="tpu_custom_call" | custom-call | flops 11811160064 | bytes 314572800 | tf_op jit(solution)/shard_map/start/pallas_call | solution.py:813
  149.4 0.9 copy.25
  150.3 0.6 slice_bitcast_fusion
  150.9 0.0 all-gather.3.cloned.1.call-done.w_ref
  150.9 121.2 %branch_sum.1 = (f32[256,2048]{1,0:T(8,128)}, bf16[256,2048]{1,0:T(8,128)(2,1)}, bf16[8,256,2048]{2,1,0:T(8,128)(2,1)}, bf16[4,512,2048]{2,1,0:T(8,128)(2,1)}) custom-call(bf16[2,1024,256]{2,1,0:T(8,128)(2,1)} %get-tuple-element.54.a_ref.att_ref, bf16[256,2048]{1,0:T(8,128)(2,1)} %all-gather.3.cloned.1.call-done.w_ref, bf16[256,2048]{1,0:T(8,128)(2,1)} %bitcast.26, ...), custom_call_target="tpu_custom_call" | custom-call | flops 2147483648 | bytes 262144000 | tf_op jit(solution)/shard_map/branch_sum/pallas_call | solution.py:917
  272.2 0.0 all-gather.5.cloned.1.call-done.wd_hbm
  272.2 144.7 %feed_forward.1 = (f32[256,2048]{1,0:T(8,128)}, bf16[256,2048]{1,0:T(8,128)(2,1)}, f32[8,2048]{1,0:T(8,128)}, bf16[2048,1024]{1,0:T(8,128)(2,1)}, bf16[2048,2048...) custom-call(bf16[256,2048]{1,0:T(8,128)(2,1)} %get-tuple-element.57.x_ref, bf16[2048,2048]{1,0:T(8,128)(2,1)} %bitcast.33, ...), custom_call_target="tpu_custom_call" | custom-call | flops 60129542144 | bytes 419430400 | tf_op jit(solution)/shard_map/feed_forward/pallas_call | solution.py:1292
  416.9 102.4 %branch_back.1 = (bf16[2,1024,256]{2,1,0:T(8,128)(2,1)}, bf16[256,2048]{1,0:T(8,128)(2,1)}, bf16[256,2048]{1,0:T(8,128)(2,1)}, bf16[2,256,2048]{2,1,0:T(8,128)(2...) custom-call(bf16[256,2048]{1,0:T(8,128)(2,1)} %get-tuple-element.61.x_ref, ...), custom_call_target="tpu_custom_call" | custom-call | flops 21474836480 | bytes 262144000 | tf_op jit(solution)/shard_map/branch_back/pallas_call | solution.py:1461
  519.3 167.7 %attention_back.1 = (f32[256,2048]{1,0:T(8,128)}, bf16[64,2048]{1,0:T(8,128)(2,1)}, bf16[64,2048]{1,0:T(8,128)(2,1)}, bf16[64,2048]{1,0:T(8,128)(2,1)}, f32[64,2...) custom-call(bf16[2,1024,256]{2,1,0:T(8,128)(2,1)} %get-tuple-element, ...), custom_call_target="tpu_custom_call" | custom-call | flops 26306674688 | bytes 419430400 | tf_op jit(solution)/shard_map/attention_back/pallas_call | solution.py:1851
  687.0 0.7 slice.17
  687.7 0.1 constant_dynamic-slice_fusion
  687.8 0.5 slice_bitcast_fusion.2
  688.3 8.4 %finish.1 = (bf16[256,2048]{1,0:T(8,128)(2,1)}, f32[256,2048]{1,0:T(8,128)}, f32[64,2048]{1,0:T(8,128)}, f32[64,2048]{1,0:T(8,128)}, f32[64,2048]{1,0:T(8,128)},...) custom-call(bf16[256,2048]{1,0:T(8,128)(2,1)} %get-tuple-element.64.refs_0_, ...), custom_call_target="tpu_custom_call" | custom-call | tf_op jit(solution)/shard_map/finish/pallas_call | solution.py:1955
  (7 shorter events, 0.0 us)
Async XLA Ops:
  7.2 143.7 %all-gather.3.cloned.1.call-start = ((), (), s32[]{:S(2)}) async-start(), calls=%async_computation | async-start | bytes 1310720 | tf_op jit(solution)/shard_map/all_gather | solution.py:2008
  7.9 264.3 %all-gather.5.cloned.1.call-start = ((), (), s32[]{:S(2)}) async-start(), calls=%async_computation.1 | async-start | bytes 5242880 | tf_op jit(solution)/shard_map/all_gather | solution.py:2006
Sparse Core Ops, SparseCore 0:
  9.9 35.2 all-gather.2
  47.0 83.9 all-gather.4

commit v12 on v11

--- a/solution.py
+++ b/solution.py
@@ -474,6 +474,16 @@
     def end(self):
         self.arrived()
         self.sent()
+
+
+def load_halves(halves, target, load):
+    copies = []
+    rows = halves[0].shape[1]
+    for index, half in enumerate(halves):
+        for place in range(half.shape[0]):
+            there = pl.ds((2 * place + index) * rows, rows)
+            copies.append(pltpu.make_async_copy(half.at[place], target.at[there], load.at[index, place]))
+    return copies
 
 
 VMEM_SPEC = pl.BlockSpec(memory_space=pltpu.VMEM)
@@ -538,12 +548,13 @@
 
 
 def start_kernel(
-    seqs, chips, batches, block, tile_ref, x_ref, wq_ref, wk_ref, wv_ref, gate_hbm, up_hbm, low_ref,
-    g_ref, q_ref, out_ref, lse_ref, pad_ref, gains_ref, w_out_ref, own_units_ref,
+    seqs, chips, batches, block, tile_ref, x_ref, wq_ref, wk_ref, wv_ref, gate_hbm, up_hbm, down_hbm, low_ref,
+    g_ref, q_ref, out_ref, lse_ref, pad_ref, gains_ref, w_out_ref, own_units_ref, wd_ref,
     gate, up, units, blocks_ref, buf, normed, pad, vt, gain, gains, w,
     unit_sem, send, recv, keep, swap_send, share_send, w_recv,
     tile_send, tile_across, tile_recv, tile_back, w_keep, gain_keep,
     halo_send, halo_recv, pad_keep, unit_send, unit_recv, unit_keep,
+    down_send, down_recv, down_keep,
 ):
     line = Line(chips)
     group = 2 * chips
@@ -615,6 +626,10 @@
         pl.loop(1, count)(lambda ahead: act(lax.rem(me + ahead, count)))
 
     others(seqs, seq, lambda peer: tile_to_seq(peer, seq).start())
+    down = Share(
+        seqs, down_hbm.at[pl.ds(0, wd_ref.shape[1])], wd_ref, down_send, down_recv, down_keep
+    )
+    down.begin()
     others(group, own, lambda peer: block_swap(peer, own).start())
     spreads = [
         Spread(line, x_ref.at[pl.ds(batch * piece, piece)], buf.at[batch], send.at[batch], recv.at[batch])
@@ -648,6 +663,7 @@
         others(seqs, seq, lambda peer: block_share(seq, member, peer).start())
 
     others(group, own, pass_block)
+    down.pass_on()
     others(group, own, lambda peer: tiles_to_group(peer, peer).wait_recv())
     for column in range(width // 128):
         total = 0.0
@@ -789,6 +805,7 @@
     w_kept.wait()
     gains_kept.wait()
     unit_swap.end()
+    down.end()
     for batch in range(batches):
         pad_kept(batch).wait()
 
@@ -797,7 +814,7 @@
             kept(batch, place).wait()
 
 
-def start(seqs, chips, batches, block, tile, x, weights, unit_weights, low, collective):
+def start(seqs, chips, batches, block, tile, x, weights, unit_weights, down, low, collective):
     rows, width = x.shape
     group = 2 * chips
     length = group * rows // batches
@@ -821,9 +838,10 @@
             jax.ShapeDtypeStruct((group, seqs, 8, 128), jnp.float32),
             jax.ShapeDtypeStruct((width, cols), half),
             jax.ShapeDtypeStruct((group, share, cells), half),
+            jax.ShapeDtypeStruct((seqs, down.shape[0] // 2, width), half),
         ],
-        in_specs=[VMEM_SPEC] * 5 + [ANY_SPEC] * 2 + [VMEM_SPEC],
-        out_specs=[ANY_SPEC] + [VMEM_SPEC] * 3 + [ANY_SPEC] * 4,
+        in_specs=[VMEM_SPEC] * 5 + [ANY_SPEC] * 3 + [VMEM_SPEC],
+        out_specs=[ANY_SPEC] + [VMEM_SPEC] * 3 + [ANY_SPEC] * 5,
         scratch_shapes=[
             pltpu.VMEM((share, wide), half),
             pltpu.VMEM((share, wide), half),
@@ -855,6 +873,9 @@
             sems(group),
             sems(group),
             pltpu.SemaphoreType.DMA,
+            sems(seqs, 2),
+            sems(seqs, 2),
+            pltpu.SemaphoreType.DMA,
         ],
         compiler_params=comm_params(collective, 62),
         cost_estimate=cost(
@@ -863,13 +884,15 @@
             2 * group * rows * width * 2,
         ),
         name="start",
-    )(tile, x, *weights, *unit_weights, low)
+    )(tile, x, *weights, *unit_weights, down, low)
 
 
 def branch_kernel(
-    seqs, chips, a_ref, w_ref, d_ref, units_ref, x_ref, gain_ref, middle_ref, normed_ref, gd_ref, w_units_ref,
+    seqs, chips, a_ref, w_ref, d_ref, units_ref, down_hbm, x_ref, gain_ref,
+    middle_ref, normed_ref, gd_ref, w_units_ref, wd_ref,
     out_ref, acc, cross_out, line_out, cross_in, line_in, sum_send, sum_recv,
     send, recv, d_keep, share_send, share_recv, share_keep,
+    down_send, down_recv, down_keep,
 ):
     line = Line(chips)
     rows = out_ref.shape[0]
@@ -884,7 +907,10 @@
     spread = Spread(line, d_ref, gd_ref, send, recv)
     units = Share(seqs, units_ref, w_units_ref, share_send, share_recv, share_keep)
     d_kept = pltpu.make_async_copy(d_ref, gd_ref.at[line.own], d_keep)
+    half = wd_ref.shape[1]
+    down = Share(seqs, down_hbm.at[pl.ds(half, half)], wd_ref, down_send, down_recv, down_keep)
     units.begin()
+    down.begin()
     spread.begin()
     d_kept.start()
 
@@ -894,7 +920,11 @@
             pl.when(step < chips - 1)(lambda: spread.relay_part(step + 1, tile))
 
         reduce.level(chips - 1 - step, also)
-        pl.when(step == chips - 2)(units.pass_on)
+
+        @pl.when(step == chips - 2)
+        def _():
+            units.pass_on()
+            down.pass_on()
 
     @pl.loop(0, rows // 32)
     def _(chunk):
@@ -908,9 +938,10 @@
     reduce.sent()
     d_kept.wait()
     units.end()
-
-
-def branch_sum(seqs, chips, a, w, d_rows, units, x, gain, collective):
+    down.end()
+
+
+def branch_sum(seqs, chips, a, w, d_rows, units, down, x, gain, collective):
     rows, width = d_rows.shape
     group = 2 * chips
     half = jnp.bfloat16
@@ -921,19 +952,20 @@
             jax.ShapeDtypeStruct((rows, width), half),
             jax.ShapeDtypeStruct((group, rows, width), half),
             jax.ShapeDtypeStruct((seqs,) + units.shape, half),
+            jax.ShapeDtypeStruct((seqs, down.shape[0] // 2, width), half),
         ],
-        in_specs=[VMEM_SPEC, VMEM_SPEC, ANY_SPEC, ANY_SPEC, VMEM_SPEC, VMEM_SPEC],
-        out_specs=[VMEM_SPEC, VMEM_SPEC, ANY_SPEC, ANY_SPEC],
+        in_specs=[VMEM_SPEC, VMEM_SPEC] + [ANY_SPEC] * 3 + [VMEM_SPEC, VMEM_SPEC],
+        out_specs=[VMEM_SPEC, VMEM_SPEC] + [ANY_SPEC] * 3,
         scratch_shapes=[pltpu.VMEM((rows, width), jnp.float32)]
         + Reduce.scratch(chips, rows, width)
         + [sems(3, group, PARTS), sems(group, PARTS), pltpu.SemaphoreType.DMA]
-        + [sems(seqs, 2), sems(seqs, 2), pltpu.SemaphoreType.DMA],
+        + [sems(seqs, 2), sems(seqs, 2), pltpu.SemaphoreType.DMA] * 2,
         compiler_params=comm_params(collective),
         cost_estimate=cost(
             2 * group * rows * width * w.shape[0], 250 * MIB, 3 * group * rows * width * 2
         ),
         name="branch_sum",
-    )(a, w, d_rows, units, x, gain)
+    )(a, w, d_rows, units, down, x, gain)
 
 
 class PairReduce:
@@ -1061,10 +1093,10 @@
 
 
 def feed_kernel(
-    seqs, chips, batches, x_ref, w_hbm, wd_hbm, gd_hbm, v_ref, cot_ref, gain_ref,
+    seqs, chips, batches, x_ref, w_hbm, wd_one, wd_two, gd_hbm, v_ref, cot_ref, gain_ref,
     dm_ref, db_ref, gain_grad_ref, hidden_hbm, grad_hbm, grad_in,
     buf, d_buf, h_buf, w_ref, wd_ref, d_ref, tiles, totals, acc, keep,
-    load, d_sem, h_sem, tile_sem, send, recv, part_send, part_recv, *sums,
+    load, d_sem, h_sem, tile_sem, send, recv, part_send, part_recv, wd_load, *sums,
 ):
     line = Line(chips)
     rows, width = x_ref.shape
@@ -1075,8 +1107,7 @@
     block = tiles.shape[1]
     loads = [
         pltpu.make_async_copy(w_hbm, w_ref, load.at[0]),
-        pltpu.make_async_copy(wd_hbm, wd_ref, load.at[1]),
-    ]
+    ] + load_halves([wd_one, wd_two], wd_ref, wd_load)
     for item in loads:
         item.start()
     meet(line.greet() + greet_seq(seqs))
@@ -1182,7 +1213,7 @@
     seq = lax.axis_index("seq")
 
     near, far_off = seq_peers(seqs)
-    soon = len(near)
+    soon = seqs - 1
     order = [peer * 2 for peer in near] + [peer * 2 for peer in far_off] + [seq * 2]
     order = order + [peer * 2 + 1 for peer in near] + [peer * 2 + 1 for peer in far_off] + [seq * 2 + 1]
 
@@ -1198,7 +1229,7 @@
             tiles.at[slot], grad_hbm.at[rows_at(tile_at(turn), block)], tile_sem.at[slot]
         )
 
-    parts = ToPeers(seqs, near, grad_hbm, grad_in, part_send, part_recv)
+    parts = ToPeers(seqs, near + far_off, grad_hbm, grad_in, part_send, part_recv)
 
     def leave(turn):
         grad_stored(turn).wait()
@@ -1282,10 +1313,10 @@
     parts.end()
 
 
-def feed_forward(seqs, chips, batches, x, w, wd, group_d, middle, cot, gain, collective):
+def feed_forward(seqs, chips, batches, x, w, wd_halves, group_d, middle, cot, gain, collective):
     rows, width = x.shape
     group = 2 * chips
-    units = wd.shape[0]
+    units = w.shape[1] // 2
     piece = rows // batches
     block = width // seqs // 2
     half = jnp.bfloat16
@@ -1297,16 +1328,16 @@
             jax.ShapeDtypeStruct((8, width), jnp.float32),
             jax.ShapeDtypeStruct((group * rows, units), half),
             jax.ShapeDtypeStruct((width, 2 * units), half),
-            jax.ShapeDtypeStruct((near_count(seqs), block, 2 * units), half),
+            jax.ShapeDtypeStruct((seqs - 1, block, 2 * units), half),
         ],
-        in_specs=[VMEM_SPEC] + [ANY_SPEC] * 3 + [VMEM_SPEC] * 3,
+        in_specs=[VMEM_SPEC] + [ANY_SPEC] * 4 + [VMEM_SPEC] * 3,
         out_specs=[VMEM_SPEC] * 3 + [ANY_SPEC] * 3,
         scratch_shapes=[
             pltpu.VMEM((batches, group, piece, width), half),
             pltpu.VMEM((2, 2 * piece, width), half),
             pltpu.VMEM((2 * piece, units), half),
             pltpu.VMEM(w.shape, half),
-            pltpu.VMEM(wd.shape, half),
+            pltpu.VMEM((units, width), half),
             pltpu.VMEM((batches, group * piece, 2 * units), half),
             pltpu.VMEM((2, block, 2 * units), half),
             pltpu.VMEM((batches, piece, width), jnp.float32),
@@ -1320,6 +1351,7 @@
             sems(batches, group, PARTS // 2),
             sems(seqs),
             sems(seqs),
+            sems(2, seqs),
         ]
         + PairReduce.scratch(chips, piece, width) * batches,
         compiler_params=comm_params(collective, 63),
@@ -1327,14 +1359,14 @@
             14 * group * rows * width * units, 400 * MIB, 2 * group * rows * width * 2
         ),
         name="feed_forward",
-    )(x, w, wd, group_d, middle, cot, gain)
+    )(x, w, *wd_halves, group_d, middle, cot, gain)
 
 
 def branch_back_kernel(
-    seqs, chips, batches, x_ref, w_ref, att_ref, middle_ref, hidden_hbm, wd_hbm, units_hbm, gd_hbm,
-    d_ref, layer_ref, out_grad_ref, half_in, whole_in, down_hbm, down_in,
+    seqs, chips, batches, x_ref, w_ref, att_ref, middle_ref, hidden_hbm, wd_one, wd_two, units_hbm, gd_hbm,
+    d_ref, layer_ref, out_grad_ref, half_in, down_hbm, down_in,
     out_ref, buf, hidden_ref, wd_ref, grad_acc, rights, tiles, send, recv, load, right_sem, tile_sem,
-    part_send, part_recv, down_send, down_recv, down_keep, acc, cross_out, line_out, cross_in, line_in, sum_send, sum_recv,
+    part_send, part_recv, wd_load, down_send, down_recv, down_keep, acc, cross_out, line_out, cross_in, line_in, sum_send, sum_recv,
 ):
     line = Line(chips)
     rows = x_ref.shape[0]
@@ -1342,8 +1374,7 @@
     width = x_ref.shape[1]
     loads = [
         pltpu.make_async_copy(hidden_hbm, hidden_ref, load.at[0]),
-        pltpu.make_async_copy(wd_hbm, wd_ref, load.at[1]),
-    ]
+    ] + load_halves([wd_one, wd_two], wd_ref, wd_load)
     for item in loads:
         item.start()
 
@@ -1382,16 +1413,13 @@
     right(0).start()
     meet(line.greet() + greet_seq(seqs))
     near, far_off = seq_peers(seqs)
-    soon = len(near)
-    halves = ToPeers(
-        seqs, near, units_hbm, half_in, part_send.at[0], part_recv.at[0], half_in.shape[1]
-    )
-    wholes = ToPeers(seqs, far_off, units_hbm, whole_in, part_send.at[1], part_recv.at[1])
-    down = ToPeers(
-        seqs, near, down_hbm, down_in.at[pl.ds(0, soon)], down_send, down_recv
-    )
+    peers = near + far_off
+    halves = ToPeers(seqs, peers, units_hbm, half_in, part_send, part_recv, half_in.shape[1])
+    down = ToPeers(seqs, peers, down_hbm, down_in.at[pl.ds(0, seqs - 1)], down_send, down_recv)
     down_kept = pltpu.make_async_copy(
-        down_hbm.at[rows_at(lax.axis_index("seq"), down_in.shape[1])], down_in.at[soon], down_keep
+        down_hbm.at[rows_at(lax.axis_index("seq"), down_in.shape[1])],
+        down_in.at[seqs - 1],
+        down_keep,
     )
     spread = Spread(line, x_ref, buf, send, recv)
     reduce = Reduce(
@@ -1399,7 +1427,6 @@
     )
     spread.begin()
     halves.begin()
-    wholes.begin()
     buf[line.own] = x_ref[...]
     grad_acc[...] = jnp.zeros_like(grad_acc)
 
@@ -1445,46 +1472,46 @@
     spread.sent()
     reduce.sent()
     halves.end()
-    wholes.end()
     down.end()
     down_kept.wait()
 
 
-def branch_back(seqs, chips, batches, x, w, attended, middle, hidden, wd, unit_part, group_d, collective):
+def branch_back(seqs, chips, batches, x, w, attended, middle, hidden, wd_halves, unit_part, group_d, collective):
     rows, width = x.shape
     group = 2 * chips
     length = group * rows // batches
     span = w.shape[0]
     half = jnp.bfloat16
     part = 256 if group * rows <= 2048 else 128
-    near, run = near_count(seqs), width // seqs
+    run = width // seqs
+    units = hidden.shape[1]
     return pl.pallas_call(
         functools.partial(branch_back_kernel, seqs, chips, batches),
         out_shape=[
             jax.ShapeDtypeStruct((batches, length, span), half),
             jax.ShapeDtypeStruct((rows, width), half),
             jax.ShapeDtypeStruct((span, width), half),
-            jax.ShapeDtypeStruct((near, run // 2, unit_part.shape[1]), half),
-            jax.ShapeDtypeStruct((seqs - 1 - near, run, unit_part.shape[1]), half),
-            jax.ShapeDtypeStruct((wd.shape[0], width), half),
-            jax.ShapeDtypeStruct((near + 1, wd.shape[0] // seqs, width), half),
+            jax.ShapeDtypeStruct((seqs - 1, run // 2, unit_part.shape[1]), half),
+            jax.ShapeDtypeStruct((units, width), half),
+            jax.ShapeDtypeStruct((seqs, units // seqs, width), half),
         ],
-        in_specs=[VMEM_SPEC] * 4 + [ANY_SPEC] * 4,
-        out_specs=[VMEM_SPEC, VMEM_SPEC, VMEM_SPEC, ANY_SPEC, ANY_SPEC, ANY_SPEC, ANY_SPEC],
+        in_specs=[VMEM_SPEC] * 4 + [ANY_SPEC] * 5,
+        out_specs=[VMEM_SPEC] * 3 + [ANY_SPEC] * 3,
         scratch_shapes=[
             pltpu.VMEM((rows, width), jnp.float32),
             pltpu.VMEM((group, rows, width), half),
             pltpu.VMEM(hidden.shape, half),
-            pltpu.VMEM(wd.shape, half),
+            pltpu.VMEM((units, width), half),
             pltpu.VMEM((span, width), jnp.float32),
             pltpu.VMEM((2, group * rows, part), half),
-            pltpu.VMEM((2, wd.shape[0], part), half),
+            pltpu.VMEM((2, units, part), half),
             sems(3, group, PARTS),
             sems(group, PARTS),
             sems(2),
             sems(2),
             sems(2),
-            sems(2, seqs),
+            sems(seqs),
+            sems(seqs),
             sems(2, seqs),
             sems(seqs),
             sems(seqs),
@@ -1493,19 +1520,19 @@
         + Reduce.scratch(chips, rows, width),
         compiler_params=comm_params(collective, 62),
         cost_estimate=cost(
-            2 * group * rows * width * (2 * span + 2 * wd.shape[0]),
+            2 * group * rows * width * (2 * span + 2 * units),
             250 * MIB,
             2 * group * rows * width * 2,
         ),
         name="branch_back",
-    )(x, w, attended, middle, hidden, wd, unit_part, group_d.reshape(group * rows, width))
+    )(x, w, attended, middle, hidden, *wd_halves, unit_part, group_d.reshape(group * rows, width))
 
 
 def attention_back_kernel(
-    seqs, chips, block, q_ref, pad_ref, low_ref, lse_ref, d_ref, part_hbm, in_one, in_two, in_far,
-    w_ref, g_hbm, v_ref, dm_hbm, gain_ref, mlp_gain_ref, out_ref, down_hbm,
-    grad_hbm, wq_ref, wk_ref, wv_ref, wo_hbm, tile_ref, gate_hbm, up_hbm, down_in,
-    grad_ref, wo_ref, gate_ref, up_ref, result_sem, down_send, down_recv,
+    seqs, chips, block, q_ref, pad_ref, low_ref, lse_ref, d_ref, part_hbm, in_one, in_two,
+    w_ref, g_hbm, v_ref, dm_hbm, gain_ref, mlp_gain_ref, out_ref,
+    grad_hbm, wq_ref, wk_ref, wv_ref, wo_hbm, tile_ref, gate_hbm, up_hbm,
+    grad_ref, wo_ref, gate_ref, up_ref, result_sem,
     dk, dv, kt, heads, back_out, back_in, unit_parts, unit_sums, units, lefts, parts, sums, cols, out_in,
     totals, gain_acc, gain_out, gain_in, gain_sum, gain_back, acc, keep,
     halo_send, halo_recv, unit_load, unit_send, unit_recv, unit_keep, dm_load, left_sem,
@@ -1539,31 +1566,21 @@
     def load_units(turn):
         member = lax.rem(own + turn, group)
         unit_loaded(turn, 0, part_hbm.at[rows_at(seq * group + member, share)]).start()
-        soon = in_one.shape[0]
         for index in range(seqs - 1):
 
-            def fetch(source, index=index):
-                unit_loaded(turn, index + 1, source).start()
-
-            if index < soon:
-
-                @pl.when(member < chips)
-                def _(index=index, fetch=fetch):
-                    fetch(in_one.at[index, rows_at(member, share)])
-
-                @pl.when(member >= chips)
-                def _(index=index, fetch=fetch):
-                    fetch(in_two.at[index, rows_at(member - chips, share)])
-
-            else:
-                fetch(in_far.at[index - soon, rows_at(member, share)])
+            @pl.when(member < chips)
+            def _(index=index):
+                unit_loaded(turn, index + 1, in_one.at[index, rows_at(member, share)]).start()
+
+            @pl.when(member >= chips)
+            def _(index=index):
+                unit_loaded(turn, index + 1, in_two.at[index, rows_at(member - chips, share)]).start()
 
     load_units(1)
     dm_loaded = pltpu.make_async_copy(dm_hbm, grad_ref, dm_load)
     dm_loaded.start()
     meet(greet_group(group) + greet_seq(seqs))
     near, far_off = seq_peers(seqs)
-    down = ToPeers(seqs, far_off, down_hbm, down_in, down_send, down_recv)
     swap = Swap(group, unit_sums, units, unit_send, unit_recv, unit_keep)
 
     @pl.loop(1, group + 1)
@@ -1754,7 +1771,6 @@
         )
 
     heads_near.arrived()
-    down.begin()
 
     @pl.loop(0, run // 64)
     def _(chunk):
@@ -1825,15 +1841,14 @@
             pl.loop(0, need)(lambda step: halo(batch, step, seq).wait_send())
 
     heads_near.sent()
-    down.end()
     others(group, own, lambda peer: gain_group(peer, own).wait_send())
     others(group, own, lambda peer: block_swap(peer, own).wait_send())
     others(seqs, seq, lambda peer: gain_seq(peer, seq).wait_send())
 
 
 def attention_back(
-    seqs, chips, block, query, kv_pad, low, lse, d_att, part_own, parts_one, parts_two, parts_far, w, group_a,
-    x, d_middle, gain, mlp_gain, out_part, down, collective,
+    seqs, chips, block, query, kv_pad, low, lse, d_att, part_own, parts_one, parts_two, w, group_a, x,
+    d_middle, gain, mlp_gain, out_part, collective,
 ):
     batches, length, span = query.shape
     padded = kv_pad.shape[1]
@@ -1859,23 +1874,19 @@
             jax.ShapeDtypeStruct((8, 128), wide),
             jax.ShapeDtypeStruct((share, cells // 2 * group), half),
             jax.ShapeDtypeStruct((share, cells // 2 * group), half),
-            jax.ShapeDtypeStruct((seqs - 1 - near_count(seqs), down.shape[0] // seqs, width), half),
         ],
         in_specs=[VMEM_SPEC] * 5
-        + [ANY_SPEC] * 4
+        + [ANY_SPEC] * 3
         + [VMEM_SPEC, ANY_SPEC, VMEM_SPEC, ANY_SPEC]
-        + [VMEM_SPEC] * 3
-        + [ANY_SPEC],
+        + [VMEM_SPEC] * 3,
         out_specs=[ANY_SPEC, VMEM_SPEC, VMEM_SPEC, VMEM_SPEC, ANY_SPEC, VMEM_SPEC]
-        + [ANY_SPEC] * 3,
+        + [ANY_SPEC] * 2,
         scratch_shapes=[
             pltpu.VMEM((rows, width), wide),
             pltpu.VMEM((out_rows, width), wide),
             pltpu.VMEM((share, cells // 2 * group), half),
             pltpu.VMEM((share, cells // 2 * group), half),
             sems(4),
-            sems(seqs),
-            sems(seqs),
             pltpu.VMEM((padded, span), wide),
             pltpu.VMEM((padded, span), wide),
             pltpu.VMEM((span, padded), half),
@@ -1926,8 +1937,8 @@
         ),
         name="attention_back",
     )(
-        query, kv_pad, low, lse, d_att, part_own, parts_one, parts_two, parts_far, w, group_a, x,
-        d_middle, gain, mlp_gain, out_part, down,
+        query, kv_pad, low, lse, d_att, part_own, parts_one, parts_two, w, group_a, x,
+        d_middle, gain, mlp_gain, out_part,
     )
 
 
@@ -2003,7 +2014,6 @@
 
     x_rows = tokens.reshape(rows, width)
     cot_rows = cotangent.reshape(rows, width)
-    wd_part = lax.all_gather(w_down, "seq", axis=0, tiled=True)
     if aligned:
         wo_part = lax.all_gather(w_out, "seq", axis=0, tiled=True)
     else:
@@ -2024,24 +2034,25 @@
     block = min(256, length)
     low = jnp.maximum(begins - group_start + WINDOW, at[None, :] + 1) - (at // block * block)[None, :]
     low = low[:, None, :]
-    group_a, query, attended, lse, kv_pad, gains, w_heads, unit_own = start(
-        seqs, chips, batches, block, tile, x_rows, (w_query, w_key, w_value), (w_gate, w_up), low, 1
+    group_a, query, attended, lse, kv_pad, gains, w_heads, unit_own, wd_one = start(
+        seqs, chips, batches, block, tile, x_rows, (w_query, w_key, w_value), (w_gate, w_up), w_down,
+        low, 1,
     )
     gains = gains.transpose(1, 0, 2, 3).reshape(devices // fold, fold, 8, 128).sum(axis=1)
     gain_one = gains[:, 0].reshape(width)
     gain_two = gains[:, 1].reshape(width)
-    middle, normed_b, group_d, w_units = branch_sum(
-        seqs, chips, attended, wo_part, cot_rows, unit_own.reshape(group * share, -1),
+    middle, normed_b, group_d, w_units, wd_two = branch_sum(
+        seqs, chips, attended, wo_part, cot_rows, unit_own.reshape(group * share, -1), w_down,
         x_rows, gain_two[None], 3,
     )
     w_units = w_units.reshape(width, -1)
     d_middle, d_branch, mlp_gain_part, hidden, unit_part, unit_one = feed_forward(
-        seqs, chips, batches, normed_b, w_units, wd_part, group_d, middle, cot_rows,
+        seqs, chips, batches, normed_b, w_units, (wd_one, wd_two), group_d, middle, cot_rows,
         gain_two[None], 4,
     )
-    d_attended, layer_out, out_part, unit_two, unit_far, down_part, down_near = branch_back(
-        seqs, chips, batches, d_branch, wo_part, attended, middle, hidden, wd_part, unit_part,
-        group_d, 5,
+    d_attended, layer_out, out_part, unit_two, _, down_in = branch_back(
+        seqs, chips, batches, d_branch, wo_part, attended, middle, hidden, (wd_one, wd_two),
+        unit_part, group_d, 5,
     )
     if not aligned:
         whole = lax.dynamic_update_slice_in_dim(
@@ -2049,19 +2060,16 @@
         )
         out_part = lax.psum(whole, "fsdp").reshape(seqs, group, share, width)
         out_part = lax.dynamic_slice_in_dim(out_part, member, 1, 1).reshape(seqs * share, width)
-    (
-        input_grad, wq_grad, wk_grad, wv_grad, wo_grad, gain_tile, gate_grad, up_grad, down_far,
-    ) = attention_back(
+    input_grad, wq_grad, wk_grad, wv_grad, wo_grad, gain_tile, gate_grad, up_grad = attention_back(
         seqs, chips, block, query, kv_pad, low, lse, d_attended, unit_part, unit_one, unit_two,
-        unit_far, w_heads, group_a, x_rows, d_middle, gain_one[None], mlp_gain_part, out_part,
-        down_part, 6,
+        w_heads, group_a, x_rows, d_middle, gain_one[None], mlp_gain_part, out_part, 6,
     )
     gain_grads = lax.dynamic_slice_in_dim(gain_tile[:2], lax.rem(device, fold) * share, share, 1)
     wide = jnp.float32
     (layer_out, input_grad, wq_grad, wk_grad, wv_grad, wo_grad, gate_grad, up_grad, down_grad) = finish(
         share // 16,
         [layer_out, input_grad, wq_grad, wk_grad, wv_grad, wo_grad, gate_grad, up_grad],
-        [down_near, down_far],
+        [down_in],
         [jnp.bfloat16] + [wide] * 8,
     )
     return (

time: 717 us -> 720 us (level)
    pallas_call x1, Pallas kernels: 168 us -> 147 us  [attention_back(): pl.pallas_call(functools.partial(attention_back_kernel, seqs, chips, bloc...]
    pallas_call x1, Pallas kernels: 145 us -> 161 us  [feed_forward(): pl.pallas_call(functools.partial(feed_kernel, seqs, chips, batches), out_...]
    pallas_call x1, Pallas kernels: 121 us -> 130 us  [branch_sum(): pl.pallas_call(functools.partial(branch_kernel, seqs, chips), out_shape=[...]
  transfers between devices with their start and end apart: 2 -> 1, of which waited for: 0 -> 0; matrix products, arithmetic and copies ran while one was open for 1% -> 1% of each run, Pallas kernels for 37% -> 19%
where the time goes in v12:
time: 720 us; the launch traced here: 708 us
  Pallas kernels  687 us (95%)
  between operations  14.6 us (2%)
    pallas_call x1, Pallas kernels, feed_forward(): pl.pallas_call(functools.partial(feed_kernel, seqs, chips, batches), out_...  161 us
    pallas_call x1, Pallas kernels, attention_back(): pl.pallas_call(functools.partial(attention_back_kernel, seqs, chips, bloc...  147 us
    pallas_call x1, Pallas kernels, start(): pl.pallas_call(functools.partial(start_kernel, seqs, chips, batches, bloc...  137 us
    pallas_call x1, Pallas kernels, branch_sum(): pl.pallas_call(functools.partial(branch_kernel, seqs, chips), out_shape=[...  130 us
    pallas_call x1, Pallas kernels, branch_back(): pl.pallas_call(functools.partial(branch_back_kernel, seqs, chips, batches...  103 us
  transfers between devices with their start and end apart: 1, of which 0 were waited for; matrix products, arithmetic and copies ran while one was open for 1% of the time, Pallas kernels for 19%

profile of v12, /device:TPU:9, one launch (start us, length us, event | category | flops | bytes accessed | tf_op | source)
XLA Modules:
  0.0 708.4 jit_solution(12869989011511885236)
XLA Ops:
  7.2 0.0 all-gather.2.cloned.1.call-start
  7.2 0.7 all-gather.2.cloned.1.call-update
  7.9 0.7 maximum_convert_fusion
  8.6 0.1 tile.10
  8.7 0.8 reduce_window_sum.11
  9.6 0.7 sub.46
  10.3 0.1 select_reduce_fusion
  10.4 0.6 maximum_subtract_fusion.low_ref
  11.0 0.6 pad_bitcast_fusion.tile_ref
  11.6 137.3 %start.1 = (bf16[2,1024,2048]{2,1,0:T(8,128)(2,1)}, bf16[2,1024,256]{2,1,0:T(8,128)(2,1)}, bf16[2,1024,256]{2,1,0:T(8,128)(2,1)}, f32[2,4,1024]{2,1,0:T(4,128)},...) custom-call(f32[1,8,128]{2,1,0:T(8,128)} %pad_bitcast_fusion.tile_re, ...), custom_call_target="tpu_custom_call" | custom-call | flops 11811160064 | bytes 314572800 | tf_op jit(solution)/shard_map/start/pallas_call | solution.py:830
  148.9 0.9 copy.25
  149.8 0.6 slice_bitcast_fusion
  150.4 0.0 all-gather.2.cloned.1.call-done.w_ref
  150.4 129.8 %branch_sum.1 = (f32[256,2048]{1,0:T(8,128)}, bf16[256,2048]{1,0:T(8,128)(2,1)}, bf16[8,256,2048]{2,1,0:T(8,128)(2,1)}, bf16[4,512,2048]{2,1,0:T(8,128)(2,1)}, bf16[4,128,2048]{2,1,0:T(8,128)(2,1)}) custom-call(bf16[2,1024,256]{2,1,0:T(8,128)(2,1)} %get-tuple-element.53.a_ref.att_ref, bf16[256,2048]{1,0:T(8,128)(2,1)} %all-gather.2.cloned.1.call-done.w_ref, ...), custom_call_target="tpu_custom_call" | custom-call | flops 2147483648 | bytes 262144000 | tf_op jit(solution)/shard_map/branch_sum/pallas_call | solution.py:948
  280.2 160.8 %feed_forward.1 = (f32[256,2048]{1,0:T(8,128)}, bf16[256,2048]{1,0:T(8,128)(2,1)}, f32[8,2048]{1,0:T(8,128)}, bf16[2048,1024]{1,0:T(8,128)(2,1)}, bf16[2048,2048...) custom-call(bf16[256,2048]{1,0:T(8,128)(2,1)} %get-tuple-element.56.x_ref, bf16[2048,2048]{1,0:T(8,128)(2,1)} %bitcast.33, ...), custom_call_target="tpu_custom_call" | custom-call | flops 60129542144 | bytes 419430400 | tf_op jit(solution)/shard_map/feed_forward/pallas_call | solution.py:1323
  441.0 103.2 %branch_back.1 = (bf16[2,1024,256]{2,1,0:T(8,128)(2,1)}, bf16[256,2048]{1,0:T(8,128)(2,1)}, bf16[256,2048]{1,0:T(8,128)(2,1)}, bf16[3,256,2048]{2,1,0:T(8,128)(2...) custom-call(bf16[256,2048]{1,0:T(8,128)(2,1)} %get-tuple-element.62.x_ref, ...), custom_call_target="tpu_custom_call" | custom-call | flops 21474836480 | bytes 262144000 | tf_op jit(solution)/shard_map/branch_back/pallas_call | solution.py:1488
  544.2 147.1 %attention_back.1 = (f32[256,2048]{1,0:T(8,128)}, bf16[64,2048]{1,0:T(8,128)(2,1)}, bf16[64,2048]{1,0:T(8,128)(2,1)}, bf16[64,2048]{1,0:T(8,128)(2,1)}, f32[64,2...) custom-call(bf16[2,1024,256]{2,1,0:T(8,128)(2,1)} %get-tuple-element.66.q_ref, ...), custom_call_target="tpu_custom_call" | custom-call | flops 26306674688 | bytes 419430400 | tf_op jit(solution)/shard_map/attention_back/pallas_call | solution.py:1866
  691.3 0.7 slice.17
  692.0 0.1 constant_dynamic-slice_fusion
  692.0 0.5 slice_bitcast_fusion.2
  692.6 8.5 %finish.1 = (bf16[256,2048]{1,0:T(8,128)(2,1)}, f32[256,2048]{1,0:T(8,128)}, f32[64,2048]{1,0:T(8,128)}, f32[64,2048]{1,0:T(8,128)}, f32[64,2048]{1,0:T(8,128)},...) custom-call(bf16[256,2048]{1,0:T(8,128)(2,1)} %get-tuple-element.65.refs_0_, ...), custom_call_target="tpu_custom_call" | custom-call | tf_op jit(solution)/shard_map/finish/pallas_call | solution.py:1966
  (7 shorter events, 0.0 us)
Async XLA Ops:
  7.2 143.2 %all-gather.2.cloned.1.call-start = ((), (), s32[]{:S(2)}) async-start(), calls=%async_computation | async-start | bytes 1310720 | tf_op jit(solution)/shard_map/all_gather | solution.py:2018
Sparse Core Ops, SparseCore 0:
  9.9 42.3 all-gather.1

commit v13 on v12

--- a/solution.py
+++ b/solution.py
@@ -361,25 +361,27 @@
         self.seqs, self.source, self.target = seqs, source, target
         self.send, self.recv, self.keep = send, recv, keep
         self.own = lax.axis_index("seq")
-        self.half = source.shape[0] // 2
-
-    def move(self, peer, place):
+        self.parts = send.shape[2]
+        self.size = source.shape[0] // self.parts
+
+    def move(self, peer, place, part):
+        here = pl.ds(part * self.size, self.size)
         return pltpu.make_async_remote_copy(
-            src_ref=self.source,
-            dst_ref=self.target.at[place],
-            send_sem=self.send.at[peer, 0],
-            recv_sem=self.recv.at[place, 0],
+            src_ref=self.source.at[here],
+            dst_ref=self.target.at[place, here],
+            send_sem=self.send.at[peer, 0, part],
+            recv_sem=self.recv.at[place, 0, part],
             device_id={"seq": peer},
             device_id_type=MESH,
         )
 
-    def relay(self, peer, place, part):
-        here = pl.ds(part * self.half, self.half)
+    def relay(self, peer, place, part, side):
+        here = pl.ds(part * self.size + side * (self.size // 2), self.size // 2)
         return pltpu.make_async_remote_copy(
             src_ref=self.target.at[place, here],
             dst_ref=self.target.at[place, here],
-            send_sem=self.send.at[peer, 1],
-            recv_sem=self.recv.at[place, part],
+            send_sem=self.send.at[peer, 1, part],
+            recv_sem=self.recv.at[place, side, part],
             device_id={"seq": peer},
             device_id_type=MESH,
         )
@@ -394,40 +396,45 @@
 
     def begin(self):
         self.kept().start()
+        for part in range(self.parts):
+            if self.seqs == 4:
+                one, two, _ = self.near()
+                self.move(one, self.own, part).start()
+                self.move(two, self.own, part).start()
+            else:
+                pl.loop(1, self.seqs)(
+                    lambda ahead, part=part: self.move(
+                        lax.rem(self.own + ahead, self.seqs), self.own, part
+                    ).start()
+                )
+
+    def pass_on(self, parts):
         if self.seqs == 4:
             one, two, _ = self.near()
-            self.move(one, self.own).start()
-            self.move(two, self.own).start()
-        else:
-            pl.loop(1, self.seqs)(
-                lambda ahead: self.move(lax.rem(self.own + ahead, self.seqs), self.own).start()
-            )
-
-    def pass_on(self):
-        if self.seqs == 4:
-            one, two, _ = self.near()
-            self.move(one, one).wait_recv()
-            self.relay(two, one, 0).start()
-            self.move(two, two).wait_recv()
-            self.relay(one, two, 1).start()
+            for part in parts:
+                self.move(one, one, part).wait_recv()
+                self.relay(two, one, part, 0).start()
+                self.move(two, two, part).wait_recv()
+                self.relay(one, two, part, 1).start()
 
     def end(self):
         self.kept().wait()
-        if self.seqs == 4:
-            one, two, far = self.near()
-            self.relay(two, far, 0).wait_recv()
-            self.relay(one, far, 1).wait_recv()
-            self.move(one, self.own).wait_send()
-            self.move(two, self.own).wait_send()
-            self.relay(two, one, 0).wait_send()
-            self.relay(one, two, 1).wait_send()
-        else:
-
-            @pl.loop(1, self.seqs)
-            def _(ahead):
-                peer = lax.rem(self.own + ahead, self.seqs)
-                self.move(peer, peer).wait_recv()
-                self.move(peer, self.own).wait_send()
+        for part in range(self.parts):
+            if self.seqs == 4:
+                one, two, far = self.near()
+                self.relay(two, far, part, 0).wait_recv()
+                self.relay(one, far, part, 1).wait_recv()
+                self.move(one, self.own, part).wait_send()
+                self.move(two, self.own, part).wait_send()
+                self.relay(two, one, part, 0).wait_send()
+                self.relay(one, two, part, 1).wait_send()
+            else:
+
+                @pl.loop(1, self.seqs)
+                def _(ahead, part=part):
+                    peer = lax.rem(self.own + ahead, self.seqs)
+                    self.move(peer, peer, part).wait_recv()
+                    self.move(peer, self.own, part).wait_send()
 
 
 def seq_peers(seqs):
@@ -663,7 +670,7 @@
         others(seqs, seq, lambda peer: block_share(seq, member, peer).start())
 
     others(group, own, pass_block)
-    down.pass_on()
+    down.pass_on([0])
     others(group, own, lambda peer: tiles_to_group(peer, peer).wait_recv())
     for column in range(width // 128):
         total = 0.0
@@ -873,8 +880,8 @@
             sems(group),
             sems(group),
             pltpu.SemaphoreType.DMA,
-            sems(seqs, 2),
-            sems(seqs, 2),
+            sems(seqs, 2, 1),
+            sems(seqs, 2, 1),
             pltpu.SemaphoreType.DMA,
         ],
         compiler_params=comm_params(collective, 62),
@@ -921,10 +928,12 @@
 
         reduce.level(chips - 1 - step, also)
 
-        @pl.when(step == chips - 2)
+        pl.when(step == chips // 2 - 1)(lambda: units.pass_on([0, 1]))
+
+        @pl.when(step == chips // 2)
         def _():
-            units.pass_on()
-            down.pass_on()
+            units.pass_on([2, 3])
+            down.pass_on([0])
 
     @pl.loop(0, rows // 32)
     def _(chunk):
@@ -959,7 +968,8 @@
         scratch_shapes=[pltpu.VMEM((rows, width), jnp.float32)]
         + Reduce.scratch(chips, rows, width)
         + [sems(3, group, PARTS), sems(group, PARTS), pltpu.SemaphoreType.DMA]
-        + [sems(seqs, 2), sems(seqs, 2), pltpu.SemaphoreType.DMA] * 2,
+        + [sems(seqs, 2, PARTS), sems(seqs, 2, PARTS), pltpu.SemaphoreType.DMA]
+        + [sems(seqs, 2, 1), sems(seqs, 2, 1), pltpu.SemaphoreType.DMA],
         compiler_params=comm_params(collective),
         cost_estimate=cost(
             2 * group * rows * width * w.shape[0], 250 * MIB, 3 * group * rows * width * 2
@@ -1213,7 +1223,7 @@
     seq = lax.axis_index("seq")
 
     near, far_off = seq_peers(seqs)
-    soon = seqs - 1
+    soon = len(near)
     order = [peer * 2 for peer in near] + [peer * 2 for peer in far_off] + [seq * 2]
     order = order + [peer * 2 + 1 for peer in near] + [peer * 2 + 1 for peer in far_off] + [seq * 2 + 1]
 
@@ -1229,7 +1239,7 @@
             tiles.at[slot], grad_hbm.at[rows_at(tile_at(turn), block)], tile_sem.at[slot]
         )
 
-    parts = ToPeers(seqs, near + far_off, grad_hbm, grad_in, part_send, part_recv)
+    parts = ToPeers(seqs, near, grad_hbm, grad_in, part_send, part_recv)
 
     def leave(turn):
         grad_stored(turn).wait()
@@ -1328,7 +1338,7 @@
             jax.ShapeDtypeStruct((8, width), jnp.float32),
             jax.ShapeDtypeStruct((group * rows, units), half),
             jax.ShapeDtypeStruct((width, 2 * units), half),
-            jax.ShapeDtypeStruct((seqs - 1, block, 2 * units), half),
+            jax.ShapeDtypeStruct((near_count(seqs), block, 2 * units), half),
         ],
         in_specs=[VMEM_SPEC] + [ANY_SPEC] * 4 + [VMEM_SPEC] * 3,
         out_specs=[VMEM_SPEC] * 3 + [ANY_SPEC] * 3,
@@ -1364,7 +1374,7 @@
 
 def branch_back_kernel(
     seqs, chips, batches, x_ref, w_ref, att_ref, middle_ref, hidden_hbm, wd_one, wd_two, units_hbm, gd_hbm,
-    d_ref, layer_ref, out_grad_ref, half_in, down_hbm, down_in,
+    d_ref, layer_ref, out_grad_ref, half_in, whole_in, down_hbm, down_in,
     out_ref, buf, hidden_ref, wd_ref, grad_acc, rights, tiles, send, recv, load, right_sem, tile_sem,
     part_send, part_recv, wd_load, down_send, down_recv, down_keep, acc, cross_out, line_out, cross_in, line_in, sum_send, sum_recv,
 ):
@@ -1413,13 +1423,16 @@
     right(0).start()
     meet(line.greet() + greet_seq(seqs))
     near, far_off = seq_peers(seqs)
-    peers = near + far_off
-    halves = ToPeers(seqs, peers, units_hbm, half_in, part_send, part_recv, half_in.shape[1])
-    down = ToPeers(seqs, peers, down_hbm, down_in.at[pl.ds(0, seqs - 1)], down_send, down_recv)
+    soon = len(near)
+    halves = ToPeers(
+        seqs, near, units_hbm, half_in, part_send.at[0], part_recv.at[0], half_in.shape[1]
+    )
+    wholes = ToPeers(seqs, far_off, units_hbm, whole_in, part_send.at[1], part_recv.at[1])
+    down = ToPeers(
+        seqs, near, down_hbm, down_in.at[pl.ds(0, soon)], down_send, down_recv
+    )
     down_kept = pltpu.make_async_copy(
-        down_hbm.at[rows_at(lax.axis_index("seq"), down_in.shape[1])],
-        down_in.at[seqs - 1],
-        down_keep,
+        down_hbm.at[rows_at(lax.axis_index("seq"), down_in.shape[1])], down_in.at[soon], down_keep
     )
     spread = Spread(line, x_ref, buf, send, recv)
     reduce = Reduce(
@@ -1427,6 +1440,7 @@
     )
     spread.begin()
     halves.begin()
+    wholes.begin()
     buf[line.own] = x_ref[...]
     grad_acc[...] = jnp.zeros_like(grad_acc)
 
@@ -1472,6 +1486,7 @@
     spread.sent()
     reduce.sent()
     halves.end()
+    wholes.end()
     down.end()
     down_kept.wait()
 
@@ -1483,7 +1498,7 @@
     span = w.shape[0]
     half = jnp.bfloat16
     part = 256 if group * rows <= 2048 else 128
-    run = width // seqs
+    near, run = near_count(seqs), width // seqs
     units = hidden.shape[1]
     return pl.pallas_call(
         functools.partial(branch_back_kernel, seqs, chips, batches),
@@ -1491,12 +1506,13 @@
             jax.ShapeDtypeStruct((batches, length, span), half),
             jax.ShapeDtypeStruct((rows, width), half),
             jax.ShapeDtypeStruct((span, width), half),
-            jax.ShapeDtypeStruct((seqs - 1, run // 2, unit_part.shape[1]), half),
+            jax.ShapeDtypeStruct((near, run // 2, unit_part.shape[1]), half),
+            jax.ShapeDtypeStruct((seqs - 1 - near, run, unit_part.shape[1]), half),
             jax.ShapeDtypeStruct((units, width), half),
-            jax.ShapeDtypeStruct((seqs, units // seqs, width), half),
+            jax.ShapeDtypeStruct((near + 1, units // seqs, width), half),
         ],
         in_specs=[VMEM_SPEC] * 4 + [ANY_SPEC] * 5,
-        out_specs=[VMEM_SPEC] * 3 + [ANY_SPEC] * 3,
+        out_specs=[VMEM_SPEC, VMEM_SPEC, VMEM_SPEC, ANY_SPEC, ANY_SPEC, ANY_SPEC, ANY_SPEC],
         scratch_shapes=[
             pltpu.VMEM((rows, width), jnp.float32),
             pltpu.VMEM((group, rows, width), half),
@@ -1510,8 +1526,8 @@
             sems(2),
             sems(2),
             sems(2),
-            sems(seqs),
-            sems(seqs),
+            sems(2, seqs),
+            sems(2, seqs),
             sems(2, seqs),
             sems(seqs),
             sems(seqs),
@@ -1529,10 +1545,10 @@
 
 
 def attention_back_kernel(
-    seqs, chips, block, q_ref, pad_ref, low_ref, lse_ref, d_ref, part_hbm, in_one, in_two,
-    w_ref, g_hbm, v_ref, dm_hbm, gain_ref, mlp_gain_ref, out_ref,
-    grad_hbm, wq_ref, wk_ref, wv_ref, wo_hbm, tile_ref, gate_hbm, up_hbm,
-    grad_ref, wo_ref, gate_ref, up_ref, result_sem,
+    seqs, chips, block, q_ref, pad_ref, low_ref, lse_ref, d_ref, part_hbm, in_one, in_two, in_far,
+    w_ref, g_hbm, v_ref, dm_hbm, gain_ref, mlp_gain_ref, out_ref, down_hbm,
+    grad_hbm, wq_ref, wk_ref, wv_ref, wo_hbm, tile_ref, gate_hbm, up_hbm, down_in,
+    grad_ref, wo_ref, gate_ref, up_ref, result_sem, down_send, down_recv,
     dk, dv, kt, heads, back_out, back_in, unit_parts, unit_sums, units, lefts, parts, sums, cols, out_in,
     totals, gain_acc, gain_out, gain_in, gain_sum, gain_back, acc, keep,
     halo_send, halo_recv, unit_load, unit_send, unit_recv, unit_keep, dm_load, left_sem,
@@ -1566,21 +1582,32 @@
     def load_units(turn):
         member = lax.rem(own + turn, group)
         unit_loaded(turn, 0, part_hbm.at[rows_at(seq * group + member, share)]).start()
+        soon = in_one.shape[0]
         for index in range(seqs - 1):
 
-            @pl.when(member < chips)
-            def _(index=index):
-                unit_loaded(turn, index + 1, in_one.at[index, rows_at(member, share)]).start()
-
-            @pl.when(member >= chips)
-            def _(index=index):
-                unit_loaded(turn, index + 1, in_two.at[index, rows_at(member - chips, share)]).start()
+            def fetch(source, index=index):
+                unit_loaded(turn, index + 1, source).start()
+
+            if index < soon:
+
+                @pl.when(member < chips)
+                def _(index=index, fetch=fetch):
+                    fetch(in_one.at[index, rows_at(member, share)])
+
+                @pl.when(member >= chips)
+                def _(index=index, fetch=fetch):
+                    fetch(in_two.at[index, rows_at(member - chips, share)])
+
+            else:
+                fetch(in_far.at[index - soon, rows_at(member, share)])
 
     load_units(1)
     dm_loaded = pltpu.make_async_copy(dm_hbm, grad_ref, dm_load)
     dm_loaded.start()
     meet(greet_group(group) + greet_seq(seqs))
     near, far_off = seq_peers(seqs)
+    down = ToPeers(seqs, far_off, down_hbm, down_in, down_send, down_recv)
+    down.begin()
     swap = Swap(group, unit_sums, units, unit_send, unit_recv, unit_keep)
 
     @pl.loop(1, group + 1)
@@ -1841,14 +1868,15 @@
             pl.loop(0, need)(lambda step: halo(batch, step, seq).wait_send())
 
     heads_near.sent()
+    down.end()
     others(group, own, lambda peer: gain_group(peer, own).wait_send())
     others(group, own, lambda peer: block_swap(peer, own).wait_send())
     others(seqs, seq, lambda peer: gain_seq(peer, seq).wait_send())
 
 
 def attention_back(
-    seqs, chips, block, query, kv_pad, low, lse, d_att, part_own, parts_one, parts_two, w, group_a, x,
-    d_middle, gain, mlp_gain, out_part, collective,
+    seqs, chips, block, query, kv_pad, low, lse, d_att, part_own, parts_one, parts_two, parts_far, w, group_a,
+    x, d_middle, gain, mlp_gain, out_part, down, collective,
 ):
     batches, length, span = query.shape
     padded = kv_pad.shape[1]
@@ -1874,19 +1902,23 @@
             jax.ShapeDtypeStruct((8, 128), wide),
             jax.ShapeDtypeStruct((share, cells // 2 * group), half),
             jax.ShapeDtypeStruct((share, cells // 2 * group), half),
+            jax.ShapeDtypeStruct((seqs - 1 - near_count(seqs), down.shape[0] // seqs, width), half),
         ],
         in_specs=[VMEM_SPEC] * 5
-        + [ANY_SPEC] * 3
+        + [ANY_SPEC] * 4
         + [VMEM_SPEC, ANY_SPEC, VMEM_SPEC, ANY_SPEC]
-        + [VMEM_SPEC] * 3,
+        + [VMEM_SPEC] * 3
+        + [ANY_SPEC],
         out_specs=[ANY_SPEC, VMEM_SPEC, VMEM_SPEC, VMEM_SPEC, ANY_SPEC, VMEM_SPEC]
-        + [ANY_SPEC] * 2,
+        + [ANY_SPEC] * 3,
         scratch_shapes=[
             pltpu.VMEM((rows, width), wide),
             pltpu.VMEM((out_rows, width), wide),
             pltpu.VMEM((share, cells // 2 * group), half),
             pltpu.VMEM((share, cells // 2 * group), half),
             sems(4),
+            sems(seqs),
+            sems(seqs),
             pltpu.VMEM((padded, span), wide),
             pltpu.VMEM((padded, span), wide),
             pltpu.VMEM((span, padded), half),
@@ -1937,8 +1969,8 @@
         ),
         name="attention_back",
     )(
-        query, kv_pad, low, lse, d_att, part_own, parts_one, parts_two, w, group_a, x,
-        d_middle, gain, mlp_gain, out_part,
+        query, kv_pad, low, lse, d_att, part_own, parts_one, parts_two, parts_far, w, group_a, x,
+        d_middle, gain, mlp_gain, out_part, down,
     )
 
 
@@ -2050,7 +2082,7 @@
         seqs, chips, batches, normed_b, w_units, (wd_one, wd_two), group_d, middle, cot_rows,
         gain_two[None], 4,
     )
-    d_attended, layer_out, out_part, unit_two, _, down_in = branch_back(
+    d_attended, layer_out, out_part, unit_two, unit_far, down_part, down_near = branch_back(
         seqs, chips, batches, d_branch, wo_part, attended, middle, hidden, (wd_one, wd_two),
         unit_part, group_d, 5,
     )
@@ -2060,16 +2092,19 @@
         )
         out_part = lax.psum(whole, "fsdp").reshape(seqs, group, share, width)
         out_part = lax.dynamic_slice_in_dim(out_part, member, 1, 1).reshape(seqs * share, width)
-    input_grad, wq_grad, wk_grad, wv_grad, wo_grad, gain_tile, gate_grad, up_grad = attention_back(
+    (
+        input_grad, wq_grad, wk_grad, wv_grad, wo_grad, gain_tile, gate_grad, up_grad, down_far,
+    ) = attention_back(
         seqs, chips, block, query, kv_pad, low, lse, d_attended, unit_part, unit_one, unit_two,
-        w_heads, group_a, x_rows, d_middle, gain_one[None], mlp_gain_part, out_part, 6,
+        unit_far, w_heads, group_a, x_rows, d_middle, gain_one[None], mlp_gain_part, out_part,
+        down_part, 6,
     )
     gain_grads = lax.dynamic_slice_in_dim(gain_tile[:2], lax.rem(device, fold) * share, share, 1)
     wide = jnp.float32
     (layer_out, input_grad, wq_grad, wk_grad, wv_grad, wo_grad, gate_grad, up_grad, down_grad) = finish(
         share // 16,
         [layer_out, input_grad, wq_grad, wk_grad, wv_grad, wo_grad, gate_grad, up_grad],
-        [down_in],
+        [down_near, down_far],
         [jnp.bfloat16] + [wide] * 8,
     )
     return (

time: 720 us -> 717 us (level)
    pallas_call x1, Pallas kernels: 161 us -> 146 us  [feed_forward(): pl.pallas_call(functools.partial(feed_kernel, seqs, chips, batches), out_...]
    pallas_call x1, Pallas kernels: 147 us -> 159 us  [attention_back(): pl.pallas_call(functools.partial(attention_back_kernel, seqs, chips, bloc...]
where the time goes in v13:
time: 717 us; the launch traced here: 705 us
  Pallas kernels  684 us (95%)
  between operations  14.6 us (2%)
    pallas_call x1, Pallas kernels, attention_back(): pl.pallas_call(functools.partial(attention_back_kernel, seqs, chips, bloc...  159 us
    pallas_call x1, Pallas kernels, feed_forward(): pl.pallas_call(functools.partial(feed_kernel, seqs, chips, batches), out_...  146 us
    pallas_call x1, Pallas kernels, start(): pl.pallas_call(functools.partial(start_kernel, seqs, chips, batches, bloc...  137 us
    pallas_call x1, Pallas kernels, branch_sum(): pl.pallas_call(functools.partial(branch_kernel, seqs, chips), out_shape=[...  130 us
    pallas_call x1, Pallas kernels, branch_back(): pl.pallas_call(functools.partial(branch_back_kernel, seqs, chips, batches...  103 us
  transfers between devices with their start and end apart: 1, of which 0 were waited for; matrix products, arithmetic and copies ran while one was open for 1% of the time, Pallas kernels for 19%

profile of v13, /device:TPU:9, one launch (start us, length us, event | category | flops | bytes accessed | tf_op | source)
XLA Modules:
  0.0 705.3 jit_solution(7730300111026723718)
XLA Ops:
  7.2 0.0 all-gather.2.cloned.1.call-start
  7.2 0.7 all-gather.2.cloned.1.call-update
  7.9 0.7 maximum_convert_fusion
  8.6 0.1 tile.10
  8.7 0.8 reduce_window_sum.11
  9.6 0.7 sub.46
  10.3 0.1 select_reduce_fusion
  10.4 0.6 maximum_subtract_fusion.low_ref
  11.0 0.6 pad_bitcast_fusion.tile_ref
  11.6 137.2 %start.1 = (bf16[2,1024,2048]{2,1,0:T(8,128)(2,1)}, bf16[2,1024,256]{2,1,0:T(8,128)(2,1)}, bf16[2,1024,256]{2,1,0:T(8,128)(2,1)}, f32[2,4,1024]{2,1,0:T(4,128)},...) custom-call(f32[1,8,128]{2,1,0:T(8,128)} %pad_bitcast_fusion.tile_re, ...), custom_call_target="tpu_custom_call" | custom-call | flops 11811160064 | bytes 314572800 | tf_op jit(solution)/shard_map/start/pallas_call | solution.py:837
  148.8 0.9 copy.25
  149.8 0.6 slice_bitcast_fusion
  150.4 0.0 all-gather.2.cloned.1.call-done.w_ref
  150.4 130.2 %branch_sum.1 = (f32[256,2048]{1,0:T(8,128)}, bf16[256,2048]{1,0:T(8,128)(2,1)}, bf16[8,256,2048]{2,1,0:T(8,128)(2,1)}, bf16[4,512,2048]{2,1,0:T(8,128)(2,1)}, bf16[4,128,2048]{2,1,0:T(8,128)(2,1)}) custom-call(bf16[2,1024,256]{2,1,0:T(8,128)(2,1)} %get-tuple-element.56.a_ref.att_ref, bf16[256,2048]{1,0:T(8,128)(2,1)} %all-gather.2.cloned.1.call-done.w_ref, ...), custom_call_target="tpu_custom_call" | custom-call | flops 2147483648 | bytes 262144000 | tf_op jit(solution)/shard_map/branch_sum/pallas_call | solution.py:957
  280.6 145.6 %feed_forward.1 = (f32[256,2048]{1,0:T(8,128)}, bf16[256,2048]{1,0:T(8,128)(2,1)}, f32[8,2048]{1,0:T(8,128)}, bf16[2048,1024]{1,0:T(8,128)(2,1)}, bf16[2048,2048...) custom-call(bf16[256,2048]{1,0:T(8,128)(2,1)} %get-tuple-element.59.x_ref, bf16[2048,2048]{1,0:T(8,128)(2,1)} %bitcast.33, ...), custom_call_target="tpu_custom_call" | custom-call | flops 60129542144 | bytes 419430400 | tf_op jit(solution)/shard_map/feed_forward/pallas_call | solution.py:1333
  426.2 102.8 %branch_back.1 = (bf16[2,1024,256]{2,1,0:T(8,128)(2,1)}, bf16[256,2048]{1,0:T(8,128)(2,1)}, bf16[256,2048]{1,0:T(8,128)(2,1)}, bf16[2,256,2048]{2,1,0:T(8,128)(2...) custom-call(bf16[256,2048]{1,0:T(8,128)(2,1)} %get-tuple-element.65.x_ref, ...), custom_call_target="tpu_custom_call" | custom-call | flops 21474836480 | bytes 262144000 | tf_op jit(solution)/shard_map/branch_back/pallas_call | solution.py:1503
  529.0 159.2 %attention_back.1 = (f32[256,2048]{1,0:T(8,128)}, bf16[64,2048]{1,0:T(8,128)(2,1)}, bf16[64,2048]{1,0:T(8,128)(2,1)}, bf16[64,2048]{1,0:T(8,128)(2,1)}, f32[64,2...) custom-call(bf16[2,1024,256]{2,1,0:T(8,128)(2,1)} %get-tuple-element, ...), custom_call_target="tpu_custom_call" | custom-call | flops 26306674688 | bytes 419430400 | tf_op jit(solution)/shard_map/attention_back/pallas_call | solution.py:1894
  688.3 0.7 slice.17
  689.0 0.1 constant_dynamic-slice_fusion
  689.0 0.5 slice_bitcast_fusion.2
  689.6 8.4 %finish.1 = (bf16[256,2048]{1,0:T(8,128)(2,1)}, f32[256,2048]{1,0:T(8,128)}, f32[64,2048]{1,0:T(8,128)}, f32[64,2048]{1,0:T(8,128)}, f32[64,2048]{1,0:T(8,128)},...) custom-call(bf16[256,2048]{1,0:T(8,128)(2,1)} %get-tuple-element.68.refs_0_, ...), custom_call_target="tpu_custom_call" | custom-call | tf_op jit(solution)/shard_map/finish/pallas_call | solution.py:1998
  (7 shorter events, 0.0 us)
Async XLA Ops:
  7.2 143.2 %all-gather.2.cloned.1.call-start = ((), (), s32[]{:S(2)}) async-start(), calls=%async_computation | async-start | bytes 1310720 | tf_op jit(solution)/shard_map/all_gather | solution.py:2050
Sparse Core Ops, SparseCore 0:
  9.9 42.3 all-gather.1

commit v14 on v13

--- a/solution.py
+++ b/solution.py
@@ -481,16 +481,6 @@
     def end(self):
         self.arrived()
         self.sent()
-
-
-def load_halves(halves, target, load):
-    copies = []
-    rows = halves[0].shape[1]
-    for index, half in enumerate(halves):
-        for place in range(half.shape[0]):
-            there = pl.ds((2 * place + index) * rows, rows)
-            copies.append(pltpu.make_async_copy(half.at[place], target.at[there], load.at[index, place]))
-    return copies
 
 
 VMEM_SPEC = pl.BlockSpec(memory_space=pltpu.VMEM)
@@ -633,9 +623,7 @@
         pl.loop(1, count)(lambda ahead: act(lax.rem(me + ahead, count)))
 
     others(seqs, seq, lambda peer: tile_to_seq(peer, seq).start())
-    down = Share(
-        seqs, down_hbm.at[pl.ds(0, wd_ref.shape[1])], wd_ref, down_send, down_recv, down_keep
-    )
+    down = Share(seqs, down_hbm, wd_ref, down_send, down_recv, down_keep)
     down.begin()
     others(group, own, lambda peer: block_swap(peer, own).start())
     spreads = [
@@ -845,7 +833,7 @@
             jax.ShapeDtypeStruct((group, seqs, 8, 128), jnp.float32),
             jax.ShapeDtypeStruct((width, cols), half),
             jax.ShapeDtypeStruct((group, share, cells), half),
-            jax.ShapeDtypeStruct((seqs, down.shape[0] // 2, width), half),
+            jax.ShapeDtypeStruct((seqs,) + down.shape, half),
         ],
         in_specs=[VMEM_SPEC] * 5 + [ANY_SPEC] * 3 + [VMEM_SPEC],
         out_specs=[ANY_SPEC] + [VMEM_SPEC] * 3 + [ANY_SPEC] * 5,
@@ -895,11 +883,10 @@
 
 
 def branch_kernel(
-    seqs, chips, a_ref, w_ref, d_ref, units_ref, down_hbm, x_ref, gain_ref,
-    middle_ref, normed_ref, gd_ref, w_units_ref, wd_ref,
+    seqs, chips, a_ref, w_ref, d_ref, units_ref, x_ref, gain_ref,
+    middle_ref, normed_ref, gd_ref, w_units_ref,
     out_ref, acc, cross_out, line_out, cross_in, line_in, sum_send, sum_recv,
     send, recv, d_keep, share_send, share_recv, share_keep,
-    down_send, down_recv, down_keep,
 ):
     line = Line(chips)
     rows = out_ref.shape[0]
@@ -914,10 +901,7 @@
     spread = Spread(line, d_ref, gd_ref, send, recv)
     units = Share(seqs, units_ref, w_units_ref, share_send, share_recv, share_keep)
     d_kept = pltpu.make_async_copy(d_ref, gd_ref.at[line.own], d_keep)
-    half = wd_ref.shape[1]
-    down = Share(seqs, down_hbm.at[pl.ds(half, half)], wd_ref, down_send, down_recv, down_keep)
     units.begin()
-    down.begin()
     spread.begin()
     d_kept.start()
 
@@ -928,12 +912,7 @@
 
         reduce.level(chips - 1 - step, also)
 
-        pl.when(step == chips // 2 - 1)(lambda: units.pass_on([0, 1]))
-
-        @pl.when(step == chips // 2)
-        def _():
-            units.pass_on([2, 3])
-            down.pass_on([0])
+        pl.when(step == chips // 2)(lambda: units.pass_on(range(units.parts)))
 
     @pl.loop(0, rows // 32)
     def _(chunk):
@@ -947,10 +926,9 @@
     reduce.sent()
     d_kept.wait()
     units.end()
-    down.end()
-
-
-def branch_sum(seqs, chips, a, w, d_rows, units, down, x, gain, collective):
+
+
+def branch_sum(seqs, chips, a, w, d_rows, units, x, gain, collective):
     rows, width = d_rows.shape
     group = 2 * chips
     half = jnp.bfloat16
@@ -961,21 +939,19 @@
             jax.ShapeDtypeStruct((rows, width), half),
             jax.ShapeDtypeStruct((group, rows, width), half),
             jax.ShapeDtypeStruct((seqs,) + units.shape, half),
-            jax.ShapeDtypeStruct((seqs, down.shape[0] // 2, width), half),
         ],
-        in_specs=[VMEM_SPEC, VMEM_SPEC] + [ANY_SPEC] * 3 + [VMEM_SPEC, VMEM_SPEC],
-        out_specs=[VMEM_SPEC, VMEM_SPEC] + [ANY_SPEC] * 3,
+        in_specs=[VMEM_SPEC, VMEM_SPEC] + [ANY_SPEC] * 2 + [VMEM_SPEC, VMEM_SPEC],
+        out_specs=[VMEM_SPEC, VMEM_SPEC] + [ANY_SPEC] * 2,
         scratch_shapes=[pltpu.VMEM((rows, width), jnp.float32)]
         + Reduce.scratch(chips, rows, width)
         + [sems(3, group, PARTS), sems(group, PARTS), pltpu.SemaphoreType.DMA]
-        + [sems(seqs, 2, PARTS), sems(seqs, 2, PARTS), pltpu.SemaphoreType.DMA]
         + [sems(seqs, 2, 1), sems(seqs, 2, 1), pltpu.SemaphoreType.DMA],
         compiler_params=comm_params(collective),
         cost_estimate=cost(
             2 * group * rows * width * w.shape[0], 250 * MIB, 3 * group * rows * width * 2
         ),
         name="branch_sum",
-    )(a, w, d_rows, units, down, x, gain)
+    )(a, w, d_rows, units, x, gain)
 
 
 class PairReduce:
@@ -1103,7 +1079,7 @@
 
 
 def feed_kernel(
-    seqs, chips, batches, x_ref, w_hbm, wd_one, wd_two, gd_hbm, v_ref, cot_ref, gain_ref,
+    seqs, chips, batches, x_ref, w_hbm, wd_hbm, gd_hbm, v_ref, cot_ref, gain_ref,
     dm_ref, db_ref, gain_grad_ref, hidden_hbm, grad_hbm, grad_in,
     buf, d_buf, h_buf, w_ref, wd_ref, d_ref, tiles, totals, acc, keep,
     load, d_sem, h_sem, tile_sem, send, recv, part_send, part_recv, wd_load, *sums,
@@ -1117,7 +1093,8 @@
     block = tiles.shape[1]
     loads = [
         pltpu.make_async_copy(w_hbm, w_ref, load.at[0]),
-    ] + load_halves([wd_one, wd_two], wd_ref, wd_load)
+        pltpu.make_async_copy(wd_hbm, wd_ref, wd_load),
+    ]
     for item in loads:
         item.start()
     meet(line.greet() + greet_seq(seqs))
@@ -1323,7 +1300,7 @@
     parts.end()
 
 
-def feed_forward(seqs, chips, batches, x, w, wd_halves, group_d, middle, cot, gain, collective):
+def feed_forward(seqs, chips, batches, x, w, wd, group_d, middle, cot, gain, collective):
     rows, width = x.shape
     group = 2 * chips
     units = w.shape[1] // 2
@@ -1340,7 +1317,7 @@
             jax.ShapeDtypeStruct((width, 2 * units), half),
             jax.ShapeDtypeStruct((near_count(seqs), block, 2 * units), half),
         ],
-        in_specs=[VMEM_SPEC] + [ANY_SPEC] * 4 + [VMEM_SPEC] * 3,
+        in_specs=[VMEM_SPEC] + [ANY_SPEC] * 3 + [VMEM_SPEC] * 3,
         out_specs=[VMEM_SPEC] * 3 + [ANY_SPEC] * 3,
         scratch_shapes=[
             pltpu.VMEM((batches, group, piece, width), half),
@@ -1361,7 +1338,7 @@
             sems(batches, group, PARTS // 2),
             sems(seqs),
             sems(seqs),
-            sems(2, seqs),
+            pltpu.SemaphoreType.DMA,
         ]
         + PairReduce.scratch(chips, piece, width) * batches,
         compiler_params=comm_params(collective, 63),
@@ -1369,11 +1346,11 @@
             14 * group * rows * width * units, 400 * MIB, 2 * group * rows * width * 2
         ),
         name="feed_forward",
-    )(x, w, *wd_halves, group_d, middle, cot, gain)
+    )(x, w, wd, group_d, middle, cot, gain)
 
 
 def branch_back_kernel(
-    seqs, chips, batches, x_ref, w_ref, att_ref, middle_ref, hidden_hbm, wd_one, wd_two, units_hbm, gd_hbm,
+    seqs, chips, batches, x_ref, w_ref, att_ref, middle_ref, hidden_hbm, wd_hbm, units_hbm, gd_hbm,
     d_ref, layer_ref, out_grad_ref, half_in, whole_in, down_hbm, down_in,
     out_ref, buf, hidden_ref, wd_ref, grad_acc, rights, tiles, send, recv, load, right_sem, tile_sem,
     part_send, part_recv, wd_load, down_send, down_recv, down_keep, acc, cross_out, line_out, cross_in, line_in, sum_send, sum_recv,
@@ -1384,7 +1361,8 @@
     width = x_ref.shape[1]
     loads = [
         pltpu.make_async_copy(hidden_hbm, hidden_ref, load.at[0]),
-    ] + load_halves([wd_one, wd_two], wd_ref, wd_load)
+        pltpu.make_async_copy(wd_hbm, wd_ref, wd_load),
+    ]
     for item in loads:
         item.start()
 
@@ -1491,7 +1469,7 @@
     down_kept.wait()
 
 
-def branch_back(seqs, chips, batches, x, w, attended, middle, hidden, wd_halves, unit_part, group_d, collective):
+def branch_back(seqs, chips, batches, x, w, attended, middle, hidden, wd, unit_part, group_d, collective):
     rows, width = x.shape
     group = 2 * chips
     length = group * rows // batches
@@ -1511,7 +1489,7 @@
             jax.ShapeDtypeStruct((units, width), half),
             jax.ShapeDtypeStruct((near + 1, units // seqs, width), half),
         ],
-        in_specs=[VMEM_SPEC] * 4 + [ANY_SPEC] * 5,
+        in_specs=[VMEM_SPEC] * 4 + [ANY_SPEC] * 4,
         out_specs=[VMEM_SPEC, VMEM_SPEC, VMEM_SPEC, ANY_SPEC, ANY_SPEC, ANY_SPEC, ANY_SPEC],
         scratch_shapes=[
             pltpu.VMEM((rows, width), jnp.float32),
@@ -1528,7 +1506,7 @@
             sems(2),
             sems(2, seqs),
             sems(2, seqs),
-            sems(2, seqs),
+            pltpu.SemaphoreType.DMA,
             sems(seqs),
             sems(seqs),
             pltpu.SemaphoreType.DMA,
@@ -1541,7 +1519,7 @@
             2 * group * rows * width * 2,
         ),
         name="branch_back",
-    )(x, w, attended, middle, hidden, *wd_halves, unit_part, group_d.reshape(group * rows, width))
+    )(x, w, attended, middle, hidden, wd, unit_part, group_d.reshape(group * rows, width))
 
 
 def attention_back_kernel(
@@ -2066,24 +2044,25 @@
     block = min(256, length)
     low = jnp.maximum(begins - group_start + WINDOW, at[None, :] + 1) - (at // block * block)[None, :]
     low = low[:, None, :]
-    group_a, query, attended, lse, kv_pad, gains, w_heads, unit_own, wd_one = start(
+    group_a, query, attended, lse, kv_pad, gains, w_heads, unit_own, wd_part = start(
         seqs, chips, batches, block, tile, x_rows, (w_query, w_key, w_value), (w_gate, w_up), w_down,
         low, 1,
     )
     gains = gains.transpose(1, 0, 2, 3).reshape(devices // fold, fold, 8, 128).sum(axis=1)
     gain_one = gains[:, 0].reshape(width)
     gain_two = gains[:, 1].reshape(width)
-    middle, normed_b, group_d, w_units, wd_two = branch_sum(
-        seqs, chips, attended, wo_part, cot_rows, unit_own.reshape(group * share, -1), w_down,
+    wd_part = wd_part.reshape(-1, width)
+    middle, normed_b, group_d, w_units = branch_sum(
+        seqs, chips, attended, wo_part, cot_rows, unit_own.reshape(group * share, -1),
         x_rows, gain_two[None], 3,
     )
     w_units = w_units.reshape(width, -1)
     d_middle, d_branch, mlp_gain_part, hidden, unit_part, unit_one = feed_forward(
-        seqs, chips, batches, normed_b, w_units, (wd_one, wd_two), group_d, middle, cot_rows,
+        seqs, chips, batches, normed_b, w_units, wd_part, group_d, middle, cot_rows,
         gain_two[None], 4,
     )
     d_attended, layer_out, out_part, unit_two, unit_far, down_part, down_near = branch_back(
-        seqs, chips, batches, d_branch, wo_part, attended, middle, hidden, (wd_one, wd_two),
+        seqs, chips, batches, d_branch, wo_part, attended, middle, hidden, wd_part,
         unit_part, group_d, 5,
     )
     if not aligned:

time: 717 us -> 705 us (0.983)
  Pallas kernels: 684 us -> 672 us
    pallas_call x1, Pallas kernels: 130 us -> 119 us  [branch_sum(): pl.pallas_call(functools.partial(branch_kernel, seqs, chips), out_shape=[...]
  transfers between devices with their start and end apart: 1 -> 1, of which waited for: 0 -> 0; matrix products, arithmetic and copies ran while one was open for 1% -> 1% of each run, Pallas kernels for 19% -> 20%
where the time goes in v14:
time: 705 us; the launch traced here: 694 us
  Pallas kernels  672 us (95%)
  between operations  14.6 us (2%)
    pallas_call x1, Pallas kernels, attention_back(): pl.pallas_call(functools.partial(attention_back_kernel, seqs, chips, bloc...  160 us
    pallas_call x1, Pallas kernels, feed_forward(): pl.pallas_call(functools.partial(feed_kernel, seqs, chips, batches), out_...  144 us
    pallas_call x1, Pallas kernels, start(): pl.pallas_call(functools.partial(start_kernel, seqs, chips, batches, bloc...  139 us
    pallas_call x1, Pallas kernels, branch_sum(): pl.pallas_call(functools.partial(branch_kernel, seqs, chips), out_shape=[...  119 us
    pallas_call x1, Pallas kernels, branch_back(): pl.pallas_call(functools.partial(branch_back_kernel, seqs, chips, batches...  101 us
  transfers between devices with their start and end apart: 1, of which 0 were waited for; matrix products, arithmetic and copies ran while one was open for 1% of the time, Pallas kernels for 20%

profile of v14, /device:TPU:9, one launch (start us, length us, event | category | flops | bytes accessed | tf_op | source)
XLA Modules:
  0.0 693.8 jit_solution(17230523697521517684)
XLA Ops:
  7.2 0.0 all-gather.2.cloned.1.call-start
  7.2 0.7 all-gather.2.cloned.1.call-update
  7.9 0.7 maximum_convert_fusion
  8.6 0.1 tile.10
  8.7 0.8 reduce_window_sum.11
  9.6 0.7 sub.46
  10.3 0.1 select_reduce_fusion
  10.4 0.6 maximum_subtract_fusion.low_ref
  11.0 0.6 pad_bitcast_fusion.tile_ref
  11.6 138.9 %start.1 = (bf16[2,1024,2048]{2,1,0:T(8,128)(2,1)}, bf16[2,1024,256]{2,1,0:T(8,128)(2,1)}, bf16[2,1024,256]{2,1,0:T(8,128)(2,1)}, f32[2,4,1024]{2,1,0:T(4,128)},...) custom-call(f32[1,8,128]{2,1,0:T(8,128)} %pad_bitcast_fusion.tile_re, ...), custom_call_target="tpu_custom_call" | custom-call | flops 11811160064 | bytes 314572800 | tf_op jit(solution)/shard_map/start/pallas_call | solution.py:825
  150.5 0.9 copy.25
  151.4 0.6 slice_bitcast_fusion
  152.0 0.0 all-gather.2.cloned.1.call-done.w_ref
  152.0 119.0 %branch_sum.1 = (f32[256,2048]{1,0:T(8,128)}, bf16[256,2048]{1,0:T(8,128)(2,1)}, bf16[8,256,2048]{2,1,0:T(8,128)(2,1)}, bf16[4,512,2048]{2,1,0:T(8,128)(2,1)}) custom-call(bf16[2,1024,256]{2,1,0:T(8,128)(2,1)} %get-tuple-element.55.a_ref.att_ref, bf16[256,2048]{1,0:T(8,128)(2,1)} %all-gather.2.cloned.1.call-done.w_ref, bf16[256,2048]{1,0:T(8,128)(2,1)} %bitcast.27, ...), custom_call_target="tpu_custom_call" | custom-call | flops 2147483648 | bytes 262144000 | tf_op jit(solution)/shard_map/branch_sum/pallas_call | solution.py:935
  271.1 144.0 %feed_forward.1 = (f32[256,2048]{1,0:T(8,128)}, bf16[256,2048]{1,0:T(8,128)(2,1)}, f32[8,2048]{1,0:T(8,128)}, bf16[2048,1024]{1,0:T(8,128)(2,1)}, bf16[2048,2048...) custom-call(bf16[256,2048]{1,0:T(8,128)(2,1)} %get-tuple-element.58.x_ref, bf16[2048,2048]{1,0:T(8,128)(2,1)} %bitcast.34, ...), custom_call_target="tpu_custom_call" | custom-call | flops 60129542144 | bytes 419430400 | tf_op jit(solution)/shard_map/feed_forward/pallas_call | solution.py:1310
  415.0 101.4 %branch_back.1 = (bf16[2,1024,256]{2,1,0:T(8,128)(2,1)}, bf16[256,2048]{1,0:T(8,128)(2,1)}, bf16[256,2048]{1,0:T(8,128)(2,1)}, bf16[2,256,2048]{2,1,0:T(8,128)(2...) custom-call(bf16[256,2048]{1,0:T(8,128)(2,1)} %get-tuple-element.63.x_ref, ...), custom_call_target="tpu_custom_call" | custom-call | flops 21474836480 | bytes 262144000 | tf_op jit(solution)/shard_map/branch_back/pallas_call | solution.py:1481
  516.4 160.3 %attention_back.1 = (f32[256,2048]{1,0:T(8,128)}, bf16[64,2048]{1,0:T(8,128)(2,1)}, bf16[64,2048]{1,0:T(8,128)(2,1)}, bf16[64,2048]{1,0:T(8,128)(2,1)}, f32[64,2...) custom-call(bf16[2,1024,256]{2,1,0:T(8,128)(2,1)} %get-tuple-element, ...), custom_call_target="tpu_custom_call" | custom-call | flops 26306674688 | bytes 419430400 | tf_op jit(solution)/shard_map/attention_back/pallas_call | solution.py:1872
  676.8 0.7 slice.17
  677.5 0.1 constant_dynamic-slice_fusion
  677.5 0.5 slice_bitcast_fusion.2
  678.1 8.4 %finish.1 = (bf16[256,2048]{1,0:T(8,128)(2,1)}, f32[256,2048]{1,0:T(8,128)}, f32[64,2048]{1,0:T(8,128)}, f32[64,2048]{1,0:T(8,128)}, f32[64,2048]{1,0:T(8,128)},...) custom-call(bf16[256,2048]{1,0:T(8,128)(2,1)} %get-tuple-element.66.refs_0_, ...), custom_call_target="tpu_custom_call" | custom-call | tf_op jit(solution)/shard_map/finish/pallas_call | solution.py:1976
  (7 shorter events, 0.0 us)
Async XLA Ops:
  7.2 144.9 %all-gather.2.cloned.1.call-start = ((), (), s32[]{:S(2)}) async-start(), calls=%async_computation | async-start | bytes 1310720 | tf_op jit(solution)/shard_map/all_gather | solution.py:2028
Sparse Core Ops, SparseCore 0:
  9.9 36.6 all-gather.1

commit v15 on v13

--- a/solution.py
+++ b/solution.py
@@ -847,7 +847,7 @@
             jax.ShapeDtypeStruct((group, share, cells), half),
             jax.ShapeDtypeStruct((seqs, down.shape[0] // 2, width), half),
         ],
-        in_specs=[VMEM_SPEC] * 5 + [ANY_SPEC] * 3 + [VMEM_SPEC],
+        in_specs=[VMEM_SPEC] * 5 + [ANY_SPEC] * 2 + [VMEM_SPEC] * 2,
         out_specs=[ANY_SPEC] + [VMEM_SPEC] * 3 + [ANY_SPEC] * 5,
         scratch_shapes=[
             pltpu.VMEM((share, wide), half),
@@ -916,24 +916,23 @@
     d_kept = pltpu.make_async_copy(d_ref, gd_ref.at[line.own], d_keep)
     half = wd_ref.shape[1]
     down = Share(seqs, down_hbm.at[pl.ds(half, half)], wd_ref, down_send, down_recv, down_keep)
+    down.begin()
     units.begin()
-    down.begin()
     spread.begin()
     d_kept.start()
 
     @pl.loop(0, chips)
     def _(step):
         def also(tile):
+            @pl.when((step == chips // 2) & (tile == 0))
+            def _():
+                down.pass_on([0])
+                units.pass_on([0])
+
             pl.when(step < chips - 1)(lambda: spread.relay_part(step + 1, tile))
 
         reduce.level(chips - 1 - step, also)
 
-        pl.when(step == chips // 2 - 1)(lambda: units.pass_on([0, 1]))
-
-        @pl.when(step == chips // 2)
-        def _():
-            units.pass_on([2, 3])
-            down.pass_on([0])
 
     @pl.loop(0, rows // 32)
     def _(chunk):
@@ -963,13 +962,12 @@
             jax.ShapeDtypeStruct((seqs,) + units.shape, half),
             jax.ShapeDtypeStruct((seqs, down.shape[0] // 2, width), half),
         ],
-        in_specs=[VMEM_SPEC, VMEM_SPEC] + [ANY_SPEC] * 3 + [VMEM_SPEC, VMEM_SPEC],
+        in_specs=[VMEM_SPEC] * 7,
         out_specs=[VMEM_SPEC, VMEM_SPEC] + [ANY_SPEC] * 3,
         scratch_shapes=[pltpu.VMEM((rows, width), jnp.float32)]
         + Reduce.scratch(chips, rows, width)
         + [sems(3, group, PARTS), sems(group, PARTS), pltpu.SemaphoreType.DMA]
-        + [sems(seqs, 2, PARTS), sems(seqs, 2, PARTS), pltpu.SemaphoreType.DMA]
-        + [sems(seqs, 2, 1), sems(seqs, 2, 1), pltpu.SemaphoreType.DMA],
+        + [sems(seqs, 2, 1), sems(seqs, 2, 1), pltpu.SemaphoreType.DMA] * 2,
         compiler_params=comm_params(collective),
         cost_estimate=cost(
             2 * group * rows * width * w.shape[0], 250 * MIB, 3 * group * rows * width * 2

time: 717 us -> 699 us (0.975)
  Pallas kernels: 684 us -> 666 us
    pallas_call x1, Pallas kernels: 130 us -> 114 us  [branch_sum(): pl.pallas_call(functools.partial(branch_kernel, seqs, chips), out_shape=[...]
  transfers between devices with their start and end apart: 1 -> 1, of which waited for: 0 -> 0; matrix products, arithmetic and copies ran while one was open for 1% -> 1% of each run, Pallas kernels for 19% -> 20%
where the time goes in v15:
time: 699 us; the launch traced here: 688 us
  Pallas kernels  666 us (95%)
  between operations  14.6 us (2%)
    pallas_call x1, Pallas kernels, attention_back(): pl.pallas_call(functools.partial(attention_back_kernel, seqs, chips, bloc...  160 us
    pallas_call x1, Pallas kernels, feed_forward(): pl.pallas_call(functools.partial(feed_kernel, seqs, chips, batches), out_...  145 us
    pallas_call x1, Pallas kernels, start(): pl.pallas_call(functools.partial(start_kernel, seqs, chips, batches, bloc...  138 us
    pallas_call x1, Pallas kernels, branch_sum(): pl.pallas_call(functools.partial(branch_kernel, seqs, chips), out_shape=[...  114 us
    pallas_call x1, Pallas kernels, branch_back(): pl.pallas_call(functools.partial(branch_back_kernel, seqs, chips, batches...  101 us
  transfers between devices with their start and end apart: 1, of which 0 were waited for; matrix products, arithmetic and copies ran while one was open for 1% of the time, Pallas kernels for 20%

profile of v15, /device:TPU:9, one launch (start us, length us, event | category | flops | bytes accessed | tf_op | source)
XLA Modules:
  0.0 687.9 jit_solution(7501461030783873717)
XLA Ops:
  7.2 0.0 all-gather.2.cloned.1.call-start
  7.2 0.7 all-gather.2.cloned.1.call-update
  7.9 0.7 maximum_convert_fusion
  8.6 0.1 tile.10
  8.7 0.8 reduce_window_sum.11
  9.6 0.7 sub.46
  10.3 0.1 select_reduce_fusion
  10.4 0.6 maximum_subtract_fusion.low_ref
  11.0 0.6 pad_bitcast_fusion.tile_ref
  11.6 137.5 %start.1 = (bf16[2,1024,2048]{2,1,0:T(8,128)(2,1)}, bf16[2,1024,256]{2,1,0:T(8,128)(2,1)}, bf16[2,1024,256]{2,1,0:T(8,128)(2,1)}, f32[2,4,1024]{2,1,0:T(4,128)},...) custom-call(f32[1,8,128]{2,1,0:T(8,128)} %pad_bitcast_fusion.tile_re, ...), custom_call_target="tpu_custom_call" | custom-call | flops 11811160064 | bytes 314572800 | tf_op jit(solution)/shard_map/start/pallas_call | solution.py:837
  149.1 0.9 copy.25
  150.1 0.6 slice_bitcast_fusion
  150.7 0.0 all-gather.2.cloned.1.call-done.w_ref
  150.7 114.3 %branch_sum.1 = (f32[256,2048]{1,0:T(8,128)}, bf16[256,2048]{1,0:T(8,128)(2,1)}, bf16[8,256,2048]{2,1,0:T(8,128)(2,1)}, bf16[4,512,2048]{2,1,0:T(8,128)(2,1)}, bf16[4,128,2048]{2,1,0:T(8,128)(2,1)}) custom-call(bf16[2,1024,256]{2,1,0:T(8,128)(2,1)} %get-tuple-element.56.a_ref.att_ref, bf16[256,2048]{1,0:T(8,128)(2,1)} %all-gather.2.cloned.1.call-done.w_ref, ...), custom_call_target="tpu_custom_call" | custom-call | flops 2147483648 | bytes 262144000 | tf_op jit(solution)/shard_map/branch_sum/pallas_call | solution.py:956
  265.0 144.8 %feed_forward.1 = (f32[256,2048]{1,0:T(8,128)}, bf16[256,2048]{1,0:T(8,128)(2,1)}, f32[8,2048]{1,0:T(8,128)}, bf16[2048,1024]{1,0:T(8,128)(2,1)}, bf16[2048,2048...) custom-call(bf16[256,2048]{1,0:T(8,128)(2,1)} %get-tuple-element.59.x_ref, bf16[2048,2048]{1,0:T(8,128)(2,1)} %bitcast.33, ...), custom_call_target="tpu_custom_call" | custom-call | flops 60129542144 | bytes 419430400 | tf_op jit(solution)/shard_map/feed_forward/pallas_call | solution.py:1331
  409.8 101.0 %branch_back.1 = (bf16[2,1024,256]{2,1,0:T(8,128)(2,1)}, bf16[256,2048]{1,0:T(8,128)(2,1)}, bf16[256,2048]{1,0:T(8,128)(2,1)}, bf16[2,256,2048]{2,1,0:T(8,128)(2...) custom-call(bf16[256,2048]{1,0:T(8,128)(2,1)} %get-tuple-element.65.x_ref, ...), custom_call_target="tpu_custom_call" | custom-call | flops 21474836480 | bytes 262144000 | tf_op jit(solution)/shard_map/branch_back/pallas_call | solution.py:1501
  510.9 160.0 %attention_back.1 = (f32[256,2048]{1,0:T(8,128)}, bf16[64,2048]{1,0:T(8,128)(2,1)}, bf16[64,2048]{1,0:T(8,128)(2,1)}, bf16[64,2048]{1,0:T(8,128)(2,1)}, f32[64,2...) custom-call(bf16[2,1024,256]{2,1,0:T(8,128)(2,1)} %get-tuple-element, ...), custom_call_target="tpu_custom_call" | custom-call | flops 26306674688 | bytes 419430400 | tf_op jit(solution)/shard_map/attention_back/pallas_call | solution.py:1892
  670.9 0.7 slice.17
  671.6 0.1 constant_dynamic-slice_fusion
  671.7 0.5 slice_bitcast_fusion.2
  672.2 8.4 %finish.1 = (bf16[256,2048]{1,0:T(8,128)(2,1)}, f32[256,2048]{1,0:T(8,128)}, f32[64,2048]{1,0:T(8,128)}, f32[64,2048]{1,0:T(8,128)}, f32[64,2048]{1,0:T(8,128)},...) custom-call(bf16[256,2048]{1,0:T(8,128)(2,1)} %get-tuple-element.68.refs_0_, ...), custom_call_target="tpu_custom_call" | custom-call | tf_op jit(solution)/shard_map/finish/pallas_call | solution.py:1996
  (7 shorter events, 0.0 us)
Async XLA Ops:
  7.2 143.5 %all-gather.2.cloned.1.call-start = ((), (), s32[]{:S(2)}) async-start(), calls=%async_computation | async-start | bytes 1310720 | tf_op jit(solution)/shard_map/all_gather | solution.py:2048
Sparse Core Ops, SparseCore 0:
  9.9 42.3 all-gather.1

commit v16 on v15

--- a/solution.py
+++ b/solution.py
@@ -1372,9 +1372,9 @@
 
 def branch_back_kernel(
     seqs, chips, batches, x_ref, w_ref, att_ref, middle_ref, hidden_hbm, wd_one, wd_two, units_hbm, gd_hbm,
-    d_ref, layer_ref, out_grad_ref, half_in, whole_in, down_hbm, down_in,
+    d_ref, layer_ref, out_grad_ref, half_in, whole_in, down_hbm, down_in, far_in,
     out_ref, buf, hidden_ref, wd_ref, grad_acc, rights, tiles, send, recv, load, right_sem, tile_sem,
-    part_send, part_recv, wd_load, down_send, down_recv, down_keep, acc, cross_out, line_out, cross_in, line_in, sum_send, sum_recv,
+    part_send, part_recv, wd_load, down_send, down_recv, far_send, far_recv, down_keep, acc, cross_out, line_out, cross_in, line_in, sum_send, sum_recv,
 ):
     line = Line(chips)
     rows = x_ref.shape[0]
@@ -1429,6 +1429,7 @@
     down = ToPeers(
         seqs, near, down_hbm, down_in.at[pl.ds(0, soon)], down_send, down_recv
     )
+    down_far = ToPeers(seqs, far_off, down_hbm, far_in, far_send, far_recv)
     down_kept = pltpu.make_async_copy(
         down_hbm.at[rows_at(lax.axis_index("seq"), down_in.shape[1])], down_in.at[soon], down_keep
     )
@@ -1461,6 +1462,7 @@
     stored(count - 2).wait()
     stored(count - 1).wait()
     down.begin()
+    down_far.begin()
     down_kept.start()
     spread.relay(1)
     spread.each(0, use)
@@ -1486,6 +1488,7 @@
     halves.end()
     wholes.end()
     down.end()
+    down_far.end()
     down_kept.wait()
 
 
@@ -1508,9 +1511,10 @@
             jax.ShapeDtypeStruct((seqs - 1 - near, run, unit_part.shape[1]), half),
             jax.ShapeDtypeStruct((units, width), half),
             jax.ShapeDtypeStruct((near + 1, units // seqs, width), half),
+            jax.ShapeDtypeStruct((seqs - 1 - near, units // seqs // 2, width), half),
         ],
         in_specs=[VMEM_SPEC] * 4 + [ANY_SPEC] * 5,
-        out_specs=[VMEM_SPEC, VMEM_SPEC, VMEM_SPEC, ANY_SPEC, ANY_SPEC, ANY_SPEC, ANY_SPEC],
+        out_specs=[VMEM_SPEC] * 3 + [ANY_SPEC] * 5,
         scratch_shapes=[
             pltpu.VMEM((rows, width), jnp.float32),
             pltpu.VMEM((group, rows, width), half),
@@ -1527,6 +1531,8 @@
             sems(2, seqs),
             sems(2, seqs),
             sems(2, seqs),
+            sems(seqs),
+            sems(seqs),
             sems(seqs),
             sems(seqs),
             pltpu.SemaphoreType.DMA,
@@ -1604,7 +1610,9 @@
     dm_loaded.start()
     meet(greet_group(group) + greet_seq(seqs))
     near, far_off = seq_peers(seqs)
-    down = ToPeers(seqs, far_off, down_hbm, down_in, down_send, down_recv)
+    down = ToPeers(
+        seqs, far_off, down_hbm, down_in, down_send, down_recv, down_in.shape[1]
+    )
     down.begin()
     swap = Swap(group, unit_sums, units, unit_send, unit_recv, unit_keep)
 
@@ -1900,7 +1908,9 @@
             jax.ShapeDtypeStruct((8, 128), wide),
             jax.ShapeDtypeStruct((share, cells // 2 * group), half),
             jax.ShapeDtypeStruct((share, cells // 2 * group), half),
-            jax.ShapeDtypeStruct((seqs - 1 - near_count(seqs), down.shape[0] // seqs, width), half),
+            jax.ShapeDtypeStruct(
+                (seqs - 1 - near_count(seqs), down.shape[0] // seqs // 2, width), half
+            ),
         ],
         in_specs=[VMEM_SPEC] * 5
         + [ANY_SPEC] * 4
@@ -2080,7 +2090,7 @@
         seqs, chips, batches, normed_b, w_units, (wd_one, wd_two), group_d, middle, cot_rows,
         gain_two[None], 4,
     )
-    d_attended, layer_out, out_part, unit_two, unit_far, down_part, down_near = branch_back(
+    d_attended, layer_out, out_part, unit_two, unit_far, down_part, down_near, far_one = branch_back(
         seqs, chips, batches, d_branch, wo_part, attended, middle, hidden, (wd_one, wd_two),
         unit_part, group_d, 5,
     )
@@ -2091,7 +2101,7 @@
         out_part = lax.psum(whole, "fsdp").reshape(seqs, group, share, width)
         out_part = lax.dynamic_slice_in_dim(out_part, member, 1, 1).reshape(seqs * share, width)
     (
-        input_grad, wq_grad, wk_grad, wv_grad, wo_grad, gain_tile, gate_grad, up_grad, down_far,
+        input_grad, wq_grad, wk_grad, wv_grad, wo_grad, gain_tile, gate_grad, up_grad, far_two,
     ) = attention_back(
         seqs, chips, block, query, kv_pad, low, lse, d_attended, unit_part, unit_one, unit_two,
         unit_far, w_heads, group_a, x_rows, d_middle, gain_one[None], mlp_gain_part, out_part,
@@ -2102,7 +2112,7 @@
     (layer_out, input_grad, wq_grad, wk_grad, wv_grad, wo_grad, gate_grad, up_grad, down_grad) = finish(
         share // 16,
         [layer_out, input_grad, wq_grad, wk_grad, wv_grad, wo_grad, gate_grad, up_grad],
-        [down_near, down_far],
+        [down_near, jnp.concatenate([far_one, far_two], axis=1)],
         [jnp.bfloat16] + [wide] * 8,
     )
     return (

time: 699 us -> 696 us (level)
    pallas_call x1, Pallas kernels: 160 us -> 145 us  [attention_back(): pl.pallas_call(functools.partial(attention_back_kernel, seqs, chips, bloc...]
    pallas_call x1, Pallas kernels: 101 us -> 111 us  [branch_back(): pl.pallas_call(functools.partial(branch_back_kernel, seqs, chips, batches...]
where the time goes in v16:
time: 696 us; the launch traced here: 685 us
  Pallas kernels  661 us (95%)
  between operations  14.6 us (2%)
    pallas_call x1, Pallas kernels, attention_back(): pl.pallas_call(functools.partial(attention_back_kernel, seqs, chips, bloc...  145 us
    pallas_call x1, Pallas kernels, feed_forward(): pl.pallas_call(functools.partial(feed_kernel, seqs, chips, batches), out_...  145 us
    pallas_call x1, Pallas kernels, start(): pl.pallas_call(functools.partial(start_kernel, seqs, chips, batches, bloc...  138 us
    pallas_call x1, Pallas kernels, branch_sum(): pl.pallas_call(functools.partial(branch_kernel, seqs, chips), out_shape=[...  114 us
    pallas_call x1, Pallas kernels, branch_back(): pl.pallas_call(functools.partial(branch_back_kernel, seqs, chips, batches...  111 us
  transfers between devices with their start and end apart: 1, of which 0 were waited for; matrix products, arithmetic and copies ran while one was open for 1% of the time, Pallas kernels for 20%

profile of v16, /device:TPU:9, one launch (start us, length us, event | category | flops | bytes accessed | tf_op | source)
XLA Modules:
  0.0 685.0 jit_solution(15877295348848573935)
XLA Ops:
  7.2 0.0 all-gather.2.cloned.1.call-start
  7.2 0.7 all-gather.2.cloned.1.call-update
  7.9 0.7 maximum_convert_fusion
  8.6 0.1 tile.10
  8.7 0.8 reduce_window_sum.11
  9.6 0.7 sub.46
  10.3 0.1 select_reduce_fusion
  10.4 0.6 maximum_subtract_fusion.low_ref
  11.0 0.6 pad_bitcast_fusion.tile_ref
  11.6 137.5 %start.1 = (bf16[2,1024,2048]{2,1,0:T(8,128)(2,1)}, bf16[2,1024,256]{2,1,0:T(8,128)(2,1)}, bf16[2,1024,256]{2,1,0:T(8,128)(2,1)}, f32[2,4,1024]{2,1,0:T(4,128)},...) custom-call(f32[1,8,128]{2,1,0:T(8,128)} %pad_bitcast_fusion.tile_re, ...), custom_call_target="tpu_custom_call" | custom-call | flops 11811160064 | bytes 314572800 | tf_op jit(solution)/shard_map/start/pallas_call | solution.py:837
  149.1 0.9 copy.25
  150.1 0.6 slice_bitcast_fusion
  150.7 0.0 all-gather.2.cloned.1.call-done.w_ref
  150.7 114.3 %branch_sum.1 = (f32[256,2048]{1,0:T(8,128)}, bf16[256,2048]{1,0:T(8,128)(2,1)}, bf16[8,256,2048]{2,1,0:T(8,128)(2,1)}, bf16[4,512,2048]{2,1,0:T(8,128)(2,1)}, bf16[4,128,2048]{2,1,0:T(8,128)(2,1)}) custom-call(bf16[2,1024,256]{2,1,0:T(8,128)(2,1)} %get-tuple-element.57.a_ref.att_ref, bf16[256,2048]{1,0:T(8,128)(2,1)} %all-gather.2.cloned.1.call-done.w_ref, ...), custom_call_target="tpu_custom_call" | custom-call | flops 2147483648 | bytes 262144000 | tf_op jit(solution)/shard_map/branch_sum/pallas_call | solution.py:956
  265.0 144.8 %feed_forward.1 = (f32[256,2048]{1,0:T(8,128)}, bf16[256,2048]{1,0:T(8,128)(2,1)}, f32[8,2048]{1,0:T(8,128)}, bf16[2048,1024]{1,0:T(8,128)(2,1)}, bf16[2048,2048...) custom-call(bf16[256,2048]{1,0:T(8,128)(2,1)} %get-tuple-element.60.x_ref, bf16[2048,2048]{1,0:T(8,128)(2,1)} %bitcast.33, ...), custom_call_target="tpu_custom_call" | custom-call | flops 60129542144 | bytes 419430400 | tf_op jit(solution)/shard_map/feed_forward/pallas_call | solution.py:1331
  409.8 110.9 %branch_back.1 = (bf16[2,1024,256]{2,1,0:T(8,128)(2,1)}, bf16[256,2048]{1,0:T(8,128)(2,1)}, bf16[256,2048]{1,0:T(8,128)(2,1)}, bf16[2,256,2048]{2,1,0:T(8,128)(2...) custom-call(bf16[256,2048]{1,0:T(8,128)(2,1)} %get-tuple-element.66., ...), custom_call_target="tpu_custom_call" | custom-call | flops 21474836480 | bytes 262144000 | tf_op jit(solution)/shard_map/branch_back/pallas_call | solution.py:1504
  520.7 0.0 copy-start
  520.7 145.2 %attention_back.1 = (f32[256,2048]{1,0:T(8,128)}, bf16[64,2048]{1,0:T(8,128)(2,1)}, bf16[64,2048]{1,0:T(8,128)(2,1)}, bf16[64,2048]{1,0:T(8,128)(2,1)}, f32[64,2...) custom-call(bf16[2,1024,256]{2,1,0:T(8,128)(2,1)} %get-tuple-element, ...), custom_call_target="tpu_custom_call" | custom-call | flops 26306674688 | bytes 419430400 | tf_op jit(solution)/shard_map/attention_back/pallas_call | solution.py:1900
  665.9 0.7 slice.17
  666.6 0.1 constant_dynamic-slice_fusion
  666.7 0.5 slice_bitcast_fusion.2
  667.2 0.0 copy-done
  667.2 2.1 pad_maximum_fusion.refs_9_
  669.3 8.4 %finish.1 = (bf16[256,2048]{1,0:T(8,128)(2,1)}, f32[256,2048]{1,0:T(8,128)}, f32[64,2048]{1,0:T(8,128)}, f32[64,2048]{1,0:T(8,128)}, f32[64,2048]{1,0:T(8,128)},...) custom-call(bf16[256,2048]{1,0:T(8,128)(2,1)} %get-tuple-element.69.refs_0_, ...), custom_call_target="tpu_custom_call" | custom-call | tf_op jit(solution)/shard_map/finish/pallas_call | solution.py:2006
  (7 shorter events, 0.0 us)
Async XLA Ops:
  7.2 143.5 %all-gather.2.cloned.1.call-start = ((), (), s32[]{:S(2)}) async-start(), calls=%async_computation | async-start | bytes 1310720 | tf_op jit(solution)/shard_map/all_gather | solution.py:2058
  520.7 146.5 %copy-start = (bf16[1,128,2048]{2,1,0:T(8,128)(2,1)S(1)}, bf16[1,128,2048]{2,1,0:T(8,128)(2,1)}, u32[]{:S(2)}) copy-start(bf16[1,128,2048]{2,1,0:T(8,128)(2,1)} %get-tuple-element.91) | copy-start | bytes 1572868
Sparse Core Ops, SparseCore 0:
  9.9 42.3 all-gather.1

commit v17 on v16

--- a/solution.py
+++ b/solution.py
@@ -1511,7 +1511,7 @@
             jax.ShapeDtypeStruct((seqs - 1 - near, run, unit_part.shape[1]), half),
             jax.ShapeDtypeStruct((units, width), half),
             jax.ShapeDtypeStruct((near + 1, units // seqs, width), half),
-            jax.ShapeDtypeStruct((seqs - 1 - near, units // seqs // 2, width), half),
+            jax.ShapeDtypeStruct((seqs - 1 - near, units // seqs // 4, width), half),
         ],
         in_specs=[VMEM_SPEC] * 4 + [ANY_SPEC] * 5,
         out_specs=[VMEM_SPEC] * 3 + [ANY_SPEC] * 5,
@@ -1611,7 +1611,7 @@
     meet(greet_group(group) + greet_seq(seqs))
     near, far_off = seq_peers(seqs)
     down = ToPeers(
-        seqs, far_off, down_hbm, down_in, down_send, down_recv, down_in.shape[1]
+        seqs, far_off, down_hbm, down_in, down_send, down_recv, down_in.shape[1] // 3
     )
     down.begin()
     swap = Swap(group, unit_sums, units, unit_send, unit_recv, unit_keep)
@@ -1909,7 +1909,7 @@
             jax.ShapeDtypeStruct((share, cells // 2 * group), half),
             jax.ShapeDtypeStruct((share, cells // 2 * group), half),
             jax.ShapeDtypeStruct(
-                (seqs - 1 - near_count(seqs), down.shape[0] // seqs // 2, width), half
+                (seqs - 1 - near_count(seqs), down.shape[0] // seqs // 4 * 3, width), half
             ),
         ],
         in_specs=[VMEM_SPEC] * 5

time: 696 us -> 697 us (level)
  no operation moved by 1% of the time
where the time goes in v17:
time: 697 us; the launch traced here: 685 us
  Pallas kernels  661 us (95%)
  between operations  14.6 us (2%)
    pallas_call x1, Pallas kernels, attention_back(): pl.pallas_call(functools.partial(attention_back_kernel, seqs, chips, bloc...  151 us
    pallas_call x1, Pallas kernels, feed_forward(): pl.pallas_call(functools.partial(feed_kernel, seqs, chips, batches), out_...  145 us
    pallas_call x1, Pallas kernels, start(): pl.pallas_call(functools.partial(start_kernel, seqs, chips, batches, bloc...  138 us
    pallas_call x1, Pallas kernels, branch_sum(): pl.pallas_call(functools.partial(branch_kernel, seqs, chips), out_shape=[...  114 us
    pallas_call x1, Pallas kernels, branch_back(): pl.pallas_call(functools.partial(branch_back_kernel, seqs, chips, batches...  105 us
  transfers between devices with their start and end apart: 1, of which 0 were waited for; matrix products, arithmetic and copies ran while one was open for 1% of the time, Pallas kernels for 20%

profile of v17, /device:TPU:9, one launch (start us, length us, event | category | flops | bytes accessed | tf_op | source)
XLA Modules:
  0.0 685.1 jit_solution(12731259089296917212)
XLA Ops:
  7.2 0.0 all-gather.2.cloned.1.call-start
  7.2 0.7 all-gather.2.cloned.1.call-update
  7.9 0.7 maximum_convert_fusion
  8.6 0.1 tile.10
  8.7 0.8 reduce_window_sum.11
  9.6 0.7 sub.46
  10.3 0.1 select_reduce_fusion
  10.4 0.6 maximum_subtract_fusion.low_ref
  11.0 0.6 pad_bitcast_fusion.tile_ref
  11.6 137.5 %start.1 = (bf16[2,1024,2048]{2,1,0:T(8,128)(2,1)}, bf16[2,1024,256]{2,1,0:T(8,128)(2,1)}, bf16[2,1024,256]{2,1,0:T(8,128)(2,1)}, f32[2,4,1024]{2,1,0:T(4,128)},...) custom-call(f32[1,8,128]{2,1,0:T(8,128)} %pad_bitcast_fusion.tile_re, ...), custom_call_target="tpu_custom_call" | custom-call | flops 11811160064 | bytes 314572800 | tf_op jit(solution)/shard_map/start/pallas_call | solution.py:837
  149.1 0.9 copy.25
  150.1 0.6 slice_bitcast_fusion
  150.7 0.0 all-gather.2.cloned.1.call-done.w_ref
  150.7 114.3 %branch_sum.1 = (f32[256,2048]{1,0:T(8,128)}, bf16[256,2048]{1,0:T(8,128)(2,1)}, bf16[8,256,2048]{2,1,0:T(8,128)(2,1)}, bf16[4,512,2048]{2,1,0:T(8,128)(2,1)}, bf16[4,128,2048]{2,1,0:T(8,128)(2,1)}) custom-call(bf16[2,1024,256]{2,1,0:T(8,128)(2,1)} %get-tuple-element.57.a_ref.att_ref, bf16[256,2048]{1,0:T(8,128)(2,1)} %all-gather.2.cloned.1.call-done.w_ref, ...), custom_call_target="tpu_custom_call" | custom-call | flops 2147483648 | bytes 262144000 | tf_op jit(solution)/shard_map/branch_sum/pallas_call | solution.py:956
  265.0 144.8 %feed_forward.1 = (f32[256,2048]{1,0:T(8,128)}, bf16[256,2048]{1,0:T(8,128)(2,1)}, f32[8,2048]{1,0:T(8,128)}, bf16[2048,1024]{1,0:T(8,128)(2,1)}, bf16[2048,2048...) custom-call(bf16[256,2048]{1,0:T(8,128)(2,1)} %get-tuple-element.60.x_ref, bf16[2048,2048]{1,0:T(8,128)(2,1)} %bitcast.33, ...), custom_call_target="tpu_custom_call" | custom-call | flops 60129542144 | bytes 419430400 | tf_op jit(solution)/shard_map/feed_forward/pallas_call | solution.py:1331
  409.8 105.3 %branch_back.1 = (bf16[2,1024,256]{2,1,0:T(8,128)(2,1)}, bf16[256,2048]{1,0:T(8,128)(2,1)}, bf16[256,2048]{1,0:T(8,128)(2,1)}, bf16[2,256,2048]{2,1,0:T(8,128)(2...) custom-call(bf16[256,2048]{1,0:T(8,128)(2,1)} %get-tuple-element.66., ...), custom_call_target="tpu_custom_call" | custom-call | flops 21474836480 | bytes 262144000 | tf_op jit(solution)/shard_map/branch_back/pallas_call | solution.py:1504
  515.1 0.0 copy-start
  515.1 150.7 %attention_back.1 = (f32[256,2048]{1,0:T(8,128)}, bf16[64,2048]{1,0:T(8,128)(2,1)}, bf16[64,2048]{1,0:T(8,128)(2,1)}, bf16[64,2048]{1,0:T(8,128)(2,1)}, f32[64,2...) custom-call(bf16[2,1024,256]{2,1,0:T(8,128)(2,1)} %get-tuple-element, ...), custom_call_target="tpu_custom_call" | custom-call | flops 26306674688 | bytes 419430400 | tf_op jit(solution)/shard_map/attention_back/pallas_call | solution.py:1900
  665.8 0.7 slice.17
  666.5 0.1 constant_dynamic-slice_fusion
  666.6 0.5 slice_bitcast_fusion.2
  667.1 0.0 copy-done
  667.1 2.2 pad_maximum_fusion.refs_9_
  669.3 8.4 %finish.1 = (bf16[256,2048]{1,0:T(8,128)(2,1)}, f32[256,2048]{1,0:T(8,128)}, f32[64,2048]{1,0:T(8,128)}, f32[64,2048]{1,0:T(8,128)}, f32[64,2048]{1,0:T(8,128)},...) custom-call(bf16[256,2048]{1,0:T(8,128)(2,1)} %get-tuple-element.69.refs_0_, ...), custom_call_target="tpu_custom_call" | custom-call | tf_op jit(solution)/shard_map/finish/pallas_call | solution.py:2006
  (7 shorter events, 0.0 us)
Async XLA Ops:
  7.2 143.5 %all-gather.2.cloned.1.call-start = ((), (), s32[]{:S(2)}) async-start(), calls=%async_computation | async-start | bytes 1310720 | tf_op jit(solution)/shard_map/all_gather | solution.py:2058
  515.1 152.0 %copy-start = (bf16[1,64,2048]{2,1,0:T(8,128)(2,1)S(1)}, bf16[1,64,2048]{2,1,0:T(8,128)(2,1)}, u32[]{:S(2)}) copy-start(bf16[1,64,2048]{2,1,0:T(8,128)(2,1)} %get-tuple-element.91) | copy-start | bytes 786436
Sparse Core Ops, SparseCore 0:
  9.9 42.3 all-gather.1
